TPU v7x, 32 devices: a whole 2x2x4 slice. The times are simulated.
32 devices in a mesh: dp: 8 (over z, x), shard: 4 (over y, core).
Axes of the slice: x: 2, y: 2, z: 4, core: 2. Of those that a mesh axis runs over, the one named last changes fastest.
Arguments:
- tokens: bfloat16 [2048, 2048], P(('dp', 'shard')), may hold values from -6 to 6
- router_probs: float32 [2048, 8], P(('dp', 'shard')), may hold values from 0.05 to 1
- expert_ids: int32 [2048, 8], P(('dp', 'shard')), may hold values from 0 to 15, all different within a row; in each aligned block of 64 rows (0 to 63, 64 to 127, ...) at most 64 rows name the same one
- old_place: int32 [16], replicated, may hold values from 0 to 15, as said below
- new_place: int32 [16], replicated, may hold values from 0 to 15, as said below
- w_gate: bfloat16 [16, 2048, 1024], P('dp', 'shard'), may hold values from -0.125 to 0.125
- w_up: bfloat16 [16, 2048, 1024], P('dp', 'shard'), may hold values from -0.125 to 0.125
- w_down: bfloat16 [16, 2048, 1024], P('dp', 'shard'), may hold values from -0.1875 to 0.1875
Outputs:
- moe_output: bfloat16 [2048, 2048], P(('dp', 'shard'))
- new_gate: bfloat16 [16, 2048, 1024], P('dp', 'shard')
- new_up: bfloat16 [16, 2048, 1024], P('dp', 'shard')
- new_down: bfloat16 [16, 2048, 1024], P('dp', 'shard')
Inputs may be any that keep to these rules, and one draw needn't show every extreme that they name: `expert_ids`: each token names 8 different experts; among the tokens of one device no expert is named by more than 64 tokens, a bound that some block reaches. `old_place`: a permutation of the 16 experts over the 16 slots. `new_place`: equal to old_place except at exactly one of the slots 2 k and 2 k + 1 for each k; the expert leaving the refilled slot of k moves to the refilled slot of (k + 1) mod (8), so that new_place is again a permutation.
All inputs are finite; a program needn't handle non-finite values.
Results may differ from a plain program's by a relative error of at most 0.0064.
Values may be sent and summed in bfloat16 or wider, within the bound.
No kernel may reach another device: no remote copies, remote signals or barrier semaphores. Data moves between devices by JAX's collectives and lax.ppermute only.
A program may use at most 128 MiB of HBM per device.

v0:
```python
import jax
import jax.numpy as jnp
from jax import lax
from jax.sharding import PartitionSpec as P


def partner_2(x, axis, apart):
    return lax.ppermute(x, axis, [(i, i ^ 1 << apart) for i in range(lax.axis_size(axis))])


def passed_along(x, axis, by):
    size = lax.axis_size(axis)
    return lax.ppermute(x, axis, [(i, (i + by) % size) for i in range(size)])


def lookup(lookup_keys, lookup_table, entry_count):
    matches = lookup_keys[..., None] == jnp.arange(entry_count, dtype=jnp.int32)
    return jnp.sum(jnp.where(matches, lookup_table, 0), axis=-1)


def widen(pieces, half_count):
    return jnp.repeat(pieces, half_count, axis=0)


def pair_halves(upper_half, own_rows, other_rows):
    return jnp.where(
        upper_half,
        jnp.stack([other_rows, own_rows], axis=1),
        jnp.stack([own_rows, other_rows], axis=1),
    )


def local(tokens, router_probs, expert_ids, old_place, new_place, w_gate, w_up, w_down):
    slot_count = old_place.shape[0]
    tok_count, top_count = expert_ids.shape
    model_width = tokens.shape[1]
    n_shard = lax.axis_size("shard")
    half_count = n_shard // 2
    partner_bit = n_shard.bit_length() - 2
    column = lax.axis_index("shard")
    row_id = lax.axis_index("dp")
    n_rows = lax.axis_size("dp")
    upper_half = column >= half_count
    capacity = max(2, 2 * tok_count * top_count // slot_count)
    places = slot_count * capacity
    full_gate, full_up, full_down = (
        lax.all_to_all(widen(w_gate, half_count), "shard", split_axis=0, concat_axis=1, tiled=True),
        lax.all_to_all(widen(w_up, half_count), "shard", split_axis=0, concat_axis=1, tiled=True),
        lax.all_to_all(widen(w_down, half_count), "shard", split_axis=0, concat_axis=1, tiled=True),
    )
    full_gate = full_gate[0]
    full_up = full_up[0]
    full_down = full_down[0]
    slot_index = jnp.arange(slot_count, dtype=jnp.int32)
    owner_slot = jnp.sum(
        jnp.where(old_place[None, :] == slot_index[:, None], slot_index[None, :], 0), axis=1
    )
    slot_ids = lookup(expert_ids, owner_slot, slot_count)
    gate_weights = (router_probs / jnp.sum(router_probs, axis=1, keepdims=True)).astype(
        jnp.bfloat16
    )
    flat_slots = slot_ids.reshape(-1)
    members = (flat_slots[:, None] == slot_index[None, :]).astype(jnp.int32)
    earlier = jnp.cumsum(members, axis=0) - members
    slot_rank = jnp.sum(earlier * members, axis=1)
    position = (flat_slots * capacity + slot_rank).reshape(tok_count, top_count)
    matches = position[:, :, None] == jnp.arange(places, dtype=jnp.int32)[None, None, :]
    chosen = jnp.any(matches, axis=1).astype(jnp.bfloat16)
    outgoing = lax.dot_general(
        chosen, tokens, (((0,), (0,)), ((), ())), preferred_element_type=jnp.float32
    ).astype(jnp.bfloat16)
    outgoing = outgoing.reshape(n_rows, 2, capacity, model_width)
    arrived = lax.all_to_all(outgoing, "dp", split_axis=0, concat_axis=0, tiled=True)
    own_rows = jnp.where(upper_half, arrived[:, 1], arrived[:, 0])
    other_rows = jnp.where(upper_half, arrived[:, 0], arrived[:, 1])
    partner = partner_2(other_rows, "shard", partner_bit)
    work_rows = jnp.stack([own_rows, partner], axis=0)
    flat_rows = work_rows.reshape(-1, model_width)
    gate_part = jnp.dot(flat_rows, full_gate, preferred_element_type=jnp.float32)
    up_part = jnp.dot(flat_rows, full_up, preferred_element_type=jnp.float32)
    hidden = (jax.nn.silu(gate_part) * up_part).astype(jnp.bfloat16)
    result = lax.dot_general(
        hidden, full_down, (((1,), (1,)), ((), ())), preferred_element_type=jnp.float32
    ).astype(jnp.bfloat16)
    result = result.reshape(2, n_rows, capacity, model_width)
    returned_other = partner_2(result[1], "shard", partner_bit)
    returned = lax.all_to_all(
        pair_halves(upper_half, result[0], returned_other),
        "dp",
        split_axis=0,
        concat_axis=0,
        tiled=True,
    )
    combine = jnp.sum(
        jnp.where(matches, gate_weights[:, :, None], jnp.zeros((), jnp.bfloat16)), axis=1
    )
    moe_output = jnp.dot(
        combine, returned.reshape(places, model_width), preferred_element_type=jnp.float32
    ).astype(jnp.bfloat16)
    base_slot = 2 * row_id
    second_old = lax.dynamic_index_in_dim(old_place, base_slot + 1, 0, keepdims=False)
    second_new = lax.dynamic_index_in_dim(new_place, base_slot + 1, 0, keepdims=False)
    second_moved = second_new != second_old
    leave_gate = jnp.where(second_moved, w_gate[1], w_gate[0])
    leave_up = jnp.where(second_moved, w_up[1], w_up[0])
    leave_down = jnp.where(second_moved, w_down[1], w_down[0])
    arrive_gate, arrive_up, arrive_down = passed_along((leave_gate, leave_up, leave_down), "dp", 1)
    new_gate = jnp.stack(
        [
            jnp.where(second_moved, w_gate[0], arrive_gate),
            jnp.where(second_moved, arrive_gate, w_gate[1]),
        ],
        axis=0,
    )
    new_up = jnp.stack(
        [jnp.where(second_moved, w_up[0], arrive_up), jnp.where(second_moved, arrive_up, w_up[1])],
        axis=0,
    )
    new_down = jnp.stack(
        [
            jnp.where(second_moved, w_down[0], arrive_down),
            jnp.where(second_moved, arrive_down, w_down[1]),
        ],
        axis=0,
    )
    return (moe_output, new_gate, new_up, new_down)


def solution(mesh):
    in_specs = (
        P(("dp", "shard"), None),
        P(("dp", "shard"), None),
        P(("dp", "shard"), None),
        P(),
        P(),
        P("dp", "shard", None),
        P("dp", "shard", None),
        P("dp", "shard", None),
    )
    out_specs = (
        P(("dp", "shard"), None),
        P("dp", "shard", None),
        P("dp", "shard", None),
        P("dp", "shard", None),
    )
    return jax.shard_map(local, mesh=mesh, in_specs=in_specs, out_specs=out_specs, check_vma=False)
```

profile of v0, /device:TPU:17, one launch (start us, length us, event | category | flops | bytes accessed | tf_op | source)
XLA Modules:
  0.0 540.4 jit_solution(950117085348618171)
XLA Ops:
  0.6 4.2 broadcast_in_dim.56
  4.9 5.6 %all-to-all-start.1 = ((bf16[4,512,1024]{2,1,0:T(8,128)(2,1)}), bf16[4,512,1024]{2,1,0:T(8,128)(2,1)}, u32[]{:S(2)}, u32[]{:S(2)}) async-start(bf16[4,512,1024]{2,1,0:T(8,128)(2,1)} %bitcast.103), calls=%async_computation.1 | async-start | bytes 8388608 | tf_op jit(solution)/shard_map/all_to_all | solution.py:47
  13.5 3.3 convolution_convert_fusion
  16.7 41.1 %all-to-all-done.1 = bf16[4,512,1024]{2,1,0:T(8,128)(2,1)} async-done(((bf16[4,512,1024]{2,1,0:T(8,128)(2,1)}), bf16[4,512,1024]{2,1,0:T(8,128)(2,1)}, u32[]{:S(2)}, u32[]{:S(2)}) %all-to-all-start.1) | async-done | bytes 4194336 | tf_op jit(solution)/shard_map/all_to_all | solution.py:47
  57.9 96.7 %all_to_all.37 = bf16[8,2,64,2048]{3,2,1,0:T(8,128)(2,1)} all-to-all(bf16[8,2,64,2048]{3,2,1,0:T(8,128)(2,1)} %bitcast.106), channel_id=1, replica_groups=mesh['dp'=8,'shard'=4] {'dp'}, dimensions={0} | all-to-all | bytes 8388608 | tf_op jit(solution)/shard_map/all_to_all | solution.py:73
  154.6 2.5 broadcast_in_dim.57
  157.1 6.5 %all-to-all-start.2 = ((bf16[4,512,1024]{2,1,0:T(8,128)(2,1)}), bf16[4,512,1024]{2,1,0:T(8,128)(2,1)}, u32[]{:S(2)}, u32[]{:S(2)}) async-start(bf16[4,512,1024]{2,1,0:T(8,128)(2,1)} %bitcast.104), calls=%async_computation.2 | async-start | bytes 8388608 | tf_op jit(solution)/shard_map/all_to_all | solution.py:48
  163.6 3.9 fusion
  168.9 42.1 %all-to-all-done.2 = bf16[4,512,1024]{2,1,0:T(8,128)(2,1)} async-done(((bf16[4,512,1024]{2,1,0:T(8,128)(2,1)}), bf16[4,512,1024]{2,1,0:T(8,128)(2,1)}, u32[]{:S(2)}, u32[]{:S(2)}) %all-to-all-start.2) | async-done | bytes 4194336 | tf_op jit(solution)/shard_map/all_to_all | solution.py:48
  211.0 2.5 broadcast_in_dim.58
  213.5 6.2 %all-to-all-start.3 = ((bf16[4,512,1024]{2,1,0:T(8,128)(2,1)}), bf16[4,512,1024]{2,1,0:T(8,128)(2,1)}, u32[]{:S(2)}, u32[]{:S(2)}) async-start(bf16[4,512,1024]{2,1,0:T(8,128)(2,1)} %bitcast.105), calls=%async_computation.3 | async-start | bytes 8388608 | tf_op jit(solution)/shard_map/all_to_all | solution.py:49
  219.7 2.4 fusion.1
  222.2 33.7 %collective-permute-done = bf16[8,64,2048]{2,1,0:T(8,128)(2,1)} collective-permute-done((bf16[8,64,2048]{2,1,0:T(8,128)(2,1)}, bf16[8,64,2048]{2,1,0:T(8,128)(2,1)}, u32[]{:S(2)}, u32[]{:S(2)}) %collective-permute-start) | collective-permute-done | bytes 2097184 | tf_op jit(solution)/shard_map/ppermute | solution.py:8
  255.9 2.0 pad_maximum_fusion
  257.9 2.0 copy-done.9
  259.9 8.2 %fusion.17 = f32[1024,1024]{1,0:T(8,128)} fusion(bf16[1024,2048]{1,0:T(8,128)(2,1)S(1)} %bitcast.108, bf16[2048,1024]{1,0:T(8,128)(2,1)} %bitcast.10), kind=kOutput, calls=%fused_computation.49 | convolution fusion | flops 4294967296 | bytes 12582912 | tf_op jit(solution)/shard_map/dot_general | solution.py:79
  268.1 32.8 %all-to-all-done.3 = bf16[4,512,1024]{2,1,0:T(8,128)(2,1)} async-done(((bf16[4,512,1024]{2,1,0:T(8,128)(2,1)}), bf16[4,512,1024]{2,1,0:T(8,128)(2,1)}, u32[]{:S(2)}, u32[]{:S(2)}) %all-to-all-start.3) | async-done | bytes 4194336 | tf_op jit(solution)/shard_map/all_to_all | solution.py:49
  300.9 15.1 %convolution_convert_fusion.1 = bf16[1024,2048]{1,0:T(8,128)(2,1)} fusion(bf16[2048,1024]{1,0:T(8,128)(2,1)} %bitcast.14, f32[1024,1024]{1,0:T(8,128)} %fusion.17, bf16[1024,2048]{1,0:T(8,128)(2,1)} %bitcast.109, bf16[2048,1024]{1,0:T(8,128)(2,1)} %bitcast.12), kind=kOutput, calls=%fused_computation.5 | convolution fusion | flops 8598323200 | bytes 20971520 | tf_op jit(solution)/shard_map/dot_general | solution.py:82
  316.0 2.7 fusion.16
  319.1 45.9 %collective-permute-done.1 = bf16[8,64,2048]{2,1,0:T(8,128)(2,1)S(1)} collective-permute-done((bf16[8,64,2048]{2,1,0:T(8,128)(2,1)S(1)}, bf16[8,64,2048]{2,1,0:T(8,128)(2,1)S(1)}, u32[]{:S(2)}, u32[]{:S(2)}) %collective-permute-start.1) | collective-permute-done | bytes 2097184 | tf_op jit(solution)/shard_map/ppermute | solution.py:8
  365.1 2.3 maximum_select_fusion
  367.3 6.4 %all-to-all-start.4 = ((bf16[8,2,64,2048]{3,2,1,0:T(8,128)(2,1)}), bf16[8,2,64,2048]{3,2,1,0:T(8,128)(2,1)}, u32[]{:S(2)}, u32[]{:S(2)}) async-start(bf16[8,2,64,2048]{3,2,1,0:T(8,128)(2,1)} %maximum_select_fusion), calls=%async_computation.4 | async-start | bytes 8388608 | tf_op jit(solution)/shard_map/all_to_all | solution.py:87
  381.0 1.4 collective-permute-start.4
  383.3 105.5 %collective-permute-done.2 = bf16[512,1024]{1,0:T(8,128)(2,1)} collective-permute-done((bf16[512,1024]{1,0:T(8,128)(2,1)}, bf16[512,1024]{1,0:T(8,128)(2,1)}, u32[]{:S(2)}, u32[]{:S(2)}) %collective-permute-start.2) | collective-permute-done | bytes 1048608 | tf_op jit(solution)/shard_map/ppermute | solution.py:13
  490.2 1.5 pad_maximum_fusion.1
  491.7 19.6 %collective-permute-done.3 = bf16[512,1024]{1,0:T(8,128)(2,1)} collective-permute-done((bf16[512,1024]{1,0:T(8,128)(2,1)}, bf16[512,1024]{1,0:T(8,128)(2,1)}, u32[]{:S(2)}, u32[]{:S(2)}) %collective-permute-start.3) | collective-permute-done | bytes 1048608 | tf_op jit(solution)/shard_map/ppermute | solution.py:13
  511.2 1.4 fusion.8
  512.6 1.5 pad_maximum_fusion.2
  514.1 19.6 %collective-permute-done.4 = bf16[512,1024]{1,0:T(8,128)(2,1)} collective-permute-done((bf16[512,1024]{1,0:T(8,128)(2,1)S(1)}, bf16[512,1024]{1,0:T(8,128)(2,1)}, u32[]{:S(2)}, u32[]{:S(2)}) %collective-permute-start.4) | collective-permute-done | bytes 1048608 | tf_op jit(solution)/shard_map/ppermute | solution.py:13
  533.7 1.4 fusion.6
  535.1 1.5 pad_maximum_fusion.3
  536.6 3.7 convolution_convert_fusion.2
  (62 shorter events, 12.9 us)
Async XLA Ops:
  0.6 12.8 %copy-start = (bf16[64,2048]{1,0:T(8,128)(2,1)S(1)}, bf16[64,2048]{1,0:T(8,128)(2,1)}, u32[]{:S(2)}) copy-start(bf16[64,2048]{1,0:T(8,128)(2,1)} %param.8) | copy-start | bytes 786436
  4.9 5.6 %copy-start.14 = (s32[16]{0:T(128)S(1)}, s32[16]{0:T(128)}, u32[]{:S(2)}) copy-start(s32[16]{0:T(128)} %param.11) | copy-start | bytes 196
  4.9 5.7 %copy-start.13 = (s32[64,8]{0,1:T(8,128)S(1)}, s32[64,8]{0,1:T(8,128)}, u32[]{:S(2)}) copy-start(s32[64,8]{0,1:T(8,128)} %param.10) | copy-start | bytes 6148
  4.9 53.0 %all-to-all-start.1 = ((bf16[4,512,1024]{2,1,0:T(8,128)(2,1)}), bf16[4,512,1024]{2,1,0:T(8,128)(2,1)}, u32[]{:S(2)}, u32[]{:S(2)}) async-start(bf16[4,512,1024]{2,1,0:T(8,128)(2,1)} %bitcast.103), calls=%async_computation.1 | async-start | bytes 8388608 | tf_op jit(solution)/shard_map/all_to_all | solution.py:47
  12.7 141.9 %copy-start.10 = (s32[64,8]{1,0:T(8,128)}, s32[64,8]{1,0:T(8,128)S(1)}, u32[]{:S(2)}) copy-start(s32[64,8]{1,0:T(8,128)S(1)} %copy.31) | copy-start | bytes 6148
  57.9 96.7 %copy-start.3 = (bf16[2,512,1024]{2,1,0:T(8,128)(2,1)S(1)}, bf16[2,512,1024]{2,1,0:T(8,128)(2,1)}, u32[]{:S(2)}) copy-start(bf16[2,512,1024]{2,1,0:T(8,128)(2,1)} %param.14) | copy-start | bytes 6291460
  157.1 53.9 %all-to-all-start.2 = ((bf16[4,512,1024]{2,1,0:T(8,128)(2,1)}), bf16[4,512,1024]{2,1,0:T(8,128)(2,1)}, u32[]{:S(2)}, u32[]{:S(2)}) async-start(bf16[4,512,1024]{2,1,0:T(8,128)(2,1)} %bitcast.104), calls=%async_computation.2 | async-start | bytes 8388608 | tf_op jit(solution)/shard_map/all_to_all | solution.py:48
  163.6 47.4 %copy-start.6 = (bf16[2,512,1024]{2,1,0:T(8,128)(2,1)S(1)}, bf16[2,512,1024]{2,1,0:T(8,128)(2,1)}, u32[]{:S(2)}) copy-start(bf16[2,512,1024]{2,1,0:T(8,128)(2,1)} %param.15) | copy-start | bytes 6291460
  167.5 88.4 %collective-permute-start = (bf16[8,64,2048]{2,1,0:T(8,128)(2,1)}, bf16[8,64,2048]{2,1,0:T(8,128)(2,1)}, u32[]{:S(2)}, u32[]{:S(2)}) collective-permute-start(bf16[8,64,2048]{2,1,0:T(8,128)(2,1)} %fusion), channel_id=1, source_target_pairs={{0,2},{1,3},{2,0},{3,1},{4,6},{5,7},{6,4},{7,5},{8,10},{9,11},{10,... | collective-permute-start | bytes 6291464 | tf_op jit(solution)/shard_map/ppermute | solution.py:8
  213.5 87.3 %all-to-all-start.3 = ((bf16[4,512,1024]{2,1,0:T(8,128)(2,1)}), bf16[4,512,1024]{2,1,0:T(8,128)(2,1)}, u32[]{:S(2)}, u32[]{:S(2)}) async-start(bf16[4,512,1024]{2,1,0:T(8,128)(2,1)} %bitcast.105), calls=%async_computation.3 | async-start | bytes 8388608 | tf_op jit(solution)/shard_map/all_to_all | solution.py:49
  257.9 2.0 copy-start.9
  318.7 46.3 %collective-permute-start.1 = (bf16[8,64,2048]{2,1,0:T(8,128)(2,1)S(1)}, bf16[8,64,2048]{2,1,0:T(8,128)(2,1)S(1)}, u32[]{:S(2)}, u32[]{:S(2)}) collective-permute-start(bf16[8,64,2048]{2,1,0:T(8,128)(2,1)S(1)} %bitcast.111), channel_id=1, source_target_pairs={{0,2},{1,3},{2,0},{3,1},{4,6},{5,7},{6,4},{7,5},{8,10},{9,11},{10,... | collective-permute-start | bytes 6291464 | tf_op jit(solution)/shard_map/ppermute | solution.py:8
  367.3 7.0 %copy-start.15 = (s32[16]{0:T(128)S(1)}, s32[16]{0:T(128)}, u32[]{:S(2)}) copy-start(s32[16]{0:T(128)} %param.12) | copy-start | bytes 196
  367.3 8.9 %copy-start.2 = (bf16[2,512,1024]{2,1,0:T(8,128)(2,1)S(1)}, bf16[2,512,1024]{2,1,0:T(8,128)(2,1)}, u32[]{:S(2)}) copy-start(bf16[2,512,1024]{2,1,0:T(8,128)(2,1)} %param.13) | copy-start | bytes 6291460
  367.3 169.3 %all-to-all-start.4 = ((bf16[8,2,64,2048]{3,2,1,0:T(8,128)(2,1)}), bf16[8,2,64,2048]{3,2,1,0:T(8,128)(2,1)}, u32[]{:S(2)}, u32[]{:S(2)}) async-start(bf16[8,2,64,2048]{3,2,1,0:T(8,128)(2,1)} %maximum_select_fusion), calls=%async_computation.4 | async-start | bytes 8388608 | tf_op jit(solution)/shard_map/all_to_all | solution.py:87
  373.7 4.9 copy-start.4
  373.7 7.1 %copy-start.7 = (bf16[2,512,1024]{2,1,0:T(8,128)(2,1)S(1)}, bf16[2,512,1024]{2,1,0:T(8,128)(2,1)}, u32[]{:S(2)}) copy-start(bf16[2,512,1024]{2,1,0:T(8,128)(2,1)} %param.15) | copy-start | bytes 6291460
  376.3 6.1 %copy-start.12 = (f32[64,8]{0,1:T(8,128)S(1)}, f32[64,8]{0,1:T(8,128)}, u32[]{:S(2)}) copy-start(f32[64,8]{0,1:T(8,128)} %param.9) | copy-start | bytes 6148
  376.3 6.2 %copy-start.11 = (s32[64,8]{1,0:T(8,128)S(1)}, s32[64,8]{1,0:T(8,128)}, u32[]{:S(2)}) copy-start(s32[64,8]{1,0:T(8,128)} %copy-done.10) | copy-start | bytes 6148
  377.4 111.4 %collective-permute-start.2 = (bf16[512,1024]{1,0:T(8,128)(2,1)}, bf16[512,1024]{1,0:T(8,128)(2,1)}, u32[]{:S(2)}, u32[]{:S(2)}) collective-permute-start(bf16[512,1024]{1,0:T(8,128)(2,1)} %bitcast_select_fusion.9), channel_id=1, source_target_pairs={{0,4},{4,8},{8,12},{12,16},{16,20},{20,24},{24,28},{28,0},{1,5},{5... | collective-permute-start | bytes 3145736 | tf_op jit(solution)/shard_map/ppermute | solution.py:13
  379.7 131.6 %collective-permute-start.3 = (bf16[512,1024]{1,0:T(8,128)(2,1)}, bf16[512,1024]{1,0:T(8,128)(2,1)}, u32[]{:S(2)}, u32[]{:S(2)}) collective-permute-start(bf16[512,1024]{1,0:T(8,128)(2,1)} %bitcast_select_fusion.6), channel_id=1, source_target_pairs={{0,4},{4,8},{8,12},{12,16},{16,20},{20,24},{24,28},{28,0},{1,5},{5... | collective-permute-start | bytes 3145736 | tf_op jit(solution)/shard_map/ppermute | solution.py:13
  381.0 152.7 %collective-permute-start.4 = (bf16[512,1024]{1,0:T(8,128)(2,1)S(1)}, bf16[512,1024]{1,0:T(8,128)(2,1)}, u32[]{:S(2)}, u32[]{:S(2)}) collective-permute-start(bf16[512,1024]{1,0:T(8,128)(2,1)S(1)} %bitcast_select_fusion.3), channel_id=1, source_target_pairs={{0,4},{4,8},{8,12},{12,16},{16,20},{20,24},{24,28},{28,0},{1,5},{5... | collective-permute-start | bytes 3145736 | tf_op jit(solution)/shard_map/ppermute | solution.py:13
  383.3 128.0 %copy-start.5 = (bf16[2,512,1024]{2,1,0:T(8,128)(2,1)S(1)}, bf16[2,512,1024]{2,1,0:T(8,128)(2,1)}, u32[]{:S(2)}) copy-start(bf16[2,512,1024]{2,1,0:T(8,128)(2,1)} %param.14) | copy-start | bytes 6291460
  491.7 42.0 %copy-start.8 = (bf16[2,512,1024]{2,1,0:T(8,128)(2,1)S(1)}, bf16[2,512,1024]{2,1,0:T(8,128)(2,1)}, u32[]{:S(2)}) copy-start(bf16[2,512,1024]{2,1,0:T(8,128)(2,1)} %param.15) | copy-start | bytes 6291460
  535.1 5.3 copy-start.1
where the time goes:
time: 541 us; the launch traced here: 540 us
  waiting for transfers between devices  340 us (63%)
  blocking collectives  96.7 us (18%)
  matrix products  30.4 us (6%)
  starting transfers between devices  30.3 us (6%)
  other arithmetic  24.5 us (5%)
  local copies, waits for them, and re-layouts  16 us (3%)
    ppermute x3, waiting for transfers between devices, passed_along(): return lax.ppermute(x, axis, [(i, (i + by) % size) for i in range(size)])  145 us
    all_to_all x1, blocking collectives, local(): lax.all_to_all(outgoing, 'dp', split_axis=0, concat_axis=0, tiled=True)  96.7 us
    ppermute x2, waiting for transfers between devices, partner_2(): lax.ppermute(x, axis, [(i, i ^ 1 << apart) for i in range(lax.axis_size(a...  79.7 us
    all_to_all x1, waiting for transfers between devices, local(): lax.all_to_all(widen(w_up, half_count), 'shard', split_axis=0, concat_axi...  42.1 us
    all_to_all x1, waiting for transfers between devices, local(): lax.all_to_all(widen(w_gate, half_count), 'shard', split_axis=0, concat_a...  41.1 us
    all_to_all x1, waiting for transfers between devices, local(): lax.all_to_all(widen(w_down, half_count), 'shard', split_axis=0, concat_a...  32.8 us
    dot_general x1, matrix products, local(): lax.dot_general(hidden, full_down, (((1,), (1,)), ((), ())), preferred_el...  15.1 us
  transfers between devices with their start and end apart: 9, of which 8 were waited for; matrix products, arithmetic and copies ran while one was open for 7% of the time, Pallas kernels for 0%

commit v1 on v0

v1 whole, which is shorter than its diff:
```python
import jax
import jax.numpy as jnp
from jax import lax
from jax.sharding import PartitionSpec as P


def swap(x, axis, bit):
    return lax.ppermute(x, axis, [(i, i ^ bit) for i in range(lax.axis_size(axis))])


def passed_along(x, axis, by):
    size = lax.axis_size(axis)
    return lax.ppermute(x, axis, [(i, (i + by) % size) for i in range(size)])


def in_order(second, own, other, axis=0):
    return jnp.where(
        second, jnp.stack([other, own], axis=axis), jnp.stack([own, other], axis=axis)
    )


def pick(w, index):
    return lax.dynamic_index_in_dim(w, index, 0, keepdims=False)


def local(tokens, router_probs, expert_ids, old_place, new_place, w_gate, w_up, w_down):
    slots = old_place.shape[0]
    tok, top = expert_ids.shape
    width = tokens.shape[1]
    ff = w_gate.shape[2]
    n_shard = lax.axis_size("shard")
    n_rows = lax.axis_size("dp")
    half = n_shard // 2
    column = lax.axis_index("shard")
    row_id = lax.axis_index("dp")
    side = column // half

    gate_weights = (router_probs / jnp.sum(router_probs, axis=1, keepdims=True)).astype(
        jnp.bfloat16
    )
    named = expert_ids[:, :, None] == old_place[None, None, :]
    coef = jnp.sum(jnp.where(named, gate_weights[:, :, None], jnp.zeros((), jnp.bfloat16)), axis=1)
    coef = jnp.pad(coef, ((0, 0), (0, 128 - slots)))
    own = jnp.concatenate([tokens, coef], axis=1)
    other = swap(own, "shard", half)
    both = in_order(side == 1, own, other).reshape(2 * tok, width + 128)
    every = lax.all_gather(both, "dp", axis=0, tiled=True)

    def slot_rows(w):
        mine, theirs = pick(w, side), pick(w, 1 - side)
        arrived = swap(theirs, "shard", half)
        rows = in_order(side == 1, mine, arrived)[:, None]
        bit = 1
        while bit < half:
            more = swap(rows, "shard", bit)
            rows = in_order((column & bit) != 0, rows, more, axis=1).reshape(
                (2, -1) + w.shape[1:]
            )
            bit *= 2
        return rows.reshape(-1, w.shape[2])

    full_gate = slot_rows(w_gate)
    full_up = slot_rows(w_up)
    down = w_down[:, None]
    bit = 1
    while bit < half:
        more = swap(down, "shard", bit)
        down = in_order((column & bit) != 0, down, more, axis=1).reshape(
            (2, -1) + w_down.shape[1:]
        )
        bit *= 2
    down = down.reshape(2, -1, ff)

    rows = every[:, :width]
    mine_coef = lax.dynamic_slice_in_dim(every, width + 2 * row_id + side, 1, 1)
    gate_part = jnp.dot(rows, full_gate, preferred_element_type=jnp.float32)
    up_part = jnp.dot(rows, full_up, preferred_element_type=jnp.float32)
    hidden = (jax.nn.silu(gate_part) * up_part * mine_coef.astype(jnp.float32)).astype(jnp.bfloat16)
    hidden_other = swap(hidden, "shard", half)
    contract = (((1,), (1,)), ((), ()))
    part = lax.dot_general(
        hidden, pick(down, side), contract, preferred_element_type=jnp.float32
    ) + lax.dot_general(
        hidden_other, pick(down, 1 - side), contract, preferred_element_type=jnp.float32
    )
    part = part.astype(jnp.bfloat16)
    total = lax.psum_scatter(part, "dp", scatter_dimension=0, tiled=True)
    total = total.reshape(2, tok, width // 2)
    kept = pick(total, side)
    arrived = swap(pick(total, 1 - side), "shard", half)
    moe_output = in_order(side == 1, kept, arrived, axis=1).reshape(tok, width)

    base_slot = 2 * row_id
    second_old = pick(old_place, base_slot + 1)
    second_new = pick(new_place, base_slot + 1)
    moved = (second_new != second_old).astype(jnp.int32)

    def refilled(w):
        arrive = passed_along(pick(w, moved), "dp", 1)
        return lax.dynamic_update_index_in_dim(w, arrive, moved, 0)

    return (moe_output, refilled(w_gate), refilled(w_up), refilled(w_down))


def solution(mesh):
    in_specs = (
        P(("dp", "shard"), None),
        P(("dp", "shard"), None),
        P(("dp", "shard"), None),
        P(),
        P(),
        P("dp", "shard", None),
        P("dp", "shard", None),
        P("dp", "shard", None),
    )
    out_specs = (
        P(("dp", "shard"), None),
        P("dp", "shard", None),
        P("dp", "shard", None),
        P("dp", "shard", None),
    )
    return jax.shard_map(local, mesh=mesh, in_specs=in_specs, out_specs=out_specs, check_vma=False)
```

time: 541 us -> 311 us (0.57)
  the two profiles are of different devices: /device:TPU:17 before, /device:TPU:0 now
where the time goes in v1:
time: 311 us
  waiting for transfers between devices  223 us (72%)
  local copies, waits for them, and re-layouts  23.7 us (8%)
  matrix products  19.3 us (6%)
  other arithmetic  16.4 us (5%)
  between operations  15.5 us (5%)
  starting transfers between devices  13.4 us (4%)
    reduce_scatter x1, waiting for transfers between devices, local(): total = lax.psum_scatter(part, 'dp', scatter_dimension=0, tiled=True)  82.9 us
    ppermute x3, waiting for transfers between devices, passed_along(): return lax.ppermute(x, axis, [(i, (i + by) % size) for i in range(size)])  70.1 us
    ppermute x8, waiting for transfers between devices, swap(): lax.ppermute(x, axis, [(i, i ^ bit) for i in range(lax.axis_size(axis))])  69.5 us
    select_n x8, other arithmetic, in_order(): jnp.where(second, jnp.stack([other, own], axis=axis), jnp.stack([own, oth...  16.2 us
    ppermute x8, starting transfers between devices, swap(): lax.ppermute(x, axis, [(i, i ^ bit) for i in range(lax.axis_size(axis))])  9.98 us
    dot_general x1, matrix products, local(): gate_part = jnp.dot(rows, full_gate, preferred_element_type=jnp.float32)  7.69 us
    dynamic_update_slice x3, local copies, waits for them, and re-layouts, refilled(): return lax.dynamic_update_index_in_dim(w, arrive, moved, 0)  6.66 us
    unnamed x36, local copies, waits for them, and re-layouts  6.61 us
  transfers between devices with their start and end apart: 13, of which 7 were waited for; matrix products, arithmetic and copies ran while one was open for 14% of the time, Pallas kernels for 0%

profile of v1, /device:TPU:0, one launch (start us, length us, event | category | flops | bytes accessed | tf_op | source)
XLA Modules:
  0.0 310.9 jit_solution(9561335166343292731)
XLA Ops:
  7.2 3.2 %copy.45 = bf16[2,512,1024]{2,1,0:T(8,128)(2,1)} copy(bf16[2,512,1024]{2,1,0:T(8,128)(2,1)} %param.14) | data formatting | bytes 4194304
  10.4 1.3 copy.44
  13.8 3.0 collective-permute-start
  16.9 6.7 %collective-permute-done = bf16[64,2176]{1,0:T(8,128)(2,1)S(1)} collective-permute-done((bf16[64,2176]{1,0:T(8,128)(2,1)S(1)}, bf16[64,2176]{1,0:T(8,128)(2,1)S(1)}, u32[]{:S(2)}, u32[]{:S(2)}) %collective-permute-start) | collective-permute-done | bytes 278560 | tf_op jit(solution)/shard_map/ppermute | solution.py:8
  23.6 1.1 copy.30
  27.3 1.4 dynamic-slice_bitcast_fusion.1
  28.7 1.8 collective-permute-start.9
  31.5 1.5 collective-permute-start.8
  33.1 40.4 %collective-permute-done.9 = bf16[512,1024]{1,0:T(8,128)(2,1)} collective-permute-done((bf16[512,1024]{1,0:T(8,128)(2,1)S(1)}, bf16[512,1024]{1,0:T(8,128)(2,1)}, u32[]{:S(2)}, u32[]{:S(2)}) %collective-permute-start.9) | collective-permute-done | bytes 1048608 | tf_op jit(solution)/shard_map/ppermute | solution.py:13
  73.4 3.8 %bitcast_dynamic-update-slice_fusion.1 = (bf16[2,512,1024]{2,1,0:T(8,128)(2,1)}, bf16[1,1,1,512,1024]{4,3,0,2,1:T(8,128)(2,1)}, bf16[1,1,512,1024]{3,2,1,0:T(8,128)(2,1)S(1)}, bf16[512,1024]{1,0:T(8,128)(2,1)S(1)}) fusion(bf16[2,512,1024]{2,1,0:T(8,128)(2,1)} %copy.45, s32[]{:T(128)S(6)} %select_n.172, bf16[512,1024]{1,0:T(8,128)(2,1)} %collective-permute-done.9, ...), kind=kLoop, calls=%fused_computation.20 | loop fusion | bytes 7340044 | tf_op jit(solution)/shard_map/jit(dynamic_update_index_in_dim)/dynamic_update_slice | solution.py:100
  77.2 1.9 collective-permute-start.3
  79.1 29.7 %collective-permute-done.8 = bf16[512,1024]{1,0:T(8,128)(2,1)} collective-permute-done((bf16[512,1024]{1,0:T(8,128)(2,1)}, bf16[512,1024]{1,0:T(8,128)(2,1)}, u32[]{:S(2)}, u32[]{:S(2)}) %collective-permute-start.8) | collective-permute-done | bytes 1048608 | tf_op jit(solution)/shard_map/ppermute | solution.py:13
  108.9 2.8 bitcast_dynamic-update-slice_fusion.2
  111.7 1.7 collective-permute-start.1
  113.4 1.7 maximum_select_fusion.4
  115.1 16.4 %collective-permute-done.1 = bf16[512,1024]{1,0:T(8,128)(2,1)S(1)} collective-permute-done((bf16[512,1024]{1,0:T(8,128)(2,1)S(1)}, bf16[512,1024]{1,0:T(8,128)(2,1)S(1)}, u32[]{:S(2)}, u32[]{:S(2)}) %collective-permute-start.1) | collective-permute-done | bytes 1048608 | tf_op jit(solution)/shard_map/ppermute | solution.py:8
  131.5 1.7 maximum_select_fusion.3
  133.7 2.0 maximum_select_fusion.5
  136.2 3.0 maximum_select_fusion.1
  139.2 2.5 copy.33
  141.7 4.5 %maximum_select_fusion = bf16[2,2,1,512,1024]{4,3,1,0,2:T(8,128)(2,1)} fusion(bf16[2,1,1,512,1024]{4,3,1,0,2:T(8,128)(2,1)S(1)} %bitcast_select_fusion, bf16[2,1,1,512,1024]{4,3,1,0,2:T(8,128)(2,1)} %bitcast.6, pred[]{:T(512)S(6)} %ne.19), kind=kLoop, calls=%fused_computation | loop fusion | flops 6291456 | bytes 8388609 | tf_op jit(solution)/shard_map/jit(_where)/select_n | solution.py:17
  146.3 7.7 %fusion.2 = f32[1024,1024]{1,0:T(8,128)S(1)} fusion(bf16[2048,1024]{1,0:T(8,128)(2,1)} %bitcast.74, bf16[1024,2176]{0,1:T(8,128)(2,1)} %all-gather.2.cloned.1.call-done), kind=kOutput, calls=%fused_computation.8 | convolution fusion | flops 4294967296 | bytes 12582912 | tf_op jit(solution)/shard_map/dot_general | solution.py:76
  154.0 5.4 %multiply_convert_fusion = bf16[1024,1024]{1,0:T(8,128)(2,1)S(1)} fusion(f32[1024,1024]{1,0:T(8,128)S(1)} %fusion.2, bf16[2048,1024]{1,0:T(8,128)(2,1)S(1)} %bitcast.71, bf16[1024,2176]{0,1:T(8,128)(2,1)S(1)} %copy-done.14, f32[1024]{0:T(1024)S(1)} %bitcast.80), kind=kOutput, calls=%fused_computation.4 | convolution fusion | flops 4302307328 | bytes 14684160 | tf_op jit(solution)/shard_map/dot_general | solution.py:77
  159.5 1.2 collective-permute-start.6
  160.7 2.9 maximum_select_fusion.2
  164.0 43.0 %collective-permute-done.6 = bf16[1024,1024]{1,0:T(8,128)(2,1)S(1)} collective-permute-done((bf16[1024,1024]{1,0:T(8,128)(2,1)S(1)}, bf16[1024,1024]{1,0:T(8,128)(2,1)S(1)}, u32[]{:S(2)}, u32[]{:S(2)}) %collective-permute-start.6) | collective-permute-done | bytes 2097184 | tf_op jit(solution)/shard_map/ppermute | solution.py:8
  207.1 2.4 fusion.6
  209.5 3.8 %add_convert_fusion = bf16[1024,1024]{1,0:T(8,128)(2,1)} fusion(f32[1024,1024]{1,0:T(8,128)S(1)} %fusion.6, bf16[1024,1024]{1,0:T(8,128)(2,1)S(1)} %multiply_convert_fusion, bf16[2,1024,1024]{2,1,0:T(8,128)(2,1)S(1)} %bitcast.73, s32[]{:T(128)S(6)} %select_n.156), kind=kOutput, calls=%fused_computation.3 | convolution fusion | flops 2149580800 | bytes 10485764 | tf_op jit(solution)/shard_map/dot_general | solution.py:81
  213.3 1.1 dynamic-slice_bitcast_fusion
  214.4 82.9 %reduce-scatter.2.cloned.1.call-done = bf16[128,1024]{1,0:T(8,128)(2,1)} async-done(((bf16[1024,1024]{1,0:T(8,128)(2,1)}), bf16[128,1024]{1,0:T(8,128)(2,1)}) %reduce-scatter.2.cloned.1.call-update) | async-done | bytes 262160 | tf_op jit(solution)/shard_map/reduce_scatter | solution.py:87
  298.3 1.5 collective-permute-start.7
  299.9 3.4 %collective-permute-done.7 = bf16[64,1024]{1,0:T(8,128)(2,1)S(1)} collective-permute-done((bf16[64,1024]{1,0:T(8,128)(2,1)S(1)}, bf16[64,1024]{1,0:T(8,128)(2,1)S(1)}, u32[]{:S(2)}, u32[]{:S(2)}) %collective-permute-start.7) | collective-permute-done | bytes 131104 | tf_op jit(solution)/shard_map/ppermute | solution.py:8
  (63 shorter events, 7.8 us)
Async XLA Ops:
  7.2 3.3 %copy-start.8 = (bf16[2,512,1024]{2,1,0:T(8,128)(2,1)S(1)}, bf16[2,512,1024]{2,1,0:T(8,128)(2,1)}, u32[]{:S(2)}) copy-start(bf16[2,512,1024]{2,1,0:T(8,128)(2,1)} %param.13) | copy-start | bytes 6291460
  7.2 139.1 %all-gather.2.cloned.1.call-start = ((), (), s32[]{:S(2)}) async-start(), calls=%async_computation.1 | async-start | bytes 5013504 | tf_op jit(solution)/shard_map/all_gather | solution.py:47
  10.4 2.3 copy-start.9
  12.8 0.7 copy-start.11
  12.8 0.7 copy-start.12
  12.8 0.7 copy-start.13
  12.8 1.0 copy-start.10
  13.5 11.9 %copy-start.15 = (s32[16]{0:T(128)S(1)}, s32[16]{0:T(128)}, u32[]{:S(2)}) copy-start(s32[16]{0:T(128)} %param.12) | copy-start | bytes 196
  13.8 9.7 %collective-permute-start = (bf16[64,2176]{1,0:T(8,128)(2,1)S(1)}, bf16[64,2176]{1,0:T(8,128)(2,1)S(1)}, u32[]{:S(2)}, u32[]{:S(2)}) collective-permute-start(bf16[64,2176]{1,0:T(8,128)(2,1)S(1)} %get-tuple-element.12), channel_id=1, source_target_pairs={{0,2},{1,3},{2,0},{3,1},{4,6},{5,7},{6,4},{7,5},{8,10},{9,11},{10,... | collective-permute-start | bytes 835592 | tf_op jit(solution)/shard_map/ppermute | solution.py:8
  24.7 272.6 %reduce-scatter.2.cloned.1.call-start = ((), (), s32[]{:S(2)}) async-start(), calls=%async_computation.2 | async-start | bytes 2359296 | tf_op jit(solution)/shard_map/reduce_scatter | solution.py:87
  27.2 3.2 %copy-start.1 = (bf16[2,512,1024]{2,1,0:T(8,128)(2,1)S(1)}, bf16[2,512,1024]{2,1,0:T(8,128)(2,1)}, u32[]{:S(2)}) copy-start(bf16[2,512,1024]{2,1,0:T(8,128)(2,1)} %copy.44) | copy-start | bytes 6291460
  28.7 44.7 %collective-permute-start.9 = (bf16[512,1024]{1,0:T(8,128)(2,1)S(1)}, bf16[512,1024]{1,0:T(8,128)(2,1)}, u32[]{:S(2)}, u32[]{:S(2)}) collective-permute-start(bf16[512,1024]{1,0:T(8,128)(2,1)S(1)} %dynamic-slice_bitcast_fusion.1), channel_id=1, source_target_pairs={{0,4},{4,8},{8,12},{12,16},{16,20},{20,24},{24,28},{28,0},{1,5},{5... | collective-permute-start | bytes 3145736 | tf_op jit(solution)/shard_map/ppermute | solution.py:13
  31.5 77.4 %collective-permute-start.8 = (bf16[512,1024]{1,0:T(8,128)(2,1)}, bf16[512,1024]{1,0:T(8,128)(2,1)}, u32[]{:S(2)}, u32[]{:S(2)}) collective-permute-start(bf16[512,1024]{1,0:T(8,128)(2,1)} %dynamic-slice_bitcast_fusion.2), channel_id=1, source_target_pairs={{0,4},{4,8},{8,12},{12,16},{16,20},{20,24},{24,28},{28,0},{1,5},{5... | collective-permute-start | bytes 3145736 | tf_op jit(solution)/shard_map/ppermute | solution.py:13
  33.1 75.8 %copy-start.2 = (bf16[2,512,1024]{2,1,0:T(8,128)(2,1)S(1)}, bf16[2,512,1024]{2,1,0:T(8,128)(2,1)}, u32[]{:S(2)}) copy-start(bf16[2,512,1024]{2,1,0:T(8,128)(2,1)} %copy.44) | copy-start | bytes 6291460
  77.2 36.2 %collective-permute-start.3 = (bf16[512,1024]{1,0:T(8,128)(2,1)S(1)}, bf16[512,1024]{1,0:T(8,128)(2,1)S(1)}, u32[]{:S(2)}, u32[]{:S(2)}) collective-permute-start(bf16[512,1024]{1,0:T(8,128)(2,1)S(1)} %get-tuple-element.7), channel_id=1, source_target_pairs={{0,2},{1,3},{2,0},{3,1},{4,6},{5,7},{6,4},{7,5},{8,10},{9,11},{10,... | collective-permute-start | bytes 3145736 | tf_op jit(solution)/shard_map/ppermute | solution.py:8
  111.7 3.5 %copy-start.3 = (bf16[2,512,1024]{2,1,0:T(8,128)(2,1)}, bf16[2,512,1024]{2,1,0:T(8,128)(2,1)S(1)}, u32[]{:S(2)}) copy-start(bf16[2,512,1024]{2,1,0:T(8,128)(2,1)S(1)} %get-tuple-element.8) | copy-start | bytes 6291460
  111.7 19.8 %collective-permute-start.1 = (bf16[512,1024]{1,0:T(8,128)(2,1)S(1)}, bf16[512,1024]{1,0:T(8,128)(2,1)S(1)}, u32[]{:S(2)}, u32[]{:S(2)}) collective-permute-start(bf16[512,1024]{1,0:T(8,128)(2,1)S(1)} %get-tuple-element.11), channel_id=1, source_target_pairs={{0,2},{1,3},{2,0},{3,1},{4,6},{5,7},{6,4},{7,5},{8,10},{9,11},{10,... | collective-permute-start | bytes 3145736 | tf_op jit(solution)/shard_map/ppermute | solution.py:8
  115.1 21.1 %collective-permute-start.4 = (bf16[2,1,512,1024]{3,2,1,0:T(8,128)(2,1)}, bf16[2,1,512,1024]{3,2,1,0:T(8,128)(2,1)}, u32[]{:S(2)}, u32[]{:S(2)}) collective-permute-start(bf16[2,1,512,1024]{3,2,1,0:T(8,128)(2,1)} %maximum_select_fusion.4), channel_id=1, source_target_pairs={{0,1},{1,0},{2,3},{3,2},{4,5},{5,4},{6,7},{7,6},{8,9},{9,8},{10,11... | collective-permute-start | bytes 6291464 | tf_op jit(solution)/shard_map/ppermute | solution.py:8
  131.5 1.7 copy-start.4
  133.2 8.5 %collective-permute-start.2 = (bf16[2,1,512,1024]{3,2,1,0:T(8,128)(2,1)}, bf16[2,1,512,1024]{3,2,1,0:T(8,128)(2,1)}, u32[]{:S(2)}, u32[]{:S(2)}) collective-permute-start(bf16[2,1,512,1024]{3,2,1,0:T(8,128)(2,1)} %maximum_select_fusion.3), channel_id=1, source_target_pairs={{0,1},{1,0},{2,3},{3,2},{4,5},{5,4},{6,7},{7,6},{8,9},{9,8},{10,11... | collective-permute-start | bytes 6291464 | tf_op jit(solution)/shard_map/ppermute | solution.py:8
  133.2 27.5 %collective-permute-start.5 = (bf16[2,1,512,1024]{3,2,0,1:T(8,128)(2,1)S(1)}, bf16[2,1,512,1024]{3,2,0,1:T(8,128)(2,1)}, u32[]{:S(2)}, u32[]{:S(2)}) collective-permute-start(bf16[2,1,512,1024]{3,2,0,1:T(8,128)(2,1)S(1)} %bitcast.65), channel_id=1, source_target_pairs={{0,1},{1,0},{2,3},{3,2},{4,5},{5,4},{6,7},{7,6},{8,9},{9,8},{10,11... | collective-permute-start | bytes 6291464 | tf_op jit(solution)/shard_map/ppermute | solution.py:8
  133.7 2.0 copy-start.5
  133.7 2.2 copy-start.7
  146.3 7.7 %copy-start.14 = (bf16[1024,2176]{0,1:T(8,128)(2,1)S(1)}, bf16[1024,2176]{0,1:T(8,128)(2,1)}, u32[]{:S(2)}) copy-start(bf16[1024,2176]{0,1:T(8,128)(2,1)} %all-gather.2.cloned.1.call-done) | copy-start | bytes 13369348
  146.3 7.7 %copy-start.6 = (bf16[2,2,1,512,1024]{4,3,1,0,2:T(8,128)(2,1)S(1)}, bf16[2,2,1,512,1024]{4,3,1,0,2:T(8,128)(2,1)}, u32[]{:S(2)}) copy-start(bf16[2,2,1,512,1024]{4,3,1,0,2:T(8,128)(2,1)} %copy.33) | copy-start | bytes 12582916
  159.5 47.6 %collective-permute-start.6 = (bf16[1024,1024]{1,0:T(8,128)(2,1)S(1)}, bf16[1024,1024]{1,0:T(8,128)(2,1)S(1)}, u32[]{:S(2)}, u32[]{:S(2)}) collective-permute-start(bf16[1024,1024]{1,0:T(8,128)(2,1)S(1)} %multiply_convert_fusion), channel_id=1, source_target_pairs={{0,2},{1,3},{2,0},{3,1},{4,6},{5,7},{6,4},{7,5},{8,10},{9,11},{10,... | collective-permute-start | bytes 6291464 | tf_op jit(solution)/shard_map/ppermute | solution.py:8
  214.4 85.4 %collective-permute-start.10 = (bf16[512,1024]{1,0:T(8,128)(2,1)}, bf16[512,1024]{1,0:T(8,128)(2,1)S(1)}, u32[]{:S(2)}, u32[]{:S(2)}) collective-permute-start(bf16[512,1024]{1,0:T(8,128)(2,1)} %dynamic-slice_bitcast_fusion), channel_id=1, source_target_pairs={{0,4},{4,8},{8,12},{12,16},{16,20},{20,24},{24,28},{28,0},{1,5},{5... | collective-permute-start | bytes 3145736 | tf_op jit(solution)/shard_map/ppermute | solution.py:13
  298.3 5.0 %collective-permute-start.7 = (bf16[64,1024]{1,0:T(8,128)(2,1)S(1)}, bf16[64,1024]{1,0:T(8,128)(2,1)S(1)}, u32[]{:S(2)}, u32[]{:S(2)}) collective-permute-start(bf16[64,1024]{1,0:T(8,128)(2,1)S(1)} %get-tuple-element.14), channel_id=1, source_target_pairs={{0,2},{1,3},{2,0},{3,1},{4,6},{5,7},{6,4},{7,5},{8,10},{9,11},{10,... | collective-permute-start | bytes 393224 | tf_op jit(solution)/shard_map/ppermute | solution.py:8
  299.9 4.2 %copy-start = (bf16[2,512,1024]{2,1,0:T(8,128)(2,1)}, bf16[2,512,1024]{2,1,0:T(8,128)(2,1)S(1)}, u32[]{:S(2)}) copy-start(bf16[2,512,1024]{2,1,0:T(8,128)(2,1)S(1)} %bitcast_dynamic-update-slice_fusion) | copy-start | bytes 6291460
Sparse Core Ops, SparseCore 0:
  24.8 109.5 all-gather.1
  213.4 83.8 reduce-scatter.1

commit v2 on v1

v2 whole, which is shorter than its diff:
```python
import functools

import jax
import jax.numpy as jnp
from jax import lax
from jax.experimental import pallas as pl
from jax.experimental.pallas import tpu as pltpu
from jax.sharding import PartitionSpec as P

LANES = 128
VMEM_BYTES = 40 * 1024 * 1024


def swap(x, axis, bit):
    return lax.ppermute(x, axis, [(i, i ^ bit) for i in range(lax.axis_size(axis))])


def passed_along(x, axis, by):
    size = lax.axis_size(axis)
    return lax.ppermute(x, axis, [(i, (i + by) % size) for i in range(size)])


def shift_z(x, by):
    size = lax.axis_size("dp")
    return lax.ppermute(x, "dp", [(i, (i + 2 * by) % size) for i in range(size)])


def in_order(second, own, other, axis=0):
    return jnp.where(
        second, jnp.stack([other, own], axis=axis), jnp.stack([own, other], axis=axis)
    )


def pick(w, index):
    return lax.dynamic_index_in_dim(w, index, 0, keepdims=False)


def spread(pieces, half):
    bit = 1
    while bit < half:
        pieces = pieces + [swap(p, "shard", bit) for p in pieces]
        bit *= 2
    return pieces


def params():
    return pltpu.CompilerParams(vmem_limit_bytes=VMEM_BYTES)


def prep_kernel(tokens_ref, probs_ref, ids_ref, place_ref, out_ref):
    probs = probs_ref[...]
    weights = (probs / jnp.sum(probs, axis=1, keepdims=True)).astype(jnp.bfloat16)
    weights = weights.astype(jnp.float32)
    ids = ids_ref[...]
    place = place_ref[...]
    coef = jnp.zeros((ids.shape[0], LANES), jnp.float32)
    for k in range(ids.shape[1]):
        coef += jnp.where(ids[:, k : k + 1] == place, weights[:, k : k + 1], 0.0)
    width = tokens_ref.shape[1]
    out_ref[:, :width] = tokens_ref[...]
    out_ref[:, width:] = coef.astype(jnp.bfloat16)


def prep(tokens, probs, ids, old_place):
    place = jnp.pad(old_place, (0, LANES - old_place.shape[0]), constant_values=-1)[None]
    return pl.pallas_call(
        prep_kernel,
        out_shape=jax.ShapeDtypeStruct((tokens.shape[0], tokens.shape[1] + LANES), tokens.dtype),
        compiler_params=params(),
    )(tokens, probs, ids, place)


def hidden_kernel(count, meta, a_ref, b_ref, *refs):
    gates, ups, out_ref = refs[:count], refs[count : 2 * count], refs[2 * count]
    depth = gates[0].shape[-2]
    width = a_ref.shape[1] - LANES
    rows = a_ref.shape[0] + b_ref.shape[0]
    block = out_ref.shape[1]
    gate = jnp.zeros((rows, block), jnp.float32)
    up = jnp.zeros((rows, block), jnp.float32)
    for i in range(count):
        columns = pl.ds(pl.multiple_of(meta[2 + i], LANES), depth)
        x = jnp.concatenate([a_ref[:, columns], b_ref[:, columns]], axis=0)
        gate += jnp.dot(x, gates[i][...].reshape(depth, block), preferred_element_type=jnp.float32)
        up += jnp.dot(x, ups[i][...].reshape(depth, block), preferred_element_type=jnp.float32)
    coef = jnp.concatenate([a_ref[:, width:], b_ref[:, width:]], axis=0).astype(jnp.float32)
    lane = lax.broadcasted_iota(jnp.int32, coef.shape, 1)
    coef = jnp.sum(jnp.where(lane == meta[1], coef, 0.0), axis=1, keepdims=True)
    out_ref[...] = (gate / (1.0 + jnp.exp(-gate)) * up * coef).astype(out_ref.dtype)


def hidden_of(meta, a, b, gates, ups):
    count = len(gates)
    depth, ff = gates[0].shape[-2:]
    block = 256
    rows = a.shape[0] + b.shape[0]

    def weight_spec(w):
        if w.ndim == 3:
            return pl.BlockSpec((1, depth, block), lambda f, m: (m[0], 0, f))
        return pl.BlockSpec((depth, block), lambda f, m: (0, f))

    def whole(x):
        return pl.BlockSpec(x.shape, lambda f, m: (0, 0))

    return pl.pallas_call(
        functools.partial(hidden_kernel, count),
        grid_spec=pltpu.PrefetchScalarGridSpec(
            num_scalar_prefetch=1,
            grid=(ff // block,),
            in_specs=[whole(a), whole(b)] + [weight_spec(w) for w in gates + ups],
            out_specs=pl.BlockSpec((rows, block), lambda f, m: (0, f)),
        ),
        out_shape=jax.ShapeDtypeStruct((rows, ff), a.dtype),
        compiler_params=params(),
        cost_estimate=pl.CostEstimate(
            flops=4 * rows * count * depth * ff,
            bytes_accessed=4 * count * depth * ff + 4 * rows * count * depth,
            transcendentals=rows * ff,
        ),
    )(meta, a, b, *gates, *ups)


def down_kernel(count, meta, own_ref, other_ref, *refs):
    downs, out_ref = refs[:count], refs[count]
    depth = downs[0].shape[1]
    contract = (((1,), (1,)), ((), ()))
    own, other = own_ref[...], other_ref[...]
    for i in range(count):
        part = lax.dot_general(
            own, downs[i][meta[0]], contract, preferred_element_type=jnp.float32
        ) + lax.dot_general(
            other, downs[i][1 - meta[0]], contract, preferred_element_type=jnp.float32
        )
        columns = pl.ds(pl.multiple_of(meta[1 + i], LANES), depth)
        out_ref[:, columns] = part.astype(out_ref.dtype)


def down_of(meta, own, other, downs):
    count = len(downs)
    depth, ff = downs[0].shape[-2:]
    rows = own.shape[0]
    vmem = pl.BlockSpec(memory_space=pltpu.VMEM)
    return pl.pallas_call(
        functools.partial(down_kernel, count),
        in_specs=[pl.BlockSpec(memory_space=pltpu.SMEM)] + [vmem] * (2 + count),
        out_specs=vmem,
        out_shape=jax.ShapeDtypeStruct((rows, count * depth), own.dtype),
        compiler_params=params(),
        cost_estimate=pl.CostEstimate(
            flops=4 * rows * count * depth * ff,
            bytes_accessed=4 * count * depth * ff + 4 * rows * ff + 2 * rows * count * depth,
            transcendentals=0,
        ),
    )(meta, own, other, *downs)


def local(tokens, router_probs, expert_ids, old_place, new_place, w_gate, w_up, w_down):
    tok = tokens.shape[0]
    width = tokens.shape[1]
    depth = w_gate.shape[1]
    n_shard = lax.axis_size("shard")
    half = n_shard // 2
    n_z = lax.axis_size("dp") // 2
    column = lax.axis_index("shard")
    row_id = lax.axis_index("dp")
    side = column // half
    place_in_side = column % half

    own = prep(tokens, router_probs, expert_ids, old_place)
    other = swap(own, "shard", half)
    both = in_order(side == 1, own, other).reshape(2 * tok, width + LANES)

    gate_arrived = swap(pick(w_gate, 1 - side), "shard", half)
    up_arrived = swap(pick(w_up, 1 - side), "shard", half)
    gate_mine, up_mine = pick(w_gate, side), pick(w_up, side)
    gates = spread([gate_mine], half) + spread([gate_arrived], half)
    ups = spread([up_mine], half) + spread([up_arrived], half)
    gates[0], ups[0] = w_gate, w_up
    downs = spread([w_down], half)

    same = [(place_in_side ^ j) * depth for j in range(half)]
    meta_hidden = jnp.stack(
        [side, 2 * row_id + side]
        + [side * half * depth + s for s in same]
        + [(1 - side) * half * depth + s for s in same]
    ).astype(jnp.int32)
    meta_down = jnp.stack([side] + same).astype(jnp.int32)

    columns = [both] + [shift_z(both, s) for s in range(1, n_z)]
    pairs = [(c, swap(c, "dp", 1)) for c in columns]

    total = None
    for s in list(range(1, n_z)) + [0]:
        hidden = hidden_of(meta_hidden, pairs[s][0], pairs[s][1], gates, ups)
        hidden_other = swap(hidden, "shard", half)
        part = down_of(meta_down, hidden, hidden_other, downs)
        if s:
            part = shift_z(part, -s)
        part = part.astype(jnp.float32)
        total = part if total is None else total + part
    total = total.reshape(2, 2 * tok, width // 2)
    given = swap(total[1].astype(jnp.bfloat16), "dp", 1)
    total = (total[0] + given.astype(jnp.float32)).astype(jnp.bfloat16)
    total = total.reshape(2, tok, width // 2)
    kept = pick(total, side)
    arrived = swap(pick(total, 1 - side), "shard", half)
    moe_output = in_order(side == 1, kept, arrived, axis=1).reshape(tok, width)

    base_slot = 2 * row_id
    second_old = pick(old_place, base_slot + 1)
    second_new = pick(new_place, base_slot + 1)
    moved = (second_new != second_old).astype(jnp.int32)

    def refilled(w):
        arrive = passed_along(pick(w, moved), "dp", 1)
        return lax.dynamic_update_index_in_dim(w, arrive, moved, 0)

    return (moe_output, refilled(w_gate), refilled(w_up), refilled(w_down))


def solution(mesh):
    in_specs = (
        P(("dp", "shard"), None),
        P(("dp", "shard"), None),
        P(("dp", "shard"), None),
        P(),
        P(),
        P("dp", "shard", None),
        P("dp", "shard", None),
        P("dp", "shard", None),
    )
    out_specs = (
        P(("dp", "shard"), None),
        P("dp", "shard", None),
        P("dp", "shard", None),
        P("dp", "shard", None),
    )
    return jax.shard_map(local, mesh=mesh, in_specs=in_specs, out_specs=out_specs, check_vma=False)
```

time: 311 us -> 240 us (0.77)
  waiting for transfers between devices: 223 us -> 91.4 us
  starting transfers between devices: 13.4 us -> 83 us
  Pallas kernels: 0 us -> 35 us
  matrix products: 19.3 us -> 0 us
  other arithmetic: 16.4 us -> 0.59 us
  between operations: 15.5 us -> 2.23 us
    reduce_scatter x1 -> x0, waiting for transfers between devices: 82.9 us -> none  [local(): total = lax.psum_scatter(part, 'dp', scatter_dimension=0, tiled=True)]
    ppermute x8 -> x18, waiting for transfers between devices: 69.5 us -> 13.9 us  [swap(): lax.ppermute(x, axis, [(i, i ^ bit) for i in range(lax.axis_size(axis))])]
    ppermute x8 -> x18, starting transfers between devices: 9.98 us -> 56.5 us  [swap(): lax.ppermute(x, axis, [(i, i ^ bit) for i in range(lax.axis_size(axis))])]
    ppermute x0 -> x6, waiting for transfers between devices: none -> 45.3 us  [shift_z(): lax.ppermute(x, 'dp', [(i, (i + 2 * by) % size) for i in range(size)])]
    ppermute x3, waiting for transfers between devices: 70.1 us -> 32.3 us  [passed_along(): return lax.ppermute(x, axis, [(i, (i + by) % size) for i in range(size)])]
    pallas_call x0 -> x9, Pallas kernels: none -> 35 us  [the longest x4 23.1 us: hidden_of(): pl.pallas_call(functools.partial(hidden_kernel, count), grid_spec=pltpu.P...]
    ppermute x0 -> x6, starting transfers between devices: none -> 22 us  [shift_z(): lax.ppermute(x, 'dp', [(i, (i + 2 * by) % size) for i in range(size)])]
    dot_general x4 -> x0, matrix products: 19.3 us -> none  [the longest x1 7.69 us: local(): gate_part = jnp.dot(rows, full_gate, preferred_element_type=jnp.float32)]
  transfers between devices with their start and end apart: 13 -> 27, of which waited for: 7 -> 10; matrix products, arithmetic and copies ran while one was open for 14% -> 4% of each run, Pallas kernels for 0% -> 15%
where the time goes in v2:
time: 240 us; the launch traced here: 239 us
  waiting for transfers between devices  91.4 us (38%)
  starting transfers between devices  83 us (35%)
  Pallas kernels  35 us (15%)
  local copies, waits for them, and re-layouts  26.6 us (11%)
    ppermute x18, starting transfers between devices, swap(): lax.ppermute(x, axis, [(i, i ^ bit) for i in range(lax.axis_size(axis))])  56.5 us
    ppermute x6, waiting for transfers between devices, shift_z(): lax.ppermute(x, 'dp', [(i, (i + 2 * by) % size) for i in range(size)])  45.3 us
    ppermute x3, waiting for transfers between devices, passed_along(): return lax.ppermute(x, axis, [(i, (i + by) % size) for i in range(size)])  32.3 us
    pallas_call x4, Pallas kernels, hidden_of(): pl.pallas_call(functools.partial(hidden_kernel, count), grid_spec=pltpu.P...  23.1 us
    ppermute x6, starting transfers between devices, shift_z(): lax.ppermute(x, 'dp', [(i, (i + 2 * by) % size) for i in range(size)])  22 us
    unnamed x46, local copies, waits for them, and re-layouts  16.3 us
    ppermute x18, waiting for transfers between devices, swap(): lax.ppermute(x, axis, [(i, i ^ bit) for i in range(lax.axis_size(axis))])  13.9 us
    pallas_call x4, Pallas kernels, down_of(): pl.pallas_call(functools.partial(down_kernel, count), in_specs=[pl.BlockS...  11.7 us
  transfers between devices with their start and end apart: 27, of which 10 were waited for; matrix products, arithmetic and copies ran while one was open for 4% of the time, Pallas kernels for 15%

profile of v2, /device:TPU:0, one launch (start us, length us, event | category | flops | bytes accessed | tf_op | source)
XLA Modules:
  0.0 238.9 jit_solution(6257447402721111745)
XLA Ops:
  0.7 1.6 copy.24.refs_0_
  4.8 2.4 %dynamic-slice_bitcast_fusion.2 = bf16[512,1024]{1,0:T(8,128)(2,1)} fusion(bf16[2,512,1024]{2,1,0:T(8,128)(2,1)} %refs_0_.11, s32[]{:T(128)S(6)} %select_n.72), kind=kLoop, calls=%fused_computation.5 | loop fusion | bytes 2097156 | tf_op jit(solution)/shard_map/jit(dynamic_index_in_dim)/squeeze | solution.py:35
  7.2 2.9 %collective-permute-start.24 = (bf16[512,1024]{1,0:T(8,128)(2,1)}, bf16[512,1024]{1,0:T(8,128)(2,1)}, u32[]{:S(2)}, u32[]{:S(2)}) collective-permute-start(bf16[512,1024]{1,0:T(8,128)(2,1)} %dynamic-slice_bitcast_fusion.2), channel_id=1, source_target_pairs={{0,4},{4,8},{8,12},{12,16},{16,20},{20,24},{24,28},{28,0},{1,5},{5... | collective-permute-start | bytes 3145736 | tf_op jit(solution)/shard_map/ppermute | solution.py:20
  14.7 3.1 %copy.20 = bf16[2,512,1024]{2,1,0:T(8,128)(2,1)} copy(bf16[2,512,1024]{2,1,0:T(8,128)(2,1)} %refs_0_.11) | data formatting | bytes 4194304
  17.8 3.2 %collective-permute-done = bf16[64,2176]{1,0:T(8,128)(2,1)S(1)} collective-permute-done((bf16[64,2176]{1,0:T(8,128)(2,1)S(1)}, bf16[64,2176]{1,0:T(8,128)(2,1)S(1)}, u32[]{:S(2)}, u32[]{:S(2)}) %collective-permute-start) | collective-permute-done | bytes 278560 | tf_op jit(solution)/shard_map/ppermute | solution.py:15
  21.2 1.6 collective-permute-start.1
  22.8 14.7 %collective-permute-done.24 = bf16[512,1024]{1,0:T(8,128)(2,1)} collective-permute-done((bf16[512,1024]{1,0:T(8,128)(2,1)}, bf16[512,1024]{1,0:T(8,128)(2,1)}, u32[]{:S(2)}, u32[]{:S(2)}) %collective-permute-start.24) | collective-permute-done | bytes 1048608 | tf_op jit(solution)/shard_map/ppermute | solution.py:20
  37.5 3.1 %bitcast_dynamic-update-slice_fusion.2 = (bf16[2,512,1024]{2,1,0:T(8,128)(2,1)}, bf16[512,1024]{1,0:T(8,128)(2,1)S(1)}, bf16[512,1024]{1,0:T(8,128)(2,1)S(1)}) fusion(bf16[2,512,1024]{2,1,0:T(8,128)(2,1)} %copy.20, s32[]{:T(128)S(6)} %select_n.72, bf16[512,1024]{1,0:T(8,128)(2,1)} %collective-permute-done.24, s32[]{:T(128)S(6)} %select_n.68, s32[]{:T(128)S(6)} %select_n.67), kind=kLoop, calls=%fused_computation.2 | loop fusion | bytes 6291468 | tf_op jit(solution)/shard_map/jit(dynamic_update_index_in_dim)/dynamic_update_slice | solution.py:217
  40.6 1.7 collective-permute-start.4
  42.3 17.6 %collective-permute-done.25 = bf16[512,1024]{1,0:T(8,128)(2,1)} collective-permute-done((bf16[512,1024]{1,0:T(8,128)(2,1)}, bf16[512,1024]{1,0:T(8,128)(2,1)}, u32[]{:S(2)}, u32[]{:S(2)}) %collective-permute-start.25) | collective-permute-done | bytes 1048608 | tf_op jit(solution)/shard_map/ppermute | solution.py:20
  61.5 1.8 collective-permute-start.7
  65.5 7.0 %collective-permute-start.2 = (bf16[128,2176]{1,0:T(8,128)(2,1)S(1)}, bf16[128,2176]{1,0:T(8,128)(2,1)S(1)}, u32[]{:S(2)}, u32[]{:S(2)}) collective-permute-start(bf16[128,2176]{1,0:T(8,128)(2,1)S(1)} %collective-permute-done.1.a_ref), channel_id=1, source_target_pairs={{0,4},{4,0},{8,12},{12,8},{16,20},{20,16},{24,28},{28,24},{1,5},{5... | collective-permute-start | bytes 1671176 | tf_op jit(solution)/shard_map/ppermute | solution.py:15
  73.3 14.3 %collective-permute-done.12.a_ref = bf16[128,2176]{1,0:T(8,128)(2,1)} collective-permute-done((bf16[128,2176]{1,0:T(8,128)(2,1)S(1)}, bf16[128,2176]{1,0:T(8,128)(2,1)}, u32[]{:S(2)}, u32[]{:S(2)}) %collective-permute-start.12) | collective-permute-done | bytes 557088 | tf_op jit(solution)/shard_map/ppermute | solution.py:25
  91.3 7.9 %collective-permute-start.13 = (bf16[128,2176]{1,0:T(8,128)(2,1)}, bf16[128,2176]{1,0:T(8,128)(2,1)}, u32[]{:S(2)}, u32[]{:S(2)}) collective-permute-start(bf16[128,2176]{1,0:T(8,128)(2,1)} %collective-permute-done.12.a_ref), channel_id=1, source_target_pairs={{0,4},{4,0},{8,12},{12,8},{16,20},{20,16},{24,28},{28,24},{1,5},{5... | collective-permute-start | bytes 1671176 | tf_op jit(solution)/shard_map/ppermute | solution.py:15
  100.3 2.0 collective-permute-start.17
  102.4 3.6 %collective-permute-start.20 = (bf16[128,2176]{1,0:T(8,128)(2,1)}, bf16[128,2176]{1,0:T(8,128)(2,1)S(1)}, u32[]{:S(2)}, u32[]{:S(2)}) collective-permute-start(bf16[128,2176]{1,0:T(8,128)(2,1)} %bitcast.46), channel_id=1, source_target_pairs={{0,4},{4,0},{8,12},{12,8},{16,20},{20,16},{24,28},{28,24},{1,5},{5... | collective-permute-start | bytes 1671176 | tf_op jit(solution)/shard_map/ppermute | solution.py:15
  105.9 1.6 copy-done.1
  107.5 1.6 copy-done.3
  113.7 5.6 %shard_map.112.own_ref = bf16[256,1024]{1,0:T(8,128)(2,1)S(1)} custom-call(s32[6]{0:T(128)S(1)} %stack.68.meta, bf16[128,2176]{1,0:T(8,128)(2,1)S(1)} %copy-done.13, bf16[128,2176]{1,0:T(8,128)(2,1)S(1)} %copy-done.15, bf16[2,512,1024]{2,1,0:T(8,128)(2,1)S(1)} %copy-done.1, bf16[512,1024]{1,0:T(8,128)(2,1)S(1)} %copy-done.7, ...), custom_call_target="tpu_custom_call" | custom-call | flops 2147483648 | bytes 10485760 | tf_op jit(solution)/shard_map/pallas_call | solution.py:106
  120.8 6.0 %shard_map.114.own_ref = bf16[256,1024]{1,0:T(8,128)(2,1)S(1)} custom-call(s32[6]{0:T(128)S(1)} %stack.68.meta, bf16[128,2176]{1,0:T(8,128)(2,1)} %collective-permute-done.12.a_ref, bf16[128,2176]{1,0:T(8,128)(2,1)} %collective-permute-done.13.b_ref, bf16[2,512,1024]{2,1,0:T(8,128)(2,1)S(1)} %copy-done.1, bf16[512,1024]{1,0:T(8,128)(2,1)S(1)} %copy-done.7, ...), custom_call_target="tpu_custom_call" | custom-call | flops 2147483648 | bytes 10485760 | tf_op jit(solution)/shard_map/pallas_call | solution.py:106
  127.4 6.0 %shard_map.116.own_ref = bf16[256,1024]{1,0:T(8,128)(2,1)S(1)} custom-call(s32[6]{0:T(128)S(1)} %stack.68.meta, bf16[128,2176]{1,0:T(8,128)(2,1)} %collective-permute-done.16.a_ref, bf16[128,2176]{1,0:T(8,128)(2,1)} %collective-permute-done.17.b_ref, bf16[2,512,1024]{2,1,0:T(8,128)(2,1)S(1)} %copy-done.1, bf16[512,1024]{1,0:T(8,128)(2,1)S(1)} %copy-done.7, ...), custom_call_target="tpu_custom_call" | custom-call | flops 2147483648 | bytes 10485760 | tf_op jit(solution)/shard_map/pallas_call | solution.py:106
  136.3 5.6 %shard_map.118.own_ref = bf16[256,1024]{1,0:T(8,128)(2,1)S(1)} custom-call(s32[6]{0:T(128)S(1)} %stack.68.meta, bf16[128,2176]{1,0:T(8,128)(2,1)S(1)} %bitcast.47, bf16[128,2176]{1,0:T(8,128)(2,1)S(1)} %collective-permute-done.20.b_ref, bf16[2,512,1024]{2,1,0:T(8,128)(2,1)S(1)} %copy-done.1, bf16[512,1024]{1,0:T(8,128)(2,1)S(1)} %copy-done.7, ...), custom_call_target="tpu_custom_call" | custom-call | flops 2147483648 | bytes 10485760 | tf_op jit(solution)/shard_map/pallas_call | solution.py:106
  143.5 2.9 %shard_map.113 = bf16[256,1024]{1,0:T(8,128)(2,1)S(1)} custom-call(s32[3]{0:T(128)S(1)} %pad_add_fusion.meta, bf16[256,1024]{1,0:T(8,128)(2,1)S(1)} %shard_map.112.own_ref, bf16[256,1024]{1,0:T(8,128)(2,1)S(1)} %collective-permute-done.9.other_ref, bf16[2,512,1024]{2,1,0:T(8,128)(2,1)S(1)} %copy.24.refs_0_, bf16[2,512,1024]{2,1,0:T(8,128)(2,1)} %collective-permute-done.10.refs_1_), custom_call_target="tpu_custom_call" | custom-call | flops 1073741824 | bytes 5767168 | tf_op jit(solution)/shard_map/pallas_call | solution.py:144
  146.4 13.5 %collective-permute-start.11 = (bf16[256,1024]{1,0:T(8,128)(2,1)S(1)}, bf16[256,1024]{1,0:T(8,128)(2,1)S(1)}, u32[]{:S(2)}, u32[]{:S(2)}) collective-permute-start(bf16[256,1024]{1,0:T(8,128)(2,1)S(1)} %shard_map.113), channel_id=1, source_target_pairs={{0,24},{4,28},{8,0},{12,4},{16,8},{20,12},{24,16},{28,20},{1,25},{... | collective-permute-start | bytes 1572872 | tf_op jit(solution)/shard_map/ppermute | solution.py:25
  159.9 2.9 %shard_map.115 = bf16[256,1024]{1,0:T(8,128)(2,1)S(1)} custom-call(s32[3]{0:T(128)S(1)} %pad_add_fusion.meta, bf16[256,1024]{1,0:T(8,128)(2,1)S(1)} %shard_map.114.own_ref, bf16[256,1024]{1,0:T(8,128)(2,1)S(1)} %collective-permute-done.14.other_ref, bf16[2,512,1024]{2,1,0:T(8,128)(2,1)S(1)} %copy.24.refs_0_, ...), custom_call_target="tpu_custom_call" | custom-call | flops 1073741824 | bytes 5767168 | tf_op jit(solution)/shard_map/pallas_call | solution.py:144
  162.9 2.9 %shard_map.117 = bf16[256,1024]{1,0:T(8,128)(2,1)S(1)} custom-call(s32[3]{0:T(128)S(1)} %pad_add_fusion.meta, bf16[256,1024]{1,0:T(8,128)(2,1)S(1)} %shard_map.116.own_ref, bf16[256,1024]{1,0:T(8,128)(2,1)S(1)} %collective-permute-done.18.other_ref, bf16[2,512,1024]{2,1,0:T(8,128)(2,1)S(1)} %copy.24.refs_0_, ...), custom_call_target="tpu_custom_call" | custom-call | flops 1073741824 | bytes 5767168 | tf_op jit(solution)/shard_map/pallas_call | solution.py:144
  165.8 4.7 %collective-permute-start.19 = (bf16[256,1024]{1,0:T(8,128)(2,1)S(1)}, bf16[256,1024]{1,0:T(8,128)(2,1)S(1)}, u32[]{:S(2)}, u32[]{:S(2)}) collective-permute-start(bf16[256,1024]{1,0:T(8,128)(2,1)S(1)} %shard_map.117), channel_id=1, source_target_pairs={{0,8},{4,12},{8,16},{12,20},{16,24},{20,28},{24,0},{28,4},{1,9},{5... | collective-permute-start | bytes 1572872 | tf_op jit(solution)/shard_map/ppermute | solution.py:25
  170.6 2.9 %shard_map.119 = bf16[256,1024]{1,0:T(8,128)(2,1)S(1)} custom-call(s32[3]{0:T(128)S(1)} %pad_add_fusion.meta, bf16[256,1024]{1,0:T(8,128)(2,1)S(1)} %shard_map.118.own_ref, bf16[256,1024]{1,0:T(8,128)(2,1)S(1)} %collective-permute-done.21.other_ref, bf16[2,512,1024]{2,1,0:T(8,128)(2,1)S(1)} %copy.24.refs_0_, ...), custom_call_target="tpu_custom_call" | custom-call | flops 1073741824 | bytes 5767168 | tf_op jit(solution)/shard_map/pallas_call | solution.py:144
  173.6 30.7 %collective-permute-done.15 = bf16[256,1024]{1,0:T(8,128)(2,1)S(1)} collective-permute-done((bf16[256,1024]{1,0:T(8,128)(2,1)S(1)}, bf16[256,1024]{1,0:T(8,128)(2,1)S(1)}, u32[]{:S(2)}, u32[]{:S(2)}) %collective-permute-start.15) | collective-permute-done | bytes 524320 | tf_op jit(solution)/shard_map/ppermute | solution.py:25
  204.6 24.0 %collective-permute-start.22 = (bf16[128,1024]{1,0:T(8,128)(2,1)S(1)}, bf16[128,1024]{1,0:T(8,128)(2,1)S(1)}, u32[]{:S(2)}, u32[]{:S(2)}) collective-permute-start(bf16[128,1024]{1,0:T(8,128)(2,1)S(1)} %slice.17), channel_id=1, source_target_pairs={{0,4},{4,0},{8,12},{12,8},{16,20},{20,16},{24,28},{28,24},{1,5},{5... | collective-permute-start | bytes 786440 | tf_op jit(solution)/shard_map/ppermute | solution.py:15
  228.5 4.5 %collective-permute-done.22 = bf16[128,1024]{1,0:T(8,128)(2,1)S(1)} collective-permute-done((bf16[128,1024]{1,0:T(8,128)(2,1)S(1)}, bf16[128,1024]{1,0:T(8,128)(2,1)S(1)}, u32[]{:S(2)}, u32[]{:S(2)}) %collective-permute-start.22) | collective-permute-done | bytes 262176 | tf_op jit(solution)/shard_map/ppermute | solution.py:15
  233.8 4.3 %collective-permute-done.23 = bf16[64,1024]{1,0:T(8,128)(2,1)S(1)} collective-permute-done((bf16[64,1024]{1,0:T(8,128)(2,1)S(1)}, bf16[64,1024]{1,0:T(8,128)(2,1)S(1)}, u32[]{:S(2)}, u32[]{:S(2)}) %collective-permute-start.23) | collective-permute-done | bytes 131104 | tf_op jit(solution)/shard_map/ppermute | solution.py:15
  (95 shorter events, 28.5 us)
Async XLA Ops:
  4.8 8.1 %copy-start.16 = (bf16[64,2048]{1,0:T(8,128)(2,1)S(1)}, bf16[64,2048]{1,0:T(8,128)(2,1)}, u32[]{:S(2)}) copy-start(bf16[64,2048]{1,0:T(8,128)(2,1)} %tokens_ref.1) | copy-start | bytes 786436
  7.2 30.3 %collective-permute-start.24 = (bf16[512,1024]{1,0:T(8,128)(2,1)}, bf16[512,1024]{1,0:T(8,128)(2,1)}, u32[]{:S(2)}, u32[]{:S(2)}) collective-permute-start(bf16[512,1024]{1,0:T(8,128)(2,1)} %dynamic-slice_bitcast_fusion.2), channel_id=1, source_target_pairs={{0,4},{4,8},{8,12},{12,16},{16,20},{20,24},{24,28},{28,0},{1,5},{5... | collective-permute-start | bytes 3145736 | tf_op jit(solution)/shard_map/ppermute | solution.py:20
  11.2 48.8 %collective-permute-start.25 = (bf16[512,1024]{1,0:T(8,128)(2,1)}, bf16[512,1024]{1,0:T(8,128)(2,1)}, u32[]{:S(2)}, u32[]{:S(2)}) collective-permute-start(bf16[512,1024]{1,0:T(8,128)(2,1)} %dynamic-slice_bitcast_fusion.1), channel_id=1, source_target_pairs={{0,4},{4,8},{8,12},{12,16},{16,20},{20,24},{24,28},{28,0},{1,5},{5... | collective-permute-start | bytes 3145736 | tf_op jit(solution)/shard_map/ppermute | solution.py:20
  13.2 7.9 %collective-permute-start = (bf16[64,2176]{1,0:T(8,128)(2,1)S(1)}, bf16[64,2176]{1,0:T(8,128)(2,1)S(1)}, u32[]{:S(2)}, u32[]{:S(2)}) collective-permute-start(bf16[64,2176]{1,0:T(8,128)(2,1)S(1)} %shard_map.111), channel_id=1, source_target_pairs={{0,2},{1,3},{2,0},{3,1},{4,6},{5,7},{6,4},{7,5},{8,10},{9,11},{10,... | collective-permute-start | bytes 835592 | tf_op jit(solution)/shard_map/ppermute | solution.py:15
  21.2 43.0 %copy-start.10 = (bf16[2,64,2176]{2,1,0:T(8,128)(2,1)}, bf16[2,64,2176]{2,1,0:T(8,128)(2,1)S(1)}, u32[]{:S(2)}) copy-start(bf16[2,64,2176]{2,1,0:T(8,128)(2,1)S(1)} %maximum_select_fusion) | copy-start | bytes 1671172
  21.2 38.8 %copy-start.5 = (bf16[2,512,1024]{2,1,0:T(8,128)(2,1)S(1)}, bf16[2,512,1024]{2,1,0:T(8,128)(2,1)}, u32[]{:S(2)}) copy-start(bf16[2,512,1024]{2,1,0:T(8,128)(2,1)} %refs_4_.7) | copy-start | bytes 6291460
  21.2 44.3 %collective-permute-start.1 = (bf16[128,2176]{1,0:T(8,128)(2,1)S(1)}, bf16[128,2176]{1,0:T(8,128)(2,1)S(1)}, u32[]{:S(2)}, u32[]{:S(2)}) collective-permute-start(bf16[128,2176]{1,0:T(8,128)(2,1)S(1)} %bitcast.43), channel_id=1, source_target_pairs={{0,8},{4,12},{8,16},{12,20},{16,24},{20,28},{24,0},{28,4},{1,9},{5... | collective-permute-start | bytes 1671176 | tf_op jit(solution)/shard_map/ppermute | solution.py:25
  40.6 48.7 %collective-permute-start.4 = (bf16[512,1024]{1,0:T(8,128)(2,1)S(1)}, bf16[512,1024]{1,0:T(8,128)(2,1)S(1)}, u32[]{:S(2)}, u32[]{:S(2)}) collective-permute-start(bf16[512,1024]{1,0:T(8,128)(2,1)S(1)} %get-tuple-element.8), channel_id=1, source_target_pairs={{0,2},{1,3},{2,0},{3,1},{4,6},{5,7},{6,4},{7,5},{8,10},{9,11},{10,... | collective-permute-start | bytes 3145736 | tf_op jit(solution)/shard_map/ppermute | solution.py:15
  61.5 26.7 %copy-start.4 = (bf16[2,512,1024]{2,1,0:T(8,128)(2,1)}, bf16[2,512,1024]{2,1,0:T(8,128)(2,1)S(1)}, u32[]{:S(2)}) copy-start(bf16[2,512,1024]{2,1,0:T(8,128)(2,1)S(1)} %get-tuple-element.4) | copy-start | bytes 6291460
  61.5 28.0 %collective-permute-start.7 = (bf16[512,1024]{1,0:T(8,128)(2,1)S(1)}, bf16[512,1024]{1,0:T(8,128)(2,1)}, u32[]{:S(2)}, u32[]{:S(2)}) collective-permute-start(bf16[512,1024]{1,0:T(8,128)(2,1)S(1)} %get-tuple-element.5), channel_id=1, source_target_pairs={{0,2},{1,3},{2,0},{3,1},{4,6},{5,7},{6,4},{7,5},{8,10},{9,11},{10,... | collective-permute-start | bytes 3145736 | tf_op jit(solution)/shard_map/ppermute | solution.py:15
  63.3 24.4 %collective-permute-start.12 = (bf16[128,2176]{1,0:T(8,128)(2,1)S(1)}, bf16[128,2176]{1,0:T(8,128)(2,1)}, u32[]{:S(2)}, u32[]{:S(2)}) collective-permute-start(bf16[128,2176]{1,0:T(8,128)(2,1)S(1)} %bitcast.44), channel_id=1, source_target_pairs={{0,16},{4,20},{8,24},{12,28},{16,0},{20,4},{24,8},{28,12},{1,17},{... | collective-permute-start | bytes 1671176 | tf_op jit(solution)/shard_map/ppermute | solution.py:25
  64.1 23.8 %collective-permute-start.16 = (bf16[128,2176]{1,0:T(8,128)(2,1)S(1)}, bf16[128,2176]{1,0:T(8,128)(2,1)}, u32[]{:S(2)}, u32[]{:S(2)}) collective-permute-start(bf16[128,2176]{1,0:T(8,128)(2,1)S(1)} %bitcast.45), channel_id=1, source_target_pairs={{0,24},{4,28},{8,0},{12,4},{16,8},{20,12},{24,16},{28,20},{1,25},{... | collective-permute-start | bytes 1671176 | tf_op jit(solution)/shard_map/ppermute | solution.py:25
  65.5 22.7 %collective-permute-start.2 = (bf16[128,2176]{1,0:T(8,128)(2,1)S(1)}, bf16[128,2176]{1,0:T(8,128)(2,1)S(1)}, u32[]{:S(2)}, u32[]{:S(2)}) collective-permute-start(bf16[128,2176]{1,0:T(8,128)(2,1)S(1)} %collective-permute-done.1.a_ref), channel_id=1, source_target_pairs={{0,4},{4,0},{8,12},{12,8},{16,20},{20,16},{24,28},{28,24},{1,5},{5... | collective-permute-start | bytes 1671176 | tf_op jit(solution)/shard_map/ppermute | solution.py:15
  87.7 2.7 %collective-permute-start.3 = (bf16[512,1024]{1,0:T(8,128)(2,1)S(1)}, bf16[512,1024]{1,0:T(8,128)(2,1)S(1)}, u32[]{:S(2)}, u32[]{:S(2)}) collective-permute-start(bf16[512,1024]{1,0:T(8,128)(2,1)S(1)} %get-tuple-element.9), channel_id=1, source_target_pairs={{0,1},{1,0},{2,3},{3,2},{4,5},{5,4},{6,7},{7,6},{8,9},{9,8},{10,11... | collective-permute-start | bytes 3145736 | tf_op jit(solution)/shard_map/ppermute | solution.py:15
  88.0 11.3 %collective-permute-start.6 = (bf16[512,1024]{1,0:T(8,128)(2,1)S(1)}, bf16[512,1024]{1,0:T(8,128)(2,1)S(1)}, u32[]{:S(2)}, u32[]{:S(2)}) collective-permute-start(bf16[512,1024]{1,0:T(8,128)(2,1)S(1)} %get-tuple-element.6), channel_id=1, source_target_pairs={{0,1},{1,0},{2,3},{3,2},{4,5},{5,4},{6,7},{7,6},{8,9},{9,8},{10,11... | collective-permute-start | bytes 3145736 | tf_op jit(solution)/shard_map/ppermute | solution.py:15
  89.0 54.4 %collective-permute-start.10 = (bf16[2,512,1024]{2,1,0:T(8,128)(2,1)S(1)}, bf16[2,512,1024]{2,1,0:T(8,128)(2,1)}, u32[]{:S(2)}, u32[]{:S(2)}) collective-permute-start(bf16[2,512,1024]{2,1,0:T(8,128)(2,1)S(1)} %copy.24.refs_0_), channel_id=1, source_target_pairs={{0,1},{1,0},{2,3},{3,2},{4,5},{5,4},{6,7},{7,6},{8,9},{9,8},{10,11... | collective-permute-start | bytes 6291464 | tf_op jit(solution)/shard_map/ppermute | solution.py:15
  89.3 13.1 %collective-permute-start.5 = (bf16[512,1024]{1,0:T(8,128)(2,1)S(1)}, bf16[512,1024]{1,0:T(8,128)(2,1)}, u32[]{:S(2)}, u32[]{:S(2)}) collective-permute-start(bf16[512,1024]{1,0:T(8,128)(2,1)S(1)} %collective-permute-done.4.refs_2_), channel_id=1, source_target_pairs={{0,1},{1,0},{2,3},{3,2},{4,5},{5,4},{6,7},{7,6},{8,9},{9,8},{10,11... | collective-permute-start | bytes 3145736 | tf_op jit(solution)/shard_map/ppermute | solution.py:15
  89.5 16.4 %collective-permute-start.8 = (bf16[512,1024]{1,0:T(8,128)(2,1)}, bf16[512,1024]{1,0:T(8,128)(2,1)}, u32[]{:S(2)}, u32[]{:S(2)}) collective-permute-start(bf16[512,1024]{1,0:T(8,128)(2,1)} %collective-permute-done.7.refs_6_), channel_id=1, source_target_pairs={{0,1},{1,0},{2,3},{3,2},{4,5},{5,4},{6,7},{7,6},{8,9},{9,8},{10,11... | collective-permute-start | bytes 3145736 | tf_op jit(solution)/shard_map/ppermute | solution.py:15
  91.3 29.5 %collective-permute-start.13 = (bf16[128,2176]{1,0:T(8,128)(2,1)}, bf16[128,2176]{1,0:T(8,128)(2,1)}, u32[]{:S(2)}, u32[]{:S(2)}) collective-permute-start(bf16[128,2176]{1,0:T(8,128)(2,1)} %collective-permute-done.12.a_ref), channel_id=1, source_target_pairs={{0,4},{4,0},{8,12},{12,8},{16,20},{20,16},{24,28},{28,24},{1,5},{5... | collective-permute-start | bytes 1671176 | tf_op jit(solution)/shard_map/ppermute | solution.py:15
  100.3 27.1 %collective-permute-start.17 = (bf16[128,2176]{1,0:T(8,128)(2,1)}, bf16[128,2176]{1,0:T(8,128)(2,1)}, u32[]{:S(2)}, u32[]{:S(2)}) collective-permute-start(bf16[128,2176]{1,0:T(8,128)(2,1)} %collective-permute-done.16.a_ref), channel_id=1, source_target_pairs={{0,4},{4,0},{8,12},{12,8},{16,20},{20,16},{24,28},{28,24},{1,5},{5... | collective-permute-start | bytes 1671176 | tf_op jit(solution)/shard_map/ppermute | solution.py:15
  102.4 33.9 %collective-permute-start.20 = (bf16[128,2176]{1,0:T(8,128)(2,1)}, bf16[128,2176]{1,0:T(8,128)(2,1)S(1)}, u32[]{:S(2)}, u32[]{:S(2)}) collective-permute-start(bf16[128,2176]{1,0:T(8,128)(2,1)} %bitcast.46), channel_id=1, source_target_pairs={{0,4},{4,0},{8,12},{12,8},{16,20},{20,16},{24,28},{28,24},{1,5},{5... | collective-permute-start | bytes 1671176 | tf_op jit(solution)/shard_map/ppermute | solution.py:15
  119.3 24.2 %collective-permute-start.9 = (bf16[256,1024]{1,0:T(8,128)(2,1)S(1)}, bf16[256,1024]{1,0:T(8,128)(2,1)S(1)}, u32[]{:S(2)}, u32[]{:S(2)}) collective-permute-start(bf16[256,1024]{1,0:T(8,128)(2,1)S(1)} %shard_map.112.own_ref), channel_id=1, source_target_pairs={{0,2},{1,3},{2,0},{3,1},{4,6},{5,7},{6,4},{7,5},{8,10},{9,11},{10,... | collective-permute-start | bytes 1572872 | tf_op jit(solution)/shard_map/ppermute | solution.py:15
  126.8 9.5 %copy-start.11 = (bf16[2,64,2176]{2,1,0:T(8,128)(2,1)S(1)}, bf16[2,64,2176]{2,1,0:T(8,128)(2,1)}, u32[]{:S(2)}) copy-start(bf16[2,64,2176]{2,1,0:T(8,128)(2,1)} %copy-done.10) | copy-start | bytes 1671172
  126.8 33.0 %collective-permute-start.14 = (bf16[256,1024]{1,0:T(8,128)(2,1)S(1)}, bf16[256,1024]{1,0:T(8,128)(2,1)S(1)}, u32[]{:S(2)}, u32[]{:S(2)}) collective-permute-start(bf16[256,1024]{1,0:T(8,128)(2,1)S(1)} %shard_map.114.own_ref), channel_id=1, source_target_pairs={{0,2},{1,3},{2,0},{3,1},{4,6},{5,7},{6,4},{7,5},{8,10},{9,11},{10,... | collective-permute-start | bytes 1572872 | tf_op jit(solution)/shard_map/ppermute | solution.py:15
  133.4 29.5 %collective-permute-start.18 = (bf16[256,1024]{1,0:T(8,128)(2,1)S(1)}, bf16[256,1024]{1,0:T(8,128)(2,1)S(1)}, u32[]{:S(2)}, u32[]{:S(2)}) collective-permute-start(bf16[256,1024]{1,0:T(8,128)(2,1)S(1)} %shard_map.116.own_ref), channel_id=1, source_target_pairs={{0,2},{1,3},{2,0},{3,1},{4,6},{5,7},{6,4},{7,5},{8,10},{9,11},{10,... | collective-permute-start | bytes 1572872 | tf_op jit(solution)/shard_map/ppermute | solution.py:15
  141.9 28.8 %collective-permute-start.21 = (bf16[256,1024]{1,0:T(8,128)(2,1)S(1)}, bf16[256,1024]{1,0:T(8,128)(2,1)S(1)}, u32[]{:S(2)}, u32[]{:S(2)}) collective-permute-start(bf16[256,1024]{1,0:T(8,128)(2,1)S(1)} %shard_map.118.own_ref), channel_id=1, source_target_pairs={{0,2},{1,3},{2,0},{3,1},{4,6},{5,7},{6,4},{7,5},{8,10},{9,11},{10,... | collective-permute-start | bytes 1572872 | tf_op jit(solution)/shard_map/ppermute | solution.py:15
  146.4 27.2 %collective-permute-start.11 = (bf16[256,1024]{1,0:T(8,128)(2,1)S(1)}, bf16[256,1024]{1,0:T(8,128)(2,1)S(1)}, u32[]{:S(2)}, u32[]{:S(2)}) collective-permute-start(bf16[256,1024]{1,0:T(8,128)(2,1)S(1)} %shard_map.113), channel_id=1, source_target_pairs={{0,24},{4,28},{8,0},{12,4},{16,8},{20,12},{24,16},{28,20},{1,25},{... | collective-permute-start | bytes 1572872 | tf_op jit(solution)/shard_map/ppermute | solution.py:25
  162.8 41.4 %collective-permute-start.15 = (bf16[256,1024]{1,0:T(8,128)(2,1)S(1)}, bf16[256,1024]{1,0:T(8,128)(2,1)S(1)}, u32[]{:S(2)}, u32[]{:S(2)}) collective-permute-start(bf16[256,1024]{1,0:T(8,128)(2,1)S(1)} %shard_map.115), channel_id=1, source_target_pairs={{0,16},{4,20},{8,24},{12,28},{16,0},{20,4},{24,8},{28,12},{1,17},{... | collective-permute-start | bytes 1572872 | tf_op jit(solution)/shard_map/ppermute | solution.py:25
  165.8 38.4 %collective-permute-start.19 = (bf16[256,1024]{1,0:T(8,128)(2,1)S(1)}, bf16[256,1024]{1,0:T(8,128)(2,1)S(1)}, u32[]{:S(2)}, u32[]{:S(2)}) collective-permute-start(bf16[256,1024]{1,0:T(8,128)(2,1)S(1)} %shard_map.117), channel_id=1, source_target_pairs={{0,8},{4,12},{8,16},{12,20},{16,24},{20,28},{24,0},{28,4},{1,9},{5... | collective-permute-start | bytes 1572872 | tf_op jit(solution)/shard_map/ppermute | solution.py:25
  170.6 63.2 %collective-permute-start.26 = (bf16[512,1024]{1,0:T(8,128)(2,1)S(1)}, bf16[512,1024]{1,0:T(8,128)(2,1)S(1)}, u32[]{:S(2)}, u32[]{:S(2)}) collective-permute-start(bf16[512,1024]{1,0:T(8,128)(2,1)S(1)} %dynamic-slice_bitcast_fusion), channel_id=1, source_target_pairs={{0,4},{4,8},{8,12},{12,16},{16,20},{20,24},{24,28},{28,0},{1,5},{5... | collective-permute-start | bytes 3145736 | tf_op jit(solution)/shard_map/ppermute | solution.py:20
  204.6 28.5 %collective-permute-start.22 = (bf16[128,1024]{1,0:T(8,128)(2,1)S(1)}, bf16[128,1024]{1,0:T(8,128)(2,1)S(1)}, u32[]{:S(2)}, u32[]{:S(2)}) collective-permute-start(bf16[128,1024]{1,0:T(8,128)(2,1)S(1)} %slice.17), channel_id=1, source_target_pairs={{0,4},{4,0},{8,12},{12,8},{16,20},{20,16},{24,28},{28,24},{1,5},{5... | collective-permute-start | bytes 786440 | tf_op jit(solution)/shard_map/ppermute | solution.py:15
  233.1 5.0 %collective-permute-start.23 = (bf16[64,1024]{1,0:T(8,128)(2,1)S(1)}, bf16[64,1024]{1,0:T(8,128)(2,1)S(1)}, u32[]{:S(2)}, u32[]{:S(2)}) collective-permute-start(bf16[64,1024]{1,0:T(8,128)(2,1)S(1)} %get-tuple-element.10), channel_id=1, source_target_pairs={{0,2},{1,3},{2,0},{3,1},{4,6},{5,7},{6,4},{7,5},{8,10},{9,11},{10,... | collective-permute-start | bytes 393224 | tf_op jit(solution)/shard_map/ppermute | solution.py:15
  (16 other events, 41.8 us)

commit v3 on v2

v3 whole, which is shorter than its diff:
```python
import functools

import jax
import jax.numpy as jnp
from jax import lax
from jax.experimental import pallas as pl
from jax.experimental.pallas import tpu as pltpu
from jax.sharding import PartitionSpec as P

LANES = 128
VMEM_BYTES = 20 * 1024 * 1024
MOST = 56 * 1024 * 1024


def swap(x, axis, bit):
    return lax.ppermute(x, axis, [(i, i ^ bit) for i in range(lax.axis_size(axis))])


def passed_along(x, axis, by):
    size = lax.axis_size(axis)
    return lax.ppermute(x, axis, [(i, (i + by) % size) for i in range(size)])


def shift_z(x, by):
    size = lax.axis_size("dp")
    return lax.ppermute(x, "dp", [(i, (i + 2 * by) % size) for i in range(size)])


def in_order(second, own, other, axis=0):
    return jnp.where(
        second, jnp.stack([other, own], axis=axis), jnp.stack([own, other], axis=axis)
    )


def pick(w, index):
    return lax.dynamic_index_in_dim(w, index, 0, keepdims=False)


def spread(pieces, half):
    bit = 1
    while bit < half:
        pieces = pieces + [swap(p, "shard", bit) for p in pieces]
        bit *= 2
    return pieces


def params(amount=VMEM_BYTES):
    return pltpu.CompilerParams(vmem_limit_bytes=amount)


def first_kernel(
    meta, tokens_ref, probs_ref, ids_ref, place_ref, gate_ref, up_ref, out_ref, sent_ref, sems
):
    copies = [
        pltpu.make_async_copy(w.at[1 - meta[0]], sent_ref.at[i], sems.at[i])
        for i, w in enumerate((gate_ref, up_ref))
    ]
    for c in copies:
        c.start()
    probs = probs_ref[...]
    weights = (probs / jnp.sum(probs, axis=1, keepdims=True)).astype(jnp.bfloat16)
    weights = weights.astype(jnp.float32)
    ids = ids_ref[...]
    place = place_ref[...]
    coef = jnp.zeros((ids.shape[0], LANES), jnp.float32)
    for k in range(ids.shape[1]):
        coef += jnp.where(ids[:, k : k + 1] == place, weights[:, k : k + 1], 0.0)
    width = tokens_ref.shape[1]
    out_ref[:, :width] = tokens_ref[...]
    out_ref[:, width:] = coef.astype(jnp.bfloat16)
    for c in copies:
        c.wait()


def first(meta, tokens, probs, ids, old_place, w_gate, w_up):
    place = jnp.pad(old_place, (0, LANES - old_place.shape[0]), constant_values=-1)[None]
    vmem = pl.BlockSpec(memory_space=pltpu.VMEM)
    anywhere = pl.BlockSpec(memory_space=pltpu.HBM)
    return pl.pallas_call(
        first_kernel,
        in_specs=[pl.BlockSpec(memory_space=pltpu.SMEM)] + [vmem] * 4 + [anywhere] * 2,
        out_specs=(vmem, anywhere),
        out_shape=(
            jax.ShapeDtypeStruct((tokens.shape[0], tokens.shape[1] + LANES), tokens.dtype),
            jax.ShapeDtypeStruct((2,) + w_gate.shape[1:], w_gate.dtype),
        ),
        scratch_shapes=[pltpu.SemaphoreType.DMA((2,))],
        compiler_params=params(MOST),
    )(meta, tokens, probs, ids, place, w_gate, w_up)


def mine_kernel(meta, gate_ref, up_ref, mine_ref, sems):
    copies = [
        pltpu.make_async_copy(w.at[meta[0]], mine_ref.at[i], sems.at[i])
        for i, w in enumerate((gate_ref, up_ref))
    ]
    for c in copies:
        c.start()
    for c in copies:
        c.wait()


def mine_of(meta, w_gate, w_up):
    anywhere = pl.BlockSpec(memory_space=pltpu.HBM)
    return pl.pallas_call(
        mine_kernel,
        in_specs=[pl.BlockSpec(memory_space=pltpu.SMEM)] + [anywhere] * 2,
        out_specs=anywhere,
        out_shape=jax.ShapeDtypeStruct((2,) + w_gate.shape[1:], w_gate.dtype),
        scratch_shapes=[pltpu.SemaphoreType.DMA((2,))],
        compiler_params=params(MOST),
    )(meta, w_gate, w_up)


def leave_kernel(meta, gate_ref, up_ref, down_ref, after_ref, leave_ref, *refs):
    news, sems = refs[:3], refs[3]
    copies = []
    for i, w in enumerate((gate_ref, up_ref, down_ref)):
        copies.append((w.at[meta[1]], leave_ref.at[i]))
        copies.append((w.at[1 - meta[1]], news[i].at[1 - meta[1]]))
    copies = [pltpu.make_async_copy(a, b, sems.at[i]) for i, (a, b) in enumerate(copies)]
    for c in copies:
        c.start()
    for c in copies:
        c.wait()


def leave_of(meta, w_gate, w_up, w_down, after):
    anywhere = pl.BlockSpec(memory_space=pltpu.HBM)
    slot = w_gate.shape[1:]
    return pl.pallas_call(
        leave_kernel,
        in_specs=[pl.BlockSpec(memory_space=pltpu.SMEM)] + [anywhere] * 4,
        out_specs=(anywhere,) * 4,
        out_shape=(jax.ShapeDtypeStruct((3,) + slot, w_gate.dtype),)
        + (jax.ShapeDtypeStruct((2,) + slot, w_gate.dtype),) * 3,
        scratch_shapes=[pltpu.SemaphoreType.DMA((6,))],
        compiler_params=params(MOST),
    )(meta, w_gate, w_up, w_down, after)


def join_kernel(*refs):
    pass


def joined(x, after):
    anywhere = pl.BlockSpec(memory_space=pltpu.HBM)
    return pl.pallas_call(
        join_kernel,
        in_specs=[anywhere] * (1 + len(after)),
        out_specs=anywhere,
        out_shape=jax.ShapeDtypeStruct(x.shape, x.dtype),
        input_output_aliases={0: 0},
        compiler_params=params(),
    )(x, *after)


def refill_kernel(meta, arrive_ref, *refs):
    news, sems = refs[3:6], refs[6]
    copies = [
        pltpu.make_async_copy(arrive_ref.at[i], news[i].at[meta[1]], sems.at[i]) for i in range(3)
    ]
    for c in copies:
        c.start()
    for c in copies:
        c.wait()


def refill(meta, arrive, news):
    anywhere = pl.BlockSpec(memory_space=pltpu.HBM)
    return pl.pallas_call(
        refill_kernel,
        in_specs=[pl.BlockSpec(memory_space=pltpu.SMEM)] + [anywhere] * 4,
        out_specs=(anywhere,) * 3,
        out_shape=tuple(jax.ShapeDtypeStruct(w.shape, w.dtype) for w in news),
        input_output_aliases={2: 0, 3: 1, 4: 2},
        scratch_shapes=[pltpu.SemaphoreType.DMA((3,))],
        compiler_params=params(MOST),
    )(meta, arrive, *news)


def hidden_kernel(meta, a_ref, b_ref, mine_ref, *refs):
    others, out_ref = refs[:-1], refs[-1]
    half, _, depth, block = mine_ref.shape
    width = a_ref.shape[1] - LANES
    rows = a_ref.shape[0] + b_ref.shape[0]
    gate = jnp.zeros((rows, block), jnp.float32)
    up = jnp.zeros((rows, block), jnp.float32)
    for i in range(2 * half):
        columns = pl.ds(pl.multiple_of(meta[2 + i], LANES), depth)
        x = jnp.concatenate([a_ref[:, columns], b_ref[:, columns]], axis=0)
        w = mine_ref.at[i] if i < half else others[i - half]
        gate += jnp.dot(x, w[0], preferred_element_type=jnp.float32)
        up += jnp.dot(x, w[1], preferred_element_type=jnp.float32)
    coef = jnp.concatenate([a_ref[:, width:], b_ref[:, width:]], axis=0).astype(jnp.float32)
    lane = lax.broadcasted_iota(jnp.int32, coef.shape, 1)
    coef = jnp.sum(jnp.where(lane == meta[1], coef, 0.0), axis=1, keepdims=True)
    out_ref[...] = (gate / (1.0 + jnp.exp(-gate)) * up * coef).astype(out_ref.dtype)


def hidden_of(meta, a, b, mine, others):
    half, _, depth, ff = mine.shape
    block = 256
    rows = a.shape[0] + b.shape[0]

    def whole(x):
        return pl.BlockSpec(x.shape, lambda f, m: (0, 0))

    own = pl.BlockSpec((half, 2, depth, block), lambda f, m: (0, 0, 0, f))
    other = pl.BlockSpec((2, depth, block), lambda f, m: (0, 0, f))
    return pl.pallas_call(
        hidden_kernel,
        grid_spec=pltpu.PrefetchScalarGridSpec(
            num_scalar_prefetch=1,
            grid=(ff // block,),
            in_specs=[whole(a), whole(b), own] + [other] * half,
            out_specs=pl.BlockSpec((rows, block), lambda f, m: (0, f)),
        ),
        out_shape=jax.ShapeDtypeStruct((rows, ff), a.dtype),
        compiler_params=params(),
        cost_estimate=pl.CostEstimate(flops=0, bytes_accessed=0, transcendentals=0),
    )(meta, a, b, mine, *others)


def down_kernel(meta, own_ref, other_ref, downs_ref, out_ref):
    half, _, depth, _ = downs_ref.shape
    contract = (((1,), (1,)), ((), ()))
    own, other = own_ref[...], other_ref[...]
    for i in range(half):
        part = lax.dot_general(
            own, downs_ref[i, meta[0]], contract, preferred_element_type=jnp.float32
        ) + lax.dot_general(
            other, downs_ref[i, 1 - meta[0]], contract, preferred_element_type=jnp.float32
        )
        out_ref[:, i * depth : (i + 1) * depth] = part.astype(out_ref.dtype)


def down_of(meta, own, other, downs):
    half, _, depth, ff = downs.shape
    rows = own.shape[0]
    vmem = pl.BlockSpec(memory_space=pltpu.VMEM)
    return pl.pallas_call(
        down_kernel,
        in_specs=[pl.BlockSpec(memory_space=pltpu.SMEM)] + [vmem] * 3,
        out_specs=vmem,
        out_shape=jax.ShapeDtypeStruct((rows, half * depth), own.dtype),
        compiler_params=params(),
        cost_estimate=pl.CostEstimate(flops=0, bytes_accessed=0, transcendentals=0),
    )(meta, own, other, downs)


def local(tokens, router_probs, expert_ids, old_place, new_place, w_gate, w_up, w_down):
    tok = tokens.shape[0]
    width = tokens.shape[1]
    depth = w_gate.shape[1]
    n_shard = lax.axis_size("shard")
    half = n_shard // 2
    n_z = lax.axis_size("dp") // 2
    column = lax.axis_index("shard")
    row_id = lax.axis_index("dp")
    side = column // half
    place_in_side = column % half

    base_slot = 2 * row_id
    moved = (pick(old_place, base_slot + 1) != pick(new_place, base_slot + 1)).astype(jnp.int32)
    groups = [[g * half + j for j in range(half)] for g in range(2)]
    flipped = [(place_in_side ^ j) * depth for j in range(half)]
    straight = [jnp.int32(j * depth) for j in range(half)]
    meta_copy = jnp.stack([side, moved]).astype(jnp.int32)
    meta_hidden = jnp.stack(
        [side, base_slot + side]
        + [side * half * depth + s for s in straight]
        + [(1 - side) * half * depth + s for s in flipped]
    ).astype(jnp.int32)
    meta_down = side.reshape(1).astype(jnp.int32)

    own, sent = first(meta_copy, tokens, router_probs, expert_ids, old_place, w_gate, w_up)
    other = swap(own, "shard", half)
    both = in_order(side == 1, own, other).reshape(2 * tok, width + LANES)
    columns = [both] + [shift_z(both, s) for s in range(1, n_z)]
    pairs = [(c, swap(c, "dp", 1)) for c in columns]

    mine = mine_of(meta_copy, w_gate, w_up)
    mine = lax.all_gather(mine, "shard", axis_index_groups=groups)
    downs = lax.all_gather(w_down, "shard", axis_index_groups=groups)
    arrived = joined(swap(sent, "shard", half), columns[2:] + [pairs[0][1], pairs[1][1]])
    others = spread([arrived], half)
    leave, *news = leave_of(meta_copy, w_gate, w_up, w_down, other)

    total = None
    for s in list(range(1, n_z)) + [0]:
        hidden = hidden_of(meta_hidden, pairs[s][0], pairs[s][1], mine, others)
        hidden_other = swap(hidden, "shard", half)
        part = down_of(meta_down, hidden, hidden_other, downs)
        if s:
            part = shift_z(part, -s)
        part = part.astype(jnp.float32)
        total = part if total is None else total + part
    total = total.reshape(2, 2 * tok, width // 2)
    given = swap(total[1].astype(jnp.bfloat16), "dp", 1)
    total = (total[0] + given.astype(jnp.float32)).astype(jnp.bfloat16)
    total = total.reshape(2, tok, width // 2)
    kept = pick(total, side)
    arrived = swap(pick(total, 1 - side), "shard", half)
    moe_output = in_order(side == 1, kept, arrived, axis=1).reshape(tok, width)

    new_gate, new_up, new_down = refill(meta_copy, passed_along(leave, "dp", 1), news)
    return (moe_output, new_gate, new_up, new_down)


def solution(mesh):
    in_specs = (
        P(("dp", "shard"), None),
        P(("dp", "shard"), None),
        P(("dp", "shard"), None),
        P(),
        P(),
        P("dp", "shard", None),
        P("dp", "shard", None),
        P("dp", "shard", None),
    )
    out_specs = (
        P(("dp", "shard"), None),
        P("dp", "shard", None),
        P("dp", "shard", None),
        P("dp", "shard", None),
    )
    return jax.shard_map(local, mesh=mesh, in_specs=in_specs, out_specs=out_specs, check_vma=False)
```

time: 240 us -> 728 us (3.03); the launches traced: 239 us -> 718 us
  Pallas kernels: 35 us -> 455 us
  waiting for transfers between devices: 91.4 us -> 197 us
  starting transfers between devices: 83 us -> 37.1 us
  local copies, waits for them, and re-layouts: 26.6 us -> 12.7 us
  between operations: 2.23 us -> 15.6 us
    pallas_call x9 -> x13, Pallas kernels: 35 us -> 455 us  [the longest x1 192 us: leave_of(): pl.pallas_call(leave_kernel, in_specs=[pl.BlockSpec(memory_space=pltpu.SM...]
    ppermute x18 -> x13, waiting for transfers between devices: 13.9 us -> 149 us  [swap(): lax.ppermute(x, axis, [(i, i ^ bit) for i in range(lax.axis_size(axis))])]
    ppermute x3 -> x1, waiting for transfers between devices: 32.3 us -> 0.01 us  [passed_along(): return lax.ppermute(x, axis, [(i, (i + by) % size) for i in range(size)])]
    ppermute x18 -> x13, starting transfers between devices: 56.5 us -> 24.6 us  [swap(): lax.ppermute(x, axis, [(i, i ^ bit) for i in range(lax.axis_size(axis))])]
    ppermute x6, starting transfers between devices: 22 us -> 11 us  [shift_z(): lax.ppermute(x, 'dp', [(i, (i + 2 * by) % size) for i in range(size)])]
    unnamed x46 -> x32, local copies, waits for them, and re-layouts: 16.3 us -> 8.79 us
  transfers between devices with their start and end apart: 27 -> 22, of which waited for: 10 -> 9; matrix products, arithmetic and copies ran while one was open for 4% -> 0% of each run, Pallas kernels for 15% -> 54%
where the time goes in v3:
time: 728 us; the launch traced here: 718 us
  Pallas kernels  455 us (62%)
  waiting for transfers between devices  197 us (27%)
  starting transfers between devices  37.1 us (5%)
  between operations  15.6 us (2%)
  local copies, waits for them, and re-layouts  12.7 us (2%)
    pallas_call x1, Pallas kernels, leave_of(): pl.pallas_call(leave_kernel, in_specs=[pl.BlockSpec(memory_space=pltpu.SM...  192 us
    ppermute x13, waiting for transfers between devices, swap(): lax.ppermute(x, axis, [(i, i ^ bit) for i in range(lax.axis_size(axis))])  149 us
    pallas_call x1, Pallas kernels, refill(): pl.pallas_call(refill_kernel, in_specs=[pl.BlockSpec(memory_space=pltpu.S...  97.1 us
    pallas_call x1, Pallas kernels, first(): pl.pallas_call(first_kernel, in_specs=[pl.BlockSpec(memory_space=pltpu.SM...  66.3 us
    pallas_call x1, Pallas kernels, mine_of(): pl.pallas_call(mine_kernel, in_specs=[pl.BlockSpec(memory_space=pltpu.SME...  65.3 us
    ppermute x6, waiting for transfers between devices, shift_z(): lax.ppermute(x, 'dp', [(i, (i + 2 * by) % size) for i in range(size)])  47.5 us
    pallas_call x4, Pallas kernels, hidden_of(): pl.pallas_call(hidden_kernel, grid_spec=pltpu.PrefetchScalarGridSpec(num_...  25.1 us
    ppermute x13, starting transfers between devices, swap(): lax.ppermute(x, axis, [(i, i ^ bit) for i in range(lax.axis_size(axis))])  24.6 us
  transfers between devices with their start and end apart: 22, of which 9 were waited for; matrix products, arithmetic and copies ran while one was open for 0% of the time, Pallas kernels for 54%

profile of v3, /device:TPU:0, one launch (start us, length us, event | category | flops | bytes accessed | tf_op | source)
XLA Modules:
  0.0 718.5 jit_solution(5067579777875687386)
XLA Ops:
  11.7 65.3 %shard_map.112 = bf16[2,512,1024]{2,1,0:T(8,128)(2,1)} custom-call(s32[2]{0:T(128)} %pad_add_fusion.meta, bf16[2,512,1024]{2,1,0:T(8,128)(2,1)} %gate_ref.5, bf16[2,512,1024]{2,1,0:T(8,128)(2,1)} %up_ref.5), custom_call_target="tpu_custom_call" | custom-call | tf_op jit(solution)/shard_map/pallas_call | solution.py:105
  79.7 66.3 %shard_map.111 = (bf16[64,2176]{1,0:T(8,128)(2,1)}, bf16[2,512,1024]{2,1,0:T(8,128)(2,1)}) custom-call(s32[2]{0:T(128)} %pad_add_fusion.meta, bf16[64,2048]{1,0:T(8,128)(2,1)} %tokens_ref.1, f32[64,8]{1,0:T(8,128)} %copy.23.probs_ref, s32[64,8]{1,0:T(8,128)} %copy.24.ids_ref, s32[1,128]{1,0:T(1,128)} %pad_bitcast_fusion.place_ref, ...), custom_call_target="tpu_custom_call" | custom-call | tf_op jit(solution)/shard_map/pallas_call | solution.py:79
  146.0 3.0 collective-permute-start.3
  149.2 51.7 %collective-permute-done.after_ref = bf16[64,2176]{1,0:T(8,128)(2,1)S(1)} collective-permute-done((bf16[64,2176]{1,0:T(8,128)(2,1)}, bf16[64,2176]{1,0:T(8,128)(2,1)S(1)}, u32[]{:S(2)}, u32[]{:S(2)}) %collective-permute-start) | collective-permute-done | bytes 278560 | tf_op jit(solution)/shard_map/ppermute | solution.py:16
  201.0 1.9 collective-permute-start.1
  204.3 2.6 collective-permute-start.4
  209.1 9.5 %collective-permute-done.1.a_ref = bf16[128,2176]{1,0:T(8,128)(2,1)S(1)} collective-permute-done((bf16[128,2176]{1,0:T(8,128)(2,1)S(1)}, bf16[128,2176]{1,0:T(8,128)(2,1)S(1)}, u32[]{:S(2)}, u32[]{:S(2)}) %collective-permute-start.1) | collective-permute-done | bytes 557088 | tf_op jit(solution)/shard_map/ppermute | solution.py:26
  218.5 1.7 collective-permute-start.2
  221.0 19.6 %collective-permute-done.4.refs_1_.a_ref = bf16[128,2176]{1,0:T(8,128)(2,1)S(1)} collective-permute-done((bf16[128,2176]{1,0:T(8,128)(2,1)S(1)}, bf16[128,2176]{1,0:T(8,128)(2,1)S(1)}, u32[]{:S(2)}, u32[]{:S(2)}) %collective-permute-start.4) | collective-permute-done | bytes 557088 | tf_op jit(solution)/shard_map/ppermute | solution.py:26
  241.5 192.4 %shard_map.122 = (bf16[3,512,1024]{2,1,0:T(8,128)(2,1)}, bf16[2,512,1024]{2,1,0:T(8,128)(2,1)}, bf16[2,512,1024]{2,1,0:T(8,128)(2,1)}, bf16[2,512,1024]{2,1,0:T(8,128)(2,1)}) custom-call(s32[2]{0:T(128)} %pad_add_fusion.meta, bf16[2,512,1024]{2,1,0:T(8,128)(2,1)} %gate_ref.5, bf16[2,512,1024]{2,1,0:T(8,128)(2,1)} %up_ref.5, bf16[2,512,1024]{2,1,0:T(8,128)(2,1)} %down_ref.1, ...), custom_call_target="tpu_custom_call" | custom-call | tf_op jit(solution)/shard_map/pallas_call | solution.py:131
  433.9 1.5 collective-permute-start.19
  435.4 12.5 %collective-permute-start.13 = (bf16[128,2176]{1,0:T(8,128)(2,1)}, bf16[128,2176]{1,0:T(8,128)(2,1)}, u32[]{:S(2)}, u32[]{:S(2)}) collective-permute-start(bf16[128,2176]{1,0:T(8,128)(2,1)} %collective-permute-done.5.refs_2_.a_ref), channel_id=1, source_target_pairs={{0,4},{4,0},{8,12},{12,8},{16,20},{20,16},{24,28},{28,24},{1,5},{5... | collective-permute-start | bytes 1671176 | tf_op jit(solution)/shard_map/ppermute | solution.py:16
  448.0 81.0 %collective-permute-done.13.b_ref = bf16[128,2176]{1,0:T(8,128)(2,1)} collective-permute-done((bf16[128,2176]{1,0:T(8,128)(2,1)}, bf16[128,2176]{1,0:T(8,128)(2,1)}, u32[]{:S(2)}, u32[]{:S(2)}) %collective-permute-start.13) | collective-permute-done | bytes 557088 | tf_op jit(solution)/shard_map/ppermute | solution.py:16
  529.0 2.2 copy-done
  531.2 6.5 shard_map.118.own_ref
  540.6 6.4 shard_map.116.own_ref
  547.0 1.5 collective-permute-start.11
  548.5 6.6 shard_map.114.own_ref
  555.6 5.6 shard_map.120.own_ref
  561.1 1.6 collective-permute-start.16
  562.7 2.2 copy-done.2
  564.9 2.5 shard_map.119
  567.4 1.5 collective-permute-start.15
  568.9 2.5 shard_map.117
  571.4 1.6 collective-permute-start.12
  573.0 2.3 collective-permute-done.8.other_ref
  575.3 2.5 shard_map.115
  577.8 2.1 collective-permute-start.9
  579.9 4.9 collective-permute-done.16.other_ref
  586.1 18.4 %collective-permute-done.12 = bf16[256,1024]{1,0:T(8,128)(2,1)S(1)} collective-permute-done((bf16[256,1024]{1,0:T(8,128)(2,1)S(1)}, bf16[256,1024]{1,0:T(8,128)(2,1)S(1)}, u32[]{:S(2)}, u32[]{:S(2)}) %collective-permute-start.12) | collective-permute-done | bytes 524320 | tf_op jit(solution)/shard_map/ppermute | solution.py:26
  605.0 8.1 %collective-permute-done.17 = bf16[128,1024]{1,0:T(8,128)(2,1)S(1)} collective-permute-done((bf16[128,1024]{1,0:T(8,128)(2,1)S(1)}, bf16[128,1024]{1,0:T(8,128)(2,1)S(1)}, u32[]{:S(2)}, u32[]{:S(2)}) %collective-permute-start.17) | collective-permute-done | bytes 262176 | tf_op jit(solution)/shard_map/ppermute | solution.py:16
  613.8 97.1 %shard_map.123 = (bf16[2,512,1024]{2,1,0:T(8,128)(2,1)}, bf16[2,512,1024]{2,1,0:T(8,128)(2,1)}, bf16[2,512,1024]{2,1,0:T(8,128)(2,1)}) custom-call(s32[2]{0:T(128)} %pad_add_fusion.meta, bf16[3,512,1024]{2,1,0:T(8,128)(2,1)} %collective-permute-done.19.arrive_ref, ...), custom_call_target="tpu_custom_call", output_to_operand_aliasing={{0}: (2, {}), {1}: (3, {}), {2}: (4, {})} | custom-call | tf_op jit(solution)/shard_map/pallas_call | solution.py:171
  (71 shorter events, 17.8 us)
Async XLA Ops:
  7.2 521.9 %all-gather.5.cloned.1.call-start = ((), (), s32[]{:S(2)}) async-start(), calls=%async_computation | async-start | bytes 6291456 | tf_op jit(solution)/shard_map/all_gather | solution.py:284
  77.0 2.1 copy-start.14
  77.1 485.6 %all-gather.7.cloned.1.call-start = ((), (), s32[]{:S(2)}) async-start(), calls=%async_computation.1 | async-start | bytes 6291456 | tf_op jit(solution)/shard_map/all_gather | solution.py:285
  146.0 54.9 %copy-start.11 = (bf16[64,2176]{1,0:T(8,128)(2,1)S(1)}, bf16[64,2176]{1,0:T(8,128)(2,1)}, u32[]{:S(2)}) copy-start(bf16[64,2176]{1,0:T(8,128)(2,1)} %get-tuple-element.13) | copy-start | bytes 835588
  146.0 94.6 %collective-permute-start.3 = (bf16[2,512,1024]{2,1,0:T(8,128)(2,1)}, bf16[2,512,1024]{2,1,0:T(8,128)(2,1)S(1)}, u32[]{:S(2)}, u32[]{:S(2)}) collective-permute-start(bf16[2,512,1024]{2,1,0:T(8,128)(2,1)} %get-tuple-element.14), channel_id=1, source_target_pairs={{0,2},{1,3},{2,0},{3,1},{4,6},{5,7},{6,4},{7,5},{8,10},{9,11},{10,... | collective-permute-start | bytes 6291464 | tf_op jit(solution)/shard_map/ppermute | solution.py:16
  149.0 51.8 %collective-permute-start = (bf16[64,2176]{1,0:T(8,128)(2,1)}, bf16[64,2176]{1,0:T(8,128)(2,1)S(1)}, u32[]{:S(2)}, u32[]{:S(2)}) collective-permute-start(bf16[64,2176]{1,0:T(8,128)(2,1)} %get-tuple-element.13), channel_id=1, source_target_pairs={{0,2},{1,3},{2,0},{3,1},{4,6},{5,7},{6,4},{7,5},{8,10},{9,11},{10,... | collective-permute-start | bytes 835592 | tf_op jit(solution)/shard_map/ppermute | solution.py:16
  200.9 39.8 %copy-start.10 = (bf16[64,2176]{1,0:T(8,128)(2,1)}, bf16[64,2176]{1,0:T(8,128)(2,1)S(1)}, u32[]{:S(2)}) copy-start(bf16[64,2176]{1,0:T(8,128)(2,1)S(1)} %collective-permute-done.after_ref) | copy-start | bytes 835588
  201.0 17.6 %collective-permute-start.1 = (bf16[128,2176]{1,0:T(8,128)(2,1)S(1)}, bf16[128,2176]{1,0:T(8,128)(2,1)S(1)}, u32[]{:S(2)}, u32[]{:S(2)}) collective-permute-start(bf16[128,2176]{1,0:T(8,128)(2,1)S(1)} %bitcast.30), channel_id=1, source_target_pairs={{0,8},{4,12},{8,16},{12,20},{16,24},{20,28},{24,0},{28,4},{1,9},{5... | collective-permute-start | bytes 1671176 | tf_op jit(solution)/shard_map/ppermute | solution.py:26
  202.8 18.2 %collective-permute-start.6 = (bf16[128,2176]{1,0:T(8,128)(2,1)S(1)}, bf16[128,2176]{1,0:T(8,128)(2,1)S(1)}, u32[]{:S(2)}, u32[]{:S(2)}) collective-permute-start(bf16[128,2176]{1,0:T(8,128)(2,1)S(1)} %bitcast.31), channel_id=1, source_target_pairs={{0,4},{4,0},{8,12},{12,8},{16,20},{20,16},{24,28},{28,24},{1,5},{5... | collective-permute-start | bytes 1671176 | tf_op jit(solution)/shard_map/ppermute | solution.py:16
  204.3 36.3 %collective-permute-start.4 = (bf16[128,2176]{1,0:T(8,128)(2,1)S(1)}, bf16[128,2176]{1,0:T(8,128)(2,1)S(1)}, u32[]{:S(2)}, u32[]{:S(2)}) collective-permute-start(bf16[128,2176]{1,0:T(8,128)(2,1)S(1)} %bitcast.32), channel_id=1, source_target_pairs={{0,16},{4,20},{8,24},{12,28},{16,0},{20,4},{24,8},{28,12},{1,17},{... | collective-permute-start | bytes 1671176 | tf_op jit(solution)/shard_map/ppermute | solution.py:26
  206.9 33.7 %collective-permute-start.5 = (bf16[128,2176]{1,0:T(8,128)(2,1)S(1)}, bf16[128,2176]{1,0:T(8,128)(2,1)}, u32[]{:S(2)}, u32[]{:S(2)}) collective-permute-start(bf16[128,2176]{1,0:T(8,128)(2,1)S(1)} %bitcast.33), channel_id=1, source_target_pairs={{0,24},{4,28},{8,0},{12,4},{16,8},{20,12},{24,16},{28,20},{1,25},{... | collective-permute-start | bytes 1671176 | tf_op jit(solution)/shard_map/ppermute | solution.py:26
  218.5 22.1 %collective-permute-start.2 = (bf16[128,2176]{1,0:T(8,128)(2,1)S(1)}, bf16[128,2176]{1,0:T(8,128)(2,1)S(1)}, u32[]{:S(2)}, u32[]{:S(2)}) collective-permute-start(bf16[128,2176]{1,0:T(8,128)(2,1)S(1)} %collective-permute-done.1.a_ref), channel_id=1, source_target_pairs={{0,4},{4,0},{8,12},{12,8},{16,20},{20,16},{24,28},{28,24},{1,5},{5... | collective-permute-start | bytes 1671176 | tf_op jit(solution)/shard_map/ppermute | solution.py:16
  241.5 287.6 %collective-permute-start.7 = (bf16[2,512,1024]{2,1,0:T(8,128)(2,1)S(1)}, bf16[2,512,1024]{2,1,0:T(8,128)(2,1)}, u32[]{:S(2)}, u32[]{:S(2)}) collective-permute-start(bf16[2,512,1024]{2,1,0:T(8,128)(2,1)S(1)} %shard_map.113.refs_0_), channel_id=1, source_target_pairs={{0,1},{1,0},{2,3},{3,2},{4,5},{5,4},{6,7},{7,6},{8,9},{9,8},{10,11... | collective-permute-start | bytes 6291464 | tf_op jit(solution)/shard_map/ppermute | solution.py:16
  433.9 179.9 %collective-permute-start.19 = (bf16[3,512,1024]{2,1,0:T(8,128)(2,1)}, bf16[3,512,1024]{2,1,0:T(8,128)(2,1)}, u32[]{:S(2)}, u32[]{:S(2)}) collective-permute-start(bf16[3,512,1024]{2,1,0:T(8,128)(2,1)} %get-tuple-element.15), channel_id=1, source_target_pairs={{0,4},{4,8},{8,12},{12,16},{16,20},{20,24},{24,28},{28,0},{1,5},{5... | collective-permute-start | bytes 9437192 | tf_op jit(solution)/shard_map/ppermute | solution.py:21
  435.4 93.7 %collective-permute-start.13 = (bf16[128,2176]{1,0:T(8,128)(2,1)}, bf16[128,2176]{1,0:T(8,128)(2,1)}, u32[]{:S(2)}, u32[]{:S(2)}) collective-permute-start(bf16[128,2176]{1,0:T(8,128)(2,1)} %collective-permute-done.5.refs_2_.a_ref), channel_id=1, source_target_pairs={{0,4},{4,0},{8,12},{12,8},{16,20},{20,16},{24,28},{28,24},{1,5},{5... | collective-permute-start | bytes 1671176 | tf_op jit(solution)/shard_map/ppermute | solution.py:16
  447.9 92.7 %collective-permute-start.10 = (bf16[128,2176]{1,0:T(8,128)(2,1)S(1)}, bf16[128,2176]{1,0:T(8,128)(2,1)}, u32[]{:S(2)}, u32[]{:S(2)}) collective-permute-start(bf16[128,2176]{1,0:T(8,128)(2,1)S(1)} %collective-permute-done.4.refs_1_.a_ref), channel_id=1, source_target_pairs={{0,4},{4,0},{8,12},{12,8},{16,20},{20,16},{24,28},{28,24},{1,5},{5... | collective-permute-start | bytes 1671176 | tf_op jit(solution)/shard_map/ppermute | solution.py:16
  529.0 2.2 copy-start
  537.8 10.7 %copy-start.5 = (bf16[128,2176]{1,0:T(8,128)(2,1)S(1)}, bf16[128,2176]{1,0:T(8,128)(2,1)}, u32[]{:S(2)}) copy-start(bf16[128,2176]{1,0:T(8,128)(2,1)} %copy-done.4) | copy-start | bytes 1671172
  537.8 10.7 %copy-start.9 = (bf16[128,2176]{1,0:T(8,128)(2,1)S(1)}, bf16[128,2176]{1,0:T(8,128)(2,1)}, u32[]{:S(2)}) copy-start(bf16[128,2176]{1,0:T(8,128)(2,1)} %copy-done.8) | copy-start | bytes 1671172
  537.8 24.9 %collective-permute-start.14 = (bf16[256,1024]{1,0:T(8,128)(2,1)}, bf16[256,1024]{1,0:T(8,128)(2,1)}, u32[]{:S(2)}, u32[]{:S(2)}) collective-permute-start(bf16[256,1024]{1,0:T(8,128)(2,1)} %shard_map.118.own_ref), channel_id=1, source_target_pairs={{0,2},{1,3},{2,0},{3,1},{4,6},{5,7},{6,4},{7,5},{8,10},{9,11},{10,... | collective-permute-start | bytes 1572872 | tf_op jit(solution)/shard_map/ppermute | solution.py:16
  547.0 8.6 %copy-start.7 = (bf16[2,64,2176]{2,1,0:T(8,128)(2,1)S(1)}, bf16[2,64,2176]{2,1,0:T(8,128)(2,1)}, u32[]{:S(2)}) copy-start(bf16[2,64,2176]{2,1,0:T(8,128)(2,1)} %copy-done.6) | copy-start | bytes 1671172
  547.0 21.9 %collective-permute-start.11 = (bf16[256,1024]{1,0:T(8,128)(2,1)}, bf16[256,1024]{1,0:T(8,128)(2,1)}, u32[]{:S(2)}, u32[]{:S(2)}) collective-permute-start(bf16[256,1024]{1,0:T(8,128)(2,1)} %shard_map.116.own_ref), channel_id=1, source_target_pairs={{0,2},{1,3},{2,0},{3,1},{4,6},{5,7},{6,4},{7,5},{8,10},{9,11},{10,... | collective-permute-start | bytes 1572872 | tf_op jit(solution)/shard_map/ppermute | solution.py:16
  548.5 7.1 copy-start.1
  555.0 20.3 %collective-permute-start.8 = (bf16[256,1024]{1,0:T(8,128)(2,1)}, bf16[256,1024]{1,0:T(8,128)(2,1)}, u32[]{:S(2)}, u32[]{:S(2)}) collective-permute-start(bf16[256,1024]{1,0:T(8,128)(2,1)} %shard_map.114.own_ref), channel_id=1, source_target_pairs={{0,2},{1,3},{2,0},{3,1},{4,6},{5,7},{6,4},{7,5},{8,10},{9,11},{10,... | collective-permute-start | bytes 1572872 | tf_op jit(solution)/shard_map/ppermute | solution.py:16
  561.1 23.7 %collective-permute-start.16 = (bf16[256,1024]{1,0:T(8,128)(2,1)S(1)}, bf16[256,1024]{1,0:T(8,128)(2,1)S(1)}, u32[]{:S(2)}, u32[]{:S(2)}) collective-permute-start(bf16[256,1024]{1,0:T(8,128)(2,1)S(1)} %shard_map.120.own_ref), channel_id=1, source_target_pairs={{0,2},{1,3},{2,0},{3,1},{4,6},{5,7},{6,4},{7,5},{8,10},{9,11},{10,... | collective-permute-start | bytes 1572872 | tf_op jit(solution)/shard_map/ppermute | solution.py:16
  562.7 2.2 copy-start.2
  567.4 18.8 %collective-permute-start.15 = (bf16[256,1024]{1,0:T(8,128)(2,1)S(1)}, bf16[256,1024]{1,0:T(8,128)(2,1)S(1)}, u32[]{:S(2)}, u32[]{:S(2)}) collective-permute-start(bf16[256,1024]{1,0:T(8,128)(2,1)S(1)} %shard_map.119), channel_id=1, source_target_pairs={{0,8},{4,12},{8,16},{12,20},{16,24},{20,28},{24,0},{28,4},{1,9},{5... | collective-permute-start | bytes 1572872 | tf_op jit(solution)/shard_map/ppermute | solution.py:26
  571.4 13.5 %copy-start.3 = (bf16[4,512,1024]{2,1,0:T(8,128)(2,1)S(1)}, bf16[4,512,1024]{2,1,0:T(8,128)(2,1)}, u32[]{:S(2)}) copy-start(bf16[4,512,1024]{2,1,0:T(8,128)(2,1)} %all-gather.7.cloned.1.call-done) | copy-start | bytes 12582916
  571.4 33.1 %collective-permute-start.12 = (bf16[256,1024]{1,0:T(8,128)(2,1)S(1)}, bf16[256,1024]{1,0:T(8,128)(2,1)S(1)}, u32[]{:S(2)}, u32[]{:S(2)}) collective-permute-start(bf16[256,1024]{1,0:T(8,128)(2,1)S(1)} %shard_map.117), channel_id=1, source_target_pairs={{0,16},{4,20},{8,24},{12,28},{16,0},{20,4},{24,8},{28,12},{1,17},{... | collective-permute-start | bytes 1572872 | tf_op jit(solution)/shard_map/ppermute | solution.py:26
  577.8 26.8 %collective-permute-start.9 = (bf16[256,1024]{1,0:T(8,128)(2,1)S(1)}, bf16[256,1024]{1,0:T(8,128)(2,1)S(1)}, u32[]{:S(2)}, u32[]{:S(2)}) collective-permute-start(bf16[256,1024]{1,0:T(8,128)(2,1)S(1)} %shard_map.115), channel_id=1, source_target_pairs={{0,24},{4,28},{8,0},{12,4},{16,8},{20,12},{24,16},{28,20},{1,25},{... | collective-permute-start | bytes 1572872 | tf_op jit(solution)/shard_map/ppermute | solution.py:26
  604.9 8.2 %collective-permute-start.17 = (bf16[128,1024]{1,0:T(8,128)(2,1)S(1)}, bf16[128,1024]{1,0:T(8,128)(2,1)S(1)}, u32[]{:S(2)}, u32[]{:S(2)}) collective-permute-start(bf16[128,1024]{1,0:T(8,128)(2,1)S(1)} %slice.17), channel_id=1, source_target_pairs={{0,4},{4,0},{8,12},{12,8},{16,20},{20,16},{24,28},{28,24},{1,5},{5... | collective-permute-start | bytes 786440 | tf_op jit(solution)/shard_map/ppermute | solution.py:16
  613.2 97.7 %collective-permute-start.18 = (bf16[64,1024]{1,0:T(8,128)(2,1)S(1)}, bf16[64,1024]{1,0:T(8,128)(2,1)S(1)}, u32[]{:S(2)}, u32[]{:S(2)}) collective-permute-start(bf16[64,1024]{1,0:T(8,128)(2,1)S(1)} %get-tuple-element.22), channel_id=1, source_target_pairs={{0,2},{1,3},{2,0},{3,1},{4,6},{5,7},{6,4},{7,5},{8,10},{9,11},{10,... | collective-permute-start | bytes 393224 | tf_op jit(solution)/shard_map/ppermute | solution.py:16
  (5 other events, 4.5 us)
Sparse Core Ops, SparseCore 0:
  77.2 16.3 all-gather.4
  149.3 15.3 all-gather.6

commit v4 on v3

v4 whole, which is shorter than its diff:
```python
import functools

import jax
import jax.numpy as jnp
from jax import lax
from jax.experimental import pallas as pl
from jax.experimental.pallas import tpu as pltpu
from jax.sharding import PartitionSpec as P

LANES = 128
GROUP = 2
VMEM_BYTES = 20 * 1024 * 1024
MOST = 56 * 1024 * 1024
NOTHING = pl.CostEstimate(flops=0, bytes_accessed=0, transcendentals=0)


def swap(x, axis, bit):
    return lax.ppermute(x, axis, [(i, i ^ bit) for i in range(lax.axis_size(axis))])


def passed_along(x, axis, by):
    size = lax.axis_size(axis)
    return lax.ppermute(x, axis, [(i, (i + by) % size) for i in range(size)])


def shift_z(x, by):
    size = lax.axis_size("dp")
    return lax.ppermute(x, "dp", [(i, (i + 2 * by) % size) for i in range(size)])


def in_order(second, own, other, axis=0):
    return jnp.where(
        second, jnp.stack([other, own], axis=axis), jnp.stack([own, other], axis=axis)
    )


def spread(pieces, half):
    bit = 1
    while bit < half:
        pieces = pieces + [swap(p, "shard", bit) for p in pieces]
        bit *= 2
    return pieces


def params(amount=VMEM_BYTES):
    return pltpu.CompilerParams(vmem_limit_bytes=amount)


def position():
    half = lax.axis_size("shard") // 2
    column = lax.axis_index("shard")
    return lax.div(column, half), lax.rem(column, half), lax.axis_index("dp")


def first_kernel(tokens_ref, probs_ref, ids_ref, place_ref, out_ref, coef_ref):
    probs = probs_ref[...]
    weights = (probs / jnp.sum(probs, axis=0, keepdims=True)).astype(jnp.bfloat16)
    weights = weights.astype(jnp.float32)
    ids = ids_ref[...]
    tok, width = tokens_ref.shape
    coef_ref[...] = jnp.zeros_like(coef_ref)
    for slot in range(place_ref.shape[0]):
        named = jnp.where(ids == place_ref[slot], weights, 0.0)
        coef_ref[slot : slot + 1, :tok] = jnp.sum(named, axis=0, keepdims=True)
    out_ref[:, :width] = tokens_ref[...]
    out_ref[:, width:] = jnp.transpose(coef_ref[...])[:tok].astype(jnp.bfloat16)


def first(tokens, probs, ids, old_place):
    vmem = pl.BlockSpec(memory_space=pltpu.VMEM)
    return pl.pallas_call(
        first_kernel,
        in_specs=[vmem] * 3 + [pl.BlockSpec(memory_space=pltpu.SMEM)],
        out_specs=vmem,
        out_shape=jax.ShapeDtypeStruct((tokens.shape[0], tokens.shape[1] + LANES), tokens.dtype),
        scratch_shapes=[pltpu.VMEM((LANES, LANES), jnp.float32)],
        compiler_params=params(),
        cost_estimate=NOTHING,
    )(tokens, probs.T, ids.T, old_place)


def copy_kernel(plan, n_in, n_out, *refs):
    old_ref, new_ref = refs[:2]
    ins, refs = refs[2 : 2 + n_in], refs[-n_out - 3 :]
    outs, (held, in_sems, out_sems) = refs[:n_out], refs[n_out:]
    side, _, row = position()
    second = 2 * row + 1
    moved = (old_ref[second] != new_ref[second]).astype(jnp.int32)
    slots = {"mine": side, "theirs": 1 - side, "leaves": moved, "stays": 1 - moved}
    slots.update({i: i for i in range(3)})
    loads = [
        pltpu.make_async_copy(ins[i].at[slots[a]], held.at[n], in_sems.at[n])
        for n, (i, a, o, b) in enumerate(plan)
    ]
    stores = [
        pltpu.make_async_copy(held.at[n], outs[o].at[slots[b]], out_sems.at[n])
        for n, (i, a, o, b) in enumerate(plan)
    ]
    for c in loads:
        c.start()
    for n, c in enumerate(stores):
        loads[n].wait()
        c.start()
    for c in stores:
        c.wait()


def copies(plan, places, ins, counts, after=(), aliases=()):
    slot, kind = ins[0].shape[1:], ins[0].dtype
    smem, anywhere = pl.BlockSpec(memory_space=pltpu.SMEM), pl.BlockSpec(memory_space=pl.ANY)
    return pl.pallas_call(
        functools.partial(copy_kernel, plan, len(ins), len(counts)),
        in_specs=[smem] * 2 + [anywhere] * (len(ins) + len(aliases) + len(after)),
        out_specs=(anywhere,) * len(counts),
        out_shape=tuple(jax.ShapeDtypeStruct((n,) + slot, kind) for n in counts),
        input_output_aliases={2 + len(ins) + i: i for i in range(len(aliases))},
        scratch_shapes=[
            pltpu.VMEM((len(plan),) + slot, kind),
            pltpu.SemaphoreType.DMA((len(plan),)),
            pltpu.SemaphoreType.DMA((len(plan),)),
        ],
        compiler_params=params(MOST),
        cost_estimate=NOTHING,
    )(*places, *ins, *aliases, *after)


def join_kernel(*refs):
    pass


def joined(x, after):
    anywhere = pl.BlockSpec(memory_space=pl.ANY)
    return pl.pallas_call(
        join_kernel,
        in_specs=[anywhere] * (1 + len(after)),
        out_specs=anywhere,
        out_shape=jax.ShapeDtypeStruct(x.shape, x.dtype),
        input_output_aliases={0: 0},
        compiler_params=params(),
    )(x, *after)


def refill_kernel(meta, arrive_ref, *refs):
    news, sems = refs[3:6], refs[6]
    copies = [
        pltpu.make_async_copy(arrive_ref.at[i], news[i].at[meta[1]], sems.at[i]) for i in range(3)
    ]
    for c in copies:
        c.start()
    for c in copies:
        c.wait()


def refill(meta, arrive, news):
    anywhere = pl.BlockSpec(memory_space=pl.ANY)
    return pl.pallas_call(
        refill_kernel,
        in_specs=[pl.BlockSpec(memory_space=pltpu.SMEM)] + [anywhere] * 4,
        out_specs=(anywhere,) * 3,
        out_shape=tuple(jax.ShapeDtypeStruct(w.shape, w.dtype) for w in news),
        input_output_aliases={2: 0, 3: 1, 4: 2},
        scratch_shapes=[pltpu.SemaphoreType.DMA((3,))],
        compiler_params=params(MOST),
    )(meta, arrive, *news)


def hidden_kernel(n_pieces, *refs):
    pieces, mine_ref, others, out_ref = (
        refs[:n_pieces], refs[n_pieces], refs[n_pieces + 1 : -1], refs[-1],
    )
    half, _, depth, block = mine_ref.shape
    width = pieces[0].shape[1] - LANES
    rows = out_ref.shape[0]
    gate = jnp.zeros((rows, block), jnp.float32)
    up = jnp.zeros((rows, block), jnp.float32)
    side, place, row = position()
    for i in range(2 * half):
        if i < half:
            start = (side * half + i) * depth
        else:
            start = ((1 - side) * half + (place ^ (i - half))) * depth
        columns = pl.ds(pl.multiple_of(start, LANES), depth)
        x = jnp.concatenate([p[:, columns] for p in pieces], axis=0)
        w = mine_ref.at[i] if i < half else others[i - half]
        gate += jnp.dot(x, w[0], preferred_element_type=jnp.float32)
        up += jnp.dot(x, w[1], preferred_element_type=jnp.float32)
    coef = jnp.concatenate([p[:, width:] for p in pieces], axis=0).astype(jnp.float32)
    lane = lax.broadcasted_iota(jnp.int32, coef.shape, 1)
    coef = jnp.sum(jnp.where(lane == 2 * row + side, coef, 0.0), axis=1, keepdims=True)
    out_ref[...] = (gate / (1.0 + jnp.exp(-gate)) * up * coef).astype(out_ref.dtype)


def hidden_of(pieces, mine, others):
    half, _, depth, ff = mine.shape
    block = 256
    rows = sum(p.shape[0] for p in pieces)
    piece = pl.BlockSpec(pieces[0].shape, lambda f: (0, 0))
    own = pl.BlockSpec((half, 2, depth, block), lambda f: (0, 0, 0, f))
    other = pl.BlockSpec((2, depth, block), lambda f: (0, 0, f))
    return pl.pallas_call(
        functools.partial(hidden_kernel, len(pieces)),
        grid=(ff // block,),
        in_specs=[piece] * len(pieces) + [own] + [other] * half,
        out_specs=pl.BlockSpec((rows, block), lambda f: (0, f)),
        out_shape=jax.ShapeDtypeStruct((rows, ff), pieces[0].dtype),
        compiler_params=params(),
        cost_estimate=NOTHING,
    )(*pieces, mine, *others)


def down_kernel(own_ref, other_ref, downs_ref, *outs):
    half, _, depth, _ = downs_ref.shape
    contract = (((1,), (1,)), ((), ()))
    own, other = own_ref[...], other_ref[...]
    side = position()[0]
    rows = outs[0].shape[0]
    for i in range(half):
        part = lax.dot_general(
            own, downs_ref[i, side], contract, preferred_element_type=jnp.float32
        ) + lax.dot_general(
            other, downs_ref[i, 1 - side], contract, preferred_element_type=jnp.float32
        )
        part = part.astype(outs[0].dtype)
        for n, out in enumerate(outs):
            out[:, i * depth : (i + 1) * depth] = part[n * rows : (n + 1) * rows]


def down_of(own, other, downs):
    half, _, depth, ff = downs.shape
    rows = own.shape[0] // GROUP
    vmem = pl.BlockSpec(memory_space=pltpu.VMEM)
    return pl.pallas_call(
        down_kernel,
        in_specs=[vmem] * 3,
        out_specs=(vmem,) * GROUP,
        out_shape=(jax.ShapeDtypeStruct((rows, half * depth), own.dtype),) * GROUP,
        compiler_params=params(),
        cost_estimate=NOTHING,
    )(own, other, downs)


def local(tokens, router_probs, expert_ids, old_place, new_place, w_gate, w_up, w_down):
    tok, width = tokens.shape
    half = lax.axis_size("shard") // 2
    n_z = lax.axis_size("dp") // 2
    side = lax.axis_index("shard") // half
    groups = [[g * half + j for j in range(half)] for g in range(2)]
    places = (old_place, new_place)

    own = first(tokens, router_probs, expert_ids, old_place)
    sent, leave_gate = copies(
        ((0, "theirs", 0, 0), (1, "theirs", 0, 1), (0, "leaves", 1, 0)),
        places, (w_gate, w_up), (2, 1), (own,),
    )
    other = swap(own, "shard", half)
    both = in_order(side == 1, own, other).reshape(2 * tok, width + LANES)
    columns = [both] + [shift_z(both, s) for s in range(1, n_z)]
    arrive_gate = passed_along(leave_gate, "dp", 1)
    pairs = [(c, swap(joined(c, [arrive_gate]) if i == 0 else c, "dp", 1))
             for i, c in enumerate(columns)]

    (mine,) = copies(((0, "mine", 0, 0), (1, "mine", 0, 1)), places, (w_gate, w_up), (2,), (own,))
    mine = lax.all_gather(mine, "shard", axis_index_groups=groups)
    downs = lax.all_gather(w_down, "shard", axis_index_groups=groups)
    arrived = joined(
        swap(joined(sent, [other]), "shard", half), columns[2:] + [p[1] for p in pairs[:3]]
    )
    others = spread([arrived], half)

    leave, *news = copies(
        tuple((i, "leaves", 0, i - 1) for i in (1, 2))
        + tuple((i, "stays", i + 1, "stays") for i in range(3)),
        places, (w_gate, w_up, w_down), (2, 2, 2, 2), (pairs[-1][1],),
    )
    arrive = (arrive_gate, passed_along(leave, "dp", 1))

    total = None
    order = list(range(1, n_z)) + [0]
    groups = [order[i : i + GROUP] for i in range(0, n_z, GROUP)]
    hiddens = [hidden_of([p for s in g for p in pairs[s]], mine, others) for g in groups]
    for g, hidden in zip(groups, hiddens):
        parts = down_of(hidden, swap(hidden, "shard", half), downs)
        for s, part in zip(g, parts):
            part = (shift_z(part, -s) if s else part).astype(jnp.float32)
            total = part if total is None else total + part
    total = total.reshape(2, 2 * tok, width // 2)
    given = swap(total[1].astype(jnp.bfloat16), "dp", 1)
    total = (total[0] + given.astype(jnp.float32)).astype(jnp.bfloat16)
    total = total.reshape(2, tok, width // 2)
    kept = jnp.where(side == 1, total[1], total[0])
    arrived = swap(jnp.where(side == 1, total[0], total[1]), "shard", half)
    moe_output = in_order(side == 1, kept, arrived, axis=1).reshape(tok, width)

    news = copies(
        ((0, 0, 0, "leaves"), (1, 0, 1, "leaves"), (1, 1, 2, "leaves")),
        places, arrive, (2, 2, 2), (), news,
    )
    return (moe_output, *news)


def solution(mesh):
    in_specs = (
        P(("dp", "shard"), None),
        P(("dp", "shard"), None),
        P(("dp", "shard"), None),
        P(),
        P(),
        P("dp", "shard", None),
        P("dp", "shard", None),
        P("dp", "shard", None),
    )
    out_specs = (
        P(("dp", "shard"), None),
        P("dp", "shard", None),
        P("dp", "shard", None),
        P("dp", "shard", None),
    )
    return jax.shard_map(local, mesh=mesh, in_specs=in_specs, out_specs=out_specs, check_vma=False)
```

time: 728 us -> 285 us (0.39); the launches traced: 718 us -> 284 us
  Pallas kernels: 455 us -> 37.6 us
  waiting for transfers between devices: 197 us -> 149 us
  starting transfers between devices: 37.1 us -> 70.5 us
    pallas_call x12 -> x9, Pallas kernels: 455 us -> 37.6 us  [the longest x4 15.5 us: copies(): pl.pallas_call(functools.partial(copy_kernel, plan, len(ins), len(counts)...]
    ppermute x13 -> x11, waiting for transfers between devices: 149 us -> 83.2 us  [swap(): lax.ppermute(x, axis, [(i, i ^ bit) for i in range(lax.axis_size(axis))])]
    ppermute x13 -> x11, starting transfers between devices: 24.6 us -> 60.5 us  [swap(): lax.ppermute(x, axis, [(i, i ^ bit) for i in range(lax.axis_size(axis))])]
    ppermute x6, waiting for transfers between devices: 47.5 us -> 65.3 us  [shift_z(): lax.ppermute(x, 'dp', [(i, (i + 2 * by) % size) for i in range(size)])]
  transfers between devices with their start and end apart: 22 -> 21, of which waited for: 9 -> 12; matrix products, arithmetic and copies ran while one was open for 0% -> 0% of each run, Pallas kernels for 54% -> 12%
where the time goes in v4:
time: 285 us; the launch traced here: 284 us
  waiting for transfers between devices  149 us (52%)
  starting transfers between devices  70.5 us (25%)
  Pallas kernels  37.6 us (13%)
  between operations  14.3 us (5%)
  local copies, waits for them, and re-layouts  12.9 us (5%)
    ppermute x11, waiting for transfers between devices, swap(): lax.ppermute(x, axis, [(i, i ^ bit) for i in range(lax.axis_size(axis))])  83.2 us
    ppermute x6, waiting for transfers between devices, shift_z(): lax.ppermute(x, 'dp', [(i, (i + 2 * by) % size) for i in range(size)])  65.3 us
    ppermute x11, starting transfers between devices, swap(): lax.ppermute(x, axis, [(i, i ^ bit) for i in range(lax.axis_size(axis))])  60.5 us
    pallas_call x4, Pallas kernels, copies(): pl.pallas_call(functools.partial(copy_kernel, plan, len(ins), len(counts)...  15.5 us
    pallas_call x2, Pallas kernels, hidden_of(): pl.pallas_call(functools.partial(hidden_kernel, len(pieces)), grid=(ff //...  15 us
    unnamed x45, local copies, waits for them, and re-layouts  12.1 us
    ppermute x6, starting transfers between devices, shift_z(): lax.ppermute(x, 'dp', [(i, (i + 2 * by) % size) for i in range(size)])  6.72 us
    pallas_call x2, Pallas kernels, down_of(): pl.pallas_call(down_kernel, in_specs=[vmem] * 3, out_specs=(vmem,) * GROU...  6.42 us
  transfers between devices with their start and end apart: 21, of which 12 were waited for; matrix products, arithmetic and copies ran while one was open for 0% of the time, Pallas kernels for 12%

profile of v4, /device:TPU:0, one launch (start us, length us, event | category | flops | bytes accessed | tf_op | source)
XLA Modules:
  0.0 284.4 jit_solution(4099714935932853935)
XLA Ops:
  11.6 3.3 %shard_map.112 = bf16[2,512,1024]{2,1,0:T(8,128)(2,1)} custom-call(s32[16]{0:T(128)} %refs_0_.7, s32[16]{0:T(128)} %refs_1_.7, bf16[2,512,1024]{2,1,0:T(8,128)(2,1)} %refs_2_.5, bf16[2,512,1024]{2,1,0:T(8,128)(2,1)} %refs_3_.5, bf16[64,2176]{1,0:T(8,128)(2,1)} %copy-done.4), custom_call_target="tpu_custom_call" | custom-call | tf_op jit(solution)/shard_map/pallas_call | solution.py:111
  15.8 3.0 %collective-permute-start = (bf16[64,2176]{1,0:T(8,128)(2,1)S(1)}, bf16[64,2176]{1,0:T(8,128)(2,1)S(1)}, u32[]{:S(2)}, u32[]{:S(2)}) collective-permute-start(bf16[64,2176]{1,0:T(8,128)(2,1)S(1)} %copy-done.5), channel_id=1, source_target_pairs={{0,2},{1,3},{2,0},{3,1},{4,6},{5,7},{6,4},{7,5},{8,10},{9,11},{10,... | collective-permute-start | bytes 835592 | tf_op jit(solution)/shard_map/ppermute | solution.py:18
  18.8 3.6 %shard_map.113 = (bf16[2,512,1024]{2,1,0:T(8,128)(2,1)}, bf16[1,512,1024]{2,1,0:T(8,128)(2,1)}) custom-call(s32[16]{0:T(128)} %refs_0_.7, s32[16]{0:T(128)} %refs_1_.7, bf16[2,512,1024]{2,1,0:T(8,128)(2,1)} %refs_2_.5, bf16[2,512,1024]{2,1,0:T(8,128)(2,1)} %refs_3_.5, bf16[64,2176]{1,0:T(8,128)(2,1)} %copy-done.4), custom_call_target="tpu_custom_call" | custom-call | tf_op jit(solution)/shard_map/pallas_call | solution.py:111
  22.4 3.0 %collective-permute-done.refs_1_ = bf16[64,2176]{1,0:T(8,128)(2,1)S(1)} collective-permute-done((bf16[64,2176]{1,0:T(8,128)(2,1)S(1)}, bf16[64,2176]{1,0:T(8,128)(2,1)S(1)}, u32[]{:S(2)}, u32[]{:S(2)}) %collective-permute-start) | collective-permute-done | bytes 278560 | tf_op jit(solution)/shard_map/ppermute | solution.py:18
  25.4 1.7 collective-permute-start.5
  28.8 2.7 collective-permute-start.3
  31.4 1.6 collective-permute-start.1
  33.1 2.3 collective-permute-start.6
  35.4 32.4 %collective-permute-done.3.refs_1_.refs_2_ = bf16[128,2176]{1,0:T(8,128)(2,1)S(1)} collective-permute-done((bf16[128,2176]{1,0:T(8,128)(2,1)S(1)}, bf16[128,2176]{1,0:T(8,128)(2,1)S(1)}, u32[]{:S(2)}, u32[]{:S(2)}) %collective-permute-start.3) | collective-permute-done | bytes 557088 | tf_op jit(solution)/shard_map/ppermute | solution.py:28
  67.8 22.7 %collective-permute-start.4 = (bf16[128,2176]{1,0:T(8,128)(2,1)S(1)}, bf16[128,2176]{1,0:T(8,128)(2,1)S(1)}, u32[]{:S(2)}, u32[]{:S(2)}) collective-permute-start(bf16[128,2176]{1,0:T(8,128)(2,1)S(1)} %collective-permute-done.3.refs_1_.refs_2_), channel_id=1, source_target_pairs={{0,4},{4,0},{8,12},{12,8},{16,20},{20,16},{24,28},{28,24},{1,5},{5... | collective-permute-start | bytes 1671176 | tf_op jit(solution)/shard_map/ppermute | solution.py:18
  90.5 2.0 collective-permute-start.8
  92.5 11.4 %collective-permute-done.4.refs_5_.refs_3_ = bf16[128,2176]{1,0:T(8,128)(2,1)S(1)} collective-permute-done((bf16[128,2176]{1,0:T(8,128)(2,1)S(1)}, bf16[128,2176]{1,0:T(8,128)(2,1)S(1)}, u32[]{:S(2)}, u32[]{:S(2)}) %collective-permute-start.4) | collective-permute-done | bytes 557088 | tf_op jit(solution)/shard_map/ppermute | solution.py:18
  103.9 11.9 %collective-permute-done.2.refs_4_.refs_1_ = bf16[128,2176]{1,0:T(8,128)(2,1)S(1)} collective-permute-done((bf16[128,2176]{1,0:T(8,128)(2,1)}, bf16[128,2176]{1,0:T(8,128)(2,1)S(1)}, u32[]{:S(2)}, u32[]{:S(2)}) %collective-permute-start.2) | collective-permute-done | bytes 557088 | tf_op jit(solution)/shard_map/ppermute | solution.py:18
  115.8 11.2 %collective-permute-done.8.refs_3_ = bf16[128,2176]{1,0:T(8,128)(2,1)S(1)} collective-permute-done((bf16[128,2176]{1,0:T(8,128)(2,1)S(1)}, bf16[128,2176]{1,0:T(8,128)(2,1)S(1)}, u32[]{:S(2)}, u32[]{:S(2)}) %collective-permute-start.8) | collective-permute-done | bytes 557088 | tf_op jit(solution)/shard_map/ppermute | solution.py:18
  127.9 1.7 collective-permute-start.13
  129.6 13.3 %collective-permute-done.13.refs_1_.refs_5_ = bf16[128,2176]{1,0:T(8,128)(2,1)S(1)} collective-permute-done((bf16[128,2176]{1,0:T(8,128)(2,1)S(1)}, bf16[128,2176]{1,0:T(8,128)(2,1)S(1)}, u32[]{:S(2)}, u32[]{:S(2)}) %collective-permute-start.13) | collective-permute-done | bytes 557088 | tf_op jit(solution)/shard_map/ppermute | solution.py:18
  142.9 2.4 copy-done.2
  147.4 7.8 %shard_map.119.own_ref = bf16[512,1024]{1,0:T(8,128)(2,1)} custom-call(bf16[128,2176]{1,0:T(8,128)(2,1)S(1)} %copy-done.13, bf16[128,2176]{1,0:T(8,128)(2,1)S(1)} %collective-permute-done.13.refs_1_.refs_5_, bf16[128,2176]{1,0:T(8,128)(2,1)S(1)} %bitcast.21, bf16[128,2176]{1,0:T(8,128)(2,1)S(1)} %copy-done.17, bf16[2,2,512,1024]{3,2,1,0:T(8,128)(2,1)S(1)} %bitcast.15, ...), custom_call_target="tpu_custom_call" | custom-call | tf_op jit(solution)/shard_map/pallas_call | solution.py:200
  155.8 7.2 %shard_map.117.own_ref = bf16[512,1024]{1,0:T(8,128)(2,1)S(1)} custom-call(bf16[128,2176]{1,0:T(8,128)(2,1)} %collective-permute-done.1.refs_0_, bf16[128,2176]{1,0:T(8,128)(2,1)S(1)} %copy-done.15, bf16[128,2176]{1,0:T(8,128)(2,1)S(1)} %copy-done.9, bf16[128,2176]{1,0:T(8,128)(2,1)S(1)} %copy-done.11, bf16[2,2,512,1024]{3,2,1,0:T(8,128)(2,1)S(1)} %bitcast.16, ...), custom_call_target="tpu_custom_call" | custom-call | tf_op jit(solution)/shard_map/pallas_call | solution.py:200
  162.9 1.6 collective-permute-start.10
  164.5 5.1 %shard_map.121 = (bf16[2,512,1024]{2,1,0:T(8,128)(2,1)}, bf16[2,512,1024]{2,1,0:T(8,128)(2,1)}, bf16[2,512,1024]{2,1,0:T(8,128)(2,1)}, bf16[2,512,1024]{2,1,0:T(8,128)(2,1)}) custom-call(s32[16]{0:T(128)} %refs_0_.7, s32[16]{0:T(128)} %refs_1_.7, bf16[2,512,1024]{2,1,0:T(8,128)(2,1)} %refs_2_.5, bf16[2,512,1024]{2,1,0:T(8,128)(2,1)} %refs_3_.5, ...), custom_call_target="tpu_custom_call" | custom-call | tf_op jit(solution)/shard_map/pallas_call | solution.py:111
  169.6 1.8 collective-permute-start.18
  171.4 10.2 %collective-permute-done.14.other_ref = bf16[512,1024]{1,0:T(8,128)(2,1)} collective-permute-done((bf16[512,1024]{1,0:T(8,128)(2,1)}, bf16[512,1024]{1,0:T(8,128)(2,1)}, u32[]{:S(2)}, u32[]{:S(2)}) %collective-permute-start.14) | collective-permute-done | bytes 1048608 | tf_op jit(solution)/shard_map/ppermute | solution.py:18
  181.6 2.2 copy-done
  183.8 4.1 %shard_map.120 = (bf16[256,1024]{1,0:T(8,128)(2,1)S(1)}, bf16[256,1024]{1,0:T(8,128)(2,1)S(1)}) custom-call(bf16[512,1024]{1,0:T(8,128)(2,1)} %shard_map.119.own_ref, bf16[512,1024]{1,0:T(8,128)(2,1)} %collective-permute-done.14.other_ref, bf16[2,2,512,1024]{3,2,1,0:T(8,128)(2,1)S(1)} %bitcast.13), custom_call_target="tpu_custom_call" | custom-call | tf_op jit(solution)/shard_map/pallas_call | solution.py:232
  187.9 14.8 %collective-permute-done.10.other_ref = bf16[512,1024]{1,0:T(8,128)(2,1)S(1)} collective-permute-done((bf16[512,1024]{1,0:T(8,128)(2,1)S(1)}, bf16[512,1024]{1,0:T(8,128)(2,1)S(1)}, u32[]{:S(2)}, u32[]{:S(2)}) %collective-permute-start.10) | collective-permute-done | bytes 1048608 | tf_op jit(solution)/shard_map/ppermute | solution.py:18
  202.7 2.4 shard_map.118
  205.2 14.2 %collective-permute-done.11 = bf16[256,1024]{1,0:T(8,128)(2,1)S(1)} collective-permute-done((bf16[256,1024]{1,0:T(8,128)(2,1)S(1)}, bf16[256,1024]{1,0:T(8,128)(2,1)S(1)}, u32[]{:S(2)}, u32[]{:S(2)}) %collective-permute-start.11) | collective-permute-done | bytes 524320 | tf_op jit(solution)/shard_map/ppermute | solution.py:28
  219.5 18.7 %collective-permute-done.12 = bf16[256,1024]{1,0:T(8,128)(2,1)S(1)} collective-permute-done((bf16[256,1024]{1,0:T(8,128)(2,1)S(1)}, bf16[256,1024]{1,0:T(8,128)(2,1)S(1)}, u32[]{:S(2)}, u32[]{:S(2)}) %collective-permute-start.12) | collective-permute-done | bytes 524320 | tf_op jit(solution)/shard_map/ppermute | solution.py:28
  238.6 26.6 %collective-permute-start.16 = (bf16[128,1024]{1,0:T(8,128)(2,1)S(1)}, bf16[128,1024]{1,0:T(8,128)(2,1)S(1)}, u32[]{:S(2)}, u32[]{:S(2)}) collective-permute-start(bf16[128,1024]{1,0:T(8,128)(2,1)S(1)} %slice.35), channel_id=1, source_target_pairs={{0,4},{4,0},{8,12},{12,8},{16,20},{20,16},{24,28},{28,24},{1,5},{5... | collective-permute-start | bytes 786440 | tf_op jit(solution)/shard_map/ppermute | solution.py:18
  265.2 6.5 %collective-permute-done.16 = bf16[128,1024]{1,0:T(8,128)(2,1)S(1)} collective-permute-done((bf16[128,1024]{1,0:T(8,128)(2,1)S(1)}, bf16[128,1024]{1,0:T(8,128)(2,1)S(1)}, u32[]{:S(2)}, u32[]{:S(2)}) %collective-permute-start.16) | collective-permute-done | bytes 262176 | tf_op jit(solution)/shard_map/ppermute | solution.py:18
  272.4 3.6 %shard_map.122 = (bf16[2,512,1024]{2,1,0:T(8,128)(2,1)}, bf16[2,512,1024]{2,1,0:T(8,128)(2,1)}, bf16[2,512,1024]{2,1,0:T(8,128)(2,1)}) custom-call(s32[16]{0:T(128)} %refs_0_.7, s32[16]{0:T(128)} %refs_1_.7, bf16[1,512,1024]{2,1,0:T(8,128)(2,1)} %collective-permute-done.7.refs_1_.refs_2_, ...), custom_call_target="tpu_custom_call", output_to_operand_aliasing={{0}: (4, {}), {1}: (5, {}), {2}: (6, {})} | custom-call | tf_op jit(solution)/shard_map/pallas_call | solution.py:111
  (76 shorter events, 13.3 us)
Async XLA Ops:
  7.2 135.7 %all-gather.5.cloned.1.call-start = ((), (), s32[]{:S(2)}) async-start(), calls=%async_computation | async-start | bytes 6291456 | tf_op jit(solution)/shard_map/all_gather | solution.py:263
  14.9 156.5 %all-gather.7.cloned.1.call-start = ((), (), s32[]{:S(2)}) async-start(), calls=%async_computation.1 | async-start | bytes 6291456 | tf_op jit(solution)/shard_map/all_gather | solution.py:264
  15.8 9.6 %collective-permute-start = (bf16[64,2176]{1,0:T(8,128)(2,1)S(1)}, bf16[64,2176]{1,0:T(8,128)(2,1)S(1)}, u32[]{:S(2)}, u32[]{:S(2)}) collective-permute-start(bf16[64,2176]{1,0:T(8,128)(2,1)S(1)} %copy-done.5), channel_id=1, source_target_pairs={{0,2},{1,3},{2,0},{3,1},{4,6},{5,7},{6,4},{7,5},{8,10},{9,11},{10,... | collective-permute-start | bytes 835592 | tf_op jit(solution)/shard_map/ppermute | solution.py:18
  25.4 3.2 %copy-start.6 = (bf16[64,2176]{1,0:T(8,128)(2,1)S(1)}, bf16[64,2176]{1,0:T(8,128)(2,1)}, u32[]{:S(2)}) copy-start(bf16[64,2176]{1,0:T(8,128)(2,1)} %copy-done.4) | copy-start | bytes 835588
  25.4 101.6 %collective-permute-start.5 = (bf16[2,512,1024]{2,1,0:T(8,128)(2,1)}, bf16[2,512,1024]{2,1,0:T(8,128)(2,1)S(1)}, u32[]{:S(2)}, u32[]{:S(2)}) collective-permute-start(bf16[2,512,1024]{2,1,0:T(8,128)(2,1)} %shard_map.114), channel_id=1, source_target_pairs={{0,2},{1,3},{2,0},{3,1},{4,6},{5,7},{6,4},{7,5},{8,10},{9,11},{10,... | collective-permute-start | bytes 6291464 | tf_op jit(solution)/shard_map/ppermute | solution.py:18
  27.2 63.3 %collective-permute-start.7 = (bf16[1,512,1024]{2,1,0:T(8,128)(2,1)}, bf16[1,512,1024]{2,1,0:T(8,128)(2,1)}, u32[]{:S(2)}, u32[]{:S(2)}) collective-permute-start(bf16[1,512,1024]{2,1,0:T(8,128)(2,1)} %get-tuple-element.18), channel_id=1, source_target_pairs={{0,4},{4,8},{8,12},{12,16},{16,20},{20,24},{24,28},{28,0},{1,5},{5... | collective-permute-start | bytes 3145736 | tf_op jit(solution)/shard_map/ppermute | solution.py:23
  28.8 39.0 %collective-permute-start.3 = (bf16[128,2176]{1,0:T(8,128)(2,1)S(1)}, bf16[128,2176]{1,0:T(8,128)(2,1)S(1)}, u32[]{:S(2)}, u32[]{:S(2)}) collective-permute-start(bf16[128,2176]{1,0:T(8,128)(2,1)S(1)} %bitcast.17), channel_id=1, source_target_pairs={{0,16},{4,20},{8,24},{12,28},{16,0},{20,4},{24,8},{28,12},{1,17},{... | collective-permute-start | bytes 1671176 | tf_op jit(solution)/shard_map/ppermute | solution.py:28
  31.4 59.0 %collective-permute-start.1 = (bf16[128,2176]{1,0:T(8,128)(2,1)S(1)}, bf16[128,2176]{1,0:T(8,128)(2,1)}, u32[]{:S(2)}, u32[]{:S(2)}) collective-permute-start(bf16[128,2176]{1,0:T(8,128)(2,1)S(1)} %bitcast.18), channel_id=1, source_target_pairs={{0,8},{4,12},{8,16},{12,20},{16,24},{20,28},{24,0},{28,4},{1,9},{5... | collective-permute-start | bytes 1671176 | tf_op jit(solution)/shard_map/ppermute | solution.py:28
  33.1 59.4 %collective-permute-start.6 = (bf16[128,2176]{1,0:T(8,128)(2,1)S(1)}, bf16[128,2176]{1,0:T(8,128)(2,1)S(1)}, u32[]{:S(2)}, u32[]{:S(2)}) collective-permute-start(bf16[128,2176]{1,0:T(8,128)(2,1)S(1)} %bitcast.20), channel_id=1, source_target_pairs={{0,24},{4,28},{8,0},{12,4},{16,8},{20,12},{24,16},{28,20},{1,25},{... | collective-permute-start | bytes 1671176 | tf_op jit(solution)/shard_map/ppermute | solution.py:28
  67.8 59.3 %copy-start.8 = (bf16[128,2176]{1,0:T(8,128)(2,1)}, bf16[128,2176]{1,0:T(8,128)(2,1)S(1)}, u32[]{:S(2)}) copy-start(bf16[128,2176]{1,0:T(8,128)(2,1)S(1)} %collective-permute-done.3.refs_1_.refs_2_) | copy-start | bytes 1671172
  67.8 36.1 %collective-permute-start.4 = (bf16[128,2176]{1,0:T(8,128)(2,1)S(1)}, bf16[128,2176]{1,0:T(8,128)(2,1)S(1)}, u32[]{:S(2)}, u32[]{:S(2)}) collective-permute-start(bf16[128,2176]{1,0:T(8,128)(2,1)S(1)} %collective-permute-done.3.refs_1_.refs_2_), channel_id=1, source_target_pairs={{0,4},{4,0},{8,12},{12,8},{16,20},{20,16},{24,28},{28,24},{1,5},{5... | collective-permute-start | bytes 1671176 | tf_op jit(solution)/shard_map/ppermute | solution.py:18
  90.4 25.4 %collective-permute-start.2 = (bf16[128,2176]{1,0:T(8,128)(2,1)}, bf16[128,2176]{1,0:T(8,128)(2,1)S(1)}, u32[]{:S(2)}, u32[]{:S(2)}) collective-permute-start(bf16[128,2176]{1,0:T(8,128)(2,1)} %collective-permute-done.1.refs_0_), channel_id=1, source_target_pairs={{0,4},{4,0},{8,12},{12,8},{16,20},{20,16},{24,28},{28,24},{1,5},{5... | collective-permute-start | bytes 1671176 | tf_op jit(solution)/shard_map/ppermute | solution.py:18
  90.5 36.5 %collective-permute-start.8 = (bf16[128,2176]{1,0:T(8,128)(2,1)S(1)}, bf16[128,2176]{1,0:T(8,128)(2,1)S(1)}, u32[]{:S(2)}, u32[]{:S(2)}) collective-permute-start(bf16[128,2176]{1,0:T(8,128)(2,1)S(1)} %shard_map.115), channel_id=1, source_target_pairs={{0,4},{4,0},{8,12},{12,8},{16,20},{20,16},{24,28},{28,24},{1,5},{5... | collective-permute-start | bytes 1671176 | tf_op jit(solution)/shard_map/ppermute | solution.py:18
  92.5 35.4 %copy-start.12 = (bf16[128,2176]{1,0:T(8,128)(2,1)}, bf16[128,2176]{1,0:T(8,128)(2,1)S(1)}, u32[]{:S(2)}) copy-start(bf16[128,2176]{1,0:T(8,128)(2,1)S(1)} %collective-permute-done.6.refs_2_.refs_0_) | copy-start | bytes 1671172
  103.9 23.2 %copy-start.10 = (bf16[128,2176]{1,0:T(8,128)(2,1)}, bf16[128,2176]{1,0:T(8,128)(2,1)S(1)}, u32[]{:S(2)}) copy-start(bf16[128,2176]{1,0:T(8,128)(2,1)S(1)} %collective-permute-done.4.refs_5_.refs_3_) | copy-start | bytes 1671172
  115.8 11.2 %copy-start.14 = (bf16[128,2176]{1,0:T(8,128)(2,1)}, bf16[128,2176]{1,0:T(8,128)(2,1)S(1)}, u32[]{:S(2)}) copy-start(bf16[128,2176]{1,0:T(8,128)(2,1)S(1)} %collective-permute-done.2.refs_4_.refs_1_) | copy-start | bytes 1671172
  127.9 15.1 %collective-permute-start.9 = (bf16[2,512,1024]{2,1,0:T(8,128)(2,1)S(1)}, bf16[2,512,1024]{2,1,0:T(8,128)(2,1)}, u32[]{:S(2)}, u32[]{:S(2)}) collective-permute-start(bf16[2,512,1024]{2,1,0:T(8,128)(2,1)S(1)} %shard_map.116.refs_5_), channel_id=1, source_target_pairs={{0,1},{1,0},{2,3},{3,2},{4,5},{5,4},{6,7},{7,6},{8,9},{9,8},{10,11... | collective-permute-start | bytes 6291464 | tf_op jit(solution)/shard_map/ppermute | solution.py:18
  127.9 15.0 %collective-permute-start.13 = (bf16[128,2176]{1,0:T(8,128)(2,1)S(1)}, bf16[128,2176]{1,0:T(8,128)(2,1)S(1)}, u32[]{:S(2)}, u32[]{:S(2)}) collective-permute-start(bf16[128,2176]{1,0:T(8,128)(2,1)S(1)} %collective-permute-done.6.refs_2_.refs_0_), channel_id=1, source_target_pairs={{0,4},{4,0},{8,12},{12,8},{16,20},{20,16},{24,28},{28,24},{1,5},{5... | collective-permute-start | bytes 1671176 | tf_op jit(solution)/shard_map/ppermute | solution.py:18
  142.9 12.3 %copy-start.7 = (bf16[128,2176]{1,0:T(8,128)(2,1)}, bf16[128,2176]{1,0:T(8,128)(2,1)S(1)}, u32[]{:S(2)}) copy-start(bf16[128,2176]{1,0:T(8,128)(2,1)S(1)} %collective-permute-done.13.refs_1_.refs_5_) | copy-start | bytes 1671172
  147.4 8.3 %copy-start.3 = (bf16[4,512,1024]{2,1,0:T(8,128)(2,1)S(1)}, bf16[4,512,1024]{2,1,0:T(8,128)(2,1)}, u32[]{:S(2)}) copy-start(bf16[4,512,1024]{2,1,0:T(8,128)(2,1)} %all-gather.5.cloned.1.call-done) | copy-start | bytes 12582916
  147.4 8.3 %copy-start.9 = (bf16[128,2176]{1,0:T(8,128)(2,1)S(1)}, bf16[128,2176]{1,0:T(8,128)(2,1)}, u32[]{:S(2)}) copy-start(bf16[128,2176]{1,0:T(8,128)(2,1)} %copy-done.8) | copy-start | bytes 1671172
  147.4 8.3 %copy-start.11 = (bf16[128,2176]{1,0:T(8,128)(2,1)S(1)}, bf16[128,2176]{1,0:T(8,128)(2,1)}, u32[]{:S(2)}) copy-start(bf16[128,2176]{1,0:T(8,128)(2,1)} %copy-done.10) | copy-start | bytes 1671172
  147.4 8.3 %copy-start.15 = (bf16[128,2176]{1,0:T(8,128)(2,1)S(1)}, bf16[128,2176]{1,0:T(8,128)(2,1)}, u32[]{:S(2)}) copy-start(bf16[128,2176]{1,0:T(8,128)(2,1)} %copy-done.14) | copy-start | bytes 1671172
  155.2 26.4 %collective-permute-start.14 = (bf16[512,1024]{1,0:T(8,128)(2,1)}, bf16[512,1024]{1,0:T(8,128)(2,1)}, u32[]{:S(2)}, u32[]{:S(2)}) collective-permute-start(bf16[512,1024]{1,0:T(8,128)(2,1)} %shard_map.119.own_ref), channel_id=1, source_target_pairs={{0,2},{1,3},{2,0},{3,1},{4,6},{5,7},{6,4},{7,5},{8,10},{9,11},{10,... | collective-permute-start | bytes 3145736 | tf_op jit(solution)/shard_map/ppermute | solution.py:18
  162.9 39.8 %collective-permute-start.10 = (bf16[512,1024]{1,0:T(8,128)(2,1)S(1)}, bf16[512,1024]{1,0:T(8,128)(2,1)S(1)}, u32[]{:S(2)}, u32[]{:S(2)}) collective-permute-start(bf16[512,1024]{1,0:T(8,128)(2,1)S(1)} %shard_map.117.own_ref), channel_id=1, source_target_pairs={{0,2},{1,3},{2,0},{3,1},{4,6},{5,7},{6,4},{7,5},{8,10},{9,11},{10,... | collective-permute-start | bytes 3145736 | tf_op jit(solution)/shard_map/ppermute | solution.py:18
  169.6 102.8 %collective-permute-start.18 = (bf16[2,512,1024]{2,1,0:T(8,128)(2,1)}, bf16[2,512,1024]{2,1,0:T(8,128)(2,1)}, u32[]{:S(2)}, u32[]{:S(2)}) collective-permute-start(bf16[2,512,1024]{2,1,0:T(8,128)(2,1)} %get-tuple-element.23), channel_id=1, source_target_pairs={{0,4},{4,8},{8,12},{12,16},{16,20},{20,24},{24,28},{28,0},{1,5},{5... | collective-permute-start | bytes 6291464 | tf_op jit(solution)/shard_map/ppermute | solution.py:23
  183.8 18.9 %copy-start.1 = (bf16[4,512,1024]{2,1,0:T(8,128)(2,1)S(1)}, bf16[4,512,1024]{2,1,0:T(8,128)(2,1)}, u32[]{:S(2)}) copy-start(bf16[4,512,1024]{2,1,0:T(8,128)(2,1)} %all-gather.7.cloned.1.call-done) | copy-start | bytes 12582916
  187.9 17.4 %collective-permute-start.15 = (bf16[256,1024]{1,0:T(8,128)(2,1)S(1)}, bf16[256,1024]{1,0:T(8,128)(2,1)S(1)}, u32[]{:S(2)}, u32[]{:S(2)}) collective-permute-start(bf16[256,1024]{1,0:T(8,128)(2,1)S(1)} %get-tuple-element.21), channel_id=1, source_target_pairs={{0,8},{4,12},{8,16},{12,20},{16,24},{20,28},{24,0},{28,4},{1,9},{5... | collective-permute-start | bytes 1572872 | tf_op jit(solution)/shard_map/ppermute | solution.py:28
  205.1 14.4 %collective-permute-start.11 = (bf16[256,1024]{1,0:T(8,128)(2,1)S(1)}, bf16[256,1024]{1,0:T(8,128)(2,1)S(1)}, u32[]{:S(2)}, u32[]{:S(2)}) collective-permute-start(bf16[256,1024]{1,0:T(8,128)(2,1)S(1)} %get-tuple-element.19), channel_id=1, source_target_pairs={{0,24},{4,28},{8,0},{12,4},{16,8},{20,12},{24,16},{28,20},{1,25},{... | collective-permute-start | bytes 1572872 | tf_op jit(solution)/shard_map/ppermute | solution.py:28
  205.2 33.0 %collective-permute-start.12 = (bf16[256,1024]{1,0:T(8,128)(2,1)S(1)}, bf16[256,1024]{1,0:T(8,128)(2,1)S(1)}, u32[]{:S(2)}, u32[]{:S(2)}) collective-permute-start(bf16[256,1024]{1,0:T(8,128)(2,1)S(1)} %get-tuple-element.20), channel_id=1, source_target_pairs={{0,16},{4,20},{8,24},{12,28},{16,0},{20,4},{24,8},{28,12},{1,17},{... | collective-permute-start | bytes 1572872 | tf_op jit(solution)/shard_map/ppermute | solution.py:28
  238.6 33.1 %collective-permute-start.16 = (bf16[128,1024]{1,0:T(8,128)(2,1)S(1)}, bf16[128,1024]{1,0:T(8,128)(2,1)S(1)}, u32[]{:S(2)}, u32[]{:S(2)}) collective-permute-start(bf16[128,1024]{1,0:T(8,128)(2,1)S(1)} %slice.35), channel_id=1, source_target_pairs={{0,4},{4,0},{8,12},{12,8},{16,20},{20,16},{24,28},{28,24},{1,5},{5... | collective-permute-start | bytes 786440 | tf_op jit(solution)/shard_map/ppermute | solution.py:18
  271.8 5.0 %collective-permute-start.17 = (bf16[64,1024]{1,0:T(8,128)(2,1)S(1)}, bf16[64,1024]{1,0:T(8,128)(2,1)S(1)}, u32[]{:S(2)}, u32[]{:S(2)}) collective-permute-start(bf16[64,1024]{1,0:T(8,128)(2,1)S(1)} %get-tuple-element.30), channel_id=1, source_target_pairs={{0,2},{1,3},{2,0},{3,1},{4,6},{5,7},{6,4},{7,5},{8,10},{9,11},{10,... | collective-permute-start | bytes 393224 | tf_op jit(solution)/shard_map/ppermute | solution.py:18
  (11 other events, 12.2 us)
Sparse Core Ops, SparseCore 0:
  15.0 16.3 all-gather.4
  33.1 14.6 all-gather.6

commit v5 on v4

v5 whole, which is shorter than its diff:
```python
import functools

import jax
import jax.numpy as jnp
from jax import lax
from jax.experimental import pallas as pl
from jax.experimental.pallas import tpu as pltpu
from jax.sharding import PartitionSpec as P

LANES = 128
VMEM_BYTES = 32 * 1024 * 1024
MOST = 56 * 1024 * 1024
NOTHING = pl.CostEstimate(flops=0, bytes_accessed=0, transcendentals=0)


def swap(x, axis, bit):
    return lax.ppermute(x, axis, [(i, i ^ bit) for i in range(lax.axis_size(axis))])


def passed_along(x, axis, by):
    size = lax.axis_size(axis)
    return lax.ppermute(x, axis, [(i, (i + by) % size) for i in range(size)])


def shift_z(x, by):
    size = lax.axis_size("dp")
    return lax.ppermute(x, "dp", [(i, (i + 2 * by) % size) for i in range(size)])


def spread(pieces):
    bit = 2
    while bit < lax.axis_size("shard"):
        pieces = pieces + [swap(p, "shard", bit) for p in pieces]
        bit *= 2
    return pieces


def params(amount=VMEM_BYTES):
    return pltpu.CompilerParams(vmem_limit_bytes=amount)


def position():
    column = lax.axis_index("shard")
    return lax.div(column, 2), lax.rem(column, 2), lax.axis_index("dp")


def first_kernel(tokens_ref, probs_ref, ids_ref, place_ref, out_ref, coef_ref):
    probs = probs_ref[...]
    weights = (probs / jnp.sum(probs, axis=0, keepdims=True)).astype(jnp.bfloat16)
    weights = weights.astype(jnp.float32)
    ids = ids_ref[...]
    tok, width = tokens_ref.shape
    coef_ref[...] = jnp.zeros_like(coef_ref)
    for slot in range(place_ref.shape[0]):
        named = jnp.where(ids == place_ref[slot], weights, 0.0)
        coef_ref[slot : slot + 1, :tok] = jnp.sum(named, axis=0, keepdims=True)
    out_ref[:, :width] = tokens_ref[...]
    out_ref[:, width:] = jnp.transpose(coef_ref[...])[:tok].astype(jnp.bfloat16)


def first(tokens, probs, ids, old_place):
    vmem = pl.BlockSpec(memory_space=pltpu.VMEM)
    return pl.pallas_call(
        first_kernel,
        in_specs=[vmem] * 3 + [pl.BlockSpec(memory_space=pltpu.SMEM)],
        out_specs=vmem,
        out_shape=jax.ShapeDtypeStruct((tokens.shape[0], tokens.shape[1] + LANES), tokens.dtype),
        scratch_shapes=[pltpu.VMEM((LANES, LANES), jnp.float32)],
        compiler_params=params(),
        cost_estimate=NOTHING,
    )(tokens, probs.T, ids.T, old_place)


def copy_kernel(plan, n_in, n_out, *refs):
    old_ref, new_ref = refs[:2]
    ins, refs = refs[2 : 2 + n_in], refs[-n_out - 3 :]
    outs, (held, in_sems, out_sems) = refs[:n_out], refs[n_out:]
    _, core, row = position()
    second = 2 * row + 1
    moved = (old_ref[second] != new_ref[second]).astype(jnp.int32)
    slots = {"mine": core, "theirs": 1 - core, "leaves": moved, "stays": 1 - moved}
    slots.update({i: i for i in range(3)})
    loads = [
        pltpu.make_async_copy(ins[i].at[slots[a]], held.at[n], in_sems.at[n])
        for n, (i, a, o, b) in enumerate(plan)
    ]
    stores = [
        pltpu.make_async_copy(held.at[n], outs[o].at[slots[b]], out_sems.at[n])
        for n, (i, a, o, b) in enumerate(plan)
    ]
    for c in loads:
        c.start()
    for n, c in enumerate(stores):
        loads[n].wait()
        c.start()
    for c in stores:
        c.wait()


def copies(plan, places, ins, counts, after=(), aliases=()):
    slot, kind = ins[0].shape[1:], ins[0].dtype
    smem, anywhere = pl.BlockSpec(memory_space=pltpu.SMEM), pl.BlockSpec(memory_space=pl.ANY)
    return pl.pallas_call(
        functools.partial(copy_kernel, plan, len(ins), len(counts)),
        in_specs=[smem] * 2 + [anywhere] * (len(ins) + len(aliases) + len(after)),
        out_specs=(anywhere,) * len(counts),
        out_shape=tuple(jax.ShapeDtypeStruct((n,) + slot, kind) for n in counts),
        input_output_aliases={2 + len(ins) + i: i for i in range(len(aliases))},
        scratch_shapes=[
            pltpu.VMEM((len(plan),) + slot, kind),
            pltpu.SemaphoreType.DMA((len(plan),)),
            pltpu.SemaphoreType.DMA((len(plan),)),
        ],
        compiler_params=params(MOST),
        cost_estimate=NOTHING,
    )(*places, *ins, *aliases, *after)


def order_kernel(mine_ref, other_ref, first_ref, second_ref, held, in_sems, out_sems):
    _, core, _ = position()
    loads = [
        pltpu.make_async_copy(mine_ref.at[core], held.at[core], in_sems.at[0]),
        pltpu.make_async_copy(other_ref.at[0], held.at[1 - core], in_sems.at[1]),
    ]
    stores = [
        pltpu.make_async_copy(held.at[n], out, out_sems.at[n])
        for n, out in enumerate((first_ref, second_ref))
    ]
    for c in loads:
        c.start()
    for c in loads:
        c.wait()
    for c in stores:
        c.start()
    for c in stores:
        c.wait()


def in_order(w_down, other):
    anywhere = pl.BlockSpec(memory_space=pl.ANY)
    slot = w_down.shape[1:]
    return pl.pallas_call(
        order_kernel,
        in_specs=[anywhere] * 2,
        out_specs=(anywhere,) * 2,
        out_shape=(jax.ShapeDtypeStruct(slot, w_down.dtype),) * 2,
        scratch_shapes=[
            pltpu.VMEM((2,) + slot, w_down.dtype),
            pltpu.SemaphoreType.DMA((2,)),
            pltpu.SemaphoreType.DMA((2,)),
        ],
        compiler_params=params(MOST),
        cost_estimate=NOTHING,
    )(w_down, other)


def join_kernel(*refs):
    pass


def joined(x, *after):
    anywhere = pl.BlockSpec(memory_space=pl.ANY)
    return pl.pallas_call(
        join_kernel,
        in_specs=[anywhere] * (1 + len(after)),
        out_specs=anywhere,
        out_shape=jax.ShapeDtypeStruct(x.shape, x.dtype),
        input_output_aliases={0: 0},
        compiler_params=params(),
        cost_estimate=NOTHING,
    )(x, *after)


def hidden_kernel(n_pieces, *refs):
    pieces, weights, (out_ref, x_ref, coef_ref) = refs[:n_pieces], refs[n_pieces:-3], refs[-3:]
    _, depth, block = weights[0].shape
    rows, width = x_ref.shape
    tall = rows // n_pieces
    pair, core, row = position()

    @pl.when(pl.program_id(0) == 0)
    def _():
        for n, p in enumerate(pieces):
            x_ref[n * tall : (n + 1) * tall] = p[:, :width]
            coef = p[:, width:].astype(jnp.float32)
            lane = lax.broadcasted_iota(jnp.int32, coef.shape, 1)
            coef = jnp.sum(jnp.where(lane == 2 * row + core, coef, 0.0), axis=1, keepdims=True)
            coef_ref[n * tall : (n + 1) * tall] = jnp.broadcast_to(coef, (tall, LANES))

    tile = min(rows, 512)
    for top in range(0, rows, tile):
        gate = jnp.zeros((tile, block), jnp.float32)
        up = jnp.zeros((tile, block), jnp.float32)
        for i, w in enumerate(weights):
            start = (2 * (pair ^ (i // 2)) + (core ^ (i % 2))) * depth
            x = x_ref[top : top + tile, pl.ds(pl.multiple_of(start, LANES), depth)]
            gate += jnp.dot(x, w[0], preferred_element_type=jnp.float32)
            up += jnp.dot(x, w[1], preferred_element_type=jnp.float32)
        coef = coef_ref[top : top + tile, :1]
        hidden = gate / (1.0 + jnp.exp(-gate)) * up * coef
        out_ref[top : top + tile] = hidden.astype(out_ref.dtype)


def hidden_of(pieces, weights):
    _, depth, ff = weights[0].shape
    block = 256
    tall, wide = pieces[0].shape
    rows = tall * len(pieces)
    return pl.pallas_call(
        functools.partial(hidden_kernel, len(pieces)),
        grid=(ff // block,),
        in_specs=[pl.BlockSpec((tall, wide), lambda f: (0, 0))] * len(pieces)
        + [pl.BlockSpec((2, depth, block), lambda f: (0, 0, f))] * len(weights),
        out_specs=pl.BlockSpec((rows, block), lambda f: (0, f)),
        out_shape=jax.ShapeDtypeStruct((rows, ff), pieces[0].dtype),
        scratch_shapes=[
            pltpu.VMEM((rows, wide - LANES), pieces[0].dtype),
            pltpu.VMEM((rows, LANES), jnp.float32),
        ],
        compiler_params=params(),
        cost_estimate=NOTHING,
    )(*pieces, *weights)


def down_kernel(n_downs, hidden_ref, *refs):
    downs, (kept_ref, sent_ref) = refs[:n_downs], refs[-2:]
    depth = downs[0].shape[0]
    rows = kept_ref.shape[0]
    tile = min(rows, 512)
    contract = (((1,), (1,)), ((), ()))
    for i, w in enumerate(downs):
        for out, base in ((kept_ref, 0), (sent_ref, rows)):
            for top in range(0, rows, tile):
                part = lax.dot_general(
                    hidden_ref[base + top : base + top + tile], w[...], contract,
                    preferred_element_type=jnp.float32,
                )
                out[top : top + tile, i * depth : (i + 1) * depth] = part.astype(out.dtype)


def down_of(hidden, downs, after):
    depth, ff = downs[0].shape
    rows = hidden.shape[0] // 2
    vmem = pl.BlockSpec(memory_space=pltpu.VMEM)
    out = jax.ShapeDtypeStruct((rows, len(downs) * depth), hidden.dtype)
    return pl.pallas_call(
        functools.partial(down_kernel, len(downs)),
        in_specs=[vmem] * (1 + len(downs)) + [pl.BlockSpec(memory_space=pl.ANY)] * len(after),
        out_specs=(vmem, vmem),
        out_shape=(out, out),
        compiler_params=params(),
        cost_estimate=NOTHING,
    )(hidden, *downs, *after)


def over_core(kept, sent):
    return kept.astype(jnp.float32) + swap(sent, "shard", 1).astype(jnp.float32)


def over_x(total, tok):
    total = total.reshape(-1, 2, tok, total.shape[-1])
    given = swap(total[:, 1].astype(jnp.bfloat16), "dp", 1)
    return total[:, 0] + given.astype(jnp.float32)


def over_z(total):
    out = total[0]
    for s in range(1, total.shape[0]):
        out += shift_z(total[s].astype(jnp.bfloat16), -s).astype(jnp.float32)
    return out.astype(jnp.bfloat16)


def place_kernel(depth, *refs):
    parts, out_ref = refs[:-1], refs[-1]
    pair, _, _ = position()
    for part, (blocks) in zip(parts, out_blocks(depth, [p.shape[1] for p in parts])):
        for n, (j, core) in enumerate(blocks):
            start = pl.multiple_of((2 * (pair ^ j) + core) * depth, LANES)
            out_ref[:, pl.ds(start, depth)] = part[:, n * depth : (n + 1) * depth]


def out_blocks(depth, widths):
    own, others = [(0, 0), (0, 1)], widths[1] // depth
    return [own] + [[(j + 1, core) for j in range(others)] for core in range(2)]


def placed(parts, depth, width):
    vmem = pl.BlockSpec(memory_space=pltpu.VMEM)
    return pl.pallas_call(
        functools.partial(place_kernel, depth),
        in_specs=[vmem] * len(parts),
        out_specs=vmem,
        out_shape=jax.ShapeDtypeStruct((parts[0].shape[0], width), parts[0].dtype),
        compiler_params=params(),
        cost_estimate=NOTHING,
    )(*parts)


def local(tokens, router_probs, expert_ids, old_place, new_place, w_gate, w_up, w_down):
    tok, width = tokens.shape
    depth = w_gate.shape[1]
    n_z = lax.axis_size("dp") // 2
    places = (old_place, new_place)

    (mine,) = copies(((0, "mine", 0, 0), (1, "mine", 0, 1)), places, (w_gate, w_up), (2,))
    theirs, theirs_down = copies(
        ((0, "theirs", 0, 0), (1, "theirs", 0, 1), (2, "theirs", 1, 0)),
        places, (w_gate, w_up, w_down), (2, 1),
    )
    near_weights = [mine, swap(theirs, "shard", 1)]
    weights = spread(near_weights)
    downs = [spread([d]) for d in in_order(w_down, swap(theirs_down, "shard", 1))]

    own = first(tokens, router_probs, expert_ids, old_place)
    columns = [own] + [shift_z(own, s) for s in range(1, n_z)]
    near = [jnp.concatenate([c, swap(c, "dp", 1)], axis=0) for c in columns]
    near = [joined(p, weights[2]) for p in near]
    far = [swap(p, "shard", 1) for p in near]

    hidden = hidden_of(near + far, weights)
    groups = [[d[0] for d in downs]] + [d[1:] for d in downs]
    kept, sent = down_of(hidden, groups[0], ())
    at_core = over_core(kept, sent)
    kept, sent = down_of(hidden, groups[1], (at_core,))
    at_x = over_x(at_core, tok)
    at_core = over_core(kept, sent)
    kept, last = down_of(hidden, groups[2], (at_x, at_core))
    parts = [over_z(at_x), over_z(over_x(at_core, tok)), over_z(over_x(over_core(kept, last), tok))]
    moe_output = placed(parts, depth, width)

    leave, *news = copies(
        tuple((i, "leaves", 0, i) for i in range(3))
        + tuple((i, "stays", i + 1, "stays") for i in range(3)),
        places, (w_gate, w_up, w_down), (3, 2, 2, 2), near,
    )
    news = copies(
        tuple((0, i, i, "leaves") for i in range(3)),
        places, (passed_along(leave, "dp", 1),), (2, 2, 2), (last,), news,
    )
    return (moe_output, *news)


def solution(mesh):
    in_specs = (
        P(("dp", "shard"), None),
        P(("dp", "shard"), None),
        P(("dp", "shard"), None),
        P(),
        P(),
        P("dp", "shard", None),
        P("dp", "shard", None),
        P("dp", "shard", None),
    )
    out_specs = (
        P(("dp", "shard"), None),
        P("dp", "shard", None),
        P("dp", "shard", None),
        P("dp", "shard", None),
    )
    return jax.shard_map(local, mesh=mesh, in_specs=in_specs, out_specs=out_specs, check_vma=False)
```

time: 285 us -> 205 us (0.72)
  waiting for transfers between devices: 149 us -> 114 us
  starting transfers between devices: 70.5 us -> 44.9 us
  between operations: 14.3 us -> 1.02 us
  local copies, waits for them, and re-layouts: 12.9 us -> 0.7 us
  other arithmetic: 0.54 us -> 4.6 us
    ppermute x6 -> x12, waiting for transfers between devices: 65.3 us -> 16.3 us  [shift_z(): lax.ppermute(x, 'dp', [(i, (i + 2 * by) % size) for i in range(size)])]
    ppermute x11 -> x20, starting transfers between devices: 60.5 us -> 17.7 us  [swap(): lax.ppermute(x, axis, [(i, i ^ bit) for i in range(lax.axis_size(axis))])]
    ppermute x6 -> x12, starting transfers between devices: 6.72 us -> 25.2 us  [shift_z(): lax.ppermute(x, 'dp', [(i, (i + 2 * by) % size) for i in range(size)])]
    ppermute x11 -> x20, waiting for transfers between devices: 83.2 us -> 98.2 us  [swap(): lax.ppermute(x, axis, [(i, i ^ bit) for i in range(lax.axis_size(axis))])]
    unnamed x45 -> x18, local copies, waits for them, and re-layouts: 12.1 us -> 0.51 us
    concatenate x0 -> x4, other arithmetic: none -> 3.4 us  [local(): near = [jnp.concatenate([c, swap(c, 'dp', 1)], axis=0) for c in columns]]
    pallas_call x2 -> x5, Pallas kernels: 6.42 us -> 8.65 us  [the longest x3 4.93 us: down_of(): pl.pallas_call(functools.partial(down_kernel, len(downs)), in_specs=[vmem...]
    pallas_call x2 -> x1, Pallas kernels: 15 us -> 13 us  [hidden_of(): pl.pallas_call(functools.partial(hidden_kernel, len(pieces)), grid=(ff //...]
  transfers between devices with their start and end apart: 21 -> 33, of which waited for: 12 -> 14; matrix products, arithmetic and copies ran while one was open for 0% -> 2% of each run, Pallas kernels for 12% -> 17%
where the time goes in v5:
time: 205 us
  waiting for transfers between devices  114 us (56%)
  starting transfers between devices  44.9 us (22%)
  Pallas kernels  39 us (19%)
  other arithmetic  4.6 us (2%)
    ppermute x20, waiting for transfers between devices, swap(): lax.ppermute(x, axis, [(i, i ^ bit) for i in range(lax.axis_size(axis))])  98.2 us
    ppermute x12, starting transfers between devices, shift_z(): lax.ppermute(x, 'dp', [(i, (i + 2 * by) % size) for i in range(size)])  25.2 us
    ppermute x20, starting transfers between devices, swap(): lax.ppermute(x, axis, [(i, i ^ bit) for i in range(lax.axis_size(axis))])  17.7 us
    pallas_call x4, Pallas kernels, copies(): pl.pallas_call(functools.partial(copy_kernel, plan, len(ins), len(counts)...  16.7 us
    ppermute x12, waiting for transfers between devices, shift_z(): lax.ppermute(x, 'dp', [(i, (i + 2 * by) % size) for i in range(size)])  16.3 us
    pallas_call x1, Pallas kernels, hidden_of(): pl.pallas_call(functools.partial(hidden_kernel, len(pieces)), grid=(ff //...  13 us
    pallas_call x3, Pallas kernels, down_of(): pl.pallas_call(functools.partial(down_kernel, len(downs)), in_specs=[vmem...  4.93 us
  transfers between devices with their start and end apart: 33, of which 14 were waited for; matrix products, arithmetic and copies ran while one was open for 2% of the time, Pallas kernels for 17%

profile of v5, /device:TPU:0, one launch (start us, length us, event | category | flops | bytes accessed | tf_op | source)
XLA Modules:
  0.0 204.6 jit_solution(8556474101081719939)
XLA Ops:
  0.6 3.6 %shard_map.117 = (bf16[2,512,1024]{2,1,0:T(8,128)(2,1)}, bf16[1,512,1024]{2,1,0:T(8,128)(2,1)}) custom-call(s32[16]{0:T(128)} %refs_0_.7, s32[16]{0:T(128)} %refs_1_.7, bf16[2,512,1024]{2,1,0:T(8,128)(2,1)} %refs_2_.5, bf16[2,512,1024]{2,1,0:T(8,128)(2,1)} %refs_3_.5, bf16[2,512,1024]{2,1,0:T(8,128)(2,1)} %refs_4_.3), custom_call_target="tpu_custom_call" | custom-call | tf_op jit(solution)/shard_map/pallas_call | solution.py:103
  4.8 3.3 %shard_map.112.refs_8_ = bf16[2,512,1024]{2,1,0:T(8,128)(2,1)} custom-call(s32[16]{0:T(128)} %refs_0_.7, s32[16]{0:T(128)} %refs_1_.7, bf16[2,512,1024]{2,1,0:T(8,128)(2,1)} %refs_2_.5, bf16[2,512,1024]{2,1,0:T(8,128)(2,1)} %refs_3_.5), custom_call_target="tpu_custom_call" | custom-call | tf_op jit(solution)/shard_map/pallas_call | solution.py:103
  8.2 2.6 %collective-permute-start.1 = (bf16[2,512,1024]{2,1,0:T(8,128)(2,1)}, bf16[2,512,1024]{2,1,0:T(8,128)(2,1)S(1)}, u32[]{:S(2)}, u32[]{:S(2)}) collective-permute-start(bf16[2,512,1024]{2,1,0:T(8,128)(2,1)} %shard_map.112.refs_8_), channel_id=1, source_target_pairs={{0,2},{1,3},{2,0},{3,1},{4,6},{5,7},{6,4},{7,5},{8,10},{9,11},{10,... | collective-permute-start | bytes 6291464 | tf_op jit(solution)/shard_map/ppermute | solution.py:17
  11.4 1.6 collective-permute-start
  13.0 1.6 collective-permute-start.2
  15.1 2.6 %collective-permute-start.4 = (bf16[64,2176]{1,0:T(8,128)(2,1)S(1)}, bf16[64,2176]{1,0:T(8,128)(2,1)S(1)}, u32[]{:S(2)}, u32[]{:S(2)}) collective-permute-start(bf16[64,2176]{1,0:T(8,128)(2,1)S(1)} %shard_map.111), channel_id=1, source_target_pairs={{0,16},{4,20},{8,24},{12,28},{16,0},{20,4},{24,8},{28,12},{1,17},{... | collective-permute-start | bytes 835592 | tf_op jit(solution)/shard_map/ppermute | solution.py:27
  17.7 2.6 %collective-permute-done = bf16[64,2176]{1,0:T(8,128)(2,1)S(1)} collective-permute-done((bf16[64,2176]{1,0:T(8,128)(2,1)S(1)}, bf16[64,2176]{1,0:T(8,128)(2,1)S(1)}, u32[]{:S(2)}, u32[]{:S(2)}) %collective-permute-start) | collective-permute-done | bytes 278560 | tf_op jit(solution)/shard_map/ppermute | solution.py:17
  20.3 3.6 %collective-permute-start.6 = (bf16[64,2176]{1,0:T(8,128)(2,1)S(1)}, bf16[64,2176]{1,0:T(8,128)(2,1)S(1)}, u32[]{:S(2)}, u32[]{:S(2)}) collective-permute-start(bf16[64,2176]{1,0:T(8,128)(2,1)S(1)} %shard_map.111), channel_id=1, source_target_pairs={{0,24},{4,28},{8,0},{12,4},{16,8},{20,12},{24,16},{28,20},{1,25},{... | collective-permute-start | bytes 835592 | tf_op jit(solution)/shard_map/ppermute | solution.py:27
  26.2 9.2 %collective-permute-done.4 = bf16[64,2176]{1,0:T(8,128)(2,1)S(1)} collective-permute-done((bf16[64,2176]{1,0:T(8,128)(2,1)S(1)}, bf16[64,2176]{1,0:T(8,128)(2,1)S(1)}, u32[]{:S(2)}, u32[]{:S(2)}) %collective-permute-start.4) | collective-permute-done | bytes 278560 | tf_op jit(solution)/shard_map/ppermute | solution.py:27
  38.3 6.6 %collective-permute-done.5 = bf16[64,2176]{1,0:T(8,128)(2,1)S(1)} collective-permute-done((bf16[64,2176]{1,0:T(8,128)(2,1)S(1)}, bf16[64,2176]{1,0:T(8,128)(2,1)S(1)}, u32[]{:S(2)}, u32[]{:S(2)}) %collective-permute-start.5) | collective-permute-done | bytes 278560 | tf_op jit(solution)/shard_map/ppermute | solution.py:17
  45.7 11.8 %collective-permute-done.1.refs_1_.refs_10_ = bf16[2,512,1024]{2,1,0:T(8,128)(2,1)S(1)} collective-permute-done((bf16[2,512,1024]{2,1,0:T(8,128)(2,1)}, bf16[2,512,1024]{2,1,0:T(8,128)(2,1)S(1)}, u32[]{:S(2)}, u32[]{:S(2)}) %collective-permute-start.1) | collective-permute-done | bytes 2097184 | tf_op jit(solution)/shard_map/ppermute | solution.py:17
  59.8 6.1 %shard_map.124 = (bf16[3,512,1024]{2,1,0:T(8,128)(2,1)}, bf16[2,512,1024]{2,1,0:T(8,128)(2,1)}, bf16[2,512,1024]{2,1,0:T(8,128)(2,1)}, bf16[2,512,1024]{2,1,0:T(8,128)(2,1)}) custom-call(s32[16]{0:T(128)} %refs_0_.7, s32[16]{0:T(128)} %refs_1_.7, bf16[2,512,1024]{2,1,0:T(8,128)(2,1)} %refs_2_.5, bf16[2,512,1024]{2,1,0:T(8,128)(2,1)} %refs_3_.5, ...), custom_call_target="tpu_custom_call" | custom-call | tf_op jit(solution)/shard_map/pallas_call | solution.py:103
  66.0 2.0 collective-permute-start.32
  68.0 3.0 %shard_map.119 = (bf16[512,1024]{1,0:T(8,128)(2,1)}, bf16[512,1024]{1,0:T(8,128)(2,1)}) custom-call(bf16[2,512,1024]{2,1,0:T(8,128)(2,1)} %refs_4_.3, bf16[1,512,1024]{2,1,0:T(8,128)(2,1)} %copy-done.8), custom_call_target="tpu_custom_call" | custom-call | tf_op jit(solution)/shard_map/pallas_call | solution.py:142
  71.0 31.3 %collective-permute-done.13.refs_11_ = bf16[2,512,1024]{2,1,0:T(8,128)(2,1)} collective-permute-done((bf16[2,512,1024]{2,1,0:T(8,128)(2,1)S(1)}, bf16[2,512,1024]{2,1,0:T(8,128)(2,1)}, u32[]{:S(2)}, u32[]{:S(2)}) %collective-permute-start.13) | collective-permute-done | bytes 2097184 | tf_op jit(solution)/shard_map/ppermute | solution.py:17
  102.3 13.0 %shard_map.118.hidden_ref = bf16[1024,1024]{1,0:T(8,128)(2,1)S(1)} custom-call(bf16[128,2176]{1,0:T(8,128)(2,1)} %shard_map.113.refs_0_.refs_5_, bf16[128,2176]{1,0:T(8,128)(2,1)} %shard_map.114.refs_1_.refs_6_, bf16[128,2176]{1,0:T(8,128)(2,1)} %shard_map.115.refs_2_.refs_7_, bf16[128,2176]{1,0:T(8,128)(2,1)} %shard_map.116.refs_3_.refs_8_, ...), custom_call_target="tpu_custom_call" | custom-call | tf_op jit(solution)/shard_map/pallas_call | solution.py:209
  115.3 2.4 %shard_map.120 = (bf16[512,1024]{1,0:T(8,128)(2,1)S(1)}, bf16[512,1024]{1,0:T(8,128)(2,1)S(1)}) custom-call(bf16[1024,1024]{1,0:T(8,128)(2,1)S(1)} %shard_map.118.hidden_ref, bf16[512,1024]{1,0:T(8,128)(2,1)S(1)} %copy-done.2, bf16[512,1024]{1,0:T(8,128)(2,1)S(1)} %copy-done.1), custom_call_target="tpu_custom_call" | custom-call | tf_op jit(solution)/shard_map/pallas_call | solution.py:246
  117.8 1.8 collective-permute-start.20
  120.8 22.5 %collective-permute-done.20.refs_0_ = bf16[512,1024]{1,0:T(8,128)(2,1)S(1)} collective-permute-done((bf16[512,1024]{1,0:T(8,128)(2,1)S(1)}, bf16[512,1024]{1,0:T(8,128)(2,1)S(1)}, u32[]{:S(2)}, u32[]{:S(2)}) %collective-permute-start.20) | collective-permute-done | bytes 1048608 | tf_op jit(solution)/shard_map/ppermute | solution.py:17
  144.7 1.8 collective-permute-start.26
  148.3 12.3 %collective-permute-done.16 = bf16[4,64,1024]{2,1,0:T(8,128)(2,1)S(1)} collective-permute-done((bf16[4,64,1024]{2,1,0:T(8,128)(2,1)S(1)}, bf16[4,64,1024]{2,1,0:T(8,128)(2,1)S(1)}, u32[]{:S(2)}, u32[]{:S(2)}) %collective-permute-start.16) | collective-permute-done | bytes 524320 | tf_op jit(solution)/shard_map/ppermute | solution.py:17
  160.9 9.4 %collective-permute-done.26.refs_0_ = bf16[512,1024]{1,0:T(8,128)(2,1)S(1)} collective-permute-done((bf16[512,1024]{1,0:T(8,128)(2,1)S(1)}, bf16[512,1024]{1,0:T(8,128)(2,1)S(1)}, u32[]{:S(2)}, u32[]{:S(2)}) %collective-permute-start.26) | collective-permute-done | bytes 1048608 | tf_op jit(solution)/shard_map/ppermute | solution.py:17
  171.7 1.9 collective-permute-start.19
  173.6 2.6 %collective-permute-start.18 = (bf16[64,1024]{1,0:T(8,128)(2,1)S(1)}, bf16[64,1024]{1,0:T(8,128)(2,1)S(1)}, u32[]{:S(2)}, u32[]{:S(2)}) collective-permute-start(bf16[64,1024]{1,0:T(8,128)(2,1)S(1)} %get-tuple-element.46), channel_id=1, source_target_pairs={{0,16},{4,20},{8,24},{12,28},{16,0},{20,4},{24,8},{28,12},{1,17},{... | collective-permute-start | bytes 393224 | tf_op jit(solution)/shard_map/ppermute | solution.py:27
  177.6 1.6 collective-permute-start.22
  179.1 3.6 %shard_map.125 = (bf16[2,512,1024]{2,1,0:T(8,128)(2,1)}, bf16[2,512,1024]{2,1,0:T(8,128)(2,1)}, bf16[2,512,1024]{2,1,0:T(8,128)(2,1)}) custom-call(s32[16]{0:T(128)} %refs_0_.7, s32[16]{0:T(128)} %refs_1_.7, bf16[3,512,1024]{2,1,0:T(8,128)(2,1)} %collective-permute-done.32.refs_2_, ...), custom_call_target="tpu_custom_call", output_to_operand_aliasing={{0}: (3, {}), {1}: (4, {}), {2}: (5, {})} | custom-call | tf_op jit(solution)/shard_map/pallas_call | solution.py:103
  182.7 2.7 %collective-permute-done.18 = bf16[64,1024]{1,0:T(8,128)(2,1)S(1)} collective-permute-done((bf16[64,1024]{1,0:T(8,128)(2,1)S(1)}, bf16[64,1024]{1,0:T(8,128)(2,1)S(1)}, u32[]{:S(2)}, u32[]{:S(2)}) %collective-permute-start.18) | collective-permute-done | bytes 131104 | tf_op jit(solution)/shard_map/ppermute | solution.py:27
  185.7 1.6 collective-permute-start.28
  187.4 3.4 %collective-permute-start.25 = (bf16[64,512]{1,0:T(8,128)(2,1)S(1)}, bf16[64,512]{1,0:T(8,128)(2,1)S(1)}, u32[]{:S(2)}, u32[]{:S(2)}) collective-permute-start(bf16[64,512]{1,0:T(8,128)(2,1)S(1)} %get-tuple-element.51), channel_id=1, source_target_pairs={{0,8},{4,12},{8,16},{12,20},{16,24},{20,28},{24,0},{28,4},{1,9},{5... | collective-permute-start | bytes 196616 | tf_op jit(solution)/shard_map/ppermute | solution.py:27
  190.7 1.6 collective-permute-start.24
  194.1 3.4 %collective-permute-start.31 = (bf16[64,512]{1,0:T(8,128)(2,1)S(1)}, bf16[64,512]{1,0:T(8,128)(2,1)S(1)}, u32[]{:S(2)}, u32[]{:S(2)}) collective-permute-start(bf16[64,512]{1,0:T(8,128)(2,1)S(1)} %get-tuple-element.48), channel_id=1, source_target_pairs={{0,8},{4,12},{8,16},{12,20},{16,24},{20,28},{24,0},{28,4},{1,9},{5... | collective-permute-start | bytes 196616 | tf_op jit(solution)/shard_map/ppermute | solution.py:27
  201.2 2.6 %collective-permute-done.30 = bf16[64,512]{1,0:T(8,128)(2,1)S(1)} collective-permute-done((bf16[64,512]{1,0:T(8,128)(2,1)S(1)}, bf16[64,512]{1,0:T(8,128)(2,1)S(1)}, u32[]{:S(2)}, u32[]{:S(2)}) %collective-permute-start.30) | collective-permute-done | bytes 65568 | tf_op jit(solution)/shard_map/ppermute | solution.py:27
  (86 shorter events, 24.1 us)
Async XLA Ops:
  4.3 10.3 %collective-permute-start.12 = (bf16[2,512,1024]{2,1,0:T(8,128)(2,1)}, bf16[2,512,1024]{2,1,0:T(8,128)(2,1)S(1)}, u32[]{:S(2)}, u32[]{:S(2)}) collective-permute-start(bf16[2,512,1024]{2,1,0:T(8,128)(2,1)} %get-tuple-element.21), channel_id=1, source_target_pairs={{0,1},{1,0},{2,3},{3,2},{4,5},{5,4},{6,7},{7,6},{8,9},{9,8},{10,11... | collective-permute-start | bytes 6291464 | tf_op jit(solution)/shard_map/ppermute | solution.py:17
  8.2 49.3 %collective-permute-start.1 = (bf16[2,512,1024]{2,1,0:T(8,128)(2,1)}, bf16[2,512,1024]{2,1,0:T(8,128)(2,1)S(1)}, u32[]{:S(2)}, u32[]{:S(2)}) collective-permute-start(bf16[2,512,1024]{2,1,0:T(8,128)(2,1)} %shard_map.112.refs_8_), channel_id=1, source_target_pairs={{0,2},{1,3},{2,0},{3,1},{4,6},{5,7},{6,4},{7,5},{8,10},{9,11},{10,... | collective-permute-start | bytes 6291464 | tf_op jit(solution)/shard_map/ppermute | solution.py:17
  11.4 8.8 %collective-permute-start = (bf16[64,2176]{1,0:T(8,128)(2,1)S(1)}, bf16[64,2176]{1,0:T(8,128)(2,1)S(1)}, u32[]{:S(2)}, u32[]{:S(2)}) collective-permute-start(bf16[64,2176]{1,0:T(8,128)(2,1)S(1)} %shard_map.111), channel_id=1, source_target_pairs={{0,4},{4,0},{8,12},{12,8},{16,20},{20,16},{24,28},{28,24},{1,5},{5... | collective-permute-start | bytes 835592 | tf_op jit(solution)/shard_map/ppermute | solution.py:17
  13.0 11.4 %collective-permute-start.2 = (bf16[64,2176]{1,0:T(8,128)(2,1)S(1)}, bf16[64,2176]{1,0:T(8,128)(2,1)S(1)}, u32[]{:S(2)}, u32[]{:S(2)}) collective-permute-start(bf16[64,2176]{1,0:T(8,128)(2,1)S(1)} %shard_map.111), channel_id=1, source_target_pairs={{0,8},{4,12},{8,16},{12,20},{16,24},{20,28},{24,0},{28,4},{1,9},{5... | collective-permute-start | bytes 835592 | tf_op jit(solution)/shard_map/ppermute | solution.py:27
  14.6 87.7 %collective-permute-start.13 = (bf16[2,512,1024]{2,1,0:T(8,128)(2,1)S(1)}, bf16[2,512,1024]{2,1,0:T(8,128)(2,1)}, u32[]{:S(2)}, u32[]{:S(2)}) collective-permute-start(bf16[2,512,1024]{2,1,0:T(8,128)(2,1)S(1)} %collective-permute-done.12.refs_9_), channel_id=1, source_target_pairs={{0,2},{1,3},{2,0},{3,1},{4,6},{5,7},{6,4},{7,5},{8,10},{9,11},{10,... | collective-permute-start | bytes 6291464 | tf_op jit(solution)/shard_map/ppermute | solution.py:17
  15.1 20.3 %collective-permute-start.4 = (bf16[64,2176]{1,0:T(8,128)(2,1)S(1)}, bf16[64,2176]{1,0:T(8,128)(2,1)S(1)}, u32[]{:S(2)}, u32[]{:S(2)}) collective-permute-start(bf16[64,2176]{1,0:T(8,128)(2,1)S(1)} %shard_map.111), channel_id=1, source_target_pairs={{0,16},{4,20},{8,24},{12,28},{16,0},{20,4},{24,8},{28,12},{1,17},{... | collective-permute-start | bytes 835592 | tf_op jit(solution)/shard_map/ppermute | solution.py:27
  20.3 15.1 %collective-permute-start.6 = (bf16[64,2176]{1,0:T(8,128)(2,1)S(1)}, bf16[64,2176]{1,0:T(8,128)(2,1)S(1)}, u32[]{:S(2)}, u32[]{:S(2)}) collective-permute-start(bf16[64,2176]{1,0:T(8,128)(2,1)S(1)} %shard_map.111), channel_id=1, source_target_pairs={{0,24},{4,28},{8,0},{12,4},{16,8},{20,12},{24,16},{28,20},{1,25},{... | collective-permute-start | bytes 835592 | tf_op jit(solution)/shard_map/ppermute | solution.py:27
  24.4 11.8 %collective-permute-start.3 = (bf16[64,2176]{1,0:T(8,128)(2,1)S(1)}, bf16[64,2176]{1,0:T(8,128)(2,1)S(1)}, u32[]{:S(2)}, u32[]{:S(2)}) collective-permute-start(bf16[64,2176]{1,0:T(8,128)(2,1)S(1)} %collective-permute-done.2), channel_id=1, source_target_pairs={{0,4},{4,0},{8,12},{12,8},{16,20},{20,16},{24,28},{28,24},{1,5},{5... | collective-permute-start | bytes 835592 | tf_op jit(solution)/shard_map/ppermute | solution.py:17
  35.4 23.5 %collective-permute-start.14 = (bf16[1,512,1024]{2,1,0:T(8,128)(2,1)}, bf16[1,512,1024]{2,1,0:T(8,128)(2,1)S(1)}, u32[]{:S(2)}, u32[]{:S(2)}) collective-permute-start(bf16[1,512,1024]{2,1,0:T(8,128)(2,1)} %get-tuple-element.22), channel_id=1, source_target_pairs={{0,1},{1,0},{2,3},{3,2},{4,5},{5,4},{6,7},{7,6},{8,9},{9,8},{10,11... | collective-permute-start | bytes 3145736 | tf_op jit(solution)/shard_map/ppermute | solution.py:17
  35.4 9.5 %collective-permute-start.5 = (bf16[64,2176]{1,0:T(8,128)(2,1)S(1)}, bf16[64,2176]{1,0:T(8,128)(2,1)S(1)}, u32[]{:S(2)}, u32[]{:S(2)}) collective-permute-start(bf16[64,2176]{1,0:T(8,128)(2,1)S(1)} %collective-permute-done.4), channel_id=1, source_target_pairs={{0,4},{4,0},{8,12},{12,8},{16,20},{20,16},{24,28},{28,24},{1,5},{5... | collective-permute-start | bytes 835592 | tf_op jit(solution)/shard_map/ppermute | solution.py:17
  36.2 21.3 %collective-permute-start.7 = (bf16[64,2176]{1,0:T(8,128)(2,1)S(1)}, bf16[64,2176]{1,0:T(8,128)(2,1)S(1)}, u32[]{:S(2)}, u32[]{:S(2)}) collective-permute-start(bf16[64,2176]{1,0:T(8,128)(2,1)S(1)} %collective-permute-done.6), channel_id=1, source_target_pairs={{0,4},{4,0},{8,12},{12,8},{16,20},{20,16},{24,28},{28,24},{1,5},{5... | collective-permute-start | bytes 835592 | tf_op jit(solution)/shard_map/ppermute | solution.py:17
  57.4 8.5 %collective-permute-start.8 = (bf16[128,2176]{1,0:T(8,128)(2,1)}, bf16[128,2176]{1,0:T(8,128)(2,1)S(1)}, u32[]{:S(2)}, u32[]{:S(2)}) collective-permute-start(bf16[128,2176]{1,0:T(8,128)(2,1)} %shard_map.113.refs_0_.refs_5_), channel_id=1, source_target_pairs={{0,1},{1,0},{2,3},{3,2},{4,5},{5,4},{6,7},{7,6},{8,9},{9,8},{10,11... | collective-permute-start | bytes 1671176 | tf_op jit(solution)/shard_map/ppermute | solution.py:17
  58.3 12.7 %collective-permute-start.9 = (bf16[128,2176]{1,0:T(8,128)(2,1)}, bf16[128,2176]{1,0:T(8,128)(2,1)S(1)}, u32[]{:S(2)}, u32[]{:S(2)}) collective-permute-start(bf16[128,2176]{1,0:T(8,128)(2,1)} %shard_map.114.refs_1_.refs_6_), channel_id=1, source_target_pairs={{0,1},{1,0},{2,3},{3,2},{4,5},{5,4},{6,7},{7,6},{8,9},{9,8},{10,11... | collective-permute-start | bytes 1671176 | tf_op jit(solution)/shard_map/ppermute | solution.py:17
  58.8 12.2 %collective-permute-start.10 = (bf16[128,2176]{1,0:T(8,128)(2,1)}, bf16[128,2176]{1,0:T(8,128)(2,1)S(1)}, u32[]{:S(2)}, u32[]{:S(2)}) collective-permute-start(bf16[128,2176]{1,0:T(8,128)(2,1)} %shard_map.115.refs_2_.refs_7_), channel_id=1, source_target_pairs={{0,1},{1,0},{2,3},{3,2},{4,5},{5,4},{6,7},{7,6},{8,9},{9,8},{10,11... | collective-permute-start | bytes 1671176 | tf_op jit(solution)/shard_map/ppermute | solution.py:17
  58.9 12.1 %collective-permute-start.11 = (bf16[128,2176]{1,0:T(8,128)(2,1)}, bf16[128,2176]{1,0:T(8,128)(2,1)}, u32[]{:S(2)}, u32[]{:S(2)}) collective-permute-start(bf16[128,2176]{1,0:T(8,128)(2,1)} %shard_map.116.refs_3_.refs_8_), channel_id=1, source_target_pairs={{0,1},{1,0},{2,3},{3,2},{4,5},{5,4},{6,7},{7,6},{8,9},{9,8},{10,11... | collective-permute-start | bytes 1671176 | tf_op jit(solution)/shard_map/ppermute | solution.py:17
  66.0 111.6 %collective-permute-start.32 = (bf16[3,512,1024]{2,1,0:T(8,128)(2,1)}, bf16[3,512,1024]{2,1,0:T(8,128)(2,1)}, u32[]{:S(2)}, u32[]{:S(2)}) collective-permute-start(bf16[3,512,1024]{2,1,0:T(8,128)(2,1)} %get-tuple-element.31), channel_id=1, source_target_pairs={{0,4},{4,8},{8,12},{12,16},{16,20},{20,24},{24,28},{28,0},{1,5},{5... | collective-permute-start | bytes 9437192 | tf_op jit(solution)/shard_map/ppermute | solution.py:22
  117.8 25.6 %collective-permute-start.20 = (bf16[512,1024]{1,0:T(8,128)(2,1)S(1)}, bf16[512,1024]{1,0:T(8,128)(2,1)S(1)}, u32[]{:S(2)}, u32[]{:S(2)}) collective-permute-start(bf16[512,1024]{1,0:T(8,128)(2,1)S(1)} %copy-done.2), channel_id=1, source_target_pairs={{0,2},{1,3},{2,0},{3,1},{4,6},{5,7},{6,4},{7,5},{8,10},{9,11},{10,... | collective-permute-start | bytes 3145736 | tf_op jit(solution)/shard_map/ppermute | solution.py:17
  144.6 3.5 %collective-permute-start.21 = (bf16[512,512]{1,0:T(8,128)(2,1)S(1)}, bf16[512,512]{1,0:T(8,128)(2,1)S(1)}, u32[]{:S(2)}, u32[]{:S(2)}) collective-permute-start(bf16[512,512]{1,0:T(8,128)(2,1)S(1)} %get-tuple-element.28), channel_id=1, source_target_pairs={{0,1},{1,0},{2,3},{3,2},{4,5},{5,4},{6,7},{7,6},{8,9},{9,8},{10,11... | collective-permute-start | bytes 1572872 | tf_op jit(solution)/shard_map/ppermute | solution.py:17
  144.7 25.6 %collective-permute-start.26 = (bf16[512,1024]{1,0:T(8,128)(2,1)S(1)}, bf16[512,1024]{1,0:T(8,128)(2,1)S(1)}, u32[]{:S(2)}, u32[]{:S(2)}) collective-permute-start(bf16[512,1024]{1,0:T(8,128)(2,1)S(1)} %copy-done.1), channel_id=1, source_target_pairs={{0,2},{1,3},{2,0},{3,1},{4,6},{5,7},{6,4},{7,5},{8,10},{9,11},{10,... | collective-permute-start | bytes 3145736 | tf_op jit(solution)/shard_map/ppermute | solution.py:17
  146.6 14.1 %collective-permute-start.16 = (bf16[4,64,1024]{2,1,0:T(8,128)(2,1)S(1)}, bf16[4,64,1024]{2,1,0:T(8,128)(2,1)S(1)}, u32[]{:S(2)}, u32[]{:S(2)}) collective-permute-start(bf16[4,64,1024]{2,1,0:T(8,128)(2,1)S(1)} %fusion.1), channel_id=1, source_target_pairs={{0,4},{4,0},{8,12},{12,8},{16,20},{20,16},{24,28},{28,24},{1,5},{5... | collective-permute-start | bytes 1572872 | tf_op jit(solution)/shard_map/ppermute | solution.py:17
  171.6 13.9 %collective-permute-start.27 = (bf16[512,512]{1,0:T(8,128)(2,1)S(1)}, bf16[512,512]{1,0:T(8,128)(2,1)S(1)}, u32[]{:S(2)}, u32[]{:S(2)}) collective-permute-start(bf16[512,512]{1,0:T(8,128)(2,1)S(1)} %get-tuple-element.30.refs_6_), channel_id=1, source_target_pairs={{0,1},{1,0},{2,3},{3,2},{4,5},{5,4},{6,7},{7,6},{8,9},{9,8},{10,11... | collective-permute-start | bytes 1572872 | tf_op jit(solution)/shard_map/ppermute | solution.py:17
  171.7 11.0 %collective-permute-start.19 = (bf16[64,1024]{1,0:T(8,128)(2,1)S(1)}, bf16[64,1024]{1,0:T(8,128)(2,1)S(1)}, u32[]{:S(2)}, u32[]{:S(2)}) collective-permute-start(bf16[64,1024]{1,0:T(8,128)(2,1)S(1)} %get-tuple-element.45), channel_id=1, source_target_pairs={{0,8},{4,12},{8,16},{12,20},{16,24},{20,28},{24,0},{28,4},{1,9},{5... | collective-permute-start | bytes 393224 | tf_op jit(solution)/shard_map/ppermute | solution.py:27
  173.6 11.9 %collective-permute-start.18 = (bf16[64,1024]{1,0:T(8,128)(2,1)S(1)}, bf16[64,1024]{1,0:T(8,128)(2,1)S(1)}, u32[]{:S(2)}, u32[]{:S(2)}) collective-permute-start(bf16[64,1024]{1,0:T(8,128)(2,1)S(1)} %get-tuple-element.46), channel_id=1, source_target_pairs={{0,16},{4,20},{8,24},{12,28},{16,0},{20,4},{24,8},{28,12},{1,17},{... | collective-permute-start | bytes 393224 | tf_op jit(solution)/shard_map/ppermute | solution.py:27
  176.2 9.3 %collective-permute-start.17 = (bf16[64,1024]{1,0:T(8,128)(2,1)S(1)}, bf16[64,1024]{1,0:T(8,128)(2,1)S(1)}, u32[]{:S(2)}, u32[]{:S(2)}) collective-permute-start(bf16[64,1024]{1,0:T(8,128)(2,1)S(1)} %get-tuple-element.44), channel_id=1, source_target_pairs={{0,24},{4,28},{8,0},{12,4},{16,8},{20,12},{24,16},{28,20},{1,25},{... | collective-permute-start | bytes 393224 | tf_op jit(solution)/shard_map/ppermute | solution.py:27
  177.6 9.7 %collective-permute-start.22 = (bf16[4,64,512]{2,1,0:T(8,128)(2,1)S(1)}, bf16[4,64,512]{2,1,0:T(8,128)(2,1)S(1)}, u32[]{:S(2)}, u32[]{:S(2)}) collective-permute-start(bf16[4,64,512]{2,1,0:T(8,128)(2,1)S(1)} %fusion.4), channel_id=1, source_target_pairs={{0,4},{4,0},{8,12},{12,8},{16,20},{20,16},{24,28},{28,24},{1,5},{5... | collective-permute-start | bytes 786440 | tf_op jit(solution)/shard_map/ppermute | solution.py:17
  185.7 8.3 %collective-permute-start.28 = (bf16[4,64,512]{2,1,0:T(8,128)(2,1)S(1)}, bf16[4,64,512]{2,1,0:T(8,128)(2,1)S(1)}, u32[]{:S(2)}, u32[]{:S(2)}) collective-permute-start(bf16[4,64,512]{2,1,0:T(8,128)(2,1)S(1)} %fusion.5), channel_id=1, source_target_pairs={{0,4},{4,0},{8,12},{12,8},{16,20},{20,16},{24,28},{28,24},{1,5},{5... | collective-permute-start | bytes 786440 | tf_op jit(solution)/shard_map/ppermute | solution.py:17
  187.4 11.4 %collective-permute-start.25 = (bf16[64,512]{1,0:T(8,128)(2,1)S(1)}, bf16[64,512]{1,0:T(8,128)(2,1)S(1)}, u32[]{:S(2)}, u32[]{:S(2)}) collective-permute-start(bf16[64,512]{1,0:T(8,128)(2,1)S(1)} %get-tuple-element.51), channel_id=1, source_target_pairs={{0,8},{4,12},{8,16},{12,20},{16,24},{20,28},{24,0},{28,4},{1,9},{5... | collective-permute-start | bytes 196616 | tf_op jit(solution)/shard_map/ppermute | solution.py:27
  190.7 9.2 %collective-permute-start.24 = (bf16[64,512]{1,0:T(8,128)(2,1)S(1)}, bf16[64,512]{1,0:T(8,128)(2,1)S(1)}, u32[]{:S(2)}, u32[]{:S(2)}) collective-permute-start(bf16[64,512]{1,0:T(8,128)(2,1)S(1)} %get-tuple-element.52), channel_id=1, source_target_pairs={{0,16},{4,20},{8,24},{12,28},{16,0},{20,4},{24,8},{28,12},{1,17},{... | collective-permute-start | bytes 196616 | tf_op jit(solution)/shard_map/ppermute | solution.py:27
  192.4 7.6 %collective-permute-start.23 = (bf16[64,512]{1,0:T(8,128)(2,1)S(1)}, bf16[64,512]{1,0:T(8,128)(2,1)S(1)}, u32[]{:S(2)}, u32[]{:S(2)}) collective-permute-start(bf16[64,512]{1,0:T(8,128)(2,1)S(1)} %get-tuple-element.50), channel_id=1, source_target_pairs={{0,24},{4,28},{8,0},{12,4},{16,8},{20,12},{24,16},{28,20},{1,25},{... | collective-permute-start | bytes 196616 | tf_op jit(solution)/shard_map/ppermute | solution.py:27
  194.1 7.1 %collective-permute-start.31 = (bf16[64,512]{1,0:T(8,128)(2,1)S(1)}, bf16[64,512]{1,0:T(8,128)(2,1)S(1)}, u32[]{:S(2)}, u32[]{:S(2)}) collective-permute-start(bf16[64,512]{1,0:T(8,128)(2,1)S(1)} %get-tuple-element.48), channel_id=1, source_target_pairs={{0,8},{4,12},{8,16},{12,20},{16,24},{20,28},{24,0},{28,4},{1,9},{5... | collective-permute-start | bytes 196616 | tf_op jit(solution)/shard_map/ppermute | solution.py:27
  197.5 6.3 %collective-permute-start.30 = (bf16[64,512]{1,0:T(8,128)(2,1)S(1)}, bf16[64,512]{1,0:T(8,128)(2,1)S(1)}, u32[]{:S(2)}, u32[]{:S(2)}) collective-permute-start(bf16[64,512]{1,0:T(8,128)(2,1)S(1)} %get-tuple-element.49), channel_id=1, source_target_pairs={{0,16},{4,20},{8,24},{12,28},{16,0},{20,4},{24,8},{28,12},{1,17},{... | collective-permute-start | bytes 196616 | tf_op jit(solution)/shard_map/ppermute | solution.py:27
  198.8 5.0 %collective-permute-start.29 = (bf16[64,512]{1,0:T(8,128)(2,1)S(1)}, bf16[64,512]{1,0:T(8,128)(2,1)S(1)}, u32[]{:S(2)}, u32[]{:S(2)}) collective-permute-start(bf16[64,512]{1,0:T(8,128)(2,1)S(1)} %get-tuple-element.47), channel_id=1, source_target_pairs={{0,24},{4,28},{8,0},{12,4},{16,8},{20,12},{24,16},{28,20},{1,25},{... | collective-permute-start | bytes 196616 | tf_op jit(solution)/shard_map/ppermute | solution.py:27
  (10 other events, 162.2 us)

commit v6 on v5

--- a/solution.py
+++ b/solution.py
@@ -218,7 +218,7 @@
             pltpu.VMEM((rows, LANES), jnp.float32),
         ],
         compiler_params=params(),
-        cost_estimate=NOTHING,
+        cost_estimate=pl.CostEstimate(flops=1, bytes_accessed=1, transcendentals=0),
     )(*pieces, *weights)
 
 
@@ -249,7 +249,7 @@
         out_specs=(vmem, vmem),
         out_shape=(out, out),
         compiler_params=params(),
-        cost_estimate=NOTHING,
+        cost_estimate=pl.CostEstimate(flops=1, bytes_accessed=1, transcendentals=0),
     )(hidden, *downs, *after)
 
 
@@ -318,24 +318,26 @@
     far = [swap(p, "shard", 1) for p in near]
 
     hidden = hidden_of(near + far, weights)
-    groups = [[d[0] for d in downs]] + [d[1:] for d in downs]
-    kept, sent = down_of(hidden, groups[0], ())
-    at_core = over_core(kept, sent)
-    kept, sent = down_of(hidden, groups[1], (at_core,))
-    at_x = over_x(at_core, tok)
-    at_core = over_core(kept, sent)
-    kept, last = down_of(hidden, groups[2], (at_x, at_core))
-    parts = [over_z(at_x), over_z(over_x(at_core, tok)), over_z(over_x(over_core(kept, last), tok))]
-    moe_output = placed(parts, depth, width)
-
     leave, *news = copies(
         tuple((i, "leaves", 0, i) for i in range(3))
         + tuple((i, "stays", i + 1, "stays") for i in range(3)),
         places, (w_gate, w_up, w_down), (3, 2, 2, 2), near,
     )
+    arrive = passed_along(leave, "dp", 1)
+
+    groups = [[d[0] for d in downs]] + [d[1:] for d in downs]
+    kept, sent = down_of(hidden, groups[0], ())
+    at_core = over_core(kept, sent)
+    kept, sent = down_of(hidden, groups[1], (sent,))
+    at_x = over_x(at_core, tok)
+    at_core = over_core(kept, sent)
+    kept, last = down_of(hidden, groups[2], (sent, arrive, at_x))
+    parts = [over_z(at_x), over_z(over_x(at_core, tok)), over_z(over_x(over_core(kept, last), tok))]
+    moe_output = placed(parts, depth, width)
+
     news = copies(
         tuple((0, i, i, "leaves") for i in range(3)),
-        places, (passed_along(leave, "dp", 1),), (2, 2, 2), (last,), news,
+        places, (arrive,), (2, 2, 2), (last,), news,
     )
     return (moe_output, *news)
 

time: 205 us -> 185 us (0.902)
  waiting for transfers between devices: 114 us -> 99.8 us
  starting transfers between devices: 44.9 us -> 39 us
  local copies, waits for them, and re-layouts: 0.7 us -> 3.93 us
  other arithmetic: 4.6 us -> 2.16 us
    ppermute x20, waiting for transfers between devices: 98.2 us -> 80.6 us  [swap(): lax.ppermute(x, axis, [(i, i ^ bit) for i in range(lax.axis_size(axis))])]
    ppermute x12, starting transfers between devices: 25.2 us -> 20.5 us  [shift_z(): lax.ppermute(x, 'dp', [(i, (i + 2 * by) % size) for i in range(size)])]
    unnamed x18 -> x30, local copies, waits for them, and re-layouts: 0.51 us -> 3.74 us
    ppermute x12, waiting for transfers between devices: 16.3 us -> 19.2 us  [shift_z(): lax.ppermute(x, 'dp', [(i, (i + 2 * by) % size) for i in range(size)])]
    concatenate x4, other arithmetic: 3.4 us -> 0.98 us  [local(): near = [jnp.concatenate([c, swap(c, 'dp', 1)], axis=0) for c in columns]]
  transfers between devices with their start and end apart: 33 -> 33, of which waited for: 14 -> 12; matrix products, arithmetic and copies ran while one was open for 2% -> 1% of each run, Pallas kernels for 17% -> 19%
where the time goes in v6:
time: 185 us
  waiting for transfers between devices  99.8 us (54%)
  starting transfers between devices  39 us (21%)
  Pallas kernels  38.7 us (21%)
  local copies, waits for them, and re-layouts  3.93 us (2%)
  other arithmetic  2.16 us (1%)
    ppermute x20, waiting for transfers between devices, swap(): lax.ppermute(x, axis, [(i, i ^ bit) for i in range(lax.axis_size(axis))])  80.6 us
    ppermute x12, starting transfers between devices, shift_z(): lax.ppermute(x, 'dp', [(i, (i + 2 * by) % size) for i in range(size)])  20.5 us
    ppermute x12, waiting for transfers between devices, shift_z(): lax.ppermute(x, 'dp', [(i, (i + 2 * by) % size) for i in range(size)])  19.2 us
    pallas_call x4, Pallas kernels, copies(): pl.pallas_call(functools.partial(copy_kernel, plan, len(ins), len(counts)...  16.7 us
    ppermute x20, starting transfers between devices, swap(): lax.ppermute(x, axis, [(i, i ^ bit) for i in range(lax.axis_size(axis))])  16.6 us
    pallas_call x1, Pallas kernels, hidden_of(): pl.pallas_call(functools.partial(hidden_kernel, len(pieces)), grid=(ff //...  12.7 us
    pallas_call x3, Pallas kernels, down_of(): pl.pallas_call(functools.partial(down_kernel, len(downs)), in_specs=[vmem...  4.94 us
    unnamed x30, local copies, waits for them, and re-layouts  3.74 us
  transfers between devices with their start and end apart: 33, of which 12 were waited for; matrix products, arithmetic and copies ran while one was open for 1% of the time, Pallas kernels for 19%

profile of v6, /device:TPU:0, one launch (start us, length us, event | category | flops | bytes accessed | tf_op | source)
XLA Modules:
  0.0 184.7 jit_solution(17681836388232152633)
XLA Ops:
  0.6 3.6 %shard_map.117 = (bf16[2,512,1024]{2,1,0:T(8,128)(2,1)}, bf16[1,512,1024]{2,1,0:T(8,128)(2,1)}) custom-call(s32[16]{0:T(128)} %refs_0_.7, s32[16]{0:T(128)} %refs_1_.7, bf16[2,512,1024]{2,1,0:T(8,128)(2,1)} %refs_2_.5, bf16[2,512,1024]{2,1,0:T(8,128)(2,1)} %refs_3_.5, bf16[2,512,1024]{2,1,0:T(8,128)(2,1)} %refs_4_.3), custom_call_target="tpu_custom_call" | custom-call | tf_op jit(solution)/shard_map/pallas_call | solution.py:103
  4.8 3.3 %shard_map.112.refs_8_ = bf16[2,512,1024]{2,1,0:T(8,128)(2,1)} custom-call(s32[16]{0:T(128)} %refs_0_.7, s32[16]{0:T(128)} %refs_1_.7, bf16[2,512,1024]{2,1,0:T(8,128)(2,1)} %refs_2_.5, bf16[2,512,1024]{2,1,0:T(8,128)(2,1)} %refs_3_.5), custom_call_target="tpu_custom_call" | custom-call | tf_op jit(solution)/shard_map/pallas_call | solution.py:103
  8.2 2.6 %collective-permute-start.1 = (bf16[2,512,1024]{2,1,0:T(8,128)(2,1)}, bf16[2,512,1024]{2,1,0:T(8,128)(2,1)S(1)}, u32[]{:S(2)}, u32[]{:S(2)}) collective-permute-start(bf16[2,512,1024]{2,1,0:T(8,128)(2,1)} %shard_map.112.refs_8_), channel_id=1, source_target_pairs={{0,2},{1,3},{2,0},{3,1},{4,6},{5,7},{6,4},{7,5},{8,10},{9,11},{10,... | collective-permute-start | bytes 6291464 | tf_op jit(solution)/shard_map/ppermute | solution.py:17
  11.4 1.6 collective-permute-start
  13.0 1.6 collective-permute-start.2
  14.6 2.6 %collective-permute-start.4 = (bf16[64,2176]{1,0:T(8,128)(2,1)S(1)}, bf16[64,2176]{1,0:T(8,128)(2,1)S(1)}, u32[]{:S(2)}, u32[]{:S(2)}) collective-permute-start(bf16[64,2176]{1,0:T(8,128)(2,1)S(1)} %shard_map.111), channel_id=1, source_target_pairs={{0,16},{4,20},{8,24},{12,28},{16,0},{20,4},{24,8},{28,12},{1,17},{... | collective-permute-start | bytes 835592 | tf_op jit(solution)/shard_map/ppermute | solution.py:27
  17.2 3.1 %collective-permute-done = bf16[64,2176]{1,0:T(8,128)(2,1)S(1)} collective-permute-done((bf16[64,2176]{1,0:T(8,128)(2,1)S(1)}, bf16[64,2176]{1,0:T(8,128)(2,1)S(1)}, u32[]{:S(2)}, u32[]{:S(2)}) %collective-permute-start) | collective-permute-done | bytes 278560 | tf_op jit(solution)/shard_map/ppermute | solution.py:17
  20.3 3.6 %collective-permute-start.6 = (bf16[64,2176]{1,0:T(8,128)(2,1)S(1)}, bf16[64,2176]{1,0:T(8,128)(2,1)S(1)}, u32[]{:S(2)}, u32[]{:S(2)}) collective-permute-start(bf16[64,2176]{1,0:T(8,128)(2,1)S(1)} %shard_map.111), channel_id=1, source_target_pairs={{0,24},{4,28},{8,0},{12,4},{16,8},{20,12},{24,16},{28,20},{1,25},{... | collective-permute-start | bytes 835592 | tf_op jit(solution)/shard_map/ppermute | solution.py:27
  26.8 8.6 %collective-permute-done.4 = bf16[64,2176]{1,0:T(8,128)(2,1)S(1)} collective-permute-done((bf16[64,2176]{1,0:T(8,128)(2,1)S(1)}, bf16[64,2176]{1,0:T(8,128)(2,1)S(1)}, u32[]{:S(2)}, u32[]{:S(2)}) %collective-permute-start.4) | collective-permute-done | bytes 278560 | tf_op jit(solution)/shard_map/ppermute | solution.py:27
  37.5 20.0 %collective-permute-done.1.refs_1_.refs_10_ = bf16[2,512,1024]{2,1,0:T(8,128)(2,1)S(1)} collective-permute-done((bf16[2,512,1024]{2,1,0:T(8,128)(2,1)}, bf16[2,512,1024]{2,1,0:T(8,128)(2,1)S(1)}, u32[]{:S(2)}, u32[]{:S(2)}) %collective-permute-start.1) | collective-permute-done | bytes 2097184 | tf_op jit(solution)/shard_map/ppermute | solution.py:17
  59.4 6.1 %shard_map.122 = (bf16[3,512,1024]{2,1,0:T(8,128)(2,1)}, bf16[2,512,1024]{2,1,0:T(8,128)(2,1)}, bf16[2,512,1024]{2,1,0:T(8,128)(2,1)}, bf16[2,512,1024]{2,1,0:T(8,128)(2,1)}) custom-call(s32[16]{0:T(128)} %refs_0_.7, s32[16]{0:T(128)} %refs_1_.7, bf16[2,512,1024]{2,1,0:T(8,128)(2,1)} %refs_2_.5, bf16[2,512,1024]{2,1,0:T(8,128)(2,1)} %refs_3_.5, ...), custom_call_target="tpu_custom_call" | custom-call | tf_op jit(solution)/shard_map/pallas_call | solution.py:103
  65.6 2.0 %collective-permute-start.27 = (bf16[3,512,1024]{2,1,0:T(8,128)(2,1)}, bf16[3,512,1024]{2,1,0:T(8,128)(2,1)S(1)}, u32[]{:S(2)}, u32[]{:S(2)}) collective-permute-start(bf16[3,512,1024]{2,1,0:T(8,128)(2,1)} %get-tuple-element.29), channel_id=1, source_target_pairs={{0,4},{4,8},{8,12},{12,16},{16,20},{20,24},{24,28},{28,0},{1,5},{5... | collective-permute-start | bytes 9437192 | tf_op jit(solution)/shard_map/ppermute | solution.py:22
  68.3 2.9 %shard_map.119 = (bf16[512,1024]{1,0:T(8,128)(2,1)}, bf16[512,1024]{1,0:T(8,128)(2,1)}) custom-call(bf16[2,512,1024]{2,1,0:T(8,128)(2,1)} %refs_4_.3, bf16[1,512,1024]{2,1,0:T(8,128)(2,1)} %collective-permute-done.14.other_ref), custom_call_target="tpu_custom_call" | custom-call | tf_op jit(solution)/shard_map/pallas_call | solution.py:142
  71.2 1.6 collective-permute-start.20
  72.8 29.7 %collective-permute-done.13.refs_11_ = bf16[2,512,1024]{2,1,0:T(8,128)(2,1)} collective-permute-done((bf16[2,512,1024]{2,1,0:T(8,128)(2,1)}, bf16[2,512,1024]{2,1,0:T(8,128)(2,1)}, u32[]{:S(2)}, u32[]{:S(2)}) %collective-permute-start.13) | collective-permute-done | bytes 2097184 | tf_op jit(solution)/shard_map/ppermute | solution.py:17
  102.5 1.6 copy-done.7
  104.1 12.7 %shard_map.118.hidden_ref = bf16[1024,1024]{1,0:T(8,128)(2,1)S(1)} custom-call(bf16[128,2176]{1,0:T(8,128)(2,1)} %shard_map.113.refs_0_.refs_5_, bf16[128,2176]{1,0:T(8,128)(2,1)S(1)} %copy-done.2, bf16[128,2176]{1,0:T(8,128)(2,1)S(1)} %copy-done.4, bf16[128,2176]{1,0:T(8,128)(2,1)S(1)} %copy-done.6, bf16[128,2176]{1,0:T(8,128)(2,1)S(1)} %collective-permute-done.8.refs_4_, ...), custom_call_target="tpu_custom_call" | custom-call | flops 1 | bytes 1 | tf_op jit(solution)/shard_map/pallas_call | solution.py:209
  116.8 2.4 %shard_map.120 = (bf16[512,1024]{1,0:T(8,128)(2,1)S(1)}, bf16[512,1024]{1,0:T(8,128)(2,1)S(1)}) custom-call(bf16[1024,1024]{1,0:T(8,128)(2,1)S(1)} %shard_map.118.hidden_ref, bf16[512,1024]{1,0:T(8,128)(2,1)S(1)} %copy-done.9, bf16[512,1024]{1,0:T(8,128)(2,1)S(1)} %copy-done.8), custom_call_target="tpu_custom_call" | custom-call | flops 1 | bytes 1 | tf_op jit(solution)/shard_map/pallas_call | solution.py:246
  119.3 2.0 %collective-permute-start.26 = (bf16[512,1024]{1,0:T(8,128)(2,1)S(1)}, bf16[512,1024]{1,0:T(8,128)(2,1)S(1)}, u32[]{:S(2)}, u32[]{:S(2)}) collective-permute-start(bf16[512,1024]{1,0:T(8,128)(2,1)S(1)} %copy-done.8), channel_id=1, source_target_pairs={{0,2},{1,3},{2,0},{3,1},{4,6},{5,7},{6,4},{7,5},{8,10},{9,11},{10,... | collective-permute-start | bytes 3145736 | tf_op jit(solution)/shard_map/ppermute | solution.py:17
  121.3 3.6 %collective-permute-done.20.refs_0_ = bf16[512,1024]{1,0:T(8,128)(2,1)S(1)} collective-permute-done((bf16[512,1024]{1,0:T(8,128)(2,1)}, bf16[512,1024]{1,0:T(8,128)(2,1)S(1)}, u32[]{:S(2)}, u32[]{:S(2)}) %collective-permute-start.20) | collective-permute-done | bytes 1048608 | tf_op jit(solution)/shard_map/ppermute | solution.py:17
  126.7 2.0 %collective-permute-start.16 = (bf16[4,64,1024]{2,1,0:T(8,128)(2,1)S(1)}, bf16[4,64,1024]{2,1,0:T(8,128)(2,1)S(1)}, u32[]{:S(2)}, u32[]{:S(2)}) collective-permute-start(bf16[4,64,1024]{2,1,0:T(8,128)(2,1)S(1)} %fusion.1), channel_id=1, source_target_pairs={{0,4},{4,0},{8,12},{12,8},{16,20},{20,16},{24,28},{28,24},{1,5},{5... | collective-permute-start | bytes 1572872 | tf_op jit(solution)/shard_map/ppermute | solution.py:17
  130.3 20.5 %collective-permute-done.16 = bf16[4,64,1024]{2,1,0:T(8,128)(2,1)S(1)} collective-permute-done((bf16[4,64,1024]{2,1,0:T(8,128)(2,1)S(1)}, bf16[4,64,1024]{2,1,0:T(8,128)(2,1)S(1)}, u32[]{:S(2)}, u32[]{:S(2)}) %collective-permute-start.16) | collective-permute-done | bytes 524320 | tf_op jit(solution)/shard_map/ppermute | solution.py:17
  152.7 3.7 %collective-permute-done.22 = bf16[4,64,512]{2,1,0:T(8,128)(2,1)S(1)} collective-permute-done((bf16[4,64,512]{2,1,0:T(8,128)(2,1)S(1)}, bf16[4,64,512]{2,1,0:T(8,128)(2,1)S(1)}, u32[]{:S(2)}, u32[]{:S(2)}) %collective-permute-start.22) | collective-permute-done | bytes 262176 | tf_op jit(solution)/shard_map/ppermute | solution.py:17
  156.6 2.3 %collective-permute-start.24 = (bf16[64,512]{1,0:T(8,128)(2,1)S(1)}, bf16[64,512]{1,0:T(8,128)(2,1)S(1)}, u32[]{:S(2)}, u32[]{:S(2)}) collective-permute-start(bf16[64,512]{1,0:T(8,128)(2,1)S(1)} %get-tuple-element.52), channel_id=1, source_target_pairs={{0,16},{4,20},{8,24},{12,28},{16,0},{20,4},{24,8},{28,12},{1,17},{... | collective-permute-start | bytes 196616 | tf_op jit(solution)/shard_map/ppermute | solution.py:27
  158.9 1.6 collective-permute-start.23
  161.1 2.3 %collective-permute-done.25 = bf16[64,512]{1,0:T(8,128)(2,1)S(1)} collective-permute-done((bf16[64,512]{1,0:T(8,128)(2,1)S(1)}, bf16[64,512]{1,0:T(8,128)(2,1)S(1)}, u32[]{:S(2)}, u32[]{:S(2)}) %collective-permute-start.25) | collective-permute-done | bytes 65568 | tf_op jit(solution)/shard_map/ppermute | solution.py:27
  163.4 1.8 collective-permute-done.24
  169.2 3.6 %shard_map.125 = (bf16[2,512,1024]{2,1,0:T(8,128)(2,1)}, bf16[2,512,1024]{2,1,0:T(8,128)(2,1)}, bf16[2,512,1024]{2,1,0:T(8,128)(2,1)}) custom-call(s32[16]{0:T(128)} %refs_0_.7, s32[16]{0:T(128)} %refs_1_.7, bf16[3,512,1024]{2,1,0:T(8,128)(2,1)} %copy-done, ...), custom_call_target="tpu_custom_call", output_to_operand_aliasing={{0}: (3, {}), {1}: (4, {}), {2}: (5, {})} | custom-call | tf_op jit(solution)/shard_map/pallas_call | solution.py:103
  173.8 1.6 collective-permute-start.31
  175.4 2.5 %collective-permute-start.30 = (bf16[64,512]{1,0:T(8,128)(2,1)S(1)}, bf16[64,512]{1,0:T(8,128)(2,1)S(1)}, u32[]{:S(2)}, u32[]{:S(2)}) collective-permute-start(bf16[64,512]{1,0:T(8,128)(2,1)S(1)} %get-tuple-element.47), channel_id=1, source_target_pairs={{0,24},{4,28},{8,0},{12,4},{16,8},{20,12},{24,16},{28,20},{1,25},{... | collective-permute-start | bytes 196616 | tf_op jit(solution)/shard_map/ppermute | solution.py:27
  178.0 1.7 collective-permute-done.32
  179.7 4.2 %collective-permute-done.31 = bf16[64,512]{1,0:T(8,128)(2,1)S(1)} collective-permute-done((bf16[64,512]{1,0:T(8,128)(2,1)S(1)}, bf16[64,512]{1,0:T(8,128)(2,1)S(1)}, u32[]{:S(2)}, u32[]{:S(2)}) %collective-permute-start.31) | collective-permute-done | bytes 65568 | tf_op jit(solution)/shard_map/ppermute | solution.py:27
  (98 shorter events, 20.7 us)
Async XLA Ops:
  4.3 21.1 %collective-permute-start.12 = (bf16[2,512,1024]{2,1,0:T(8,128)(2,1)}, bf16[2,512,1024]{2,1,0:T(8,128)(2,1)}, u32[]{:S(2)}, u32[]{:S(2)}) collective-permute-start(bf16[2,512,1024]{2,1,0:T(8,128)(2,1)} %get-tuple-element.21), channel_id=1, source_target_pairs={{0,1},{1,0},{2,3},{3,2},{4,5},{5,4},{6,7},{7,6},{8,9},{9,8},{10,11... | collective-permute-start | bytes 6291464 | tf_op jit(solution)/shard_map/ppermute | solution.py:17
  8.2 49.3 %collective-permute-start.1 = (bf16[2,512,1024]{2,1,0:T(8,128)(2,1)}, bf16[2,512,1024]{2,1,0:T(8,128)(2,1)S(1)}, u32[]{:S(2)}, u32[]{:S(2)}) collective-permute-start(bf16[2,512,1024]{2,1,0:T(8,128)(2,1)} %shard_map.112.refs_8_), channel_id=1, source_target_pairs={{0,2},{1,3},{2,0},{3,1},{4,6},{5,7},{6,4},{7,5},{8,10},{9,11},{10,... | collective-permute-start | bytes 6291464 | tf_op jit(solution)/shard_map/ppermute | solution.py:17
  11.4 8.8 %collective-permute-start = (bf16[64,2176]{1,0:T(8,128)(2,1)S(1)}, bf16[64,2176]{1,0:T(8,128)(2,1)S(1)}, u32[]{:S(2)}, u32[]{:S(2)}) collective-permute-start(bf16[64,2176]{1,0:T(8,128)(2,1)S(1)} %shard_map.111), channel_id=1, source_target_pairs={{0,4},{4,0},{8,12},{12,8},{16,20},{20,16},{24,28},{28,24},{1,5},{5... | collective-permute-start | bytes 835592 | tf_op jit(solution)/shard_map/ppermute | solution.py:17
  13.0 11.4 %collective-permute-start.2 = (bf16[64,2176]{1,0:T(8,128)(2,1)S(1)}, bf16[64,2176]{1,0:T(8,128)(2,1)S(1)}, u32[]{:S(2)}, u32[]{:S(2)}) collective-permute-start(bf16[64,2176]{1,0:T(8,128)(2,1)S(1)} %shard_map.111), channel_id=1, source_target_pairs={{0,8},{4,12},{8,16},{12,20},{16,24},{20,28},{24,0},{28,4},{1,9},{5... | collective-permute-start | bytes 835592 | tf_op jit(solution)/shard_map/ppermute | solution.py:27
  14.6 20.8 %collective-permute-start.4 = (bf16[64,2176]{1,0:T(8,128)(2,1)S(1)}, bf16[64,2176]{1,0:T(8,128)(2,1)S(1)}, u32[]{:S(2)}, u32[]{:S(2)}) collective-permute-start(bf16[64,2176]{1,0:T(8,128)(2,1)S(1)} %shard_map.111), channel_id=1, source_target_pairs={{0,16},{4,20},{8,24},{12,28},{16,0},{20,4},{24,8},{28,12},{1,17},{... | collective-permute-start | bytes 835592 | tf_op jit(solution)/shard_map/ppermute | solution.py:27
  20.3 15.1 %collective-permute-start.6 = (bf16[64,2176]{1,0:T(8,128)(2,1)S(1)}, bf16[64,2176]{1,0:T(8,128)(2,1)S(1)}, u32[]{:S(2)}, u32[]{:S(2)}) collective-permute-start(bf16[64,2176]{1,0:T(8,128)(2,1)S(1)} %shard_map.111), channel_id=1, source_target_pairs={{0,24},{4,28},{8,0},{12,4},{16,8},{20,12},{24,16},{28,20},{1,25},{... | collective-permute-start | bytes 835592 | tf_op jit(solution)/shard_map/ppermute | solution.py:27
  24.4 11.8 %collective-permute-start.3 = (bf16[64,2176]{1,0:T(8,128)(2,1)S(1)}, bf16[64,2176]{1,0:T(8,128)(2,1)S(1)}, u32[]{:S(2)}, u32[]{:S(2)}) collective-permute-start(bf16[64,2176]{1,0:T(8,128)(2,1)S(1)} %collective-permute-done.2), channel_id=1, source_target_pairs={{0,4},{4,0},{8,12},{12,8},{16,20},{20,16},{24,28},{28,24},{1,5},{5... | collective-permute-start | bytes 835592 | tf_op jit(solution)/shard_map/ppermute | solution.py:17
  25.4 77.1 %collective-permute-start.13 = (bf16[2,512,1024]{2,1,0:T(8,128)(2,1)}, bf16[2,512,1024]{2,1,0:T(8,128)(2,1)}, u32[]{:S(2)}, u32[]{:S(2)}) collective-permute-start(bf16[2,512,1024]{2,1,0:T(8,128)(2,1)} %collective-permute-done.12.refs_9_), channel_id=1, source_target_pairs={{0,2},{1,3},{2,0},{3,1},{4,6},{5,7},{6,4},{7,5},{8,10},{9,11},{10,... | collective-permute-start | bytes 6291464 | tf_op jit(solution)/shard_map/ppermute | solution.py:17
  35.4 32.4 %collective-permute-start.14 = (bf16[1,512,1024]{2,1,0:T(8,128)(2,1)}, bf16[1,512,1024]{2,1,0:T(8,128)(2,1)}, u32[]{:S(2)}, u32[]{:S(2)}) collective-permute-start(bf16[1,512,1024]{2,1,0:T(8,128)(2,1)} %get-tuple-element.22), channel_id=1, source_target_pairs={{0,1},{1,0},{2,3},{3,2},{4,5},{5,4},{6,7},{7,6},{8,9},{9,8},{10,11... | collective-permute-start | bytes 3145736 | tf_op jit(solution)/shard_map/ppermute | solution.py:17
  35.4 22.1 %collective-permute-start.5 = (bf16[64,2176]{1,0:T(8,128)(2,1)S(1)}, bf16[64,2176]{1,0:T(8,128)(2,1)S(1)}, u32[]{:S(2)}, u32[]{:S(2)}) collective-permute-start(bf16[64,2176]{1,0:T(8,128)(2,1)S(1)} %collective-permute-done.4), channel_id=1, source_target_pairs={{0,4},{4,0},{8,12},{12,8},{16,20},{20,16},{24,28},{28,24},{1,5},{5... | collective-permute-start | bytes 835592 | tf_op jit(solution)/shard_map/ppermute | solution.py:17
  36.2 21.3 %collective-permute-start.7 = (bf16[64,2176]{1,0:T(8,128)(2,1)S(1)}, bf16[64,2176]{1,0:T(8,128)(2,1)S(1)}, u32[]{:S(2)}, u32[]{:S(2)}) collective-permute-start(bf16[64,2176]{1,0:T(8,128)(2,1)S(1)} %collective-permute-done.6), channel_id=1, source_target_pairs={{0,4},{4,0},{8,12},{12,8},{16,20},{20,16},{24,28},{28,24},{1,5},{5... | collective-permute-start | bytes 835592 | tf_op jit(solution)/shard_map/ppermute | solution.py:17
  57.5 10.6 %collective-permute-start.8 = (bf16[128,2176]{1,0:T(8,128)(2,1)}, bf16[128,2176]{1,0:T(8,128)(2,1)S(1)}, u32[]{:S(2)}, u32[]{:S(2)}) collective-permute-start(bf16[128,2176]{1,0:T(8,128)(2,1)} %shard_map.113.refs_0_.refs_5_), channel_id=1, source_target_pairs={{0,1},{1,0},{2,3},{3,2},{4,5},{5,4},{6,7},{7,6},{8,9},{9,8},{10,11... | collective-permute-start | bytes 1671176 | tf_op jit(solution)/shard_map/ppermute | solution.py:17
  65.6 85.5 %collective-permute-start.27 = (bf16[3,512,1024]{2,1,0:T(8,128)(2,1)}, bf16[3,512,1024]{2,1,0:T(8,128)(2,1)S(1)}, u32[]{:S(2)}, u32[]{:S(2)}) collective-permute-start(bf16[3,512,1024]{2,1,0:T(8,128)(2,1)} %get-tuple-element.29), channel_id=1, source_target_pairs={{0,4},{4,8},{8,12},{12,16},{16,20},{20,24},{24,28},{28,0},{1,5},{5... | collective-permute-start | bytes 9437192 | tf_op jit(solution)/shard_map/ppermute | solution.py:22
  67.5 3.7 %collective-permute-start.9 = (bf16[128,2176]{1,0:T(8,128)(2,1)}, bf16[128,2176]{1,0:T(8,128)(2,1)S(1)}, u32[]{:S(2)}, u32[]{:S(2)}) collective-permute-start(bf16[128,2176]{1,0:T(8,128)(2,1)} %copy-done.1), channel_id=1, source_target_pairs={{0,1},{1,0},{2,3},{3,2},{4,5},{5,4},{6,7},{7,6},{8,9},{9,8},{10,11... | collective-permute-start | bytes 1671176 | tf_op jit(solution)/shard_map/ppermute | solution.py:17
  67.8 5.1 %collective-permute-start.10 = (bf16[128,2176]{1,0:T(8,128)(2,1)}, bf16[128,2176]{1,0:T(8,128)(2,1)}, u32[]{:S(2)}, u32[]{:S(2)}) collective-permute-start(bf16[128,2176]{1,0:T(8,128)(2,1)} %copy-done.3), channel_id=1, source_target_pairs={{0,1},{1,0},{2,3},{3,2},{4,5},{5,4},{6,7},{7,6},{8,9},{9,8},{10,11... | collective-permute-start | bytes 1671176 | tf_op jit(solution)/shard_map/ppermute | solution.py:17
  68.1 4.8 %collective-permute-start.11 = (bf16[128,2176]{1,0:T(8,128)(2,1)}, bf16[128,2176]{1,0:T(8,128)(2,1)}, u32[]{:S(2)}, u32[]{:S(2)}) collective-permute-start(bf16[128,2176]{1,0:T(8,128)(2,1)} %copy-done.5), channel_id=1, source_target_pairs={{0,1},{1,0},{2,3},{3,2},{4,5},{5,4},{6,7},{7,6},{8,9},{9,8},{10,11... | collective-permute-start | bytes 1671176 | tf_op jit(solution)/shard_map/ppermute | solution.py:17
  71.2 53.6 %collective-permute-start.20 = (bf16[512,1024]{1,0:T(8,128)(2,1)}, bf16[512,1024]{1,0:T(8,128)(2,1)S(1)}, u32[]{:S(2)}, u32[]{:S(2)}) collective-permute-start(bf16[512,1024]{1,0:T(8,128)(2,1)} %get-tuple-element.23.refs_0_), channel_id=1, source_target_pairs={{0,2},{1,3},{2,0},{3,1},{4,6},{5,7},{6,4},{7,5},{8,10},{9,11},{10,... | collective-permute-start | bytes 3145736 | tf_op jit(solution)/shard_map/ppermute | solution.py:17
  119.2 7.0 %collective-permute-start.15 = (bf16[512,1024]{1,0:T(8,128)(2,1)S(1)}, bf16[512,1024]{1,0:T(8,128)(2,1)S(1)}, u32[]{:S(2)}, u32[]{:S(2)}) collective-permute-start(bf16[512,1024]{1,0:T(8,128)(2,1)S(1)} %get-tuple-element.26.refs_1_), channel_id=1, source_target_pairs={{0,1},{1,0},{2,3},{3,2},{4,5},{5,4},{6,7},{7,6},{8,9},{9,8},{10,11... | collective-permute-start | bytes 3145736 | tf_op jit(solution)/shard_map/ppermute | solution.py:17
  119.3 31.8 %collective-permute-start.26 = (bf16[512,1024]{1,0:T(8,128)(2,1)S(1)}, bf16[512,1024]{1,0:T(8,128)(2,1)S(1)}, u32[]{:S(2)}, u32[]{:S(2)}) collective-permute-start(bf16[512,1024]{1,0:T(8,128)(2,1)S(1)} %copy-done.8), channel_id=1, source_target_pairs={{0,2},{1,3},{2,0},{3,1},{4,6},{5,7},{6,4},{7,5},{8,10},{9,11},{10,... | collective-permute-start | bytes 3145736 | tf_op jit(solution)/shard_map/ppermute | solution.py:17
  126.7 24.1 %collective-permute-start.16 = (bf16[4,64,1024]{2,1,0:T(8,128)(2,1)S(1)}, bf16[4,64,1024]{2,1,0:T(8,128)(2,1)S(1)}, u32[]{:S(2)}, u32[]{:S(2)}) collective-permute-start(bf16[4,64,1024]{2,1,0:T(8,128)(2,1)S(1)} %fusion.1), channel_id=1, source_target_pairs={{0,4},{4,0},{8,12},{12,8},{16,20},{20,16},{24,28},{28,24},{1,5},{5... | collective-permute-start | bytes 1572872 | tf_op jit(solution)/shard_map/ppermute | solution.py:17
  128.9 27.5 %collective-permute-start.22 = (bf16[4,64,512]{2,1,0:T(8,128)(2,1)S(1)}, bf16[4,64,512]{2,1,0:T(8,128)(2,1)S(1)}, u32[]{:S(2)}, u32[]{:S(2)}) collective-permute-start(bf16[4,64,512]{2,1,0:T(8,128)(2,1)S(1)} %fusion.4), channel_id=1, source_target_pairs={{0,4},{4,0},{8,12},{12,8},{16,20},{20,16},{24,28},{28,24},{1,5},{5... | collective-permute-start | bytes 786440 | tf_op jit(solution)/shard_map/ppermute | solution.py:17
  152.7 7.8 %collective-permute-start.28 = (bf16[512,512]{1,0:T(8,128)(2,1)S(1)}, bf16[512,512]{1,0:T(8,128)(2,1)S(1)}, u32[]{:S(2)}, u32[]{:S(2)}) collective-permute-start(bf16[512,512]{1,0:T(8,128)(2,1)S(1)} %get-tuple-element.31.refs_6_), channel_id=1, source_target_pairs={{0,1},{1,0},{2,3},{3,2},{4,5},{5,4},{6,7},{7,6},{8,9},{9,8},{10,11... | collective-permute-start | bytes 1572872 | tf_op jit(solution)/shard_map/ppermute | solution.py:17
  156.5 6.8 %collective-permute-start.25 = (bf16[64,512]{1,0:T(8,128)(2,1)S(1)}, bf16[64,512]{1,0:T(8,128)(2,1)S(1)}, u32[]{:S(2)}, u32[]{:S(2)}) collective-permute-start(bf16[64,512]{1,0:T(8,128)(2,1)S(1)} %get-tuple-element.51), channel_id=1, source_target_pairs={{0,8},{4,12},{8,16},{12,20},{16,24},{20,28},{24,0},{28,4},{1,9},{5... | collective-permute-start | bytes 196616 | tf_op jit(solution)/shard_map/ppermute | solution.py:27
  156.6 8.6 %collective-permute-start.24 = (bf16[64,512]{1,0:T(8,128)(2,1)S(1)}, bf16[64,512]{1,0:T(8,128)(2,1)S(1)}, u32[]{:S(2)}, u32[]{:S(2)}) collective-permute-start(bf16[64,512]{1,0:T(8,128)(2,1)S(1)} %get-tuple-element.52), channel_id=1, source_target_pairs={{0,16},{4,20},{8,24},{12,28},{16,0},{20,4},{24,8},{28,12},{1,17},{... | collective-permute-start | bytes 196616 | tf_op jit(solution)/shard_map/ppermute | solution.py:27
  158.9 6.3 %collective-permute-start.23 = (bf16[64,512]{1,0:T(8,128)(2,1)S(1)}, bf16[64,512]{1,0:T(8,128)(2,1)S(1)}, u32[]{:S(2)}, u32[]{:S(2)}) collective-permute-start(bf16[64,512]{1,0:T(8,128)(2,1)S(1)} %get-tuple-element.50), channel_id=1, source_target_pairs={{0,24},{4,28},{8,0},{12,4},{16,8},{20,12},{24,16},{28,20},{1,25},{... | collective-permute-start | bytes 196616 | tf_op jit(solution)/shard_map/ppermute | solution.py:27
  160.6 12.1 %collective-permute-start.29 = (bf16[4,64,512]{2,1,0:T(8,128)(2,1)S(1)}, bf16[4,64,512]{2,1,0:T(8,128)(2,1)S(1)}, u32[]{:S(2)}, u32[]{:S(2)}) collective-permute-start(bf16[4,64,512]{2,1,0:T(8,128)(2,1)S(1)} %fusion.5), channel_id=1, source_target_pairs={{0,4},{4,0},{8,12},{12,8},{16,20},{20,16},{24,28},{28,24},{1,5},{5... | collective-permute-start | bytes 786440 | tf_op jit(solution)/shard_map/ppermute | solution.py:17
  165.3 10.2 %collective-permute-start.19 = (bf16[64,1024]{1,0:T(8,128)(2,1)S(1)}, bf16[64,1024]{1,0:T(8,128)(2,1)S(1)}, u32[]{:S(2)}, u32[]{:S(2)}) collective-permute-start(bf16[64,1024]{1,0:T(8,128)(2,1)S(1)} %get-tuple-element.45), channel_id=1, source_target_pairs={{0,8},{4,12},{8,16},{12,20},{16,24},{20,28},{24,0},{28,4},{1,9},{5... | collective-permute-start | bytes 393224 | tf_op jit(solution)/shard_map/ppermute | solution.py:27
  166.7 11.2 %collective-permute-start.18 = (bf16[64,1024]{1,0:T(8,128)(2,1)S(1)}, bf16[64,1024]{1,0:T(8,128)(2,1)S(1)}, u32[]{:S(2)}, u32[]{:S(2)}) collective-permute-start(bf16[64,1024]{1,0:T(8,128)(2,1)S(1)} %get-tuple-element.46), channel_id=1, source_target_pairs={{0,16},{4,20},{8,24},{12,28},{16,0},{20,4},{24,8},{28,12},{1,17},{... | collective-permute-start | bytes 393224 | tf_op jit(solution)/shard_map/ppermute | solution.py:27
  168.0 9.9 %collective-permute-start.17 = (bf16[64,1024]{1,0:T(8,128)(2,1)S(1)}, bf16[64,1024]{1,0:T(8,128)(2,1)S(1)}, u32[]{:S(2)}, u32[]{:S(2)}) collective-permute-start(bf16[64,1024]{1,0:T(8,128)(2,1)S(1)} %get-tuple-element.44), channel_id=1, source_target_pairs={{0,24},{4,28},{8,0},{12,4},{16,8},{20,12},{24,16},{28,20},{1,25},{... | collective-permute-start | bytes 393224 | tf_op jit(solution)/shard_map/ppermute | solution.py:27
  172.9 6.8 %collective-permute-start.32 = (bf16[64,512]{1,0:T(8,128)(2,1)S(1)}, bf16[64,512]{1,0:T(8,128)(2,1)S(1)}, u32[]{:S(2)}, u32[]{:S(2)}) collective-permute-start(bf16[64,512]{1,0:T(8,128)(2,1)S(1)} %get-tuple-element.48), channel_id=1, source_target_pairs={{0,8},{4,12},{8,16},{12,20},{16,24},{20,28},{24,0},{28,4},{1,9},{5... | collective-permute-start | bytes 196616 | tf_op jit(solution)/shard_map/ppermute | solution.py:27
  173.8 10.1 %collective-permute-start.31 = (bf16[64,512]{1,0:T(8,128)(2,1)S(1)}, bf16[64,512]{1,0:T(8,128)(2,1)S(1)}, u32[]{:S(2)}, u32[]{:S(2)}) collective-permute-start(bf16[64,512]{1,0:T(8,128)(2,1)S(1)} %get-tuple-element.49), channel_id=1, source_target_pairs={{0,16},{4,20},{8,24},{12,28},{16,0},{20,4},{24,8},{28,12},{1,17},{... | collective-permute-start | bytes 196616 | tf_op jit(solution)/shard_map/ppermute | solution.py:27
  175.4 8.5 %collective-permute-start.30 = (bf16[64,512]{1,0:T(8,128)(2,1)S(1)}, bf16[64,512]{1,0:T(8,128)(2,1)S(1)}, u32[]{:S(2)}, u32[]{:S(2)}) collective-permute-start(bf16[64,512]{1,0:T(8,128)(2,1)S(1)} %get-tuple-element.47), channel_id=1, source_target_pairs={{0,24},{4,28},{8,0},{12,4},{16,8},{20,12},{24,16},{28,20},{1,25},{... | collective-permute-start | bytes 196616 | tf_op jit(solution)/shard_map/ppermute | solution.py:27
  (16 other events, 178.5 us)

commit v7 on v6

--- a/solution.py
+++ b/solution.py
@@ -22,9 +22,8 @@
     return lax.ppermute(x, axis, [(i, (i + by) % size) for i in range(size)])
 
 
-def shift_z(x, by):
-    size = lax.axis_size("dp")
-    return lax.ppermute(x, "dp", [(i, (i + 2 * by) % size) for i in range(size)])
+def flip_z(x, bits):
+    return swap(x, "dp", 2 * bits)
 
 
 def spread(pieces):
@@ -159,6 +158,8 @@
 
 
 def joined(x, *after):
+    if not after:
+        return x
     anywhere = pl.BlockSpec(memory_space=pl.ANY)
     return pl.pallas_call(
         join_kernel,
@@ -257,17 +258,18 @@
     return kept.astype(jnp.float32) + swap(sent, "shard", 1).astype(jnp.float32)
 
 
-def over_x(total, tok):
+def over_x(total, tok, *after):
     total = total.reshape(-1, 2, tok, total.shape[-1])
-    given = swap(total[:, 1].astype(jnp.bfloat16), "dp", 1)
+    given = swap(joined(total[:, 1].astype(jnp.bfloat16), *after), "dp", 1)
     return total[:, 0] + given.astype(jnp.float32)
 
 
 def over_z(total):
-    out = total[0]
-    for s in range(1, total.shape[0]):
-        out += shift_z(total[s].astype(jnp.bfloat16), -s).astype(jnp.float32)
-    return out.astype(jnp.bfloat16)
+    while total.shape[0] > 1:
+        half = total.shape[0] // 2
+        given = flip_z(total[half:].astype(jnp.bfloat16), half)
+        total = total[:half] + given.astype(jnp.float32)
+    return total[0].astype(jnp.bfloat16)
 
 
 def place_kernel(depth, *refs):
@@ -305,16 +307,16 @@
     (mine,) = copies(((0, "mine", 0, 0), (1, "mine", 0, 1)), places, (w_gate, w_up), (2,))
     theirs, theirs_down = copies(
         ((0, "theirs", 0, 0), (1, "theirs", 0, 1), (2, "theirs", 1, 0)),
-        places, (w_gate, w_up, w_down), (2, 1),
+        places, (w_gate, w_up, w_down), (2, 1), (mine,),
     )
     near_weights = [mine, swap(theirs, "shard", 1)]
     weights = spread(near_weights)
     downs = [spread([d]) for d in in_order(w_down, swap(theirs_down, "shard", 1))]
 
     own = first(tokens, router_probs, expert_ids, old_place)
-    columns = [own] + [shift_z(own, s) for s in range(1, n_z)]
-    near = [jnp.concatenate([c, swap(c, "dp", 1)], axis=0) for c in columns]
-    near = [joined(p, weights[2]) for p in near]
+    columns = [own] + [flip_z(own, j) for j in range(1, n_z)]
+    across = [swap(c, "dp", 1) for c in columns]
+    near = [joined(jnp.concatenate(p, axis=0), weights[2]) for p in zip(columns, across)]
     far = [swap(p, "shard", 1) for p in near]
 
     hidden = hidden_of(near + far, weights)
@@ -325,20 +327,26 @@
     )
     arrive = passed_along(leave, "dp", 1)
 
+    leave, *news = copies(
+        tuple((i, "leaves", 0, i) for i in range(3))
+        + tuple((i, "stays", i + 1, "stays") for i in range(3)),
+        places, (w_gate, w_up, w_down), (3, 2, 2, 2), across,
+    )
+    arrive = passed_along(leave, "dp", 1)
+    news = copies(
+        tuple((0, i, i, "leaves") for i in range(3)), places, (arrive,), (2, 2, 2), (), news
+    )
+
     groups = [[d[0] for d in downs]] + [d[1:] for d in downs]
     kept, sent = down_of(hidden, groups[0], ())
     at_core = over_core(kept, sent)
-    kept, sent = down_of(hidden, groups[1], (sent,))
-    at_x = over_x(at_core, tok)
-    at_core = over_core(kept, sent)
-    kept, last = down_of(hidden, groups[2], (sent, arrive, at_x))
-    parts = [over_z(at_x), over_z(over_x(at_core, tok)), over_z(over_x(over_core(kept, last), tok))]
+    kept, sent = down_of(hidden, groups[1], (sent, news[0]))
+    own_part = over_z(over_x(at_core, tok, sent))
+    at_x = over_x(over_core(kept, sent), tok)
+    kept, sent = down_of(hidden, groups[2], (sent, own_part, at_x))
+    parts = [own_part, over_z(at_x), over_z(over_x(over_core(kept, sent), tok))]
     moe_output = placed(parts, depth, width)
 
-    news = copies(
-        tuple((0, i, i, "leaves") for i in range(3)),
-        places, (arrive,), (2, 2, 2), (last,), news,
-    )
     return (moe_output, *news)
 
 

time: 185 us -> 203 us (1.097)
  waiting for transfers between devices: 99.8 us -> 123 us
  starting transfers between devices: 39 us -> 26.1 us
  local copies, waits for them, and re-layouts: 3.93 us -> 8.51 us
    ppermute x20 -> x29, waiting for transfers between devices: 80.6 us -> 119 us  [swap(): lax.ppermute(x, axis, [(i, i ^ bit) for i in range(lax.axis_size(axis))])]
    ppermute x12 -> x0, starting transfers between devices: 20.5 us -> none  [shift_z(): lax.ppermute(x, 'dp', [(i, (i + 2 * by) % size) for i in range(size)])]
    ppermute x12 -> x0, waiting for transfers between devices: 19.2 us -> none  [shift_z(): lax.ppermute(x, 'dp', [(i, (i + 2 * by) % size) for i in range(size)])]
    ppermute x20 -> x29, starting transfers between devices: 16.6 us -> 24.6 us  [swap(): lax.ppermute(x, axis, [(i, i ^ bit) for i in range(lax.axis_size(axis))])]
    unnamed x30 -> x44, local copies, waits for them, and re-layouts: 3.74 us -> 8.27 us
    ppermute x1, waiting for transfers between devices: 0.01 us -> 4.29 us  [passed_along(): return lax.ppermute(x, axis, [(i, (i + by) % size) for i in range(size)])]
  transfers between devices with their start and end apart: 33 -> 30, of which waited for: 12 -> 15; matrix products, arithmetic and copies ran while one was open for 1% -> 1% of each run, Pallas kernels for 19% -> 15%
where the time goes in v7:
time: 203 us; the launch traced here: 202 us
  waiting for transfers between devices  123 us (61%)
  Pallas kernels  39.8 us (20%)
  starting transfers between devices  26.1 us (13%)
  local copies, waits for them, and re-layouts  8.51 us (4%)
  other arithmetic  3.26 us (2%)
    ppermute x29, waiting for transfers between devices, swap(): lax.ppermute(x, axis, [(i, i ^ bit) for i in range(lax.axis_size(axis))])  119 us
    ppermute x29, starting transfers between devices, swap(): lax.ppermute(x, axis, [(i, i ^ bit) for i in range(lax.axis_size(axis))])  24.6 us
    pallas_call x4, Pallas kernels, copies(): pl.pallas_call(functools.partial(copy_kernel, plan, len(ins), len(counts)...  16.7 us
    pallas_call x1, Pallas kernels, hidden_of(): pl.pallas_call(functools.partial(hidden_kernel, len(pieces)), grid=(ff //...  12.5 us
    unnamed x44, local copies, waits for them, and re-layouts  8.27 us
    pallas_call x3, Pallas kernels, down_of(): pl.pallas_call(functools.partial(down_kernel, len(downs)), in_specs=[vmem...  6.16 us
    ppermute x1, waiting for transfers between devices, passed_along(): return lax.ppermute(x, axis, [(i, (i + by) % size) for i in range(size)])  4.29 us
  transfers between devices with their start and end apart: 30, of which 15 were waited for; matrix products, arithmetic and copies ran while one was open for 1% of the time, Pallas kernels for 15%

profile of v7, /device:TPU:0, one launch (start us, length us, event | category | flops | bytes accessed | tf_op | source)
XLA Modules:
  0.0 202.1 jit_solution(6891331793150277180)
XLA Ops:
  0.6 3.3 %shard_map.112.refs_5_.refs_8_ = bf16[2,512,1024]{2,1,0:T(8,128)(2,1)} custom-call(s32[16]{0:T(128)} %refs_0_.7, s32[16]{0:T(128)} %refs_1_.7, bf16[2,512,1024]{2,1,0:T(8,128)(2,1)} %refs_2_.5, bf16[2,512,1024]{2,1,0:T(8,128)(2,1)} %refs_3_.5), custom_call_target="tpu_custom_call" | custom-call | tf_op jit(solution)/shard_map/pallas_call | solution.py:102
  4.0 3.7 %shard_map.117 = (bf16[2,512,1024]{2,1,0:T(8,128)(2,1)}, bf16[1,512,1024]{2,1,0:T(8,128)(2,1)}) custom-call(s32[16]{0:T(128)} %refs_0_.7, s32[16]{0:T(128)} %refs_1_.7, bf16[2,512,1024]{2,1,0:T(8,128)(2,1)} %refs_2_.5, bf16[2,512,1024]{2,1,0:T(8,128)(2,1)} %refs_3_.5, bf16[2,512,1024]{2,1,0:T(8,128)(2,1)} %refs_4_.3, ...), custom_call_target="tpu_custom_call" | custom-call | tf_op jit(solution)/shard_map/pallas_call | solution.py:102
  8.2 2.6 %collective-permute-start.1 = (bf16[2,512,1024]{2,1,0:T(8,128)(2,1)S(1)}, bf16[2,512,1024]{2,1,0:T(8,128)(2,1)S(1)}, u32[]{:S(2)}, u32[]{:S(2)}) collective-permute-start(bf16[2,512,1024]{2,1,0:T(8,128)(2,1)S(1)} %copy-done), channel_id=1, source_target_pairs={{0,2},{1,3},{2,0},{3,1},{4,6},{5,7},{6,4},{7,5},{8,10},{9,11},{10,... | collective-permute-start | bytes 6291464 | tf_op jit(solution)/shard_map/ppermute | solution.py:17
  11.5 2.7 %collective-permute-start.4 = (bf16[64,2176]{1,0:T(8,128)(2,1)S(1)}, bf16[64,2176]{1,0:T(8,128)(2,1)S(1)}, u32[]{:S(2)}, u32[]{:S(2)}) collective-permute-start(bf16[64,2176]{1,0:T(8,128)(2,1)S(1)} %shard_map.111), channel_id=1, source_target_pairs={{0,16},{4,20},{8,24},{12,28},{16,0},{20,4},{24,8},{28,12},{1,17},{... | collective-permute-start | bytes 835592 | tf_op jit(solution)/shard_map/ppermute | solution.py:17
  15.7 18.2 %collective-permute-done.4 = bf16[64,2176]{1,0:T(8,128)(2,1)S(1)} collective-permute-done((bf16[64,2176]{1,0:T(8,128)(2,1)S(1)}, bf16[64,2176]{1,0:T(8,128)(2,1)S(1)}, u32[]{:S(2)}, u32[]{:S(2)}) %collective-permute-start.4) | collective-permute-done | bytes 278560 | tf_op jit(solution)/shard_map/ppermute | solution.py:17
  33.9 1.5 collective-permute-start
  36.0 1.5 collective-permute-start.7
  37.5 6.1 %collective-permute-done.refs_5_ = bf16[64,2176]{1,0:T(8,128)(2,1)S(1)} collective-permute-done((bf16[64,2176]{1,0:T(8,128)(2,1)S(1)}, bf16[64,2176]{1,0:T(8,128)(2,1)S(1)}, u32[]{:S(2)}, u32[]{:S(2)}) %collective-permute-start) | collective-permute-done | bytes 278560 | tf_op jit(solution)/shard_map/ppermute | solution.py:17
  43.5 1.5 collective-permute-start.3
  45.0 4.5 %collective-permute-done.5.refs_7_ = bf16[64,2176]{1,0:T(8,128)(2,1)S(1)} collective-permute-done((bf16[64,2176]{1,0:T(8,128)(2,1)S(1)}, bf16[64,2176]{1,0:T(8,128)(2,1)S(1)}, u32[]{:S(2)}, u32[]{:S(2)}) %collective-permute-start.5) | collective-permute-done | bytes 278560 | tf_op jit(solution)/shard_map/ppermute | solution.py:17
  49.5 6.0 %collective-permute-done.7.refs_8_ = bf16[64,2176]{1,0:T(8,128)(2,1)S(1)} collective-permute-done((bf16[64,2176]{1,0:T(8,128)(2,1)S(1)}, bf16[64,2176]{1,0:T(8,128)(2,1)S(1)}, u32[]{:S(2)}, u32[]{:S(2)}) %collective-permute-start.7) | collective-permute-done | bytes 278560 | tf_op jit(solution)/shard_map/ppermute | solution.py:17
  55.5 3.5 %collective-permute-done.3.refs_6_ = bf16[64,2176]{1,0:T(8,128)(2,1)S(1)} collective-permute-done((bf16[64,2176]{1,0:T(8,128)(2,1)S(1)}, bf16[64,2176]{1,0:T(8,128)(2,1)S(1)}, u32[]{:S(2)}, u32[]{:S(2)}) %collective-permute-start.3) | collective-permute-done | bytes 278560 | tf_op jit(solution)/shard_map/ppermute | solution.py:17
  59.7 6.1 %shard_map.121 = (bf16[3,512,1024]{2,1,0:T(8,128)(2,1)}, bf16[2,512,1024]{2,1,0:T(8,128)(2,1)}, bf16[2,512,1024]{2,1,0:T(8,128)(2,1)}, bf16[2,512,1024]{2,1,0:T(8,128)(2,1)}) custom-call(s32[16]{0:T(128)} %refs_0_.7, s32[16]{0:T(128)} %refs_1_.7, bf16[2,512,1024]{2,1,0:T(8,128)(2,1)} %refs_2_.5, bf16[2,512,1024]{2,1,0:T(8,128)(2,1)} %refs_3_.5, ...), custom_call_target="tpu_custom_call" | custom-call | tf_op jit(solution)/shard_map/pallas_call | solution.py:102
  65.8 1.5 collective-permute-start.17
  73.2 3.0 %shard_map.119 = (bf16[512,1024]{1,0:T(8,128)(2,1)}, bf16[512,1024]{1,0:T(8,128)(2,1)}) custom-call(bf16[2,512,1024]{2,1,0:T(8,128)(2,1)} %refs_4_.3, bf16[1,512,1024]{2,1,0:T(8,128)(2,1)} %copy-done.21), custom_call_target="tpu_custom_call" | custom-call | tf_op jit(solution)/shard_map/pallas_call | solution.py:141
  77.0 1.5 collective-permute-start.16
  78.6 37.7 %collective-permute-done.13.refs_11_ = bf16[2,512,1024]{2,1,0:T(8,128)(2,1)} collective-permute-done((bf16[2,512,1024]{2,1,0:T(8,128)(2,1)}, bf16[2,512,1024]{2,1,0:T(8,128)(2,1)}, u32[]{:S(2)}, u32[]{:S(2)}) %collective-permute-start.13) | collective-permute-done | bytes 2097184 | tf_op jit(solution)/shard_map/ppermute | solution.py:17
  119.4 12.5 %shard_map.118.hidden_ref = bf16[1024,1024]{1,0:T(8,128)(2,1)S(1)} custom-call(bf16[128,2176]{1,0:T(8,128)(2,1)S(1)} %shard_map.113.refs_0_, bf16[128,2176]{1,0:T(8,128)(2,1)S(1)} %shard_map.114.refs_1_, bf16[128,2176]{1,0:T(8,128)(2,1)S(1)} %shard_map.115.refs_2_, bf16[128,2176]{1,0:T(8,128)(2,1)S(1)} %copy-done.3, ...), custom_call_target="tpu_custom_call" | custom-call | flops 1 | bytes 1 | tf_op jit(solution)/shard_map/pallas_call | solution.py:210
  131.9 2.4 %shard_map.120 = (bf16[512,1024]{1,0:T(8,128)(2,1)S(1)}, bf16[512,1024]{1,0:T(8,128)(2,1)S(1)}) custom-call(bf16[1024,1024]{1,0:T(8,128)(2,1)S(1)} %shard_map.118.hidden_ref, bf16[512,1024]{1,0:T(8,128)(2,1)S(1)} %copy-done.6, bf16[512,1024]{1,0:T(8,128)(2,1)S(1)} %copy-done.4), custom_call_target="tpu_custom_call" | custom-call | flops 1 | bytes 1 | tf_op jit(solution)/shard_map/pallas_call | solution.py:247
  134.4 4.3 %collective-permute-done.17.refs_2_ = bf16[3,512,1024]{2,1,0:T(8,128)(2,1)} collective-permute-done((bf16[3,512,1024]{2,1,0:T(8,128)(2,1)}, bf16[3,512,1024]{2,1,0:T(8,128)(2,1)}, u32[]{:S(2)}, u32[]{:S(2)}) %collective-permute-start.17) | collective-permute-done | bytes 3145760 | tf_op jit(solution)/shard_map/ppermute | solution.py:22
  138.7 3.6 %shard_map.122 = (bf16[2,512,1024]{2,1,0:T(8,128)(2,1)}, bf16[2,512,1024]{2,1,0:T(8,128)(2,1)}, bf16[2,512,1024]{2,1,0:T(8,128)(2,1)}) custom-call(s32[16]{0:T(128)} %refs_0_.7, s32[16]{0:T(128)} %refs_1_.7, bf16[3,512,1024]{2,1,0:T(8,128)(2,1)} %collective-permute-done.17.refs_2_, ...), custom_call_target="tpu_custom_call", output_to_operand_aliasing={{0}: (3, {}), {1}: (4, {}), {2}: (5, {})} | custom-call | tf_op jit(solution)/shard_map/pallas_call | solution.py:102
  142.3 1.6 copy-done.1
  143.9 2.5 %shard_map.123 = (bf16[512,512]{1,0:T(8,128)(2,1)S(1)}, bf16[512,512]{1,0:T(8,128)(2,1)S(1)}) custom-call(bf16[1024,1024]{1,0:T(8,128)(2,1)S(1)} %shard_map.118.hidden_ref, bf16[512,1024]{1,0:T(8,128)(2,1)} %collective-permute-done.16.refs_0_, bf16[512,1024]{1,0:T(8,128)(2,1)S(1)} %get-tuple-element.26.refs_1_, bf16[2,512,1024]{2,1,0:T(8,128)(2,1)S(1)} %copy-done.1), custom_call_target="tpu_custom_call" | custom-call | flops 1 | bytes 1 | tf_op jit(solution)/shard_map/pallas_call | solution.py:247
  148.6 10.7 %collective-permute-done.18 = bf16[4,64,1024]{2,1,0:T(8,128)(2,1)S(1)} collective-permute-done((bf16[4,64,1024]{2,1,0:T(8,128)(2,1)S(1)}, bf16[4,64,1024]{2,1,0:T(8,128)(2,1)S(1)}, u32[]{:S(2)}, u32[]{:S(2)}) %collective-permute-start.18) | collective-permute-done | bytes 524320 | tf_op jit(solution)/shard_map/ppermute | solution.py:17
  160.8 1.5 collective-permute-start.22
  162.3 9.5 %collective-permute-done.19 = bf16[2,64,1024]{2,1,0:T(8,128)(2,1)S(1)} collective-permute-done((bf16[2,64,1024]{2,1,0:T(8,128)(2,1)S(1)}, bf16[2,64,1024]{2,1,0:T(8,128)(2,1)S(1)}, u32[]{:S(2)}, u32[]{:S(2)}) %collective-permute-start.19) | collective-permute-done | bytes 262176 | tf_op jit(solution)/shard_map/ppermute | solution.py:17
  172.1 4.9 %collective-permute-done.20 = bf16[1,64,1024]{2,1,0:T(8,128)(2,1)S(1)} collective-permute-done((bf16[1,64,1024]{2,1,0:T(8,128)(2,1)S(1)}, bf16[1,64,1024]{2,1,0:T(8,128)(2,1)S(1)}, u32[]{:S(2)}, u32[]{:S(2)}) %collective-permute-start.20) | collective-permute-done | bytes 131104 | tf_op jit(solution)/shard_map/ppermute | solution.py:17
  178.3 1.9 collective-permute-done.26
  182.6 6.3 %collective-permute-done.27 = bf16[4,64,512]{2,1,0:T(8,128)(2,1)S(1)} collective-permute-done((bf16[4,64,512]{2,1,0:T(8,128)(2,1)S(1)}, bf16[4,64,512]{2,1,0:T(8,128)(2,1)S(1)}, u32[]{:S(2)}, u32[]{:S(2)}) %collective-permute-start.27) | collective-permute-done | bytes 262176 | tf_op jit(solution)/shard_map/ppermute | solution.py:17
  190.4 1.4 collective-permute-start.24
  191.8 5.2 %collective-permute-done.28 = bf16[2,64,512]{2,1,0:T(8,128)(2,1)S(1)} collective-permute-done((bf16[2,64,512]{2,1,0:T(8,128)(2,1)S(1)}, bf16[2,64,512]{2,1,0:T(8,128)(2,1)S(1)}, u32[]{:S(2)}, u32[]{:S(2)}) %collective-permute-start.28) | collective-permute-done | bytes 131104 | tf_op jit(solution)/shard_map/ppermute | solution.py:17
  197.1 4.2 %collective-permute-done.29 = bf16[1,64,512]{2,1,0:T(8,128)(2,1)S(1)} collective-permute-done((bf16[1,64,512]{2,1,0:T(8,128)(2,1)S(1)}, bf16[1,64,512]{2,1,0:T(8,128)(2,1)S(1)}, u32[]{:S(2)}, u32[]{:S(2)}) %collective-permute-start.29) | collective-permute-done | bytes 65568 | tf_op jit(solution)/shard_map/ppermute | solution.py:17
  (113 shorter events, 23.8 us)
Async XLA Ops:
  7.7 59.7 %collective-permute-start.12 = (bf16[2,512,1024]{2,1,0:T(8,128)(2,1)}, bf16[2,512,1024]{2,1,0:T(8,128)(2,1)}, u32[]{:S(2)}, u32[]{:S(2)}) collective-permute-start(bf16[2,512,1024]{2,1,0:T(8,128)(2,1)} %get-tuple-element.21), channel_id=1, source_target_pairs={{0,1},{1,0},{2,3},{3,2},{4,5},{5,4},{6,7},{7,6},{8,9},{9,8},{10,11... | collective-permute-start | bytes 6291464 | tf_op jit(solution)/shard_map/ppermute | solution.py:17
  8.2 61.7 %collective-permute-start.1 = (bf16[2,512,1024]{2,1,0:T(8,128)(2,1)S(1)}, bf16[2,512,1024]{2,1,0:T(8,128)(2,1)S(1)}, u32[]{:S(2)}, u32[]{:S(2)}) collective-permute-start(bf16[2,512,1024]{2,1,0:T(8,128)(2,1)S(1)} %copy-done), channel_id=1, source_target_pairs={{0,2},{1,3},{2,0},{3,1},{4,6},{5,7},{6,4},{7,5},{8,10},{9,11},{10,... | collective-permute-start | bytes 6291464 | tf_op jit(solution)/shard_map/ppermute | solution.py:17
  11.5 22.4 %collective-permute-start.4 = (bf16[64,2176]{1,0:T(8,128)(2,1)S(1)}, bf16[64,2176]{1,0:T(8,128)(2,1)S(1)}, u32[]{:S(2)}, u32[]{:S(2)}) collective-permute-start(bf16[64,2176]{1,0:T(8,128)(2,1)S(1)} %shard_map.111), channel_id=1, source_target_pairs={{0,16},{4,20},{8,24},{12,28},{16,0},{20,4},{24,8},{28,12},{1,17},{... | collective-permute-start | bytes 835592 | tf_op jit(solution)/shard_map/ppermute | solution.py:17
  14.1 21.3 %collective-permute-start.6 = (bf16[64,2176]{1,0:T(8,128)(2,1)S(1)}, bf16[64,2176]{1,0:T(8,128)(2,1)S(1)}, u32[]{:S(2)}, u32[]{:S(2)}) collective-permute-start(bf16[64,2176]{1,0:T(8,128)(2,1)S(1)} %shard_map.111), channel_id=1, source_target_pairs={{0,24},{4,28},{8,16},{12,20},{16,8},{20,12},{24,0},{28,4},{1,25},{... | collective-permute-start | bytes 835592 | tf_op jit(solution)/shard_map/ppermute | solution.py:17
  15.5 20.5 %collective-permute-start.2 = (bf16[64,2176]{1,0:T(8,128)(2,1)S(1)}, bf16[64,2176]{1,0:T(8,128)(2,1)S(1)}, u32[]{:S(2)}, u32[]{:S(2)}) collective-permute-start(bf16[64,2176]{1,0:T(8,128)(2,1)S(1)} %shard_map.111), channel_id=1, source_target_pairs={{0,8},{4,12},{8,0},{12,4},{16,24},{20,28},{24,16},{28,20},{1,9},{5... | collective-permute-start | bytes 835592 | tf_op jit(solution)/shard_map/ppermute | solution.py:17
  33.9 9.6 %collective-permute-start = (bf16[64,2176]{1,0:T(8,128)(2,1)S(1)}, bf16[64,2176]{1,0:T(8,128)(2,1)S(1)}, u32[]{:S(2)}, u32[]{:S(2)}) collective-permute-start(bf16[64,2176]{1,0:T(8,128)(2,1)S(1)} %shard_map.111), channel_id=1, source_target_pairs={{0,4},{4,0},{8,12},{12,8},{16,20},{20,16},{24,28},{28,24},{1,5},{5... | collective-permute-start | bytes 835592 | tf_op jit(solution)/shard_map/ppermute | solution.py:17
  35.4 14.1 %collective-permute-start.5 = (bf16[64,2176]{1,0:T(8,128)(2,1)S(1)}, bf16[64,2176]{1,0:T(8,128)(2,1)S(1)}, u32[]{:S(2)}, u32[]{:S(2)}) collective-permute-start(bf16[64,2176]{1,0:T(8,128)(2,1)S(1)} %collective-permute-done.4), channel_id=1, source_target_pairs={{0,4},{4,0},{8,12},{12,8},{16,20},{20,16},{24,28},{28,24},{1,5},{5... | collective-permute-start | bytes 835592 | tf_op jit(solution)/shard_map/ppermute | solution.py:17
  36.0 19.5 %collective-permute-start.7 = (bf16[64,2176]{1,0:T(8,128)(2,1)S(1)}, bf16[64,2176]{1,0:T(8,128)(2,1)S(1)}, u32[]{:S(2)}, u32[]{:S(2)}) collective-permute-start(bf16[64,2176]{1,0:T(8,128)(2,1)S(1)} %collective-permute-done.6), channel_id=1, source_target_pairs={{0,4},{4,0},{8,12},{12,8},{16,20},{20,16},{24,28},{28,24},{1,5},{5... | collective-permute-start | bytes 835592 | tf_op jit(solution)/shard_map/ppermute | solution.py:17
  43.5 15.4 %copy-start.17 = (bf16[64,2176]{1,0:T(8,128)(2,1)}, bf16[64,2176]{1,0:T(8,128)(2,1)S(1)}, u32[]{:S(2)}) copy-start(bf16[64,2176]{1,0:T(8,128)(2,1)S(1)} %collective-permute-done.refs_5_) | copy-start | bytes 835588
  43.5 15.4 %collective-permute-start.3 = (bf16[64,2176]{1,0:T(8,128)(2,1)S(1)}, bf16[64,2176]{1,0:T(8,128)(2,1)S(1)}, u32[]{:S(2)}, u32[]{:S(2)}) collective-permute-start(bf16[64,2176]{1,0:T(8,128)(2,1)S(1)} %collective-permute-done.2), channel_id=1, source_target_pairs={{0,4},{4,0},{8,12},{12,8},{16,20},{20,16},{24,28},{28,24},{1,5},{5... | collective-permute-start | bytes 835592 | tf_op jit(solution)/shard_map/ppermute | solution.py:17
  65.8 72.9 %collective-permute-start.17 = (bf16[3,512,1024]{2,1,0:T(8,128)(2,1)}, bf16[3,512,1024]{2,1,0:T(8,128)(2,1)}, u32[]{:S(2)}, u32[]{:S(2)}) collective-permute-start(bf16[3,512,1024]{2,1,0:T(8,128)(2,1)} %get-tuple-element.27), channel_id=1, source_target_pairs={{0,4},{4,8},{8,12},{12,16},{16,20},{20,24},{24,28},{28,0},{1,5},{5... | collective-permute-start | bytes 9437192 | tf_op jit(solution)/shard_map/ppermute | solution.py:22
  67.4 48.9 %collective-permute-start.13 = (bf16[2,512,1024]{2,1,0:T(8,128)(2,1)}, bf16[2,512,1024]{2,1,0:T(8,128)(2,1)}, u32[]{:S(2)}, u32[]{:S(2)}) collective-permute-start(bf16[2,512,1024]{2,1,0:T(8,128)(2,1)} %collective-permute-done.12.refs_9_), channel_id=1, source_target_pairs={{0,2},{1,3},{2,0},{3,1},{4,6},{5,7},{6,4},{7,5},{8,10},{9,11},{10,... | collective-permute-start | bytes 6291464 | tf_op jit(solution)/shard_map/ppermute | solution.py:17
  67.9 3.9 %collective-permute-start.14 = (bf16[1,512,1024]{2,1,0:T(8,128)(2,1)}, bf16[1,512,1024]{2,1,0:T(8,128)(2,1)S(1)}, u32[]{:S(2)}, u32[]{:S(2)}) collective-permute-start(bf16[1,512,1024]{2,1,0:T(8,128)(2,1)} %get-tuple-element.22), channel_id=1, source_target_pairs={{0,1},{1,0},{2,3},{3,2},{4,5},{5,4},{6,7},{7,6},{8,9},{9,8},{10,11... | collective-permute-start | bytes 3145736 | tf_op jit(solution)/shard_map/ppermute | solution.py:17
  69.9 2.3 %collective-permute-start.10 = (bf16[128,2176]{1,0:T(8,128)(2,1)S(1)}, bf16[128,2176]{1,0:T(8,128)(2,1)S(1)}, u32[]{:S(2)}, u32[]{:S(2)}) collective-permute-start(bf16[128,2176]{1,0:T(8,128)(2,1)S(1)} %shard_map.115.refs_2_), channel_id=1, source_target_pairs={{0,1},{1,0},{2,3},{3,2},{4,5},{5,4},{6,7},{7,6},{8,9},{9,8},{10,11... | collective-permute-start | bytes 1671176 | tf_op jit(solution)/shard_map/ppermute | solution.py:17
  70.9 5.3 %collective-permute-start.11 = (bf16[128,2176]{1,0:T(8,128)(2,1)S(1)}, bf16[128,2176]{1,0:T(8,128)(2,1)S(1)}, u32[]{:S(2)}, u32[]{:S(2)}) collective-permute-start(bf16[128,2176]{1,0:T(8,128)(2,1)S(1)} %shard_map.116.refs_3_), channel_id=1, source_target_pairs={{0,1},{1,0},{2,3},{3,2},{4,5},{5,4},{6,7},{7,6},{8,9},{9,8},{10,11... | collective-permute-start | bytes 1671176 | tf_op jit(solution)/shard_map/ppermute | solution.py:17
  71.7 6.8 %collective-permute-start.9 = (bf16[128,2176]{1,0:T(8,128)(2,1)S(1)}, bf16[128,2176]{1,0:T(8,128)(2,1)}, u32[]{:S(2)}, u32[]{:S(2)}) collective-permute-start(bf16[128,2176]{1,0:T(8,128)(2,1)S(1)} %shard_map.114.refs_1_), channel_id=1, source_target_pairs={{0,1},{1,0},{2,3},{3,2},{4,5},{5,4},{6,7},{7,6},{8,9},{9,8},{10,11... | collective-permute-start | bytes 1671176 | tf_op jit(solution)/shard_map/ppermute | solution.py:17
  72.7 5.8 %collective-permute-start.8 = (bf16[128,2176]{1,0:T(8,128)(2,1)S(1)}, bf16[128,2176]{1,0:T(8,128)(2,1)}, u32[]{:S(2)}, u32[]{:S(2)}) collective-permute-start(bf16[128,2176]{1,0:T(8,128)(2,1)S(1)} %shard_map.113.refs_0_), channel_id=1, source_target_pairs={{0,1},{1,0},{2,3},{3,2},{4,5},{5,4},{6,7},{7,6},{8,9},{9,8},{10,11... | collective-permute-start | bytes 1671176 | tf_op jit(solution)/shard_map/ppermute | solution.py:17
  77.0 65.3 %collective-permute-start.16 = (bf16[512,1024]{1,0:T(8,128)(2,1)}, bf16[512,1024]{1,0:T(8,128)(2,1)}, u32[]{:S(2)}, u32[]{:S(2)}) collective-permute-start(bf16[512,1024]{1,0:T(8,128)(2,1)} %get-tuple-element.23.refs_0_), channel_id=1, source_target_pairs={{0,2},{1,3},{2,0},{3,1},{4,6},{5,7},{6,4},{7,5},{8,10},{9,11},{10,... | collective-permute-start | bytes 3145736 | tf_op jit(solution)/shard_map/ppermute | solution.py:17
  119.4 12.5 %copy-start.6 = (bf16[512,1024]{1,0:T(8,128)(2,1)S(1)}, bf16[512,1024]{1,0:T(8,128)(2,1)}, u32[]{:S(2)}) copy-start(bf16[512,1024]{1,0:T(8,128)(2,1)} %get-tuple-element.23.refs_0_) | copy-start | bytes 3145732
  134.3 12.1 %collective-permute-start.15 = (bf16[512,1024]{1,0:T(8,128)(2,1)S(1)}, bf16[512,1024]{1,0:T(8,128)(2,1)S(1)}, u32[]{:S(2)}, u32[]{:S(2)}) collective-permute-start(bf16[512,1024]{1,0:T(8,128)(2,1)S(1)} %get-tuple-element.26.refs_1_), channel_id=1, source_target_pairs={{0,1},{1,0},{2,3},{3,2},{4,5},{5,4},{6,7},{7,6},{8,9},{9,8},{10,11... | collective-permute-start | bytes 3145736 | tf_op jit(solution)/shard_map/ppermute | solution.py:17
  146.9 12.4 %collective-permute-start.18 = (bf16[4,64,1024]{2,1,0:T(8,128)(2,1)S(1)}, bf16[4,64,1024]{2,1,0:T(8,128)(2,1)S(1)}, u32[]{:S(2)}, u32[]{:S(2)}) collective-permute-start(bf16[4,64,1024]{2,1,0:T(8,128)(2,1)S(1)} %shard_map.124), channel_id=1, source_target_pairs={{0,4},{4,0},{8,12},{12,8},{16,20},{20,16},{24,28},{28,24},{1,5},{5... | collective-permute-start | bytes 1572872 | tf_op jit(solution)/shard_map/ppermute | solution.py:17
  147.0 13.6 %collective-permute-start.21 = (bf16[512,512]{1,0:T(8,128)(2,1)S(1)}, bf16[512,512]{1,0:T(8,128)(2,1)S(1)}, u32[]{:S(2)}, u32[]{:S(2)}) collective-permute-start(bf16[512,512]{1,0:T(8,128)(2,1)S(1)} %get-tuple-element.32.refs_1_), channel_id=1, source_target_pairs={{0,1},{1,0},{2,3},{3,2},{4,5},{5,4},{6,7},{7,6},{8,9},{9,8},{10,11... | collective-permute-start | bytes 1572872 | tf_op jit(solution)/shard_map/ppermute | solution.py:17
  148.0 28.9 %collective-permute-start.25 = (bf16[512,1024]{1,0:T(8,128)(2,1)S(1)}, bf16[512,1024]{1,0:T(8,128)(2,1)S(1)}, u32[]{:S(2)}, u32[]{:S(2)}) collective-permute-start(bf16[512,1024]{1,0:T(8,128)(2,1)S(1)} %copy-done.5), channel_id=1, source_target_pairs={{0,2},{1,3},{2,0},{3,1},{4,6},{5,7},{6,4},{7,5},{8,10},{9,11},{10,... | collective-permute-start | bytes 3145736 | tf_op jit(solution)/shard_map/ppermute | solution.py:17
  159.5 12.3 %collective-permute-start.19 = (bf16[2,64,1024]{2,1,0:T(8,128)(2,1)S(1)}, bf16[2,64,1024]{2,1,0:T(8,128)(2,1)S(1)}, u32[]{:S(2)}, u32[]{:S(2)}) collective-permute-start(bf16[2,64,1024]{2,1,0:T(8,128)(2,1)S(1)} %slice.123), channel_id=1, source_target_pairs={{0,16},{4,20},{8,24},{12,28},{16,0},{20,4},{24,8},{28,12},{1,17},{... | collective-permute-start | bytes 786440 | tf_op jit(solution)/shard_map/ppermute | solution.py:17
  160.8 11.2 %collective-permute-start.22 = (bf16[4,64,512]{2,1,0:T(8,128)(2,1)S(1)}, bf16[4,64,512]{2,1,0:T(8,128)(2,1)S(1)}, u32[]{:S(2)}, u32[]{:S(2)}) collective-permute-start(bf16[4,64,512]{2,1,0:T(8,128)(2,1)S(1)} %fusion.4), channel_id=1, source_target_pairs={{0,4},{4,0},{8,12},{12,8},{16,20},{20,16},{24,28},{28,24},{1,5},{5... | collective-permute-start | bytes 786440 | tf_op jit(solution)/shard_map/ppermute | solution.py:17
  171.9 5.0 %collective-permute-start.20 = (bf16[1,64,1024]{2,1,0:T(8,128)(2,1)S(1)}, bf16[1,64,1024]{2,1,0:T(8,128)(2,1)S(1)}, u32[]{:S(2)}, u32[]{:S(2)}) collective-permute-start(bf16[1,64,1024]{2,1,0:T(8,128)(2,1)S(1)} %slice.126), channel_id=1, source_target_pairs={{0,8},{4,12},{8,0},{12,4},{16,24},{20,28},{24,16},{28,20},{1,9},{5... | collective-permute-start | bytes 393224 | tf_op jit(solution)/shard_map/ppermute | solution.py:17
  178.3 2.0 collective-permute-start.26
  180.4 8.4 %collective-permute-start.27 = (bf16[4,64,512]{2,1,0:T(8,128)(2,1)S(1)}, bf16[4,64,512]{2,1,0:T(8,128)(2,1)S(1)}, u32[]{:S(2)}, u32[]{:S(2)}) collective-permute-start(bf16[4,64,512]{2,1,0:T(8,128)(2,1)S(1)} %fusion.5), channel_id=1, source_target_pairs={{0,4},{4,0},{8,12},{12,8},{16,20},{20,16},{24,28},{28,24},{1,5},{5... | collective-permute-start | bytes 786440 | tf_op jit(solution)/shard_map/ppermute | solution.py:17
  181.3 9.0 %collective-permute-start.23 = (bf16[2,64,512]{2,1,0:T(8,128)(2,1)S(1)}, bf16[2,64,512]{2,1,0:T(8,128)(2,1)S(1)}, u32[]{:S(2)}, u32[]{:S(2)}) collective-permute-start(bf16[2,64,512]{2,1,0:T(8,128)(2,1)S(1)} %slice.125), channel_id=1, source_target_pairs={{0,16},{4,20},{8,24},{12,28},{16,0},{20,4},{24,8},{28,12},{1,17},{... | collective-permute-start | bytes 393224 | tf_op jit(solution)/shard_map/ppermute | solution.py:17
  189.0 8.0 %collective-permute-start.28 = (bf16[2,64,512]{2,1,0:T(8,128)(2,1)S(1)}, bf16[2,64,512]{2,1,0:T(8,128)(2,1)S(1)}, u32[]{:S(2)}, u32[]{:S(2)}) collective-permute-start(bf16[2,64,512]{2,1,0:T(8,128)(2,1)S(1)} %slice.124), channel_id=1, source_target_pairs={{0,16},{4,20},{8,24},{12,28},{16,0},{20,4},{24,8},{28,12},{1,17},{... | collective-permute-start | bytes 393224 | tf_op jit(solution)/shard_map/ppermute | solution.py:17
  190.4 6.7 %collective-permute-start.24 = (bf16[1,64,512]{2,1,0:T(8,128)(2,1)S(1)}, bf16[1,64,512]{2,1,0:T(8,128)(2,1)S(1)}, u32[]{:S(2)}, u32[]{:S(2)}) collective-permute-start(bf16[1,64,512]{2,1,0:T(8,128)(2,1)S(1)} %slice.128), channel_id=1, source_target_pairs={{0,8},{4,12},{8,0},{12,4},{16,24},{20,28},{24,16},{28,20},{1,9},{5... | collective-permute-start | bytes 196616 | tf_op jit(solution)/shard_map/ppermute | solution.py:17
  197.0 4.3 %collective-permute-start.29 = (bf16[1,64,512]{2,1,0:T(8,128)(2,1)S(1)}, bf16[1,64,512]{2,1,0:T(8,128)(2,1)S(1)}, u32[]{:S(2)}, u32[]{:S(2)}) collective-permute-start(bf16[1,64,512]{2,1,0:T(8,128)(2,1)S(1)} %slice.127), channel_id=1, source_target_pairs={{0,8},{4,12},{8,0},{12,4},{16,24},{20,28},{24,16},{28,20},{1,9},{5... | collective-permute-start | bytes 196616 | tf_op jit(solution)/shard_map/ppermute | solution.py:17
  (20 other events, 75.0 us)

commit v8 on v7

--- a/solution.py
+++ b/solution.py
@@ -158,8 +158,6 @@
 
 
 def joined(x, *after):
-    if not after:
-        return x
     anywhere = pl.BlockSpec(memory_space=pl.ANY)
     return pl.pallas_call(
         join_kernel,
@@ -258,9 +256,9 @@
     return kept.astype(jnp.float32) + swap(sent, "shard", 1).astype(jnp.float32)
 
 
-def over_x(total, tok, *after):
+def over_x(total, tok):
     total = total.reshape(-1, 2, tok, total.shape[-1])
-    given = swap(joined(total[:, 1].astype(jnp.bfloat16), *after), "dp", 1)
+    given = swap(total[:, 1].astype(jnp.bfloat16), "dp", 1)
     return total[:, 0] + given.astype(jnp.float32)
 
 
@@ -275,15 +273,15 @@
 def place_kernel(depth, *refs):
     parts, out_ref = refs[:-1], refs[-1]
     pair, _, _ = position()
-    for part, (blocks) in zip(parts, out_blocks(depth, [p.shape[1] for p in parts])):
+    for part, blocks in zip(parts, out_blocks(depth, [p.shape[1] for p in parts])):
         for n, (j, core) in enumerate(blocks):
             start = pl.multiple_of((2 * (pair ^ j) + core) * depth, LANES)
             out_ref[:, pl.ds(start, depth)] = part[:, n * depth : (n + 1) * depth]
 
 
 def out_blocks(depth, widths):
-    own, others = [(0, 0), (0, 1)], widths[1] // depth
-    return [own] + [[(j + 1, core) for j in range(others)] for core in range(2)]
+    others = range(1, widths[1] // depth + 1)
+    return [[(0, 0), (0, 1)] + [(j, 0) for j in others], [(j, 1) for j in others]]
 
 
 def placed(parts, depth, width):
@@ -337,14 +335,12 @@
         tuple((0, i, i, "leaves") for i in range(3)), places, (arrive,), (2, 2, 2), (), news
     )
 
-    groups = [[d[0] for d in downs]] + [d[1:] for d in downs]
+    groups = [[d[0] for d in downs] + downs[0][1:], downs[1][1:]]
     kept, sent = down_of(hidden, groups[0], ())
     at_core = over_core(kept, sent)
-    kept, sent = down_of(hidden, groups[1], (sent, news[0]))
-    own_part = over_z(over_x(at_core, tok, sent))
-    at_x = over_x(over_core(kept, sent), tok)
-    kept, sent = down_of(hidden, groups[2], (sent, own_part, at_x))
-    parts = [own_part, over_z(at_x), over_z(over_x(over_core(kept, sent), tok))]
+    at_x = over_x(at_core, tok)
+    kept, sent = down_of(hidden, groups[1], (news[0], at_x))
+    parts = [over_z(at_x), over_z(over_x(over_core(kept, sent), tok))]
     moe_output = placed(parts, depth, width)
 
     return (moe_output, *news)

time: 203 us -> 262 us (1.29)
  waiting for transfers between devices: 123 us -> 187 us
  local copies, waits for them, and re-layouts: 8.51 us -> 1.93 us
    ppermute x1, waiting for transfers between devices: 4.29 us -> 68.4 us  [passed_along(): return lax.ppermute(x, axis, [(i, (i + by) % size) for i in range(size)])]
    unnamed x44 -> x30, local copies, waits for them, and re-layouts: 8.27 us -> 1.72 us
    ppermute x29 -> x25, starting transfers between devices: 24.6 us -> 26.7 us  [swap(): lax.ppermute(x, axis, [(i, i ^ bit) for i in range(lax.axis_size(axis))])]
    pallas_call x3 -> x2, Pallas kernels: 6.16 us -> 4.74 us  [down_of(): pl.pallas_call(functools.partial(down_kernel, len(downs)), in_specs=[vmem...]
    ppermute x29 -> x25, waiting for transfers between devices: 119 us -> 119 us  [swap(): lax.ppermute(x, axis, [(i, i ^ bit) for i in range(lax.axis_size(axis))])]
  transfers between devices with their start and end apart: 30 -> 26, of which waited for: 15 -> 18; matrix products, arithmetic and copies ran while one was open for 1% -> 2% of each run, Pallas kernels for 15% -> 10%
where the time goes in v8:
time: 262 us; the launch traced here: 261 us
  waiting for transfers between devices  187 us (71%)
  Pallas kernels  37.9 us (14%)
  starting transfers between devices  28.5 us (11%)
  other arithmetic  4.68 us (2%)
    ppermute x25, waiting for transfers between devices, swap(): lax.ppermute(x, axis, [(i, i ^ bit) for i in range(lax.axis_size(axis))])  119 us
    ppermute x1, waiting for transfers between devices, passed_along(): return lax.ppermute(x, axis, [(i, (i + by) % size) for i in range(size)])  68.4 us
    ppermute x25, starting transfers between devices, swap(): lax.ppermute(x, axis, [(i, i ^ bit) for i in range(lax.axis_size(axis))])  26.7 us
    pallas_call x4, Pallas kernels, copies(): pl.pallas_call(functools.partial(copy_kernel, plan, len(ins), len(counts)...  16.8 us
    pallas_call x1, Pallas kernels, hidden_of(): pl.pallas_call(functools.partial(hidden_kernel, len(pieces)), grid=(ff //...  12.1 us
  transfers between devices with their start and end apart: 26, of which 18 were waited for; matrix products, arithmetic and copies ran while one was open for 2% of the time, Pallas kernels for 10%

profile of v8, /device:TPU:0, one launch (start us, length us, event | category | flops | bytes accessed | tf_op | source)
XLA Modules:
  0.0 261.4 jit_solution(13317990141684862307)
XLA Ops:
  0.6 3.3 %shard_map.112.refs_5_.refs_8_ = bf16[2,512,1024]{2,1,0:T(8,128)(2,1)} custom-call(s32[16]{0:T(128)} %refs_0_.7, s32[16]{0:T(128)} %refs_1_.7, bf16[2,512,1024]{2,1,0:T(8,128)(2,1)} %refs_2_.5, bf16[2,512,1024]{2,1,0:T(8,128)(2,1)} %refs_3_.5), custom_call_target="tpu_custom_call" | custom-call | tf_op jit(solution)/shard_map/pallas_call | solution.py:102
  4.0 3.8 %shard_map.117 = (bf16[2,512,1024]{2,1,0:T(8,128)(2,1)}, bf16[1,512,1024]{2,1,0:T(8,128)(2,1)}) custom-call(s32[16]{0:T(128)} %refs_0_.7, s32[16]{0:T(128)} %refs_1_.7, bf16[2,512,1024]{2,1,0:T(8,128)(2,1)} %refs_2_.5, bf16[2,512,1024]{2,1,0:T(8,128)(2,1)} %refs_3_.5, bf16[2,512,1024]{2,1,0:T(8,128)(2,1)} %refs_4_.3, ...), custom_call_target="tpu_custom_call" | custom-call | tf_op jit(solution)/shard_map/pallas_call | solution.py:102
  8.2 2.6 collective-permute-start.1
  11.5 2.7 %collective-permute-start.4 = (bf16[64,2176]{1,0:T(8,128)(2,1)S(1)}, bf16[64,2176]{1,0:T(8,128)(2,1)S(1)}, u32[]{:S(2)}, u32[]{:S(2)}) collective-permute-start(bf16[64,2176]{1,0:T(8,128)(2,1)S(1)} %shard_map.111), channel_id=1, source_target_pairs={{0,16},{4,20},{8,24},{12,28},{16,0},{20,4},{24,8},{28,12},{1,17},{... | collective-permute-start | bytes 835592 | tf_op jit(solution)/shard_map/ppermute | solution.py:17
  15.5 18.4 %collective-permute-done.4 = bf16[64,2176]{1,0:T(8,128)(2,1)S(1)} collective-permute-done((bf16[64,2176]{1,0:T(8,128)(2,1)S(1)}, bf16[64,2176]{1,0:T(8,128)(2,1)S(1)}, u32[]{:S(2)}, u32[]{:S(2)}) %collective-permute-start.4) | collective-permute-done | bytes 278560 | tf_op jit(solution)/shard_map/ppermute | solution.py:17
  33.9 1.5 collective-permute-start
  35.9 3.9 %collective-permute-start.2 = (bf16[64,2176]{1,0:T(8,128)(2,1)S(1)}, bf16[64,2176]{1,0:T(8,128)(2,1)}, u32[]{:S(2)}, u32[]{:S(2)}) collective-permute-start(bf16[64,2176]{1,0:T(8,128)(2,1)S(1)} %shard_map.111), channel_id=1, source_target_pairs={{0,8},{4,12},{8,0},{12,4},{16,24},{20,28},{24,16},{28,20},{1,9},{5... | collective-permute-start | bytes 835592 | tf_op jit(solution)/shard_map/ppermute | solution.py:17
  42.6 4.2 %collective-permute-done.2 = bf16[64,2176]{1,0:T(8,128)(2,1)} collective-permute-done((bf16[64,2176]{1,0:T(8,128)(2,1)S(1)}, bf16[64,2176]{1,0:T(8,128)(2,1)}, u32[]{:S(2)}, u32[]{:S(2)}) %collective-permute-start.2) | collective-permute-done | bytes 278560 | tf_op jit(solution)/shard_map/ppermute | solution.py:17
  46.7 1.5 collective-permute-start.7
  49.7 2.9 %shard_map.119 = (bf16[512,1024]{1,0:T(8,128)(2,1)}, bf16[512,1024]{1,0:T(8,128)(2,1)}) custom-call(bf16[2,512,1024]{2,1,0:T(8,128)(2,1)} %refs_4_.3, bf16[1,512,1024]{2,1,0:T(8,128)(2,1)} %collective-permute-done.14.other_ref), custom_call_target="tpu_custom_call" | custom-call | tf_op jit(solution)/shard_map/pallas_call | solution.py:141
  53.2 4.1 %collective-permute-done.1.refs_1_.refs_10_ = bf16[2,512,1024]{2,1,0:T(8,128)(2,1)S(1)} collective-permute-done((bf16[2,512,1024]{2,1,0:T(8,128)(2,1)S(1)}, bf16[2,512,1024]{2,1,0:T(8,128)(2,1)S(1)}, u32[]{:S(2)}, u32[]{:S(2)}) %collective-permute-start.1) | collective-permute-done | bytes 2097184 | tf_op jit(solution)/shard_map/ppermute | solution.py:17
  58.4 2.7 %collective-permute-done.3.refs_6_ = bf16[64,2176]{1,0:T(8,128)(2,1)} collective-permute-done((bf16[64,2176]{1,0:T(8,128)(2,1)}, bf16[64,2176]{1,0:T(8,128)(2,1)}, u32[]{:S(2)}, u32[]{:S(2)}) %collective-permute-start.3) | collective-permute-done | bytes 278560 | tf_op jit(solution)/shard_map/ppermute | solution.py:17
  65.8 36.6 %collective-permute-done.13.refs_11_ = bf16[2,512,1024]{2,1,0:T(8,128)(2,1)} collective-permute-done((bf16[2,512,1024]{2,1,0:T(8,128)(2,1)S(1)}, bf16[2,512,1024]{2,1,0:T(8,128)(2,1)}, u32[]{:S(2)}, u32[]{:S(2)}) %collective-permute-start.13) | collective-permute-done | bytes 2097184 | tf_op jit(solution)/shard_map/ppermute | solution.py:17
  102.4 12.1 %shard_map.118.hidden_ref = bf16[1024,1024]{1,0:T(8,128)(2,1)S(1)} custom-call(bf16[128,2176]{1,0:T(8,128)(2,1)S(1)} %shard_map.113.refs_0_, bf16[128,2176]{1,0:T(8,128)(2,1)S(1)} %shard_map.114.refs_1_, bf16[128,2176]{1,0:T(8,128)(2,1)S(1)} %shard_map.115.refs_2_, bf16[128,2176]{1,0:T(8,128)(2,1)S(1)} %shard_map.116.refs_3_, ...), custom_call_target="tpu_custom_call" | custom-call | flops 1 | bytes 1 | tf_op jit(solution)/shard_map/pallas_call | solution.py:208
  114.5 10.0 %collective-permute-done.15.refs_2_ = bf16[512,1024]{1,0:T(8,128)(2,1)S(1)} collective-permute-done((bf16[512,1024]{1,0:T(8,128)(2,1)}, bf16[512,1024]{1,0:T(8,128)(2,1)S(1)}, u32[]{:S(2)}, u32[]{:S(2)}) %collective-permute-start.15) | collective-permute-done | bytes 1048608 | tf_op jit(solution)/shard_map/ppermute | solution.py:17
  124.5 3.5 %shard_map.120 = (bf16[512,1536]{1,0:T(8,128)(2,1)S(1)}, bf16[512,1536]{1,0:T(8,128)(2,1)S(1)}) custom-call(bf16[1024,1024]{1,0:T(8,128)(2,1)S(1)} %shard_map.118.hidden_ref, bf16[512,1024]{1,0:T(8,128)(2,1)S(1)} %copy-done.6, bf16[512,1024]{1,0:T(8,128)(2,1)S(1)} %copy-done.4, bf16[512,1024]{1,0:T(8,128)(2,1)S(1)} %collective-permute-done.15.refs_2_), custom_call_target="tpu_custom_call" | custom-call | flops 1 | bytes 1 | tf_op jit(solution)/shard_map/pallas_call | solution.py:245
  128.0 6.2 %shard_map.121 = (bf16[3,512,1024]{2,1,0:T(8,128)(2,1)}, bf16[2,512,1024]{2,1,0:T(8,128)(2,1)}, bf16[2,512,1024]{2,1,0:T(8,128)(2,1)}, bf16[2,512,1024]{2,1,0:T(8,128)(2,1)}) custom-call(s32[16]{0:T(128)} %refs_0_.7, s32[16]{0:T(128)} %refs_1_.7, bf16[2,512,1024]{2,1,0:T(8,128)(2,1)} %refs_2_.5, bf16[2,512,1024]{2,1,0:T(8,128)(2,1)} %refs_3_.5, ...), custom_call_target="tpu_custom_call" | custom-call | tf_op jit(solution)/shard_map/pallas_call | solution.py:102
  134.2 1.8 collective-permute-start.21
  136.5 1.6 collective-permute-start.17
  138.1 1.5 collective-permute-start.20
  139.6 68.4 %collective-permute-done.21.refs_2_ = bf16[3,512,1024]{2,1,0:T(8,128)(2,1)S(1)} collective-permute-done((bf16[3,512,1024]{2,1,0:T(8,128)(2,1)}, bf16[3,512,1024]{2,1,0:T(8,128)(2,1)S(1)}, u32[]{:S(2)}, u32[]{:S(2)}) %collective-permute-start.21) | collective-permute-done | bytes 3145760 | tf_op jit(solution)/shard_map/ppermute | solution.py:22
  208.1 1.6 copy-done.12
  209.7 3.6 %shard_map.122 = (bf16[2,512,1024]{2,1,0:T(8,128)(2,1)}, bf16[2,512,1024]{2,1,0:T(8,128)(2,1)}, bf16[2,512,1024]{2,1,0:T(8,128)(2,1)}) custom-call(s32[16]{0:T(128)} %refs_0_.7, s32[16]{0:T(128)} %refs_1_.7, bf16[3,512,1024]{2,1,0:T(8,128)(2,1)} %copy-done.12, ...), custom_call_target="tpu_custom_call", output_to_operand_aliasing={{0}: (3, {}), {1}: (4, {}), {2}: (5, {})} | custom-call | tf_op jit(solution)/shard_map/pallas_call | solution.py:102
  213.3 10.3 %collective-permute-done.17 = bf16[4,64,1536]{2,1,0:T(8,128)(2,1)S(1)} collective-permute-done((bf16[4,64,1536]{2,1,0:T(8,128)(2,1)S(1)}, bf16[4,64,1536]{2,1,0:T(8,128)(2,1)S(1)}, u32[]{:S(2)}, u32[]{:S(2)}) %collective-permute-start.17) | collective-permute-done | bytes 786464 | tf_op jit(solution)/shard_map/ppermute | solution.py:17
  223.6 1.6 fusion.refs_2_
  226.6 1.9 collective-permute-done.22
  228.9 2.5 collective-permute-start.18
  231.4 5.8 %collective-permute-done.23 = bf16[4,64,512]{2,1,0:T(8,128)(2,1)S(1)} collective-permute-done((bf16[4,64,512]{2,1,0:T(8,128)(2,1)S(1)}, bf16[4,64,512]{2,1,0:T(8,128)(2,1)S(1)}, u32[]{:S(2)}, u32[]{:S(2)}) %collective-permute-start.23) | collective-permute-done | bytes 262176 | tf_op jit(solution)/shard_map/ppermute | solution.py:17
  237.3 1.9 collective-permute-start.24
  239.2 13.7 %collective-permute-done.18 = bf16[2,64,1536]{2,1,0:T(8,128)(2,1)S(1)} collective-permute-done((bf16[2,64,1536]{2,1,0:T(8,128)(2,1)S(1)}, bf16[2,64,1536]{2,1,0:T(8,128)(2,1)S(1)}, u32[]{:S(2)}, u32[]{:S(2)}) %collective-permute-start.18) | collective-permute-done | bytes 393248 | tf_op jit(solution)/shard_map/ppermute | solution.py:17
  253.1 2.0 collective-permute-done.24
  255.4 4.6 %collective-permute-done.19 = bf16[1,64,1536]{2,1,0:T(8,128)(2,1)S(1)} collective-permute-done((bf16[1,64,1536]{2,1,0:T(8,128)(2,1)S(1)}, bf16[1,64,1536]{2,1,0:T(8,128)(2,1)S(1)}, u32[]{:S(2)}, u32[]{:S(2)}) %collective-permute-start.19) | collective-permute-done | bytes 196640 | tf_op jit(solution)/shard_map/ppermute | solution.py:17
  (82 shorter events, 17.9 us)
Async XLA Ops:
  7.7 27.7 %collective-permute-start.12 = (bf16[2,512,1024]{2,1,0:T(8,128)(2,1)}, bf16[2,512,1024]{2,1,0:T(8,128)(2,1)S(1)}, u32[]{:S(2)}, u32[]{:S(2)}) collective-permute-start(bf16[2,512,1024]{2,1,0:T(8,128)(2,1)} %get-tuple-element.19), channel_id=1, source_target_pairs={{0,1},{1,0},{2,3},{3,2},{4,5},{5,4},{6,7},{7,6},{8,9},{9,8},{10,11... | collective-permute-start | bytes 6291464 | tf_op jit(solution)/shard_map/ppermute | solution.py:17
  8.2 49.1 %collective-permute-start.1 = (bf16[2,512,1024]{2,1,0:T(8,128)(2,1)S(1)}, bf16[2,512,1024]{2,1,0:T(8,128)(2,1)S(1)}, u32[]{:S(2)}, u32[]{:S(2)}) collective-permute-start(bf16[2,512,1024]{2,1,0:T(8,128)(2,1)S(1)} %copy-done), channel_id=1, source_target_pairs={{0,2},{1,3},{2,0},{3,1},{4,6},{5,7},{6,4},{7,5},{8,10},{9,11},{10,... | collective-permute-start | bytes 6291464 | tf_op jit(solution)/shard_map/ppermute | solution.py:17
  11.5 22.4 %collective-permute-start.4 = (bf16[64,2176]{1,0:T(8,128)(2,1)S(1)}, bf16[64,2176]{1,0:T(8,128)(2,1)S(1)}, u32[]{:S(2)}, u32[]{:S(2)}) collective-permute-start(bf16[64,2176]{1,0:T(8,128)(2,1)S(1)} %shard_map.111), channel_id=1, source_target_pairs={{0,16},{4,20},{8,24},{12,28},{16,0},{20,4},{24,8},{28,12},{1,17},{... | collective-permute-start | bytes 835592 | tf_op jit(solution)/shard_map/ppermute | solution.py:17
  14.2 35.5 %collective-permute-start.14 = (bf16[1,512,1024]{2,1,0:T(8,128)(2,1)}, bf16[1,512,1024]{2,1,0:T(8,128)(2,1)}, u32[]{:S(2)}, u32[]{:S(2)}) collective-permute-start(bf16[1,512,1024]{2,1,0:T(8,128)(2,1)} %get-tuple-element.20), channel_id=1, source_target_pairs={{0,1},{1,0},{2,3},{3,2},{4,5},{5,4},{6,7},{7,6},{8,9},{9,8},{10,11... | collective-permute-start | bytes 3145736 | tf_op jit(solution)/shard_map/ppermute | solution.py:17
  14.2 21.8 %collective-permute-start.6 = (bf16[64,2176]{1,0:T(8,128)(2,1)S(1)}, bf16[64,2176]{1,0:T(8,128)(2,1)}, u32[]{:S(2)}, u32[]{:S(2)}) collective-permute-start(bf16[64,2176]{1,0:T(8,128)(2,1)S(1)} %shard_map.111), channel_id=1, source_target_pairs={{0,24},{4,28},{8,16},{12,20},{16,8},{20,12},{24,0},{28,4},{1,25},{... | collective-permute-start | bytes 835592 | tf_op jit(solution)/shard_map/ppermute | solution.py:17
  33.9 7.1 %collective-permute-start = (bf16[64,2176]{1,0:T(8,128)(2,1)S(1)}, bf16[64,2176]{1,0:T(8,128)(2,1)S(1)}, u32[]{:S(2)}, u32[]{:S(2)}) collective-permute-start(bf16[64,2176]{1,0:T(8,128)(2,1)S(1)} %shard_map.111), channel_id=1, source_target_pairs={{0,4},{4,0},{8,12},{12,8},{16,20},{20,16},{24,28},{28,24},{1,5},{5... | collective-permute-start | bytes 835592 | tf_op jit(solution)/shard_map/ppermute | solution.py:17
  35.4 17.2 %copy-start.2 = (bf16[2,512,1024]{2,1,0:T(8,128)(2,1)}, bf16[2,512,1024]{2,1,0:T(8,128)(2,1)S(1)}, u32[]{:S(2)}) copy-start(bf16[2,512,1024]{2,1,0:T(8,128)(2,1)S(1)} %collective-permute-done.12.refs_9_) | copy-start | bytes 6291460
  35.4 66.9 %collective-permute-start.13 = (bf16[2,512,1024]{2,1,0:T(8,128)(2,1)S(1)}, bf16[2,512,1024]{2,1,0:T(8,128)(2,1)}, u32[]{:S(2)}, u32[]{:S(2)}) collective-permute-start(bf16[2,512,1024]{2,1,0:T(8,128)(2,1)S(1)} %collective-permute-done.12.refs_9_), channel_id=1, source_target_pairs={{0,2},{1,3},{2,0},{3,1},{4,6},{5,7},{6,4},{7,5},{8,10},{9,11},{10,... | collective-permute-start | bytes 6291464 | tf_op jit(solution)/shard_map/ppermute | solution.py:17
  35.9 10.8 %collective-permute-start.2 = (bf16[64,2176]{1,0:T(8,128)(2,1)S(1)}, bf16[64,2176]{1,0:T(8,128)(2,1)}, u32[]{:S(2)}, u32[]{:S(2)}) collective-permute-start(bf16[64,2176]{1,0:T(8,128)(2,1)S(1)} %shard_map.111), channel_id=1, source_target_pairs={{0,8},{4,12},{8,0},{12,4},{16,24},{20,28},{24,16},{28,20},{1,9},{5... | collective-permute-start | bytes 835592 | tf_op jit(solution)/shard_map/ppermute | solution.py:17
  41.0 11.5 %copy-start.13 = (bf16[64,2176]{1,0:T(8,128)(2,1)}, bf16[64,2176]{1,0:T(8,128)(2,1)S(1)}, u32[]{:S(2)}) copy-start(bf16[64,2176]{1,0:T(8,128)(2,1)S(1)} %collective-permute-done.refs_5_) | copy-start | bytes 835588
  41.0 7.2 %collective-permute-start.5 = (bf16[64,2176]{1,0:T(8,128)(2,1)S(1)}, bf16[64,2176]{1,0:T(8,128)(2,1)S(1)}, u32[]{:S(2)}, u32[]{:S(2)}) collective-permute-start(bf16[64,2176]{1,0:T(8,128)(2,1)S(1)} %collective-permute-done.4), channel_id=1, source_target_pairs={{0,4},{4,0},{8,12},{12,8},{16,20},{20,16},{24,28},{28,24},{1,5},{5... | collective-permute-start | bytes 835592 | tf_op jit(solution)/shard_map/ppermute | solution.py:17
  46.7 10.6 %collective-permute-start.7 = (bf16[64,2176]{1,0:T(8,128)(2,1)}, bf16[64,2176]{1,0:T(8,128)(2,1)}, u32[]{:S(2)}, u32[]{:S(2)}) collective-permute-start(bf16[64,2176]{1,0:T(8,128)(2,1)} %collective-permute-done.6), channel_id=1, source_target_pairs={{0,4},{4,0},{8,12},{12,8},{16,20},{20,16},{24,28},{28,24},{1,5},{5... | collective-permute-start | bytes 835592 | tf_op jit(solution)/shard_map/ppermute | solution.py:17
  48.2 12.8 %collective-permute-start.3 = (bf16[64,2176]{1,0:T(8,128)(2,1)}, bf16[64,2176]{1,0:T(8,128)(2,1)}, u32[]{:S(2)}, u32[]{:S(2)}) collective-permute-start(bf16[64,2176]{1,0:T(8,128)(2,1)} %collective-permute-done.2), channel_id=1, source_target_pairs={{0,4},{4,0},{8,12},{12,8},{16,20},{20,16},{24,28},{28,24},{1,5},{5... | collective-permute-start | bytes 835592 | tf_op jit(solution)/shard_map/ppermute | solution.py:17
  52.6 71.9 %collective-permute-start.15 = (bf16[512,1024]{1,0:T(8,128)(2,1)}, bf16[512,1024]{1,0:T(8,128)(2,1)S(1)}, u32[]{:S(2)}, u32[]{:S(2)}) collective-permute-start(bf16[512,1024]{1,0:T(8,128)(2,1)} %get-tuple-element.21.refs_0_), channel_id=1, source_target_pairs={{0,2},{1,3},{2,0},{3,1},{4,6},{5,7},{6,4},{7,5},{8,10},{9,11},{10,... | collective-permute-start | bytes 3145736 | tf_op jit(solution)/shard_map/ppermute | solution.py:17
  57.3 5.5 %collective-permute-start.10 = (bf16[128,2176]{1,0:T(8,128)(2,1)S(1)}, bf16[128,2176]{1,0:T(8,128)(2,1)S(1)}, u32[]{:S(2)}, u32[]{:S(2)}) collective-permute-start(bf16[128,2176]{1,0:T(8,128)(2,1)S(1)} %shard_map.115.refs_2_), channel_id=1, source_target_pairs={{0,1},{1,0},{2,3},{3,2},{4,5},{5,4},{6,7},{7,6},{8,9},{9,8},{10,11... | collective-permute-start | bytes 1671176 | tf_op jit(solution)/shard_map/ppermute | solution.py:17
  62.2 2.0 collective-permute-start.11
  62.3 40.1 %copy-start.3 = (bf16[2,512,1024]{2,1,0:T(8,128)(2,1)S(1)}, bf16[2,512,1024]{2,1,0:T(8,128)(2,1)}, u32[]{:S(2)}) copy-start(bf16[2,512,1024]{2,1,0:T(8,128)(2,1)} %copy-done.2) | copy-start | bytes 6291460
  62.3 2.7 %collective-permute-start.9 = (bf16[128,2176]{1,0:T(8,128)(2,1)S(1)}, bf16[128,2176]{1,0:T(8,128)(2,1)S(1)}, u32[]{:S(2)}, u32[]{:S(2)}) collective-permute-start(bf16[128,2176]{1,0:T(8,128)(2,1)S(1)} %shard_map.114.refs_1_), channel_id=1, source_target_pairs={{0,1},{1,0},{2,3},{3,2},{4,5},{5,4},{6,7},{7,6},{8,9},{9,8},{10,11... | collective-permute-start | bytes 1671176 | tf_op jit(solution)/shard_map/ppermute | solution.py:17
  62.8 61.7 %copy-start.4 = (bf16[512,1024]{1,0:T(8,128)(2,1)S(1)}, bf16[512,1024]{1,0:T(8,128)(2,1)}, u32[]{:S(2)}) copy-start(bf16[512,1024]{1,0:T(8,128)(2,1)} %get-tuple-element.22.refs_1_) | copy-start | bytes 3145732
  62.8 61.7 %copy-start.6 = (bf16[512,1024]{1,0:T(8,128)(2,1)S(1)}, bf16[512,1024]{1,0:T(8,128)(2,1)}, u32[]{:S(2)}) copy-start(bf16[512,1024]{1,0:T(8,128)(2,1)} %get-tuple-element.21.refs_0_) | copy-start | bytes 3145732
  62.8 3.0 %collective-permute-start.8 = (bf16[128,2176]{1,0:T(8,128)(2,1)S(1)}, bf16[128,2176]{1,0:T(8,128)(2,1)S(1)}, u32[]{:S(2)}, u32[]{:S(2)}) collective-permute-start(bf16[128,2176]{1,0:T(8,128)(2,1)S(1)} %shard_map.113.refs_0_), channel_id=1, source_target_pairs={{0,1},{1,0},{2,3},{3,2},{4,5},{5,4},{6,7},{7,6},{8,9},{9,8},{10,11... | collective-permute-start | bytes 1671176 | tf_op jit(solution)/shard_map/ppermute | solution.py:17
  127.9 8.0 %collective-permute-start.16 = (bf16[512,1536]{1,0:T(8,128)(2,1)S(1)}, bf16[512,1536]{1,0:T(8,128)(2,1)S(1)}, u32[]{:S(2)}, u32[]{:S(2)}) collective-permute-start(bf16[512,1536]{1,0:T(8,128)(2,1)S(1)} %get-tuple-element.24), channel_id=1, source_target_pairs={{0,1},{1,0},{2,3},{3,2},{4,5},{5,4},{6,7},{7,6},{8,9},{9,8},{10,11... | collective-permute-start | bytes 4718600 | tf_op jit(solution)/shard_map/ppermute | solution.py:17
  134.2 73.9 %collective-permute-start.21 = (bf16[3,512,1024]{2,1,0:T(8,128)(2,1)}, bf16[3,512,1024]{2,1,0:T(8,128)(2,1)S(1)}, u32[]{:S(2)}, u32[]{:S(2)}) collective-permute-start(bf16[3,512,1024]{2,1,0:T(8,128)(2,1)} %get-tuple-element.25), channel_id=1, source_target_pairs={{0,4},{4,8},{8,12},{12,16},{16,20},{20,24},{24,28},{28,0},{1,5},{5... | collective-permute-start | bytes 9437192 | tf_op jit(solution)/shard_map/ppermute | solution.py:22
  136.5 87.1 %collective-permute-start.17 = (bf16[4,64,1536]{2,1,0:T(8,128)(2,1)S(1)}, bf16[4,64,1536]{2,1,0:T(8,128)(2,1)S(1)}, u32[]{:S(2)}, u32[]{:S(2)}) collective-permute-start(bf16[4,64,1536]{2,1,0:T(8,128)(2,1)S(1)} %fusion.1), channel_id=1, source_target_pairs={{0,4},{4,0},{8,12},{12,8},{16,20},{20,16},{24,28},{28,24},{1,5},{5... | collective-permute-start | bytes 2359304 | tf_op jit(solution)/shard_map/ppermute | solution.py:17
  138.1 87.1 %collective-permute-start.20 = (bf16[512,1024]{1,0:T(8,128)(2,1)S(1)}, bf16[512,1024]{1,0:T(8,128)(2,1)S(1)}, u32[]{:S(2)}, u32[]{:S(2)}) collective-permute-start(bf16[512,1024]{1,0:T(8,128)(2,1)S(1)} %copy-done.5), channel_id=1, source_target_pairs={{0,2},{1,3},{2,0},{3,1},{4,6},{5,7},{6,4},{7,5},{8,10},{9,11},{10,... | collective-permute-start | bytes 3145736 | tf_op jit(solution)/shard_map/ppermute | solution.py:17
  213.3 11.9 %copy-start.1 = (bf16[2,512,1024]{2,1,0:T(8,128)(2,1)S(1)}, bf16[2,512,1024]{2,1,0:T(8,128)(2,1)}, u32[]{:S(2)}) copy-start(bf16[2,512,1024]{2,1,0:T(8,128)(2,1)} %get-tuple-element.16.refs_1_) | copy-start | bytes 6291460
  226.6 2.0 collective-permute-start.22
  228.7 8.4 %collective-permute-start.23 = (bf16[4,64,512]{2,1,0:T(8,128)(2,1)S(1)}, bf16[4,64,512]{2,1,0:T(8,128)(2,1)S(1)}, u32[]{:S(2)}, u32[]{:S(2)}) collective-permute-start(bf16[4,64,512]{2,1,0:T(8,128)(2,1)S(1)} %fusion.4), channel_id=1, source_target_pairs={{0,4},{4,0},{8,12},{12,8},{16,20},{20,16},{24,28},{28,24},{1,5},{5... | collective-permute-start | bytes 786440 | tf_op jit(solution)/shard_map/ppermute | solution.py:17
  228.9 24.0 %collective-permute-start.18 = (bf16[2,64,1536]{2,1,0:T(8,128)(2,1)S(1)}, bf16[2,64,1536]{2,1,0:T(8,128)(2,1)S(1)}, u32[]{:S(2)}, u32[]{:S(2)}) collective-permute-start(bf16[2,64,1536]{2,1,0:T(8,128)(2,1)S(1)} %slice.82), channel_id=1, source_target_pairs={{0,16},{4,20},{8,24},{12,28},{16,0},{20,4},{24,8},{28,12},{1,17},{... | collective-permute-start | bytes 1179656 | tf_op jit(solution)/shard_map/ppermute | solution.py:17
  237.3 17.8 %collective-permute-start.24 = (bf16[2,64,512]{2,1,0:T(8,128)(2,1)S(1)}, bf16[2,64,512]{2,1,0:T(8,128)(2,1)S(1)}, u32[]{:S(2)}, u32[]{:S(2)}) collective-permute-start(bf16[2,64,512]{2,1,0:T(8,128)(2,1)S(1)} %slice.84), channel_id=1, source_target_pairs={{0,16},{4,20},{8,24},{12,28},{16,0},{20,4},{24,8},{28,12},{1,17},{... | collective-permute-start | bytes 393224 | tf_op jit(solution)/shard_map/ppermute | solution.py:17
  253.0 7.0 %collective-permute-start.19 = (bf16[1,64,1536]{2,1,0:T(8,128)(2,1)S(1)}, bf16[1,64,1536]{2,1,0:T(8,128)(2,1)S(1)}, u32[]{:S(2)}, u32[]{:S(2)}) collective-permute-start(bf16[1,64,1536]{2,1,0:T(8,128)(2,1)S(1)} %slice.83), channel_id=1, source_target_pairs={{0,8},{4,12},{8,0},{12,4},{16,24},{20,28},{24,16},{28,20},{1,9},{5... | collective-permute-start | bytes 589832 | tf_op jit(solution)/shard_map/ppermute | solution.py:17
  255.1 5.5 %collective-permute-start.25 = (bf16[1,64,512]{2,1,0:T(8,128)(2,1)S(1)}, bf16[1,64,512]{2,1,0:T(8,128)(2,1)S(1)}, u32[]{:S(2)}, u32[]{:S(2)}) collective-permute-start(bf16[1,64,512]{2,1,0:T(8,128)(2,1)S(1)} %slice.85), channel_id=1, source_target_pairs={{0,8},{4,12},{8,0},{12,4},{16,24},{20,28},{24,16},{28,20},{1,9},{5... | collective-permute-start | bytes 196616 | tf_op jit(solution)/shard_map/ppermute | solution.py:17
  (9 other events, 43.4 us)

commit v9 on v8

--- a/solution.py
+++ b/solution.py
@@ -328,19 +328,23 @@
     leave, *news = copies(
         tuple((i, "leaves", 0, i) for i in range(3))
         + tuple((i, "stays", i + 1, "stays") for i in range(3)),
-        places, (w_gate, w_up, w_down), (3, 2, 2, 2), across,
+        places, (w_gate, w_up, w_down), (3, 2, 2, 2), across + [weights[2]],
     )
     arrive = passed_along(leave, "dp", 1)
     news = copies(
         tuple((0, i, i, "leaves") for i in range(3)), places, (arrive,), (2, 2, 2), (), news
     )
 
-    groups = [[d[0] for d in downs] + downs[0][1:], downs[1][1:]]
+    groups = [[d[0] for d in downs]] + [d[1:] for d in downs]
     kept, sent = down_of(hidden, groups[0], ())
     at_core = over_core(kept, sent)
+    kept, sent = down_of(hidden, groups[1], (sent,))
     at_x = over_x(at_core, tok)
-    kept, sent = down_of(hidden, groups[1], (news[0], at_x))
-    parts = [over_z(at_x), over_z(over_x(over_core(kept, sent), tok))]
+    at_core = over_core(kept, sent)
+    at_x2 = over_x(at_core, tok)
+    kept, last = down_of(hidden, groups[2], (sent, news[0], at_x, at_x2))
+    early = over_z(jnp.concatenate([at_x, at_x2], axis=-1))
+    parts = [early, over_z(over_x(over_core(kept, last), tok))]
     moe_output = placed(parts, depth, width)
 
     return (moe_output, *news)

time: 262 us -> 201 us (0.77)
  waiting for transfers between devices: 187 us -> 124 us
  Pallas kernels: 37.9 us -> 41 us
    ppermute x1, waiting for transfers between devices: 68.4 us -> 0.01 us  [passed_along(): return lax.ppermute(x, axis, [(i, (i + by) % size) for i in range(size)])]
    ppermute x25 -> x27, waiting for transfers between devices: 119 us -> 124 us  [swap(): lax.ppermute(x, axis, [(i, i ^ bit) for i in range(lax.axis_size(axis))])]
    pallas_call x2 -> x3, Pallas kernels: 4.74 us -> 7.38 us  [down_of(): pl.pallas_call(functools.partial(down_kernel, len(downs)), in_specs=[vmem...]
    ppermute x25 -> x27, starting transfers between devices: 26.7 us -> 27.5 us  [swap(): lax.ppermute(x, axis, [(i, i ^ bit) for i in range(lax.axis_size(axis))])]
  transfers between devices with their start and end apart: 26 -> 28, of which waited for: 18 -> 15; matrix products, arithmetic and copies ran while one was open for 2% -> 1% of each run, Pallas kernels for 10% -> 16%
where the time goes in v9:
time: 201 us
  waiting for transfers between devices  124 us (62%)
  Pallas kernels  41 us (20%)
  starting transfers between devices  29 us (14%)
  local copies, waits for them, and re-layouts  3.64 us (2%)
  other arithmetic  2.42 us (1%)
    ppermute x27, waiting for transfers between devices, swap(): lax.ppermute(x, axis, [(i, i ^ bit) for i in range(lax.axis_size(axis))])  124 us
    ppermute x27, starting transfers between devices, swap(): lax.ppermute(x, axis, [(i, i ^ bit) for i in range(lax.axis_size(axis))])  27.5 us
    pallas_call x4, Pallas kernels, copies(): pl.pallas_call(functools.partial(copy_kernel, plan, len(ins), len(counts)...  16.9 us
    pallas_call x1, Pallas kernels, hidden_of(): pl.pallas_call(functools.partial(hidden_kernel, len(pieces)), grid=(ff //...  12.5 us
    pallas_call x3, Pallas kernels, down_of(): pl.pallas_call(functools.partial(down_kernel, len(downs)), in_specs=[vmem...  7.38 us
  transfers between devices with their start and end apart: 28, of which 15 were waited for; matrix products, arithmetic and copies ran while one was open for 1% of the time, Pallas kernels for 16%

profile of v9, /device:TPU:0, one launch (start us, length us, event | category | flops | bytes accessed | tf_op | source)
XLA Modules:
  0.0 201.0 jit_solution(6741959153831892967)
XLA Ops:
  0.6 3.3 %shard_map.112.refs_5_.refs_8_ = bf16[2,512,1024]{2,1,0:T(8,128)(2,1)} custom-call(s32[16]{0:T(128)} %refs_0_.7, s32[16]{0:T(128)} %refs_1_.7, bf16[2,512,1024]{2,1,0:T(8,128)(2,1)} %refs_2_.5, bf16[2,512,1024]{2,1,0:T(8,128)(2,1)} %refs_3_.5), custom_call_target="tpu_custom_call" | custom-call | tf_op jit(solution)/shard_map/pallas_call | solution.py:102
  4.0 3.8 %shard_map.117 = (bf16[2,512,1024]{2,1,0:T(8,128)(2,1)}, bf16[1,512,1024]{2,1,0:T(8,128)(2,1)}) custom-call(s32[16]{0:T(128)} %refs_0_.7, s32[16]{0:T(128)} %refs_1_.7, bf16[2,512,1024]{2,1,0:T(8,128)(2,1)} %refs_2_.5, bf16[2,512,1024]{2,1,0:T(8,128)(2,1)} %refs_3_.5, bf16[2,512,1024]{2,1,0:T(8,128)(2,1)} %refs_4_.3, ...), custom_call_target="tpu_custom_call" | custom-call | tf_op jit(solution)/shard_map/pallas_call | solution.py:102
  8.2 2.6 %collective-permute-start.1 = (bf16[2,512,1024]{2,1,0:T(8,128)(2,1)S(1)}, bf16[2,512,1024]{2,1,0:T(8,128)(2,1)S(1)}, u32[]{:S(2)}, u32[]{:S(2)}) collective-permute-start(bf16[2,512,1024]{2,1,0:T(8,128)(2,1)S(1)} %copy-done.2), channel_id=1, source_target_pairs={{0,2},{1,3},{2,0},{3,1},{4,6},{5,7},{6,4},{7,5},{8,10},{9,11},{10,... | collective-permute-start | bytes 6291464 | tf_op jit(solution)/shard_map/ppermute | solution.py:17
  11.5 3.7 %collective-permute-start.6 = (bf16[64,2176]{1,0:T(8,128)(2,1)S(1)}, bf16[64,2176]{1,0:T(8,128)(2,1)S(1)}, u32[]{:S(2)}, u32[]{:S(2)}) collective-permute-start(bf16[64,2176]{1,0:T(8,128)(2,1)S(1)} %shard_map.111), channel_id=1, source_target_pairs={{0,24},{4,28},{8,16},{12,20},{16,8},{20,12},{24,0},{28,4},{1,25},{... | collective-permute-start | bytes 835592 | tf_op jit(solution)/shard_map/ppermute | solution.py:17
  15.2 1.5 collective-permute-start
  17.2 5.8 %collective-permute-done.6 = bf16[64,2176]{1,0:T(8,128)(2,1)S(1)} collective-permute-done((bf16[64,2176]{1,0:T(8,128)(2,1)S(1)}, bf16[64,2176]{1,0:T(8,128)(2,1)S(1)}, u32[]{:S(2)}, u32[]{:S(2)}) %collective-permute-start.6) | collective-permute-done | bytes 278560 | tf_op jit(solution)/shard_map/ppermute | solution.py:17
  23.0 5.9 %collective-permute-start.4 = (bf16[64,2176]{1,0:T(8,128)(2,1)S(1)}, bf16[64,2176]{1,0:T(8,128)(2,1)}, u32[]{:S(2)}, u32[]{:S(2)}) collective-permute-start(bf16[64,2176]{1,0:T(8,128)(2,1)S(1)} %shard_map.111), channel_id=1, source_target_pairs={{0,16},{4,20},{8,24},{12,28},{16,0},{20,4},{24,8},{28,12},{1,17},{... | collective-permute-start | bytes 835592 | tf_op jit(solution)/shard_map/ppermute | solution.py:17
  28.9 1.6 collective-permute-start.3
  30.5 10.6 %collective-permute-done.4 = bf16[64,2176]{1,0:T(8,128)(2,1)} collective-permute-done((bf16[64,2176]{1,0:T(8,128)(2,1)S(1)}, bf16[64,2176]{1,0:T(8,128)(2,1)}, u32[]{:S(2)}, u32[]{:S(2)}) %collective-permute-start.4) | collective-permute-done | bytes 278560 | tf_op jit(solution)/shard_map/ppermute | solution.py:17
  41.1 1.5 collective-permute-start.7
  43.2 14.2 %collective-permute-done.1.refs_1_.refs_10_.refs_9_ = bf16[2,512,1024]{2,1,0:T(8,128)(2,1)S(1)} collective-permute-done((bf16[2,512,1024]{2,1,0:T(8,128)(2,1)S(1)}, bf16[2,512,1024]{2,1,0:T(8,128)(2,1)S(1)}, u32[]{:S(2)}, u32[]{:S(2)}) %collective-permute-start.1) | collective-permute-done | bytes 2097184 | tf_op jit(solution)/shard_map/ppermute | solution.py:17
  59.5 2.9 %shard_map.119 = (bf16[512,1024]{1,0:T(8,128)(2,1)}, bf16[512,1024]{1,0:T(8,128)(2,1)}) custom-call(bf16[2,512,1024]{2,1,0:T(8,128)(2,1)} %refs_4_.3, bf16[1,512,1024]{2,1,0:T(8,128)(2,1)} %collective-permute-done.14.other_ref), custom_call_target="tpu_custom_call" | custom-call | tf_op jit(solution)/shard_map/pallas_call | solution.py:141
  62.4 2.0 %collective-permute-start.17 = (bf16[512,1024]{1,0:T(8,128)(2,1)}, bf16[512,1024]{1,0:T(8,128)(2,1)}, u32[]{:S(2)}, u32[]{:S(2)}) collective-permute-start(bf16[512,1024]{1,0:T(8,128)(2,1)} %get-tuple-element.23.refs_0_), channel_id=1, source_target_pairs={{0,2},{1,3},{2,0},{3,1},{4,6},{5,7},{6,4},{7,5},{8,10},{9,11},{10,... | collective-permute-start | bytes 3145736 | tf_op jit(solution)/shard_map/ppermute | solution.py:17
  64.4 6.3 %shard_map.122 = (bf16[3,512,1024]{2,1,0:T(8,128)(2,1)}, bf16[2,512,1024]{2,1,0:T(8,128)(2,1)}, bf16[2,512,1024]{2,1,0:T(8,128)(2,1)}, bf16[2,512,1024]{2,1,0:T(8,128)(2,1)}) custom-call(s32[16]{0:T(128)} %refs_0_.7, s32[16]{0:T(128)} %refs_1_.7, bf16[2,512,1024]{2,1,0:T(8,128)(2,1)} %refs_2_.5, bf16[2,512,1024]{2,1,0:T(8,128)(2,1)} %refs_3_.5, ...), custom_call_target="tpu_custom_call" | custom-call | tf_op jit(solution)/shard_map/pallas_call | solution.py:102
  70.7 1.5 collective-permute-start.23
  74.0 1.4 collective-permute-done.10.refs_6_
  76.2 26.1 %collective-permute-done.13.refs_11_ = bf16[2,512,1024]{2,1,0:T(8,128)(2,1)} collective-permute-done((bf16[2,512,1024]{2,1,0:T(8,128)(2,1)S(1)}, bf16[2,512,1024]{2,1,0:T(8,128)(2,1)}, u32[]{:S(2)}, u32[]{:S(2)}) %collective-permute-start.13) | collective-permute-done | bytes 2097184 | tf_op jit(solution)/shard_map/ppermute | solution.py:17
  102.4 12.5 %shard_map.118.hidden_ref = bf16[1024,1024]{1,0:T(8,128)(2,1)S(1)} custom-call(bf16[128,2176]{1,0:T(8,128)(2,1)S(1)} %shard_map.113.refs_0_, bf16[128,2176]{1,0:T(8,128)(2,1)S(1)} %shard_map.114.refs_1_, bf16[128,2176]{1,0:T(8,128)(2,1)S(1)} %shard_map.115.refs_2_, bf16[128,2176]{1,0:T(8,128)(2,1)S(1)} %shard_map.116.refs_3_, ...), custom_call_target="tpu_custom_call" | custom-call | flops 1 | bytes 1 | tf_op jit(solution)/shard_map/pallas_call | solution.py:208
  114.9 3.6 %shard_map.120 = (bf16[512,1024]{1,0:T(8,128)(2,1)S(1)}, bf16[512,1024]{1,0:T(8,128)(2,1)S(1)}) custom-call(bf16[1024,1024]{1,0:T(8,128)(2,1)S(1)} %shard_map.118.hidden_ref, bf16[512,1024]{1,0:T(8,128)(2,1)S(1)} %copy-done.6, bf16[512,1024]{1,0:T(8,128)(2,1)} %get-tuple-element.24.refs_1_), custom_call_target="tpu_custom_call" | custom-call | flops 1 | bytes 1 | tf_op jit(solution)/shard_map/pallas_call | solution.py:245
  118.5 6.0 %collective-permute-done.17.refs_0_ = bf16[512,1024]{1,0:T(8,128)(2,1)} collective-permute-done((bf16[512,1024]{1,0:T(8,128)(2,1)}, bf16[512,1024]{1,0:T(8,128)(2,1)}, u32[]{:S(2)}, u32[]{:S(2)}) %collective-permute-start.17) | collective-permute-done | bytes 1048608 | tf_op jit(solution)/shard_map/ppermute | solution.py:17
  124.6 2.5 %shard_map.121 = (bf16[512,512]{1,0:T(8,128)(2,1)S(1)}, bf16[512,512]{1,0:T(8,128)(2,1)S(1)}) custom-call(bf16[1024,1024]{1,0:T(8,128)(2,1)S(1)} %shard_map.118.hidden_ref, bf16[512,1024]{1,0:T(8,128)(2,1)} %collective-permute-done.17.refs_0_, bf16[512,1024]{1,0:T(8,128)(2,1)S(1)} %get-tuple-element.26.refs_1_), custom_call_target="tpu_custom_call" | custom-call | flops 1 | bytes 1 | tf_op jit(solution)/shard_map/pallas_call | solution.py:245
  127.2 1.8 collective-permute-start.22
  129.7 1.8 collective-permute-start.16
  131.9 28.2 %collective-permute-done.19 = bf16[4,64,512]{2,1,0:T(8,128)(2,1)S(1)} collective-permute-done((bf16[4,64,512]{2,1,0:T(8,128)(2,1)S(1)}, bf16[4,64,512]{2,1,0:T(8,128)(2,1)S(1)}, u32[]{:S(2)}, u32[]{:S(2)}) %collective-permute-start.19) | collective-permute-done | bytes 262176 | tf_op jit(solution)/shard_map/ppermute | solution.py:17
  160.2 3.6 %shard_map.123 = (bf16[2,512,1024]{2,1,0:T(8,128)(2,1)}, bf16[2,512,1024]{2,1,0:T(8,128)(2,1)}, bf16[2,512,1024]{2,1,0:T(8,128)(2,1)}) custom-call(s32[16]{0:T(128)} %refs_0_.7, s32[16]{0:T(128)} %refs_1_.7, bf16[3,512,1024]{2,1,0:T(8,128)(2,1)} %collective-permute-done.23.refs_2_, ...), custom_call_target="tpu_custom_call", output_to_operand_aliasing={{0}: (3, {}), {1}: (4, {}), {2}: (5, {})} | custom-call | tf_op jit(solution)/shard_map/pallas_call | solution.py:102
  164.1 1.4 copy-done.3
  166.8 1.9 collective-permute-done.24
  169.0 1.3 collective-permute-start.20
  170.4 6.9 %collective-permute-done.25 = bf16[4,64,512]{2,1,0:T(8,128)(2,1)S(1)} collective-permute-done((bf16[4,64,512]{2,1,0:T(8,128)(2,1)S(1)}, bf16[4,64,512]{2,1,0:T(8,128)(2,1)S(1)}, u32[]{:S(2)}, u32[]{:S(2)}) %collective-permute-start.25) | collective-permute-done | bytes 262176 | tf_op jit(solution)/shard_map/ppermute | solution.py:17
  178.2 13.7 %collective-permute-done.20 = bf16[2,64,1536]{2,1,0:T(8,128)(2,1)S(1)} collective-permute-done((bf16[2,64,1536]{2,1,0:T(8,128)(2,1)S(1)}, bf16[2,64,1536]{2,1,0:T(8,128)(2,1)S(1)}, u32[]{:S(2)}, u32[]{:S(2)}) %collective-permute-start.20) | collective-permute-done | bytes 393248 | tf_op jit(solution)/shard_map/ppermute | solution.py:17
  192.1 2.5 %collective-permute-done.26 = bf16[2,64,512]{2,1,0:T(8,128)(2,1)S(1)} collective-permute-done((bf16[2,64,512]{2,1,0:T(8,128)(2,1)S(1)}, bf16[2,64,512]{2,1,0:T(8,128)(2,1)S(1)}, u32[]{:S(2)}, u32[]{:S(2)}) %collective-permute-start.26) | collective-permute-done | bytes 131104 | tf_op jit(solution)/shard_map/ppermute | solution.py:17
  194.8 4.8 %collective-permute-done.21 = bf16[1,64,1536]{2,1,0:T(8,128)(2,1)S(1)} collective-permute-done((bf16[1,64,1536]{2,1,0:T(8,128)(2,1)S(1)}, bf16[1,64,1536]{2,1,0:T(8,128)(2,1)S(1)}, u32[]{:S(2)}, u32[]{:S(2)}) %collective-permute-start.21) | collective-permute-done | bytes 196640 | tf_op jit(solution)/shard_map/ppermute | solution.py:17
  (88 shorter events, 12.7 us)
Async XLA Ops:
  7.7 9.0 %collective-permute-start.12 = (bf16[2,512,1024]{2,1,0:T(8,128)(2,1)}, bf16[2,512,1024]{2,1,0:T(8,128)(2,1)S(1)}, u32[]{:S(2)}, u32[]{:S(2)}) collective-permute-start(bf16[2,512,1024]{2,1,0:T(8,128)(2,1)} %get-tuple-element.21), channel_id=1, source_target_pairs={{0,1},{1,0},{2,3},{3,2},{4,5},{5,4},{6,7},{7,6},{8,9},{9,8},{10,11... | collective-permute-start | bytes 6291464 | tf_op jit(solution)/shard_map/ppermute | solution.py:17
  8.2 49.1 %collective-permute-start.1 = (bf16[2,512,1024]{2,1,0:T(8,128)(2,1)S(1)}, bf16[2,512,1024]{2,1,0:T(8,128)(2,1)S(1)}, u32[]{:S(2)}, u32[]{:S(2)}) collective-permute-start(bf16[2,512,1024]{2,1,0:T(8,128)(2,1)S(1)} %copy-done.2), channel_id=1, source_target_pairs={{0,2},{1,3},{2,0},{3,1},{4,6},{5,7},{6,4},{7,5},{8,10},{9,11},{10,... | collective-permute-start | bytes 6291464 | tf_op jit(solution)/shard_map/ppermute | solution.py:17
  11.5 11.4 %collective-permute-start.6 = (bf16[64,2176]{1,0:T(8,128)(2,1)S(1)}, bf16[64,2176]{1,0:T(8,128)(2,1)S(1)}, u32[]{:S(2)}, u32[]{:S(2)}) collective-permute-start(bf16[64,2176]{1,0:T(8,128)(2,1)S(1)} %shard_map.111), channel_id=1, source_target_pairs={{0,24},{4,28},{8,16},{12,20},{16,8},{20,12},{24,0},{28,4},{1,25},{... | collective-permute-start | bytes 835592 | tf_op jit(solution)/shard_map/ppermute | solution.py:17
  15.2 13.7 %collective-permute-start.2 = (bf16[64,2176]{1,0:T(8,128)(2,1)S(1)}, bf16[64,2176]{1,0:T(8,128)(2,1)S(1)}, u32[]{:S(2)}, u32[]{:S(2)}) collective-permute-start(bf16[64,2176]{1,0:T(8,128)(2,1)S(1)} %shard_map.111), channel_id=1, source_target_pairs={{0,8},{4,12},{8,0},{12,4},{16,24},{20,28},{24,16},{28,20},{1,9},{5... | collective-permute-start | bytes 835592 | tf_op jit(solution)/shard_map/ppermute | solution.py:17
  15.2 13.7 %collective-permute-start = (bf16[64,2176]{1,0:T(8,128)(2,1)S(1)}, bf16[64,2176]{1,0:T(8,128)(2,1)S(1)}, u32[]{:S(2)}, u32[]{:S(2)}) collective-permute-start(bf16[64,2176]{1,0:T(8,128)(2,1)S(1)} %shard_map.111), channel_id=1, source_target_pairs={{0,4},{4,0},{8,12},{12,8},{16,20},{20,16},{24,28},{28,24},{1,5},{5... | collective-permute-start | bytes 835592 | tf_op jit(solution)/shard_map/ppermute | solution.py:17
  16.7 40.6 %copy-start.4 = (bf16[2,512,1024]{2,1,0:T(8,128)(2,1)}, bf16[2,512,1024]{2,1,0:T(8,128)(2,1)S(1)}, u32[]{:S(2)}) copy-start(bf16[2,512,1024]{2,1,0:T(8,128)(2,1)S(1)} %collective-permute-done.12.refs_9_) | copy-start | bytes 6291460
  16.7 85.7 %collective-permute-start.13 = (bf16[2,512,1024]{2,1,0:T(8,128)(2,1)S(1)}, bf16[2,512,1024]{2,1,0:T(8,128)(2,1)}, u32[]{:S(2)}, u32[]{:S(2)}) collective-permute-start(bf16[2,512,1024]{2,1,0:T(8,128)(2,1)S(1)} %collective-permute-done.12.refs_9_), channel_id=1, source_target_pairs={{0,2},{1,3},{2,0},{3,1},{4,6},{5,7},{6,4},{7,5},{8,10},{9,11},{10,... | collective-permute-start | bytes 6291464 | tf_op jit(solution)/shard_map/ppermute | solution.py:17
  23.0 18.1 %collective-permute-start.4 = (bf16[64,2176]{1,0:T(8,128)(2,1)S(1)}, bf16[64,2176]{1,0:T(8,128)(2,1)}, u32[]{:S(2)}, u32[]{:S(2)}) collective-permute-start(bf16[64,2176]{1,0:T(8,128)(2,1)S(1)} %shard_map.111), channel_id=1, source_target_pairs={{0,16},{4,20},{8,24},{12,28},{16,0},{20,4},{24,8},{28,12},{1,17},{... | collective-permute-start | bytes 835592 | tf_op jit(solution)/shard_map/ppermute | solution.py:17
  28.9 30.6 %collective-permute-start.14 = (bf16[1,512,1024]{2,1,0:T(8,128)(2,1)}, bf16[1,512,1024]{2,1,0:T(8,128)(2,1)}, u32[]{:S(2)}, u32[]{:S(2)}) collective-permute-start(bf16[1,512,1024]{2,1,0:T(8,128)(2,1)} %get-tuple-element.22), channel_id=1, source_target_pairs={{0,1},{1,0},{2,3},{3,2},{4,5},{5,4},{6,7},{7,6},{8,9},{9,8},{10,11... | collective-permute-start | bytes 3145736 | tf_op jit(solution)/shard_map/ppermute | solution.py:17
  28.9 28.4 %copy-start.11 = (bf16[64,2176]{1,0:T(8,128)(2,1)}, bf16[64,2176]{1,0:T(8,128)(2,1)S(1)}, u32[]{:S(2)}) copy-start(bf16[64,2176]{1,0:T(8,128)(2,1)S(1)} %collective-permute-done.refs_5_) | copy-start | bytes 835588
  28.9 13.7 %collective-permute-start.3 = (bf16[64,2176]{1,0:T(8,128)(2,1)S(1)}, bf16[64,2176]{1,0:T(8,128)(2,1)S(1)}, u32[]{:S(2)}, u32[]{:S(2)}) collective-permute-start(bf16[64,2176]{1,0:T(8,128)(2,1)S(1)} %collective-permute-done.2), channel_id=1, source_target_pairs={{0,4},{4,0},{8,12},{12,8},{16,20},{20,16},{24,28},{28,24},{1,5},{5... | collective-permute-start | bytes 835592 | tf_op jit(solution)/shard_map/ppermute | solution.py:17
  41.1 17.6 %collective-permute-start.7 = (bf16[64,2176]{1,0:T(8,128)(2,1)S(1)}, bf16[64,2176]{1,0:T(8,128)(2,1)S(1)}, u32[]{:S(2)}, u32[]{:S(2)}) collective-permute-start(bf16[64,2176]{1,0:T(8,128)(2,1)S(1)} %collective-permute-done.6), channel_id=1, source_target_pairs={{0,4},{4,0},{8,12},{12,8},{16,20},{20,16},{24,28},{28,24},{1,5},{5... | collective-permute-start | bytes 835592 | tf_op jit(solution)/shard_map/ppermute | solution.py:17
  42.6 21.8 %collective-permute-start.5 = (bf16[64,2176]{1,0:T(8,128)(2,1)}, bf16[64,2176]{1,0:T(8,128)(2,1)}, u32[]{:S(2)}, u32[]{:S(2)}) collective-permute-start(bf16[64,2176]{1,0:T(8,128)(2,1)} %collective-permute-done.4), channel_id=1, source_target_pairs={{0,4},{4,0},{8,12},{12,8},{16,20},{20,16},{24,28},{28,24},{1,5},{5... | collective-permute-start | bytes 835592 | tf_op jit(solution)/shard_map/ppermute | solution.py:17
  57.3 16.0 %collective-permute-start.8 = (bf16[128,2176]{1,0:T(8,128)(2,1)S(1)}, bf16[128,2176]{1,0:T(8,128)(2,1)}, u32[]{:S(2)}, u32[]{:S(2)}) collective-permute-start(bf16[128,2176]{1,0:T(8,128)(2,1)S(1)} %shard_map.113.refs_0_), channel_id=1, source_target_pairs={{0,1},{1,0},{2,3},{3,2},{4,5},{5,4},{6,7},{7,6},{8,9},{9,8},{10,11... | collective-permute-start | bytes 1671176 | tf_op jit(solution)/shard_map/ppermute | solution.py:17
  58.7 14.7 %collective-permute-start.9 = (bf16[128,2176]{1,0:T(8,128)(2,1)S(1)}, bf16[128,2176]{1,0:T(8,128)(2,1)}, u32[]{:S(2)}, u32[]{:S(2)}) collective-permute-start(bf16[128,2176]{1,0:T(8,128)(2,1)S(1)} %shard_map.114.refs_1_), channel_id=1, source_target_pairs={{0,1},{1,0},{2,3},{3,2},{4,5},{5,4},{6,7},{7,6},{8,9},{9,8},{10,11... | collective-permute-start | bytes 1671176 | tf_op jit(solution)/shard_map/ppermute | solution.py:17
  62.4 62.2 %collective-permute-start.17 = (bf16[512,1024]{1,0:T(8,128)(2,1)}, bf16[512,1024]{1,0:T(8,128)(2,1)}, u32[]{:S(2)}, u32[]{:S(2)}) collective-permute-start(bf16[512,1024]{1,0:T(8,128)(2,1)} %get-tuple-element.23.refs_0_), channel_id=1, source_target_pairs={{0,2},{1,3},{2,0},{3,1},{4,6},{5,7},{6,4},{7,5},{8,10},{9,11},{10,... | collective-permute-start | bytes 3145736 | tf_op jit(solution)/shard_map/ppermute | solution.py:17
  70.7 89.5 %collective-permute-start.23 = (bf16[3,512,1024]{2,1,0:T(8,128)(2,1)}, bf16[3,512,1024]{2,1,0:T(8,128)(2,1)}, u32[]{:S(2)}, u32[]{:S(2)}) collective-permute-start(bf16[3,512,1024]{2,1,0:T(8,128)(2,1)} %get-tuple-element.29), channel_id=1, source_target_pairs={{0,4},{4,8},{8,12},{12,16},{16,20},{20,24},{24,28},{28,0},{1,5},{5... | collective-permute-start | bytes 9437192 | tf_op jit(solution)/shard_map/ppermute | solution.py:22
  73.4 29.0 %copy-start.5 = (bf16[2,512,1024]{2,1,0:T(8,128)(2,1)S(1)}, bf16[2,512,1024]{2,1,0:T(8,128)(2,1)}, u32[]{:S(2)}) copy-start(bf16[2,512,1024]{2,1,0:T(8,128)(2,1)} %copy-done.4) | copy-start | bytes 6291460
  73.4 41.5 %copy-start.6 = (bf16[512,1024]{1,0:T(8,128)(2,1)S(1)}, bf16[512,1024]{1,0:T(8,128)(2,1)}, u32[]{:S(2)}) copy-start(bf16[512,1024]{1,0:T(8,128)(2,1)} %get-tuple-element.23.refs_0_) | copy-start | bytes 3145732
  73.4 2.0 %collective-permute-start.10 = (bf16[128,2176]{1,0:T(8,128)(2,1)S(1)}, bf16[128,2176]{1,0:T(8,128)(2,1)S(1)}, u32[]{:S(2)}, u32[]{:S(2)}) collective-permute-start(bf16[128,2176]{1,0:T(8,128)(2,1)S(1)} %shard_map.115.refs_2_), channel_id=1, source_target_pairs={{0,1},{1,0},{2,3},{3,2},{4,5},{5,4},{6,7},{7,6},{8,9},{9,8},{10,11... | collective-permute-start | bytes 1671176 | tf_op jit(solution)/shard_map/ppermute | solution.py:17
  73.5 2.7 %collective-permute-start.11 = (bf16[128,2176]{1,0:T(8,128)(2,1)S(1)}, bf16[128,2176]{1,0:T(8,128)(2,1)S(1)}, u32[]{:S(2)}, u32[]{:S(2)}) collective-permute-start(bf16[128,2176]{1,0:T(8,128)(2,1)S(1)} %shard_map.116.refs_3_), channel_id=1, source_target_pairs={{0,1},{1,0},{2,3},{3,2},{4,5},{5,4},{6,7},{7,6},{8,9},{9,8},{10,11... | collective-permute-start | bytes 1671176 | tf_op jit(solution)/shard_map/ppermute | solution.py:17
  118.5 10.7 %collective-permute-start.15 = (bf16[512,1024]{1,0:T(8,128)(2,1)S(1)}, bf16[512,1024]{1,0:T(8,128)(2,1)S(1)}, u32[]{:S(2)}, u32[]{:S(2)}) collective-permute-start(bf16[512,1024]{1,0:T(8,128)(2,1)S(1)} %get-tuple-element.26.refs_1_), channel_id=1, source_target_pairs={{0,1},{1,0},{2,3},{3,2},{4,5},{5,4},{6,7},{7,6},{8,9},{9,8},{10,11... | collective-permute-start | bytes 3145736 | tf_op jit(solution)/shard_map/ppermute | solution.py:17
  127.1 2.0 collective-permute-start.18
  127.2 36.9 %collective-permute-start.22 = (bf16[512,1024]{1,0:T(8,128)(2,1)}, bf16[512,1024]{1,0:T(8,128)(2,1)S(1)}, u32[]{:S(2)}, u32[]{:S(2)}) collective-permute-start(bf16[512,1024]{1,0:T(8,128)(2,1)} %get-tuple-element.24.refs_1_), channel_id=1, source_target_pairs={{0,2},{1,3},{2,0},{3,1},{4,6},{5,7},{6,4},{7,5},{8,10},{9,11},{10,... | collective-permute-start | bytes 3145736 | tf_op jit(solution)/shard_map/ppermute | solution.py:17
  129.7 34.2 %collective-permute-start.16 = (bf16[4,64,1024]{2,1,0:T(8,128)(2,1)S(1)}, bf16[4,64,1024]{2,1,0:T(8,128)(2,1)S(1)}, u32[]{:S(2)}, u32[]{:S(2)}) collective-permute-start(bf16[4,64,1024]{2,1,0:T(8,128)(2,1)S(1)} %fusion.4), channel_id=1, source_target_pairs={{0,4},{4,0},{8,12},{12,8},{16,20},{20,16},{24,28},{28,24},{1,5},{5... | collective-permute-start | bytes 1572872 | tf_op jit(solution)/shard_map/ppermute | solution.py:17
  131.5 28.6 %collective-permute-start.19 = (bf16[4,64,512]{2,1,0:T(8,128)(2,1)S(1)}, bf16[4,64,512]{2,1,0:T(8,128)(2,1)S(1)}, u32[]{:S(2)}, u32[]{:S(2)}) collective-permute-start(bf16[4,64,512]{2,1,0:T(8,128)(2,1)S(1)} %fusion.8), channel_id=1, source_target_pairs={{0,4},{4,0},{8,12},{12,8},{16,20},{20,16},{24,28},{28,24},{1,5},{5... | collective-permute-start | bytes 786440 | tf_op jit(solution)/shard_map/ppermute | solution.py:17
  166.7 2.0 collective-permute-start.24
  168.9 8.4 %collective-permute-start.25 = (bf16[4,64,512]{2,1,0:T(8,128)(2,1)S(1)}, bf16[4,64,512]{2,1,0:T(8,128)(2,1)S(1)}, u32[]{:S(2)}, u32[]{:S(2)}) collective-permute-start(bf16[4,64,512]{2,1,0:T(8,128)(2,1)S(1)} %fusion.9), channel_id=1, source_target_pairs={{0,4},{4,0},{8,12},{12,8},{16,20},{20,16},{24,28},{28,24},{1,5},{5... | collective-permute-start | bytes 786440 | tf_op jit(solution)/shard_map/ppermute | solution.py:17
  169.0 22.8 %collective-permute-start.20 = (bf16[2,64,1536]{2,1,0:T(8,128)(2,1)S(1)}, bf16[2,64,1536]{2,1,0:T(8,128)(2,1)S(1)}, u32[]{:S(2)}, u32[]{:S(2)}) collective-permute-start(bf16[2,64,1536]{2,1,0:T(8,128)(2,1)S(1)} %fusion.3), channel_id=1, source_target_pairs={{0,16},{4,20},{8,24},{12,28},{16,0},{20,4},{24,8},{28,12},{1,17},{... | collective-permute-start | bytes 1179656 | tf_op jit(solution)/shard_map/ppermute | solution.py:17
  177.4 17.2 %collective-permute-start.26 = (bf16[2,64,512]{2,1,0:T(8,128)(2,1)S(1)}, bf16[2,64,512]{2,1,0:T(8,128)(2,1)S(1)}, u32[]{:S(2)}, u32[]{:S(2)}) collective-permute-start(bf16[2,64,512]{2,1,0:T(8,128)(2,1)S(1)} %slice.100), channel_id=1, source_target_pairs={{0,16},{4,20},{8,24},{12,28},{16,0},{20,4},{24,8},{28,12},{1,17},{... | collective-permute-start | bytes 393224 | tf_op jit(solution)/shard_map/ppermute | solution.py:17
  192.0 7.5 %collective-permute-start.21 = (bf16[1,64,1536]{2,1,0:T(8,128)(2,1)S(1)}, bf16[1,64,1536]{2,1,0:T(8,128)(2,1)S(1)}, u32[]{:S(2)}, u32[]{:S(2)}) collective-permute-start(bf16[1,64,1536]{2,1,0:T(8,128)(2,1)S(1)} %slice.99), channel_id=1, source_target_pairs={{0,8},{4,12},{8,0},{12,4},{16,24},{20,28},{24,16},{28,20},{1,9},{5... | collective-permute-start | bytes 589832 | tf_op jit(solution)/shard_map/ppermute | solution.py:17
  194.7 5.6 %collective-permute-start.27 = (bf16[1,64,512]{2,1,0:T(8,128)(2,1)S(1)}, bf16[1,64,512]{2,1,0:T(8,128)(2,1)S(1)}, u32[]{:S(2)}, u32[]{:S(2)}) collective-permute-start(bf16[1,64,512]{2,1,0:T(8,128)(2,1)S(1)} %slice.101), channel_id=1, source_target_pairs={{0,8},{4,12},{8,0},{12,4},{16,24},{20,28},{24,16},{28,20},{1,9},{5... | collective-permute-start | bytes 196616 | tf_op jit(solution)/shard_map/ppermute | solution.py:17
  (10 other events, 59.4 us)

commit v10 on v9

--- a/solution.py
+++ b/solution.py
@@ -311,34 +311,33 @@
     weights = spread(near_weights)
     downs = [spread([d]) for d in in_order(w_down, swap(theirs_down, "shard", 1))]
 
+    (leave,) = copies(
+        ((0, "leaves", 0, 0),), places, (w_gate,), (1,), (mine,)
+    )
+    arrive = passed_along(leave, "dp", 1)
+
     own = first(tokens, router_probs, expert_ids, old_place)
     columns = [own] + [flip_z(own, j) for j in range(1, n_z)]
-    across = [swap(c, "dp", 1) for c in columns]
+    across = [swap(joined(c, arrive), "dp", 1) for c in columns]
     near = [joined(jnp.concatenate(p, axis=0), weights[2]) for p in zip(columns, across)]
     far = [swap(p, "shard", 1) for p in near]
 
     hidden = hidden_of(near + far, weights)
     leave, *news = copies(
-        tuple((i, "leaves", 0, i) for i in range(3))
+        ((1, "leaves", 0, 0), (2, "leaves", 0, 1))
         + tuple((i, "stays", i + 1, "stays") for i in range(3)),
-        places, (w_gate, w_up, w_down), (3, 2, 2, 2), near,
-    )
-    arrive = passed_along(leave, "dp", 1)
-
-    leave, *news = copies(
-        tuple((i, "leaves", 0, i) for i in range(3))
-        + tuple((i, "stays", i + 1, "stays") for i in range(3)),
-        places, (w_gate, w_up, w_down), (3, 2, 2, 2), across + [weights[2]],
-    )
-    arrive = passed_along(leave, "dp", 1)
+        places, (w_gate, w_up, w_down), (2, 2, 2, 2), across + [weights[2]],
+    )
+    arrive_rest = passed_along(leave, "dp", 1)
     news = copies(
-        tuple((0, i, i, "leaves") for i in range(3)), places, (arrive,), (2, 2, 2), (), news
+        ((0, 0, 0, "leaves"), (1, 0, 1, "leaves"), (1, 1, 2, "leaves")),
+        places, (arrive, arrive_rest), (2, 2, 2), (), news,
     )
 
     groups = [[d[0] for d in downs]] + [d[1:] for d in downs]
     kept, sent = down_of(hidden, groups[0], ())
     at_core = over_core(kept, sent)
-    kept, sent = down_of(hidden, groups[1], (sent,))
+    kept, sent = down_of(hidden, groups[1], (sent, arrive_rest))
     at_x = over_x(at_core, tok)
     at_core = over_core(kept, sent)
     at_x2 = over_x(at_core, tok)

time: 201 us -> 216 us (1.075)
  starting transfers between devices: 29 us -> 47.4 us
  waiting for transfers between devices: 124 us -> 116 us
  local copies, waits for them, and re-layouts: 3.64 us -> 5.91 us
    ppermute x27, waiting for transfers between devices: 124 us -> 96.2 us  [swap(): lax.ppermute(x, axis, [(i, i ^ bit) for i in range(lax.axis_size(axis))])]
    ppermute x1 -> x2, waiting for transfers between devices: 0.01 us -> 19.3 us  [passed_along(): return lax.ppermute(x, axis, [(i, (i + by) % size) for i in range(size)])]
    ppermute x27, starting transfers between devices: 27.5 us -> 44.1 us  [swap(): lax.ppermute(x, axis, [(i, i ^ bit) for i in range(lax.axis_size(axis))])]
    pallas_call x4 -> x5, Pallas kernels: 16.9 us -> 18.6 us  [copies(): pl.pallas_call(functools.partial(copy_kernel, plan, len(ins), len(counts)...]
  transfers between devices with their start and end apart: 28 -> 29, of which waited for: 15 -> 22; matrix products, arithmetic and copies ran while one was open for 1% -> 3% of each run, Pallas kernels for 16% -> 15%
where the time goes in v10:
time: 216 us
  waiting for transfers between devices  116 us (54%)
  starting transfers between devices  47.4 us (22%)
  Pallas kernels  42 us (19%)
  local copies, waits for them, and re-layouts  5.91 us (3%)
  other arithmetic  3.46 us (2%)
    ppermute x27, waiting for transfers between devices, swap(): lax.ppermute(x, axis, [(i, i ^ bit) for i in range(lax.axis_size(axis))])  96.2 us
    ppermute x27, starting transfers between devices, swap(): lax.ppermute(x, axis, [(i, i ^ bit) for i in range(lax.axis_size(axis))])  44.1 us
    ppermute x2, waiting for transfers between devices, passed_along(): return lax.ppermute(x, axis, [(i, (i + by) % size) for i in range(size)])  19.3 us
    pallas_call x5, Pallas kernels, copies(): pl.pallas_call(functools.partial(copy_kernel, plan, len(ins), len(counts)...  18.6 us
    pallas_call x1, Pallas kernels, hidden_of(): pl.pallas_call(functools.partial(hidden_kernel, len(pieces)), grid=(ff //...  12.1 us
    pallas_call x3, Pallas kernels, down_of(): pl.pallas_call(functools.partial(down_kernel, len(downs)), in_specs=[vmem...  6.91 us
  transfers between devices with their start and end apart: 29, of which 22 were waited for; matrix products, arithmetic and copies ran while one was open for 3% of the time, Pallas kernels for 15%

profile of v10, /device:TPU:0, one launch (start us, length us, event | category | flops | bytes accessed | tf_op | source)
XLA Modules:
  0.0 215.6 jit_solution(11957079335763277821)
XLA Ops:
  0.6 3.3 %shard_map.112.refs_3_.refs_5_.refs_8_ = bf16[2,512,1024]{2,1,0:T(8,128)(2,1)} custom-call(s32[16]{0:T(128)} %refs_0_.9, s32[16]{0:T(128)} %refs_1_.9, bf16[2,512,1024]{2,1,0:T(8,128)(2,1)} %refs_2_.7, bf16[2,512,1024]{2,1,0:T(8,128)(2,1)} %refs_3_.5), custom_call_target="tpu_custom_call" | custom-call | tf_op jit(solution)/shard_map/pallas_call | solution.py:102
  3.9 3.8 %shard_map.122 = (bf16[2,512,1024]{2,1,0:T(8,128)(2,1)}, bf16[1,512,1024]{2,1,0:T(8,128)(2,1)}) custom-call(s32[16]{0:T(128)} %refs_0_.9, s32[16]{0:T(128)} %refs_1_.9, bf16[2,512,1024]{2,1,0:T(8,128)(2,1)} %refs_2_.7, bf16[2,512,1024]{2,1,0:T(8,128)(2,1)} %refs_3_.5, bf16[2,512,1024]{2,1,0:T(8,128)(2,1)} %refs_4_.3, ...), custom_call_target="tpu_custom_call" | custom-call | tf_op jit(solution)/shard_map/pallas_call | solution.py:102
  8.3 2.6 %collective-permute-start.2 = (bf16[2,512,1024]{2,1,0:T(8,128)(2,1)S(1)}, bf16[2,512,1024]{2,1,0:T(8,128)(2,1)S(1)}, u32[]{:S(2)}, u32[]{:S(2)}) collective-permute-start(bf16[2,512,1024]{2,1,0:T(8,128)(2,1)S(1)} %copy-done.2), channel_id=1, source_target_pairs={{0,2},{1,3},{2,0},{3,1},{4,6},{5,7},{6,4},{7,5},{8,10},{9,11},{10,... | collective-permute-start | bytes 6291464 | tf_op jit(solution)/shard_map/ppermute | solution.py:17
  10.9 2.9 %shard_map.113 = bf16[1,512,1024]{2,1,0:T(8,128)(2,1)} custom-call(s32[16]{0:T(128)} %refs_0_.9, s32[16]{0:T(128)} %refs_1_.9, bf16[2,512,1024]{2,1,0:T(8,128)(2,1)} %refs_2_.7, bf16[2,512,1024]{2,1,0:T(8,128)(2,1)} %shard_map.112.refs_3_.refs_5_.refs_8_), custom_call_target="tpu_custom_call" | custom-call | tf_op jit(solution)/shard_map/pallas_call | solution.py:102
  16.0 1.6 collective-permute-start.3
  17.7 7.5 %collective-permute-done.3 = bf16[64,2176]{1,0:T(8,128)(2,1)S(1)} collective-permute-done((bf16[64,2176]{1,0:T(8,128)(2,1)S(1)}, bf16[64,2176]{1,0:T(8,128)(2,1)S(1)}, u32[]{:S(2)}, u32[]{:S(2)}) %collective-permute-start.3) | collective-permute-done | bytes 278560 | tf_op jit(solution)/shard_map/ppermute | solution.py:17
  25.1 2.6 %collective-permute-start.5 = (bf16[64,2176]{1,0:T(8,128)(2,1)S(1)}, bf16[64,2176]{1,0:T(8,128)(2,1)S(1)}, u32[]{:S(2)}, u32[]{:S(2)}) collective-permute-start(bf16[64,2176]{1,0:T(8,128)(2,1)S(1)} %shard_map.111), channel_id=1, source_target_pairs={{0,16},{4,20},{8,24},{12,28},{16,0},{20,4},{24,8},{28,12},{1,17},{... | collective-permute-start | bytes 835592 | tf_op jit(solution)/shard_map/ppermute | solution.py:17
  27.7 15.0 %collective-permute-done.refs_1_.refs_2_ = bf16[1,512,1024]{2,1,0:T(8,128)(2,1)S(1)} collective-permute-done((bf16[1,512,1024]{2,1,0:T(8,128)(2,1)}, bf16[1,512,1024]{2,1,0:T(8,128)(2,1)S(1)}, u32[]{:S(2)}, u32[]{:S(2)}) %collective-permute-start) | collective-permute-done | bytes 1048608 | tf_op jit(solution)/shard_map/ppermute | solution.py:22
  42.7 1.8 collective-permute-start.7
  44.6 24.5 %collective-permute-start.1 = (bf16[64,2176]{1,0:T(8,128)(2,1)S(1)}, bf16[64,2176]{1,0:T(8,128)(2,1)S(1)}, u32[]{:S(2)}, u32[]{:S(2)}) collective-permute-start(bf16[64,2176]{1,0:T(8,128)(2,1)S(1)} %shard_map.114), channel_id=1, source_target_pairs={{0,4},{4,0},{8,12},{12,8},{16,20},{20,16},{24,28},{28,24},{1,5},{5... | collective-permute-start | bytes 835592 | tf_op jit(solution)/shard_map/ppermute | solution.py:17
  70.8 2.0 collective-permute-start.6
  72.8 3.8 %collective-permute-done.1.refs_5_ = bf16[64,2176]{1,0:T(8,128)(2,1)S(1)} collective-permute-done((bf16[64,2176]{1,0:T(8,128)(2,1)S(1)}, bf16[64,2176]{1,0:T(8,128)(2,1)S(1)}, u32[]{:S(2)}, u32[]{:S(2)}) %collective-permute-start.1) | collective-permute-done | bytes 278560 | tf_op jit(solution)/shard_map/ppermute | solution.py:17
  76.6 2.1 collective-permute-start.8
  79.2 3.0 %shard_map.124 = (bf16[512,1024]{1,0:T(8,128)(2,1)}, bf16[512,1024]{1,0:T(8,128)(2,1)}) custom-call(bf16[2,512,1024]{2,1,0:T(8,128)(2,1)} %refs_4_.3, bf16[1,512,1024]{2,1,0:T(8,128)(2,1)} %copy-done.24), custom_call_target="tpu_custom_call" | custom-call | tf_op jit(solution)/shard_map/pallas_call | solution.py:141
  83.8 4.7 %collective-permute-done.6.refs_7_ = bf16[64,2176]{1,0:T(8,128)(2,1)S(1)} collective-permute-done((bf16[64,2176]{1,0:T(8,128)(2,1)S(1)}, bf16[64,2176]{1,0:T(8,128)(2,1)S(1)}, u32[]{:S(2)}, u32[]{:S(2)}) %collective-permute-start.6) | collective-permute-done | bytes 278560 | tf_op jit(solution)/shard_map/ppermute | solution.py:17
  88.5 5.3 %collective-permute-done.8.refs_8_ = bf16[64,2176]{1,0:T(8,128)(2,1)S(1)} collective-permute-done((bf16[64,2176]{1,0:T(8,128)(2,1)S(1)}, bf16[64,2176]{1,0:T(8,128)(2,1)S(1)}, u32[]{:S(2)}, u32[]{:S(2)}) %collective-permute-start.8) | collective-permute-done | bytes 278560 | tf_op jit(solution)/shard_map/ppermute | solution.py:17
  95.9 5.1 %shard_map.126 = (bf16[2,512,1024]{2,1,0:T(8,128)(2,1)}, bf16[2,512,1024]{2,1,0:T(8,128)(2,1)}, bf16[2,512,1024]{2,1,0:T(8,128)(2,1)}, bf16[2,512,1024]{2,1,0:T(8,128)(2,1)}) custom-call(s32[16]{0:T(128)} %refs_0_.9, s32[16]{0:T(128)} %refs_1_.9, bf16[2,512,1024]{2,1,0:T(8,128)(2,1)} %refs_2_.7, bf16[2,512,1024]{2,1,0:T(8,128)(2,1)} %refs_3_.5, ...), custom_call_target="tpu_custom_call" | custom-call | tf_op jit(solution)/shard_map/pallas_call | solution.py:102
  101.0 1.8 collective-permute-start.19
  108.7 18.7 %collective-permute-done.14.refs_11_ = bf16[2,512,1024]{2,1,0:T(8,128)(2,1)} collective-permute-done((bf16[2,512,1024]{2,1,0:T(8,128)(2,1)S(1)}, bf16[2,512,1024]{2,1,0:T(8,128)(2,1)}, u32[]{:S(2)}, u32[]{:S(2)}) %collective-permute-start.14) | collective-permute-done | bytes 2097184 | tf_op jit(solution)/shard_map/ppermute | solution.py:17
  127.4 12.1 %shard_map.123.hidden_ref = bf16[1024,1024]{1,0:T(8,128)(2,1)S(1)} custom-call(bf16[128,2176]{1,0:T(8,128)(2,1)S(1)} %shard_map.115.refs_0_, bf16[128,2176]{1,0:T(8,128)(2,1)S(1)} %shard_map.117.refs_1_, bf16[128,2176]{1,0:T(8,128)(2,1)S(1)} %shard_map.119.refs_2_, bf16[128,2176]{1,0:T(8,128)(2,1)S(1)} %shard_map.121.refs_3_, ...), custom_call_target="tpu_custom_call" | custom-call | flops 1 | bytes 1 | tf_op jit(solution)/shard_map/pallas_call | solution.py:208
  139.6 2.4 %shard_map.125 = (bf16[512,1024]{1,0:T(8,128)(2,1)S(1)}, bf16[512,1024]{1,0:T(8,128)(2,1)S(1)}) custom-call(bf16[1024,1024]{1,0:T(8,128)(2,1)S(1)} %shard_map.123.hidden_ref, bf16[512,1024]{1,0:T(8,128)(2,1)S(1)} %copy-done.8, bf16[512,1024]{1,0:T(8,128)(2,1)S(1)} %copy-done.7), custom_call_target="tpu_custom_call" | custom-call | flops 1 | bytes 1 | tf_op jit(solution)/shard_map/pallas_call | solution.py:245
  142.0 4.6 %collective-permute-done.18.refs_0_ = bf16[512,1024]{1,0:T(8,128)(2,1)} collective-permute-done((bf16[512,1024]{1,0:T(8,128)(2,1)}, bf16[512,1024]{1,0:T(8,128)(2,1)}, u32[]{:S(2)}, u32[]{:S(2)}) %collective-permute-start.18) | collective-permute-done | bytes 1048608 | tf_op jit(solution)/shard_map/ppermute | solution.py:17
  146.6 4.3 %collective-permute-done.19.refs_2_.refs_3_ = bf16[2,512,1024]{2,1,0:T(8,128)(2,1)S(1)} collective-permute-done((bf16[2,512,1024]{2,1,0:T(8,128)(2,1)}, bf16[2,512,1024]{2,1,0:T(8,128)(2,1)S(1)}, u32[]{:S(2)}, u32[]{:S(2)}) %collective-permute-start.19) | collective-permute-done | bytes 2097184 | tf_op jit(solution)/shard_map/ppermute | solution.py:22
  151.0 3.3 %shard_map.127 = (bf16[512,512]{1,0:T(8,128)(2,1)S(1)}, bf16[512,512]{1,0:T(8,128)(2,1)S(1)}) custom-call(bf16[1024,1024]{1,0:T(8,128)(2,1)S(1)} %shard_map.123.hidden_ref, bf16[512,1024]{1,0:T(8,128)(2,1)} %collective-permute-done.18.refs_0_, bf16[512,1024]{1,0:T(8,128)(2,1)S(1)} %get-tuple-element.26.refs_1_, ...), custom_call_target="tpu_custom_call" | custom-call | flops 1 | bytes 1 | tf_op jit(solution)/shard_map/pallas_call | solution.py:245
  158.4 2.0 collective-permute-start.21
  160.4 3.6 %shard_map.128 = (bf16[2,512,1024]{2,1,0:T(8,128)(2,1)}, bf16[2,512,1024]{2,1,0:T(8,128)(2,1)}, bf16[2,512,1024]{2,1,0:T(8,128)(2,1)}) custom-call(s32[16]{0:T(128)} %refs_0_.9, s32[16]{0:T(128)} %refs_1_.9, bf16[1,512,1024]{2,1,0:T(8,128)(2,1)} %copy-done.4, ...), custom_call_target="tpu_custom_call", output_to_operand_aliasing={{0}: (4, {}), {1}: (5, {}), {2}: (6, {})} | custom-call | tf_op jit(solution)/shard_map/pallas_call | solution.py:102
  164.1 13.4 %collective-permute-done.21 = bf16[4,64,512]{2,1,0:T(8,128)(2,1)S(1)} collective-permute-done((bf16[4,64,512]{2,1,0:T(8,128)(2,1)}, bf16[4,64,512]{2,1,0:T(8,128)(2,1)S(1)}, u32[]{:S(2)}, u32[]{:S(2)}) %collective-permute-start.21) | collective-permute-done | bytes 262176 | tf_op jit(solution)/shard_map/ppermute | solution.py:17
  181.3 1.9 collective-permute-done.25
  184.0 7.8 %collective-permute-done.26 = bf16[4,64,512]{2,1,0:T(8,128)(2,1)S(1)} collective-permute-done((bf16[4,64,512]{2,1,0:T(8,128)(2,1)S(1)}, bf16[4,64,512]{2,1,0:T(8,128)(2,1)S(1)}, u32[]{:S(2)}, u32[]{:S(2)}) %collective-permute-start.26) | collective-permute-done | bytes 262176 | tf_op jit(solution)/shard_map/ppermute | solution.py:17
  192.0 14.5 %collective-permute-done.22 = bf16[2,64,1536]{2,1,0:T(8,128)(2,1)S(1)} collective-permute-done((bf16[2,64,1536]{2,1,0:T(8,128)(2,1)S(1)}, bf16[2,64,1536]{2,1,0:T(8,128)(2,1)S(1)}, u32[]{:S(2)}, u32[]{:S(2)}) %collective-permute-start.22) | collective-permute-done | bytes 393248 | tf_op jit(solution)/shard_map/ppermute | solution.py:17
  206.6 2.5 %collective-permute-done.27 = bf16[2,64,512]{2,1,0:T(8,128)(2,1)S(1)} collective-permute-done((bf16[2,64,512]{2,1,0:T(8,128)(2,1)S(1)}, bf16[2,64,512]{2,1,0:T(8,128)(2,1)S(1)}, u32[]{:S(2)}, u32[]{:S(2)}) %collective-permute-start.27) | collective-permute-done | bytes 131104 | tf_op jit(solution)/shard_map/ppermute | solution.py:17
  209.3 4.8 %collective-permute-done.23 = bf16[1,64,1536]{2,1,0:T(8,128)(2,1)S(1)} collective-permute-done((bf16[1,64,1536]{2,1,0:T(8,128)(2,1)S(1)}, bf16[1,64,1536]{2,1,0:T(8,128)(2,1)S(1)}, u32[]{:S(2)}, u32[]{:S(2)}) %collective-permute-start.23) | collective-permute-done | bytes 196640 | tf_op jit(solution)/shard_map/ppermute | solution.py:17
  (121 shorter events, 25.1 us)
Async XLA Ops:
  7.7 70.9 %collective-permute-start.13 = (bf16[2,512,1024]{2,1,0:T(8,128)(2,1)}, bf16[2,512,1024]{2,1,0:T(8,128)(2,1)S(1)}, u32[]{:S(2)}, u32[]{:S(2)}) collective-permute-start(bf16[2,512,1024]{2,1,0:T(8,128)(2,1)} %get-tuple-element.21), channel_id=1, source_target_pairs={{0,1},{1,0},{2,3},{3,2},{4,5},{5,4},{6,7},{7,6},{8,9},{9,8},{10,11... | collective-permute-start | bytes 6291464 | tf_op jit(solution)/shard_map/ppermute | solution.py:17
  8.3 85.5 %collective-permute-start.2 = (bf16[2,512,1024]{2,1,0:T(8,128)(2,1)S(1)}, bf16[2,512,1024]{2,1,0:T(8,128)(2,1)S(1)}, u32[]{:S(2)}, u32[]{:S(2)}) collective-permute-start(bf16[2,512,1024]{2,1,0:T(8,128)(2,1)S(1)} %copy-done.2), channel_id=1, source_target_pairs={{0,2},{1,3},{2,0},{3,1},{4,6},{5,7},{6,4},{7,5},{8,10},{9,11},{10,... | collective-permute-start | bytes 6291464 | tf_op jit(solution)/shard_map/ppermute | solution.py:17
  13.8 28.9 %collective-permute-start = (bf16[1,512,1024]{2,1,0:T(8,128)(2,1)}, bf16[1,512,1024]{2,1,0:T(8,128)(2,1)S(1)}, u32[]{:S(2)}, u32[]{:S(2)}) collective-permute-start(bf16[1,512,1024]{2,1,0:T(8,128)(2,1)} %shard_map.113), channel_id=1, source_target_pairs={{0,4},{4,8},{8,12},{12,16},{16,20},{20,24},{24,28},{28,0},{1,5},{5... | collective-permute-start | bytes 3145736 | tf_op jit(solution)/shard_map/ppermute | solution.py:22
  15.3 55.4 %collective-permute-start.15 = (bf16[1,512,1024]{2,1,0:T(8,128)(2,1)}, bf16[1,512,1024]{2,1,0:T(8,128)(2,1)S(1)}, u32[]{:S(2)}, u32[]{:S(2)}) collective-permute-start(bf16[1,512,1024]{2,1,0:T(8,128)(2,1)} %get-tuple-element.22), channel_id=1, source_target_pairs={{0,1},{1,0},{2,3},{3,2},{4,5},{5,4},{6,7},{7,6},{8,9},{9,8},{10,11... | collective-permute-start | bytes 3145736 | tf_op jit(solution)/shard_map/ppermute | solution.py:17
  16.0 9.1 %collective-permute-start.3 = (bf16[64,2176]{1,0:T(8,128)(2,1)S(1)}, bf16[64,2176]{1,0:T(8,128)(2,1)S(1)}, u32[]{:S(2)}, u32[]{:S(2)}) collective-permute-start(bf16[64,2176]{1,0:T(8,128)(2,1)S(1)} %shard_map.111), channel_id=1, source_target_pairs={{0,8},{4,12},{8,0},{12,4},{16,24},{20,28},{24,16},{28,20},{1,9},{5... | collective-permute-start | bytes 835592 | tf_op jit(solution)/shard_map/ppermute | solution.py:17
  25.1 44.7 %copy-start.23 = (bf16[64,2176]{1,0:T(8,128)(2,1)}, bf16[64,2176]{1,0:T(8,128)(2,1)S(1)}, u32[]{:S(2)}) copy-start(bf16[64,2176]{1,0:T(8,128)(2,1)S(1)} %collective-permute-done.3) | copy-start | bytes 835588
  25.1 19.4 %collective-permute-start.5 = (bf16[64,2176]{1,0:T(8,128)(2,1)S(1)}, bf16[64,2176]{1,0:T(8,128)(2,1)S(1)}, u32[]{:S(2)}, u32[]{:S(2)}) collective-permute-start(bf16[64,2176]{1,0:T(8,128)(2,1)S(1)} %shard_map.111), channel_id=1, source_target_pairs={{0,16},{4,20},{8,24},{12,28},{16,0},{20,4},{24,8},{28,12},{1,17},{... | collective-permute-start | bytes 835592 | tf_op jit(solution)/shard_map/ppermute | solution.py:17
  42.7 27.1 %collective-permute-start.7 = (bf16[64,2176]{1,0:T(8,128)(2,1)S(1)}, bf16[64,2176]{1,0:T(8,128)(2,1)S(1)}, u32[]{:S(2)}, u32[]{:S(2)}) collective-permute-start(bf16[64,2176]{1,0:T(8,128)(2,1)S(1)} %shard_map.111), channel_id=1, source_target_pairs={{0,24},{4,28},{8,16},{12,20},{16,8},{20,12},{24,0},{28,4},{1,25},{... | collective-permute-start | bytes 835592 | tf_op jit(solution)/shard_map/ppermute | solution.py:17
  44.6 32.0 %collective-permute-start.1 = (bf16[64,2176]{1,0:T(8,128)(2,1)S(1)}, bf16[64,2176]{1,0:T(8,128)(2,1)S(1)}, u32[]{:S(2)}, u32[]{:S(2)}) collective-permute-start(bf16[64,2176]{1,0:T(8,128)(2,1)S(1)} %shard_map.114), channel_id=1, source_target_pairs={{0,4},{4,0},{8,12},{12,8},{16,20},{20,16},{24,28},{28,24},{1,5},{5... | collective-permute-start | bytes 835592 | tf_op jit(solution)/shard_map/ppermute | solution.py:17
  70.6 12.0 %collective-permute-start.4 = (bf16[64,2176]{1,0:T(8,128)(2,1)}, bf16[64,2176]{1,0:T(8,128)(2,1)}, u32[]{:S(2)}, u32[]{:S(2)}) collective-permute-start(bf16[64,2176]{1,0:T(8,128)(2,1)} %shard_map.116), channel_id=1, source_target_pairs={{0,4},{4,0},{8,12},{12,8},{16,20},{20,16},{24,28},{28,24},{1,5},{5... | collective-permute-start | bytes 835592 | tf_op jit(solution)/shard_map/ppermute | solution.py:17
  70.8 17.8 %collective-permute-start.6 = (bf16[64,2176]{1,0:T(8,128)(2,1)S(1)}, bf16[64,2176]{1,0:T(8,128)(2,1)S(1)}, u32[]{:S(2)}, u32[]{:S(2)}) collective-permute-start(bf16[64,2176]{1,0:T(8,128)(2,1)S(1)} %shard_map.118), channel_id=1, source_target_pairs={{0,4},{4,0},{8,12},{12,8},{16,20},{20,16},{24,28},{28,24},{1,5},{5... | collective-permute-start | bytes 835592 | tf_op jit(solution)/shard_map/ppermute | solution.py:17
  76.6 17.2 %collective-permute-start.8 = (bf16[64,2176]{1,0:T(8,128)(2,1)S(1)}, bf16[64,2176]{1,0:T(8,128)(2,1)S(1)}, u32[]{:S(2)}, u32[]{:S(2)}) collective-permute-start(bf16[64,2176]{1,0:T(8,128)(2,1)S(1)} %shard_map.120), channel_id=1, source_target_pairs={{0,4},{4,0},{8,12},{12,8},{16,20},{20,16},{24,28},{28,24},{1,5},{5... | collective-permute-start | bytes 835592 | tf_op jit(solution)/shard_map/ppermute | solution.py:17
  78.7 48.7 %collective-permute-start.14 = (bf16[2,512,1024]{2,1,0:T(8,128)(2,1)S(1)}, bf16[2,512,1024]{2,1,0:T(8,128)(2,1)}, u32[]{:S(2)}, u32[]{:S(2)}) collective-permute-start(bf16[2,512,1024]{2,1,0:T(8,128)(2,1)S(1)} %collective-permute-done.13.refs_9_), channel_id=1, source_target_pairs={{0,2},{1,3},{2,0},{3,1},{4,6},{5,7},{6,4},{7,5},{8,10},{9,11},{10,... | collective-permute-start | bytes 6291464 | tf_op jit(solution)/shard_map/ppermute | solution.py:17
  82.7 64.0 %collective-permute-start.18 = (bf16[512,1024]{1,0:T(8,128)(2,1)}, bf16[512,1024]{1,0:T(8,128)(2,1)}, u32[]{:S(2)}, u32[]{:S(2)}) collective-permute-start(bf16[512,1024]{1,0:T(8,128)(2,1)} %get-tuple-element.23.refs_0_), channel_id=1, source_target_pairs={{0,2},{1,3},{2,0},{3,1},{4,6},{5,7},{6,4},{7,5},{8,10},{9,11},{10,... | collective-permute-start | bytes 3145736 | tf_op jit(solution)/shard_map/ppermute | solution.py:17
  101.0 50.0 %collective-permute-start.19 = (bf16[2,512,1024]{2,1,0:T(8,128)(2,1)}, bf16[2,512,1024]{2,1,0:T(8,128)(2,1)S(1)}, u32[]{:S(2)}, u32[]{:S(2)}) collective-permute-start(bf16[2,512,1024]{2,1,0:T(8,128)(2,1)} %get-tuple-element.27), channel_id=1, source_target_pairs={{0,4},{4,8},{8,12},{12,16},{16,20},{20,24},{24,28},{28,0},{1,5},{5... | collective-permute-start | bytes 6291464 | tf_op jit(solution)/shard_map/ppermute | solution.py:22
  103.9 2.0 collective-permute-start.9
  104.0 2.7 %collective-permute-start.10 = (bf16[128,2176]{1,0:T(8,128)(2,1)S(1)}, bf16[128,2176]{1,0:T(8,128)(2,1)S(1)}, u32[]{:S(2)}, u32[]{:S(2)}) collective-permute-start(bf16[128,2176]{1,0:T(8,128)(2,1)S(1)} %shard_map.117.refs_1_), channel_id=1, source_target_pairs={{0,1},{1,0},{2,3},{3,2},{4,5},{5,4},{6,7},{7,6},{8,9},{9,8},{10,11... | collective-permute-start | bytes 1671176 | tf_op jit(solution)/shard_map/ppermute | solution.py:17
  105.2 34.4 %copy-start.7 = (bf16[512,1024]{1,0:T(8,128)(2,1)S(1)}, bf16[512,1024]{1,0:T(8,128)(2,1)}, u32[]{:S(2)}) copy-start(bf16[512,1024]{1,0:T(8,128)(2,1)} %get-tuple-element.24.refs_1_) | copy-start | bytes 3145732
  105.2 34.4 %copy-start.8 = (bf16[512,1024]{1,0:T(8,128)(2,1)S(1)}, bf16[512,1024]{1,0:T(8,128)(2,1)}, u32[]{:S(2)}) copy-start(bf16[512,1024]{1,0:T(8,128)(2,1)} %get-tuple-element.23.refs_0_) | copy-start | bytes 3145732
  106.0 2.0 collective-permute-start.11
  106.8 2.0 collective-permute-start.12
  141.9 14.4 %collective-permute-start.16 = (bf16[512,1024]{1,0:T(8,128)(2,1)S(1)}, bf16[512,1024]{1,0:T(8,128)(2,1)S(1)}, u32[]{:S(2)}, u32[]{:S(2)}) collective-permute-start(bf16[512,1024]{1,0:T(8,128)(2,1)S(1)} %get-tuple-element.26.refs_1_), channel_id=1, source_target_pairs={{0,1},{1,0},{2,3},{3,2},{4,5},{5,4},{6,7},{7,6},{8,9},{9,8},{10,11... | collective-permute-start | bytes 3145736 | tf_op jit(solution)/shard_map/ppermute | solution.py:17
  154.2 2.0 collective-permute-start.20
  154.3 25.6 %collective-permute-start.24 = (bf16[512,1024]{1,0:T(8,128)(2,1)S(1)}, bf16[512,1024]{1,0:T(8,128)(2,1)S(1)}, u32[]{:S(2)}, u32[]{:S(2)}) collective-permute-start(bf16[512,1024]{1,0:T(8,128)(2,1)S(1)} %copy-done.7), channel_id=1, source_target_pairs={{0,2},{1,3},{2,0},{3,1},{4,6},{5,7},{6,4},{7,5},{8,10},{9,11},{10,... | collective-permute-start | bytes 3145736 | tf_op jit(solution)/shard_map/ppermute | solution.py:17
  157.7 19.9 %collective-permute-start.17 = (bf16[4,64,1024]{2,1,0:T(8,128)(2,1)}, bf16[4,64,1024]{2,1,0:T(8,128)(2,1)}, u32[]{:S(2)}, u32[]{:S(2)}) collective-permute-start(bf16[4,64,1024]{2,1,0:T(8,128)(2,1)} %fusion.4), channel_id=1, source_target_pairs={{0,4},{4,0},{8,12},{12,8},{16,20},{20,16},{24,28},{28,24},{1,5},{5... | collective-permute-start | bytes 1572872 | tf_op jit(solution)/shard_map/ppermute | solution.py:17
  158.4 19.1 %collective-permute-start.21 = (bf16[4,64,512]{2,1,0:T(8,128)(2,1)}, bf16[4,64,512]{2,1,0:T(8,128)(2,1)S(1)}, u32[]{:S(2)}, u32[]{:S(2)}) collective-permute-start(bf16[4,64,512]{2,1,0:T(8,128)(2,1)} %fusion.8), channel_id=1, source_target_pairs={{0,4},{4,0},{8,12},{12,8},{16,20},{20,16},{24,28},{28,24},{1,5},{5... | collective-permute-start | bytes 786440 | tf_op jit(solution)/shard_map/ppermute | solution.py:17
  181.2 2.0 collective-permute-start.25
  183.4 8.4 %collective-permute-start.26 = (bf16[4,64,512]{2,1,0:T(8,128)(2,1)S(1)}, bf16[4,64,512]{2,1,0:T(8,128)(2,1)S(1)}, u32[]{:S(2)}, u32[]{:S(2)}) collective-permute-start(bf16[4,64,512]{2,1,0:T(8,128)(2,1)S(1)} %fusion.9), channel_id=1, source_target_pairs={{0,4},{4,0},{8,12},{12,8},{16,20},{20,16},{24,28},{28,24},{1,5},{5... | collective-permute-start | bytes 786440 | tf_op jit(solution)/shard_map/ppermute | solution.py:17
  183.5 23.0 %collective-permute-start.22 = (bf16[2,64,1536]{2,1,0:T(8,128)(2,1)S(1)}, bf16[2,64,1536]{2,1,0:T(8,128)(2,1)S(1)}, u32[]{:S(2)}, u32[]{:S(2)}) collective-permute-start(bf16[2,64,1536]{2,1,0:T(8,128)(2,1)S(1)} %fusion.3), channel_id=1, source_target_pairs={{0,16},{4,20},{8,24},{12,28},{16,0},{20,4},{24,8},{28,12},{1,17},{... | collective-permute-start | bytes 1179656 | tf_op jit(solution)/shard_map/ppermute | solution.py:17
  191.9 17.3 %collective-permute-start.27 = (bf16[2,64,512]{2,1,0:T(8,128)(2,1)S(1)}, bf16[2,64,512]{2,1,0:T(8,128)(2,1)S(1)}, u32[]{:S(2)}, u32[]{:S(2)}) collective-permute-start(bf16[2,64,512]{2,1,0:T(8,128)(2,1)S(1)} %slice.100), channel_id=1, source_target_pairs={{0,16},{4,20},{8,24},{12,28},{16,0},{20,4},{24,8},{28,12},{1,17},{... | collective-permute-start | bytes 393224 | tf_op jit(solution)/shard_map/ppermute | solution.py:17
  206.6 7.5 %collective-permute-start.23 = (bf16[1,64,1536]{2,1,0:T(8,128)(2,1)S(1)}, bf16[1,64,1536]{2,1,0:T(8,128)(2,1)S(1)}, u32[]{:S(2)}, u32[]{:S(2)}) collective-permute-start(bf16[1,64,1536]{2,1,0:T(8,128)(2,1)S(1)} %slice.99), channel_id=1, source_target_pairs={{0,8},{4,12},{8,0},{12,4},{16,24},{20,28},{24,16},{28,20},{1,9},{5... | collective-permute-start | bytes 589832 | tf_op jit(solution)/shard_map/ppermute | solution.py:17
  209.2 5.6 %collective-permute-start.28 = (bf16[1,64,512]{2,1,0:T(8,128)(2,1)S(1)}, bf16[1,64,512]{2,1,0:T(8,128)(2,1)S(1)}, u32[]{:S(2)}, u32[]{:S(2)}) collective-permute-start(bf16[1,64,512]{2,1,0:T(8,128)(2,1)S(1)} %slice.101), channel_id=1, source_target_pairs={{0,8},{4,12},{8,0},{12,4},{16,24},{20,28},{24,16},{28,20},{1,9},{5... | collective-permute-start | bytes 196616 | tf_op jit(solution)/shard_map/ppermute | solution.py:17
  (22 other events, 175.7 us)

commit v11 on v9

--- a/solution.py
+++ b/solution.py
@@ -305,7 +305,7 @@
     (mine,) = copies(((0, "mine", 0, 0), (1, "mine", 0, 1)), places, (w_gate, w_up), (2,))
     theirs, theirs_down = copies(
         ((0, "theirs", 0, 0), (1, "theirs", 0, 1), (2, "theirs", 1, 0)),
-        places, (w_gate, w_up, w_down), (2, 1), (mine,),
+        places, (w_gate, w_up, w_down), (2, 1),
     )
     near_weights = [mine, swap(theirs, "shard", 1)]
     weights = spread(near_weights)
@@ -318,21 +318,14 @@
     far = [swap(p, "shard", 1) for p in near]
 
     hidden = hidden_of(near + far, weights)
-    leave, *news = copies(
-        tuple((i, "leaves", 0, i) for i in range(3))
-        + tuple((i, "stays", i + 1, "stays") for i in range(3)),
-        places, (w_gate, w_up, w_down), (3, 2, 2, 2), near,
-    )
-    arrive = passed_along(leave, "dp", 1)
-
-    leave, *news = copies(
-        tuple((i, "leaves", 0, i) for i in range(3))
-        + tuple((i, "stays", i + 1, "stays") for i in range(3)),
-        places, (w_gate, w_up, w_down), (3, 2, 2, 2), across + [weights[2]],
+    (leave,) = copies(
+        tuple((i, "leaves", 0, i) for i in range(3)), places, (w_gate, w_up, w_down), (3,), across
     )
     arrive = passed_along(leave, "dp", 1)
     news = copies(
-        tuple((0, i, i, "leaves") for i in range(3)), places, (arrive,), (2, 2, 2), (), news
+        tuple((0, i, i, "leaves") for i in range(3))
+        + tuple((i + 1, "stays", i, "stays") for i in range(3)),
+        places, (arrive, w_gate, w_up, w_down), (2, 2, 2),
     )
 
     groups = [[d[0] for d in downs]] + [d[1:] for d in downs]

time: 201 us -> 191 us (0.950)
  waiting for transfers between devices: 124 us -> 115 us
  starting transfers between devices: 29 us -> 23.2 us
  other arithmetic: 2.42 us -> 5.65 us
    ppermute x27, waiting for transfers between devices: 124 us -> 111 us  [swap(): lax.ppermute(x, axis, [(i, i ^ bit) for i in range(lax.axis_size(axis))])]
    ppermute x27, starting transfers between devices: 27.5 us -> 21.6 us  [swap(): lax.ppermute(x, axis, [(i, i ^ bit) for i in range(lax.axis_size(axis))])]
    ppermute x1, waiting for transfers between devices: 0.01 us -> 4.13 us  [passed_along(): return lax.ppermute(x, axis, [(i, (i + by) % size) for i in range(size)])]
    unnamed x28 -> x34, local copies, waits for them, and re-layouts: 3.45 us -> 5.43 us
  transfers between devices with their start and end apart: 28 -> 28, of which waited for: 15 -> 18; matrix products, arithmetic and copies ran while one was open for 1% -> 3% of each run, Pallas kernels for 16% -> 18%
where the time goes in v11:
time: 191 us; the launch traced here: 190 us
  waiting for transfers between devices  115 us (60%)
  Pallas kernels  39.6 us (21%)
  starting transfers between devices  23.2 us (12%)
  other arithmetic  5.65 us (3%)
  local copies, waits for them, and re-layouts  5.61 us (3%)
    ppermute x27, waiting for transfers between devices, swap(): lax.ppermute(x, axis, [(i, i ^ bit) for i in range(lax.axis_size(axis))])  111 us
    ppermute x27, starting transfers between devices, swap(): lax.ppermute(x, axis, [(i, i ^ bit) for i in range(lax.axis_size(axis))])  21.6 us
    pallas_call x4, Pallas kernels, copies(): pl.pallas_call(functools.partial(copy_kernel, plan, len(ins), len(counts)...  16.6 us
    pallas_call x1, Pallas kernels, hidden_of(): pl.pallas_call(functools.partial(hidden_kernel, len(pieces)), grid=(ff //...  12.5 us
    pallas_call x3, Pallas kernels, down_of(): pl.pallas_call(functools.partial(down_kernel, len(downs)), in_specs=[vmem...  6.16 us
    unnamed x34, local copies, waits for them, and re-layouts  5.43 us
    ppermute x1, waiting for transfers between devices, passed_along(): return lax.ppermute(x, axis, [(i, (i + by) % size) for i in range(size)])  4.13 us
  transfers between devices with their start and end apart: 28, of which 18 were waited for; matrix products, arithmetic and copies ran while one was open for 3% of the time, Pallas kernels for 18%

profile of v11, /device:TPU:0, one launch (start us, length us, event | category | flops | bytes accessed | tf_op | source)
XLA Modules:
  0.0 190.3 jit_solution(10200176966225163670)
XLA Ops:
  0.6 3.6 %shard_map.117 = (bf16[2,512,1024]{2,1,0:T(8,128)(2,1)}, bf16[1,512,1024]{2,1,0:T(8,128)(2,1)}) custom-call(s32[16]{0:T(128)} %refs_0_.7, s32[16]{0:T(128)} %refs_1_.7, bf16[2,512,1024]{2,1,0:T(8,128)(2,1)} %refs_3_.7, bf16[2,512,1024]{2,1,0:T(8,128)(2,1)} %refs_4_.5, bf16[2,512,1024]{2,1,0:T(8,128)(2,1)} %refs_5_.1), custom_call_target="tpu_custom_call" | custom-call | tf_op jit(solution)/shard_map/pallas_call | solution.py:102
  4.8 3.3 %shard_map.112.refs_8_ = bf16[2,512,1024]{2,1,0:T(8,128)(2,1)} custom-call(s32[16]{0:T(128)} %refs_0_.7, s32[16]{0:T(128)} %refs_1_.7, bf16[2,512,1024]{2,1,0:T(8,128)(2,1)} %refs_3_.7, bf16[2,512,1024]{2,1,0:T(8,128)(2,1)} %refs_4_.5), custom_call_target="tpu_custom_call" | custom-call | tf_op jit(solution)/shard_map/pallas_call | solution.py:102
  8.1 2.6 %collective-permute-start.1 = (bf16[2,512,1024]{2,1,0:T(8,128)(2,1)}, bf16[2,512,1024]{2,1,0:T(8,128)(2,1)S(1)}, u32[]{:S(2)}, u32[]{:S(2)}) collective-permute-start(bf16[2,512,1024]{2,1,0:T(8,128)(2,1)} %shard_map.112.refs_8_), channel_id=1, source_target_pairs={{0,2},{1,3},{2,0},{3,1},{4,6},{5,7},{6,4},{7,5},{8,10},{9,11},{10,... | collective-permute-start | bytes 6291464 | tf_op jit(solution)/shard_map/ppermute | solution.py:17
  11.4 2.7 %collective-permute-start.4 = (bf16[64,2176]{1,0:T(8,128)(2,1)S(1)}, bf16[64,2176]{1,0:T(8,128)(2,1)S(1)}, u32[]{:S(2)}, u32[]{:S(2)}) collective-permute-start(bf16[64,2176]{1,0:T(8,128)(2,1)S(1)} %shard_map.111), channel_id=1, source_target_pairs={{0,16},{4,20},{8,24},{12,28},{16,0},{20,4},{24,8},{28,12},{1,17},{... | collective-permute-start | bytes 835592 | tf_op jit(solution)/shard_map/ppermute | solution.py:17
  15.6 18.2 %collective-permute-done.4 = bf16[64,2176]{1,0:T(8,128)(2,1)S(1)} collective-permute-done((bf16[64,2176]{1,0:T(8,128)(2,1)S(1)}, bf16[64,2176]{1,0:T(8,128)(2,1)S(1)}, u32[]{:S(2)}, u32[]{:S(2)}) %collective-permute-start.4) | collective-permute-done | bytes 278560 | tf_op jit(solution)/shard_map/ppermute | solution.py:17
  33.8 1.5 collective-permute-start
  35.8 1.5 collective-permute-start.7
  37.3 6.1 %collective-permute-done.refs_5_ = bf16[64,2176]{1,0:T(8,128)(2,1)S(1)} collective-permute-done((bf16[64,2176]{1,0:T(8,128)(2,1)S(1)}, bf16[64,2176]{1,0:T(8,128)(2,1)S(1)}, u32[]{:S(2)}, u32[]{:S(2)}) %collective-permute-start) | collective-permute-done | bytes 278560 | tf_op jit(solution)/shard_map/ppermute | solution.py:17
  43.4 1.5 collective-permute-start.3
  45.4 4.0 %collective-permute-done.5.refs_7_ = bf16[64,2176]{1,0:T(8,128)(2,1)S(1)} collective-permute-done((bf16[64,2176]{1,0:T(8,128)(2,1)S(1)}, bf16[64,2176]{1,0:T(8,128)(2,1)S(1)}, u32[]{:S(2)}, u32[]{:S(2)}) %collective-permute-start.5) | collective-permute-done | bytes 278560 | tf_op jit(solution)/shard_map/ppermute | solution.py:17
  49.4 6.0 %collective-permute-done.7.refs_8_ = bf16[64,2176]{1,0:T(8,128)(2,1)S(1)} collective-permute-done((bf16[64,2176]{1,0:T(8,128)(2,1)S(1)}, bf16[64,2176]{1,0:T(8,128)(2,1)S(1)}, u32[]{:S(2)}, u32[]{:S(2)}) %collective-permute-start.7) | collective-permute-done | bytes 278560 | tf_op jit(solution)/shard_map/ppermute | solution.py:17
  55.3 3.6 %collective-permute-done.3.refs_6_ = bf16[64,2176]{1,0:T(8,128)(2,1)S(1)} collective-permute-done((bf16[64,2176]{1,0:T(8,128)(2,1)S(1)}, bf16[64,2176]{1,0:T(8,128)(2,1)S(1)}, u32[]{:S(2)}, u32[]{:S(2)}) %collective-permute-start.3) | collective-permute-done | bytes 278560 | tf_op jit(solution)/shard_map/ppermute | solution.py:17
  59.7 3.6 %shard_map.122 = bf16[3,512,1024]{2,1,0:T(8,128)(2,1)} custom-call(s32[16]{0:T(128)} %refs_0_.7, s32[16]{0:T(128)} %refs_1_.7, bf16[2,512,1024]{2,1,0:T(8,128)(2,1)} %refs_3_.7, bf16[2,512,1024]{2,1,0:T(8,128)(2,1)} %refs_4_.5, bf16[2,512,1024]{2,1,0:T(8,128)(2,1)} %refs_5_.1, bf16[64,2176]{1,0:T(8,128)(2,1)} %copy-done.10, bf16[64,2176]{1,0:T(8,128)(2,1)} %copy-done.12, ...), custom_call_target="tpu_custom_call" | custom-call | tf_op jit(solution)/shard_map/pallas_call | solution.py:102
  63.3 1.5 collective-permute-start.23
  67.9 2.9 %shard_map.119 = (bf16[512,1024]{1,0:T(8,128)(2,1)}, bf16[512,1024]{1,0:T(8,128)(2,1)}) custom-call(bf16[2,512,1024]{2,1,0:T(8,128)(2,1)} %refs_5_.1, bf16[1,512,1024]{2,1,0:T(8,128)(2,1)} %collective-permute-done.14.other_ref), custom_call_target="tpu_custom_call" | custom-call | tf_op jit(solution)/shard_map/pallas_call | solution.py:141
  73.1 1.4 collective-permute-done.9.refs_5_
  75.4 26.9 %collective-permute-done.13.refs_11_ = bf16[2,512,1024]{2,1,0:T(8,128)(2,1)S(1)} collective-permute-done((bf16[2,512,1024]{2,1,0:T(8,128)(2,1)S(1)}, bf16[2,512,1024]{2,1,0:T(8,128)(2,1)S(1)}, u32[]{:S(2)}, u32[]{:S(2)}) %collective-permute-start.13) | collective-permute-done | bytes 2097184 | tf_op jit(solution)/shard_map/ppermute | solution.py:17
  103.6 1.6 copy-done.3
  105.2 12.5 %shard_map.118.hidden_ref = bf16[1024,1024]{1,0:T(8,128)(2,1)S(1)} custom-call(bf16[128,2176]{1,0:T(8,128)(2,1)S(1)} %shard_map.113.refs_0_, bf16[128,2176]{1,0:T(8,128)(2,1)S(1)} %shard_map.114.refs_1_, bf16[128,2176]{1,0:T(8,128)(2,1)S(1)} %shard_map.115.refs_2_, bf16[128,2176]{1,0:T(8,128)(2,1)S(1)} %shard_map.116.refs_3_, ...), custom_call_target="tpu_custom_call" | custom-call | flops 1 | bytes 1 | tf_op jit(solution)/shard_map/pallas_call | solution.py:208
  117.8 3.6 %shard_map.120 = (bf16[512,1024]{1,0:T(8,128)(2,1)S(1)}, bf16[512,1024]{1,0:T(8,128)(2,1)S(1)}) custom-call(bf16[1024,1024]{1,0:T(8,128)(2,1)S(1)} %shard_map.118.hidden_ref, bf16[512,1024]{1,0:T(8,128)(2,1)S(1)} %copy-done.4, bf16[512,1024]{1,0:T(8,128)(2,1)} %get-tuple-element.20.refs_1_), custom_call_target="tpu_custom_call" | custom-call | flops 1 | bytes 1 | tf_op jit(solution)/shard_map/pallas_call | solution.py:245
  121.4 3.1 %collective-permute-done.17.refs_0_ = bf16[512,1024]{1,0:T(8,128)(2,1)S(1)} collective-permute-done((bf16[512,1024]{1,0:T(8,128)(2,1)}, bf16[512,1024]{1,0:T(8,128)(2,1)S(1)}, u32[]{:S(2)}, u32[]{:S(2)}) %collective-permute-start.17) | collective-permute-done | bytes 1048608 | tf_op jit(solution)/shard_map/ppermute | solution.py:17
  126.0 1.8 collective-permute-start.22
  129.9 1.8 collective-permute-start.16
  132.1 4.1 %collective-permute-done.23.refs_2_ = bf16[3,512,1024]{2,1,0:T(8,128)(2,1)} collective-permute-done((bf16[3,512,1024]{2,1,0:T(8,128)(2,1)}, bf16[3,512,1024]{2,1,0:T(8,128)(2,1)}, u32[]{:S(2)}, u32[]{:S(2)}) %collective-permute-start.23) | collective-permute-done | bytes 3145760 | tf_op jit(solution)/shard_map/ppermute | solution.py:22
  136.2 6.1 %shard_map.123 = (bf16[2,512,1024]{2,1,0:T(8,128)(2,1)}, bf16[2,512,1024]{2,1,0:T(8,128)(2,1)}, bf16[2,512,1024]{2,1,0:T(8,128)(2,1)}) custom-call(s32[16]{0:T(128)} %refs_0_.7, s32[16]{0:T(128)} %refs_1_.7, bf16[3,512,1024]{2,1,0:T(8,128)(2,1)} %collective-permute-done.23.refs_2_, bf16[2,512,1024]{2,1,0:T(8,128)(2,1)} %refs_3_.7, ...), custom_call_target="tpu_custom_call" | custom-call | tf_op jit(solution)/shard_map/pallas_call | solution.py:102
  142.4 10.5 %collective-permute-done.19 = bf16[4,64,512]{2,1,0:T(8,128)(2,1)S(1)} collective-permute-done((bf16[4,64,512]{2,1,0:T(8,128)(2,1)S(1)}, bf16[4,64,512]{2,1,0:T(8,128)(2,1)S(1)}, u32[]{:S(2)}, u32[]{:S(2)}) %collective-permute-start.19) | collective-permute-done | bytes 262176 | tf_op jit(solution)/shard_map/ppermute | solution.py:17
  155.8 1.9 collective-permute-done.24
  158.0 1.7 collective-permute-start.20
  159.7 6.6 %collective-permute-done.25 = bf16[4,64,512]{2,1,0:T(8,128)(2,1)S(1)} collective-permute-done((bf16[4,64,512]{2,1,0:T(8,128)(2,1)S(1)}, bf16[4,64,512]{2,1,0:T(8,128)(2,1)S(1)}, u32[]{:S(2)}, u32[]{:S(2)}) %collective-permute-start.25) | collective-permute-done | bytes 262176 | tf_op jit(solution)/shard_map/ppermute | solution.py:17
  167.3 13.9 %collective-permute-done.20 = bf16[2,64,1536]{2,1,0:T(8,128)(2,1)S(1)} collective-permute-done((bf16[2,64,1536]{2,1,0:T(8,128)(2,1)S(1)}, bf16[2,64,1536]{2,1,0:T(8,128)(2,1)S(1)}, u32[]{:S(2)}, u32[]{:S(2)}) %collective-permute-start.20) | collective-permute-done | bytes 393248 | tf_op jit(solution)/shard_map/ppermute | solution.py:17
  181.4 2.5 %collective-permute-done.26 = bf16[2,64,512]{2,1,0:T(8,128)(2,1)S(1)} collective-permute-done((bf16[2,64,512]{2,1,0:T(8,128)(2,1)S(1)}, bf16[2,64,512]{2,1,0:T(8,128)(2,1)S(1)}, u32[]{:S(2)}, u32[]{:S(2)}) %collective-permute-start.26) | collective-permute-done | bytes 131104 | tf_op jit(solution)/shard_map/ppermute | solution.py:17
  184.1 4.8 %collective-permute-done.21 = bf16[1,64,1536]{2,1,0:T(8,128)(2,1)S(1)} collective-permute-done((bf16[1,64,1536]{2,1,0:T(8,128)(2,1)S(1)}, bf16[1,64,1536]{2,1,0:T(8,128)(2,1)S(1)}, u32[]{:S(2)}, u32[]{:S(2)}) %collective-permute-start.21) | collective-permute-done | bytes 196640 | tf_op jit(solution)/shard_map/ppermute | solution.py:17
  (94 shorter events, 21.8 us)
Async XLA Ops:
  4.3 40.6 %collective-permute-start.12 = (bf16[2,512,1024]{2,1,0:T(8,128)(2,1)}, bf16[2,512,1024]{2,1,0:T(8,128)(2,1)S(1)}, u32[]{:S(2)}, u32[]{:S(2)}) collective-permute-start(bf16[2,512,1024]{2,1,0:T(8,128)(2,1)} %get-tuple-element.17), channel_id=1, source_target_pairs={{0,1},{1,0},{2,3},{3,2},{4,5},{5,4},{6,7},{7,6},{8,9},{9,8},{10,11... | collective-permute-start | bytes 6291464 | tf_op jit(solution)/shard_map/ppermute | solution.py:17
  8.1 58.8 %collective-permute-start.1 = (bf16[2,512,1024]{2,1,0:T(8,128)(2,1)}, bf16[2,512,1024]{2,1,0:T(8,128)(2,1)S(1)}, u32[]{:S(2)}, u32[]{:S(2)}) collective-permute-start(bf16[2,512,1024]{2,1,0:T(8,128)(2,1)} %shard_map.112.refs_8_), channel_id=1, source_target_pairs={{0,2},{1,3},{2,0},{3,1},{4,6},{5,7},{6,4},{7,5},{8,10},{9,11},{10,... | collective-permute-start | bytes 6291464 | tf_op jit(solution)/shard_map/ppermute | solution.py:17
  11.4 22.4 %collective-permute-start.4 = (bf16[64,2176]{1,0:T(8,128)(2,1)S(1)}, bf16[64,2176]{1,0:T(8,128)(2,1)S(1)}, u32[]{:S(2)}, u32[]{:S(2)}) collective-permute-start(bf16[64,2176]{1,0:T(8,128)(2,1)S(1)} %shard_map.111), channel_id=1, source_target_pairs={{0,16},{4,20},{8,24},{12,28},{16,0},{20,4},{24,8},{28,12},{1,17},{... | collective-permute-start | bytes 835592 | tf_op jit(solution)/shard_map/ppermute | solution.py:17
  14.0 21.3 %collective-permute-start.6 = (bf16[64,2176]{1,0:T(8,128)(2,1)S(1)}, bf16[64,2176]{1,0:T(8,128)(2,1)S(1)}, u32[]{:S(2)}, u32[]{:S(2)}) collective-permute-start(bf16[64,2176]{1,0:T(8,128)(2,1)S(1)} %shard_map.111), channel_id=1, source_target_pairs={{0,24},{4,28},{8,16},{12,20},{16,8},{20,12},{24,0},{28,4},{1,25},{... | collective-permute-start | bytes 835592 | tf_op jit(solution)/shard_map/ppermute | solution.py:17
  15.4 20.5 %collective-permute-start.2 = (bf16[64,2176]{1,0:T(8,128)(2,1)S(1)}, bf16[64,2176]{1,0:T(8,128)(2,1)S(1)}, u32[]{:S(2)}, u32[]{:S(2)}) collective-permute-start(bf16[64,2176]{1,0:T(8,128)(2,1)S(1)} %shard_map.111), channel_id=1, source_target_pairs={{0,8},{4,12},{8,0},{12,4},{16,24},{20,28},{24,16},{28,20},{1,9},{5... | collective-permute-start | bytes 835592 | tf_op jit(solution)/shard_map/ppermute | solution.py:17
  33.8 9.6 %collective-permute-start = (bf16[64,2176]{1,0:T(8,128)(2,1)S(1)}, bf16[64,2176]{1,0:T(8,128)(2,1)S(1)}, u32[]{:S(2)}, u32[]{:S(2)}) collective-permute-start(bf16[64,2176]{1,0:T(8,128)(2,1)S(1)} %shard_map.111), channel_id=1, source_target_pairs={{0,4},{4,0},{8,12},{12,8},{16,20},{20,16},{24,28},{28,24},{1,5},{5... | collective-permute-start | bytes 835592 | tf_op jit(solution)/shard_map/ppermute | solution.py:17
  35.3 20.0 %copy-start.16 = (bf16[64,2176]{1,0:T(8,128)(2,1)}, bf16[64,2176]{1,0:T(8,128)(2,1)S(1)}, u32[]{:S(2)}) copy-start(bf16[64,2176]{1,0:T(8,128)(2,1)S(1)} %collective-permute-done.6) | copy-start | bytes 835588
  35.3 14.1 %collective-permute-start.5 = (bf16[64,2176]{1,0:T(8,128)(2,1)S(1)}, bf16[64,2176]{1,0:T(8,128)(2,1)S(1)}, u32[]{:S(2)}, u32[]{:S(2)}) collective-permute-start(bf16[64,2176]{1,0:T(8,128)(2,1)S(1)} %collective-permute-done.4), channel_id=1, source_target_pairs={{0,4},{4,0},{8,12},{12,8},{16,20},{20,16},{24,28},{28,24},{1,5},{5... | collective-permute-start | bytes 835592 | tf_op jit(solution)/shard_map/ppermute | solution.py:17
  35.8 29.0 %copy-start.15 = (bf16[64,2176]{1,0:T(8,128)(2,1)}, bf16[64,2176]{1,0:T(8,128)(2,1)S(1)}, u32[]{:S(2)}) copy-start(bf16[64,2176]{1,0:T(8,128)(2,1)S(1)} %collective-permute-done.2) | copy-start | bytes 835588
  35.8 19.5 %collective-permute-start.7 = (bf16[64,2176]{1,0:T(8,128)(2,1)S(1)}, bf16[64,2176]{1,0:T(8,128)(2,1)S(1)}, u32[]{:S(2)}, u32[]{:S(2)}) collective-permute-start(bf16[64,2176]{1,0:T(8,128)(2,1)S(1)} %collective-permute-done.6), channel_id=1, source_target_pairs={{0,4},{4,0},{8,12},{12,8},{16,20},{20,16},{24,28},{28,24},{1,5},{5... | collective-permute-start | bytes 835592 | tf_op jit(solution)/shard_map/ppermute | solution.py:17
  43.4 15.5 %collective-permute-start.3 = (bf16[64,2176]{1,0:T(8,128)(2,1)S(1)}, bf16[64,2176]{1,0:T(8,128)(2,1)S(1)}, u32[]{:S(2)}, u32[]{:S(2)}) collective-permute-start(bf16[64,2176]{1,0:T(8,128)(2,1)S(1)} %collective-permute-done.2), channel_id=1, source_target_pairs={{0,4},{4,0},{8,12},{12,8},{16,20},{20,16},{24,28},{28,24},{1,5},{5... | collective-permute-start | bytes 835592 | tf_op jit(solution)/shard_map/ppermute | solution.py:17
  44.9 57.4 %collective-permute-start.13 = (bf16[2,512,1024]{2,1,0:T(8,128)(2,1)S(1)}, bf16[2,512,1024]{2,1,0:T(8,128)(2,1)S(1)}, u32[]{:S(2)}, u32[]{:S(2)}) collective-permute-start(bf16[2,512,1024]{2,1,0:T(8,128)(2,1)S(1)} %collective-permute-done.12.refs_9_), channel_id=1, source_target_pairs={{0,2},{1,3},{2,0},{3,1},{4,6},{5,7},{6,4},{7,5},{8,10},{9,11},{10,... | collective-permute-start | bytes 6291464 | tf_op jit(solution)/shard_map/ppermute | solution.py:17
  49.4 18.6 %collective-permute-start.14 = (bf16[1,512,1024]{2,1,0:T(8,128)(2,1)}, bf16[1,512,1024]{2,1,0:T(8,128)(2,1)}, u32[]{:S(2)}, u32[]{:S(2)}) collective-permute-start(bf16[1,512,1024]{2,1,0:T(8,128)(2,1)} %get-tuple-element.18), channel_id=1, source_target_pairs={{0,1},{1,0},{2,3},{3,2},{4,5},{5,4},{6,7},{7,6},{8,9},{9,8},{10,11... | collective-permute-start | bytes 3145736 | tf_op jit(solution)/shard_map/ppermute | solution.py:17
  63.3 72.9 %collective-permute-start.23 = (bf16[3,512,1024]{2,1,0:T(8,128)(2,1)}, bf16[3,512,1024]{2,1,0:T(8,128)(2,1)}, u32[]{:S(2)}, u32[]{:S(2)}) collective-permute-start(bf16[3,512,1024]{2,1,0:T(8,128)(2,1)} %shard_map.122), channel_id=1, source_target_pairs={{0,4},{4,8},{8,12},{12,16},{16,20},{20,24},{24,28},{28,0},{1,5},{5... | collective-permute-start | bytes 9437192 | tf_op jit(solution)/shard_map/ppermute | solution.py:22
  66.9 5.6 %collective-permute-start.10 = (bf16[128,2176]{1,0:T(8,128)(2,1)S(1)}, bf16[128,2176]{1,0:T(8,128)(2,1)}, u32[]{:S(2)}, u32[]{:S(2)}) collective-permute-start(bf16[128,2176]{1,0:T(8,128)(2,1)S(1)} %shard_map.115.refs_2_), channel_id=1, source_target_pairs={{0,1},{1,0},{2,3},{3,2},{4,5},{5,4},{6,7},{7,6},{8,9},{9,8},{10,11... | collective-permute-start | bytes 1671176 | tf_op jit(solution)/shard_map/ppermute | solution.py:17
  67.0 5.6 %collective-permute-start.11 = (bf16[128,2176]{1,0:T(8,128)(2,1)S(1)}, bf16[128,2176]{1,0:T(8,128)(2,1)}, u32[]{:S(2)}, u32[]{:S(2)}) collective-permute-start(bf16[128,2176]{1,0:T(8,128)(2,1)S(1)} %shard_map.116.refs_3_), channel_id=1, source_target_pairs={{0,1},{1,0},{2,3},{3,2},{4,5},{5,4},{6,7},{7,6},{8,9},{9,8},{10,11... | collective-permute-start | bytes 1671176 | tf_op jit(solution)/shard_map/ppermute | solution.py:17
  70.8 53.8 %collective-permute-start.17 = (bf16[512,1024]{1,0:T(8,128)(2,1)}, bf16[512,1024]{1,0:T(8,128)(2,1)S(1)}, u32[]{:S(2)}, u32[]{:S(2)}) collective-permute-start(bf16[512,1024]{1,0:T(8,128)(2,1)} %get-tuple-element.19.refs_0_), channel_id=1, source_target_pairs={{0,2},{1,3},{2,0},{3,1},{4,6},{5,7},{6,4},{7,5},{8,10},{9,11},{10,... | collective-permute-start | bytes 3145736 | tf_op jit(solution)/shard_map/ppermute | solution.py:17
  72.5 31.1 %copy-start = (bf16[2,512,1024]{2,1,0:T(8,128)(2,1)S(1)}, bf16[2,512,1024]{2,1,0:T(8,128)(2,1)}, u32[]{:S(2)}) copy-start(bf16[2,512,1024]{2,1,0:T(8,128)(2,1)} %shard_map.112.refs_8_) | copy-start | bytes 6291460
  72.5 45.2 %copy-start.4 = (bf16[512,1024]{1,0:T(8,128)(2,1)S(1)}, bf16[512,1024]{1,0:T(8,128)(2,1)}, u32[]{:S(2)}) copy-start(bf16[512,1024]{1,0:T(8,128)(2,1)} %get-tuple-element.19.refs_0_) | copy-start | bytes 3145732
  72.5 2.0 %collective-permute-start.9 = (bf16[128,2176]{1,0:T(8,128)(2,1)S(1)}, bf16[128,2176]{1,0:T(8,128)(2,1)S(1)}, u32[]{:S(2)}, u32[]{:S(2)}) collective-permute-start(bf16[128,2176]{1,0:T(8,128)(2,1)S(1)} %shard_map.114.refs_1_), channel_id=1, source_target_pairs={{0,1},{1,0},{2,3},{3,2},{4,5},{5,4},{6,7},{7,6},{8,9},{9,8},{10,11... | collective-permute-start | bytes 1671176 | tf_op jit(solution)/shard_map/ppermute | solution.py:17
  72.6 2.7 %collective-permute-start.8 = (bf16[128,2176]{1,0:T(8,128)(2,1)S(1)}, bf16[128,2176]{1,0:T(8,128)(2,1)S(1)}, u32[]{:S(2)}, u32[]{:S(2)}) collective-permute-start(bf16[128,2176]{1,0:T(8,128)(2,1)S(1)} %shard_map.113.refs_0_), channel_id=1, source_target_pairs={{0,1},{1,0},{2,3},{3,2},{4,5},{5,4},{6,7},{7,6},{8,9},{9,8},{10,11... | collective-permute-start | bytes 1671176 | tf_op jit(solution)/shard_map/ppermute | solution.py:17
  121.4 6.6 %collective-permute-start.15 = (bf16[512,1024]{1,0:T(8,128)(2,1)S(1)}, bf16[512,1024]{1,0:T(8,128)(2,1)S(1)}, u32[]{:S(2)}, u32[]{:S(2)}) collective-permute-start(bf16[512,1024]{1,0:T(8,128)(2,1)S(1)} %get-tuple-element.22.refs_1_), channel_id=1, source_target_pairs={{0,1},{1,0},{2,3},{3,2},{4,5},{5,4},{6,7},{7,6},{8,9},{9,8},{10,11... | collective-permute-start | bytes 3145736 | tf_op jit(solution)/shard_map/ppermute | solution.py:17
  125.9 2.0 %collective-permute-start.18 = (bf16[512,512]{1,0:T(8,128)(2,1)S(1)}, bf16[512,512]{1,0:T(8,128)(2,1)S(1)}, u32[]{:S(2)}, u32[]{:S(2)}) collective-permute-start(bf16[512,512]{1,0:T(8,128)(2,1)S(1)} %get-tuple-element.24.refs_1_), channel_id=1, source_target_pairs={{0,1},{1,0},{2,3},{3,2},{4,5},{5,4},{6,7},{7,6},{8,9},{9,8},{10,11... | collective-permute-start | bytes 1572872 | tf_op jit(solution)/shard_map/ppermute | solution.py:17
  126.0 28.4 %collective-permute-start.22 = (bf16[512,1024]{1,0:T(8,128)(2,1)}, bf16[512,1024]{1,0:T(8,128)(2,1)S(1)}, u32[]{:S(2)}, u32[]{:S(2)}) collective-permute-start(bf16[512,1024]{1,0:T(8,128)(2,1)} %get-tuple-element.20.refs_1_), channel_id=1, source_target_pairs={{0,2},{1,3},{2,0},{3,1},{4,6},{5,7},{6,4},{7,5},{8,10},{9,11},{10,... | collective-permute-start | bytes 3145736 | tf_op jit(solution)/shard_map/ppermute | solution.py:17
  129.9 23.1 %collective-permute-start.16 = (bf16[4,64,1024]{2,1,0:T(8,128)(2,1)S(1)}, bf16[4,64,1024]{2,1,0:T(8,128)(2,1)S(1)}, u32[]{:S(2)}, u32[]{:S(2)}) collective-permute-start(bf16[4,64,1024]{2,1,0:T(8,128)(2,1)S(1)} %fusion.4), channel_id=1, source_target_pairs={{0,4},{4,0},{8,12},{12,8},{16,20},{20,16},{24,28},{28,24},{1,5},{5... | collective-permute-start | bytes 1572872 | tf_op jit(solution)/shard_map/ppermute | solution.py:17
  131.7 21.2 %collective-permute-start.19 = (bf16[4,64,512]{2,1,0:T(8,128)(2,1)S(1)}, bf16[4,64,512]{2,1,0:T(8,128)(2,1)S(1)}, u32[]{:S(2)}, u32[]{:S(2)}) collective-permute-start(bf16[4,64,512]{2,1,0:T(8,128)(2,1)S(1)} %fusion.8), channel_id=1, source_target_pairs={{0,4},{4,0},{8,12},{12,8},{16,20},{20,16},{24,28},{28,24},{1,5},{5... | collective-permute-start | bytes 786440 | tf_op jit(solution)/shard_map/ppermute | solution.py:17
  155.7 2.0 %collective-permute-start.24 = (bf16[512,512]{1,0:T(8,128)(2,1)S(1)}, bf16[512,512]{1,0:T(8,128)(2,1)S(1)}, u32[]{:S(2)}, u32[]{:S(2)}) collective-permute-start(bf16[512,512]{1,0:T(8,128)(2,1)S(1)} %get-tuple-element.27), channel_id=1, source_target_pairs={{0,1},{1,0},{2,3},{3,2},{4,5},{5,4},{6,7},{7,6},{8,9},{9,8},{10,11... | collective-permute-start | bytes 1572872 | tf_op jit(solution)/shard_map/ppermute | solution.py:17
  157.8 8.4 %collective-permute-start.25 = (bf16[4,64,512]{2,1,0:T(8,128)(2,1)S(1)}, bf16[4,64,512]{2,1,0:T(8,128)(2,1)S(1)}, u32[]{:S(2)}, u32[]{:S(2)}) collective-permute-start(bf16[4,64,512]{2,1,0:T(8,128)(2,1)S(1)} %fusion.9), channel_id=1, source_target_pairs={{0,4},{4,0},{8,12},{12,8},{16,20},{20,16},{24,28},{28,24},{1,5},{5... | collective-permute-start | bytes 786440 | tf_op jit(solution)/shard_map/ppermute | solution.py:17
  158.0 23.2 %collective-permute-start.20 = (bf16[2,64,1536]{2,1,0:T(8,128)(2,1)S(1)}, bf16[2,64,1536]{2,1,0:T(8,128)(2,1)S(1)}, u32[]{:S(2)}, u32[]{:S(2)}) collective-permute-start(bf16[2,64,1536]{2,1,0:T(8,128)(2,1)S(1)} %fusion.3), channel_id=1, source_target_pairs={{0,16},{4,20},{8,24},{12,28},{16,0},{20,4},{24,8},{28,12},{1,17},{... | collective-permute-start | bytes 1179656 | tf_op jit(solution)/shard_map/ppermute | solution.py:17
  166.4 17.6 %collective-permute-start.26 = (bf16[2,64,512]{2,1,0:T(8,128)(2,1)S(1)}, bf16[2,64,512]{2,1,0:T(8,128)(2,1)S(1)}, u32[]{:S(2)}, u32[]{:S(2)}) collective-permute-start(bf16[2,64,512]{2,1,0:T(8,128)(2,1)S(1)} %slice.100), channel_id=1, source_target_pairs={{0,16},{4,20},{8,24},{12,28},{16,0},{20,4},{24,8},{28,12},{1,17},{... | collective-permute-start | bytes 393224 | tf_op jit(solution)/shard_map/ppermute | solution.py:17
  181.3 7.5 %collective-permute-start.21 = (bf16[1,64,1536]{2,1,0:T(8,128)(2,1)S(1)}, bf16[1,64,1536]{2,1,0:T(8,128)(2,1)S(1)}, u32[]{:S(2)}, u32[]{:S(2)}) collective-permute-start(bf16[1,64,1536]{2,1,0:T(8,128)(2,1)S(1)} %slice.99), channel_id=1, source_target_pairs={{0,8},{4,12},{8,0},{12,4},{16,24},{20,28},{24,16},{28,20},{1,9},{5... | collective-permute-start | bytes 589832 | tf_op jit(solution)/shard_map/ppermute | solution.py:17
  184.0 5.6 %collective-permute-start.27 = (bf16[1,64,512]{2,1,0:T(8,128)(2,1)S(1)}, bf16[1,64,512]{2,1,0:T(8,128)(2,1)S(1)}, u32[]{:S(2)}, u32[]{:S(2)}) collective-permute-start(bf16[1,64,512]{2,1,0:T(8,128)(2,1)S(1)} %slice.101), channel_id=1, source_target_pairs={{0,8},{4,12},{8,0},{12,4},{16,24},{20,28},{24,16},{28,20},{1,9},{5... | collective-permute-start | bytes 196616 | tf_op jit(solution)/shard_map/ppermute | solution.py:17
  (13 other events, 72.4 us)

commit v12 on v11

--- a/solution.py
+++ b/solution.py
@@ -313,7 +313,9 @@
 
     own = first(tokens, router_probs, expert_ids, old_place)
     columns = [own] + [flip_z(own, j) for j in range(1, n_z)]
-    across = [swap(c, "dp", 1) for c in columns]
+    across = [swap(own, "dp", 1)]
+    for c in columns[1:]:
+        across.append(swap(joined(c, across[-1]), "dp", 1))
     near = [joined(jnp.concatenate(p, axis=0), weights[2]) for p in zip(columns, across)]
     far = [swap(p, "shard", 1) for p in near]
 

time: 191 us -> 190 us (level)
  starting transfers between devices: 23.2 us -> 34.1 us
  waiting for transfers between devices: 115 us -> 108 us
  other arithmetic: 5.65 us -> 2.33 us
    ppermute x27, starting transfers between devices: 21.6 us -> 32.7 us  [swap(): lax.ppermute(x, axis, [(i, i ^ bit) for i in range(lax.axis_size(axis))])]
    ppermute x1, waiting for transfers between devices: 4.13 us -> 0.01 us  [passed_along(): return lax.ppermute(x, axis, [(i, (i + by) % size) for i in range(size)])]
    ppermute x27, waiting for transfers between devices: 111 us -> 108 us  [swap(): lax.ppermute(x, axis, [(i, i ^ bit) for i in range(lax.axis_size(axis))])]
    unnamed x34 -> x33, local copies, waits for them, and re-layouts: 5.43 us -> 3.12 us
    concatenate x4, other arithmetic: 3.2 us -> 1.12 us  [local(): jnp.concatenate(p, axis=0)]
  transfers between devices with their start and end apart: 28 -> 28, of which waited for: 18 -> 20; matrix products, arithmetic and copies ran while one was open for 3% -> 2% of each run, Pallas kernels for 18% -> 18%
where the time goes in v12:
time: 190 us; the launch traced here: 189 us
  waiting for transfers between devices  108 us (57%)
  Pallas kernels  39.4 us (21%)
  starting transfers between devices  34.1 us (18%)
  local copies, waits for them, and re-layouts  4.02 us (2%)
  other arithmetic  2.33 us (1%)
    ppermute x27, waiting for transfers between devices, swap(): lax.ppermute(x, axis, [(i, i ^ bit) for i in range(lax.axis_size(axis))])  108 us
    ppermute x27, starting transfers between devices, swap(): lax.ppermute(x, axis, [(i, i ^ bit) for i in range(lax.axis_size(axis))])  32.7 us
    pallas_call x4, Pallas kernels, copies(): pl.pallas_call(functools.partial(copy_kernel, plan, len(ins), len(counts)...  16.6 us
    pallas_call x1, Pallas kernels, hidden_of(): pl.pallas_call(functools.partial(hidden_kernel, len(pieces)), grid=(ff //...  12.3 us
    pallas_call x3, Pallas kernels, down_of(): pl.pallas_call(functools.partial(down_kernel, len(downs)), in_specs=[vmem...  6.16 us
  transfers between devices with their start and end apart: 28, of which 20 were waited for; matrix products, arithmetic and copies ran while one was open for 2% of the time, Pallas kernels for 18%

profile of v12, /device:TPU:0, one launch (start us, length us, event | category | flops | bytes accessed | tf_op | source)
XLA Modules:
  0.0 189.3 jit_solution(5841767283128955891)
XLA Ops:
  0.6 3.6 %shard_map.120 = (bf16[2,512,1024]{2,1,0:T(8,128)(2,1)}, bf16[1,512,1024]{2,1,0:T(8,128)(2,1)}) custom-call(s32[16]{0:T(128)} %refs_0_.7, s32[16]{0:T(128)} %refs_1_.7, bf16[2,512,1024]{2,1,0:T(8,128)(2,1)} %refs_3_.7, bf16[2,512,1024]{2,1,0:T(8,128)(2,1)} %refs_4_.5, bf16[2,512,1024]{2,1,0:T(8,128)(2,1)} %refs_5_.1), custom_call_target="tpu_custom_call" | custom-call | tf_op jit(solution)/shard_map/pallas_call | solution.py:102
  4.8 3.3 %shard_map.112.refs_8_ = bf16[2,512,1024]{2,1,0:T(8,128)(2,1)} custom-call(s32[16]{0:T(128)} %refs_0_.7, s32[16]{0:T(128)} %refs_1_.7, bf16[2,512,1024]{2,1,0:T(8,128)(2,1)} %refs_3_.7, bf16[2,512,1024]{2,1,0:T(8,128)(2,1)} %refs_4_.5), custom_call_target="tpu_custom_call" | custom-call | tf_op jit(solution)/shard_map/pallas_call | solution.py:102
  8.1 2.6 %collective-permute-start.1 = (bf16[2,512,1024]{2,1,0:T(8,128)(2,1)}, bf16[2,512,1024]{2,1,0:T(8,128)(2,1)S(1)}, u32[]{:S(2)}, u32[]{:S(2)}) collective-permute-start(bf16[2,512,1024]{2,1,0:T(8,128)(2,1)} %shard_map.112.refs_8_), channel_id=1, source_target_pairs={{0,2},{1,3},{2,0},{3,1},{4,6},{5,7},{6,4},{7,5},{8,10},{9,11},{10,... | collective-permute-start | bytes 6291464 | tf_op jit(solution)/shard_map/ppermute | solution.py:17
  11.4 1.6 collective-permute-start.2
  14.5 2.6 %collective-permute-start.4 = (bf16[64,2176]{1,0:T(8,128)(2,1)S(1)}, bf16[64,2176]{1,0:T(8,128)(2,1)S(1)}, u32[]{:S(2)}, u32[]{:S(2)}) collective-permute-start(bf16[64,2176]{1,0:T(8,128)(2,1)S(1)} %shard_map.111), channel_id=1, source_target_pairs={{0,16},{4,20},{8,24},{12,28},{16,0},{20,4},{24,8},{28,12},{1,17},{... | collective-permute-start | bytes 835592 | tf_op jit(solution)/shard_map/ppermute | solution.py:17
  17.1 7.8 %collective-permute-done.2 = bf16[64,2176]{1,0:T(8,128)(2,1)S(1)} collective-permute-done((bf16[64,2176]{1,0:T(8,128)(2,1)S(1)}, bf16[64,2176]{1,0:T(8,128)(2,1)S(1)}, u32[]{:S(2)}, u32[]{:S(2)}) %collective-permute-start.2) | collective-permute-done | bytes 278560 | tf_op jit(solution)/shard_map/ppermute | solution.py:17
  24.9 2.5 %collective-permute-start.3 = (bf16[64,2176]{1,0:T(8,128)(2,1)S(1)}, bf16[64,2176]{1,0:T(8,128)(2,1)S(1)}, u32[]{:S(2)}, u32[]{:S(2)}) collective-permute-start(bf16[64,2176]{1,0:T(8,128)(2,1)S(1)} %shard_map.114), channel_id=1, source_target_pairs={{0,4},{4,0},{8,12},{12,8},{16,20},{20,16},{24,28},{28,24},{1,5},{5... | collective-permute-start | bytes 835592 | tf_op jit(solution)/shard_map/ppermute | solution.py:17
  27.4 2.5 %collective-permute-start.6 = (bf16[64,2176]{1,0:T(8,128)(2,1)S(1)}, bf16[64,2176]{1,0:T(8,128)(2,1)S(1)}, u32[]{:S(2)}, u32[]{:S(2)}) collective-permute-start(bf16[64,2176]{1,0:T(8,128)(2,1)S(1)} %shard_map.111), channel_id=1, source_target_pairs={{0,24},{4,28},{8,16},{12,20},{16,8},{20,12},{24,0},{28,4},{1,25},{... | collective-permute-start | bytes 835592 | tf_op jit(solution)/shard_map/ppermute | solution.py:17
  31.0 2.7 %collective-permute-done.3.refs_1_.refs_6_ = bf16[64,2176]{1,0:T(8,128)(2,1)S(1)} collective-permute-done((bf16[64,2176]{1,0:T(8,128)(2,1)S(1)}, bf16[64,2176]{1,0:T(8,128)(2,1)S(1)}, u32[]{:S(2)}, u32[]{:S(2)}) %collective-permute-start.3) | collective-permute-done | bytes 278560 | tf_op jit(solution)/shard_map/ppermute | solution.py:17
  33.6 1.7 collective-permute-start.5
  37.0 4.0 %collective-permute-done.5.refs_1_.refs_7_ = bf16[64,2176]{1,0:T(8,128)(2,1)S(1)} collective-permute-done((bf16[64,2176]{1,0:T(8,128)(2,1)S(1)}, bf16[64,2176]{1,0:T(8,128)(2,1)S(1)}, u32[]{:S(2)}, u32[]{:S(2)}) %collective-permute-start.5) | collective-permute-done | bytes 278560 | tf_op jit(solution)/shard_map/ppermute | solution.py:17
  42.5 5.1 %collective-permute-done.7.refs_8_ = bf16[64,2176]{1,0:T(8,128)(2,1)S(1)} collective-permute-done((bf16[64,2176]{1,0:T(8,128)(2,1)S(1)}, bf16[64,2176]{1,0:T(8,128)(2,1)S(1)}, u32[]{:S(2)}, u32[]{:S(2)}) %collective-permute-start.7) | collective-permute-done | bytes 278560 | tf_op jit(solution)/shard_map/ppermute | solution.py:17
  48.2 3.6 %shard_map.125 = bf16[3,512,1024]{2,1,0:T(8,128)(2,1)} custom-call(s32[16]{0:T(128)} %refs_0_.7, s32[16]{0:T(128)} %refs_1_.7, bf16[2,512,1024]{2,1,0:T(8,128)(2,1)} %refs_3_.7, bf16[2,512,1024]{2,1,0:T(8,128)(2,1)} %refs_4_.5, bf16[2,512,1024]{2,1,0:T(8,128)(2,1)} %refs_5_.1, bf16[64,2176]{1,0:T(8,128)(2,1)} %copy-done.1, bf16[64,2176]{1,0:T(8,128)(2,1)} %copy-done.3, ...), custom_call_target="tpu_custom_call" | custom-call | tf_op jit(solution)/shard_map/pallas_call | solution.py:102
  54.3 3.0 %collective-permute-done.1.refs_1_.refs_10_ = bf16[2,512,1024]{2,1,0:T(8,128)(2,1)S(1)} collective-permute-done((bf16[2,512,1024]{2,1,0:T(8,128)(2,1)}, bf16[2,512,1024]{2,1,0:T(8,128)(2,1)S(1)}, u32[]{:S(2)}, u32[]{:S(2)}) %collective-permute-start.1) | collective-permute-done | bytes 2097184 | tf_op jit(solution)/shard_map/ppermute | solution.py:17
  58.4 2.9 %shard_map.122 = (bf16[512,1024]{1,0:T(8,128)(2,1)}, bf16[512,1024]{1,0:T(8,128)(2,1)}) custom-call(bf16[2,512,1024]{2,1,0:T(8,128)(2,1)} %refs_5_.1, bf16[1,512,1024]{2,1,0:T(8,128)(2,1)} %collective-permute-done.14.other_ref), custom_call_target="tpu_custom_call" | custom-call | tf_op jit(solution)/shard_map/pallas_call | solution.py:141
  61.3 2.0 %collective-permute-start.17 = (bf16[512,1024]{1,0:T(8,128)(2,1)}, bf16[512,1024]{1,0:T(8,128)(2,1)S(1)}, u32[]{:S(2)}, u32[]{:S(2)}) collective-permute-start(bf16[512,1024]{1,0:T(8,128)(2,1)} %get-tuple-element.19.refs_0_), channel_id=1, source_target_pairs={{0,2},{1,3},{2,0},{3,1},{4,6},{5,7},{6,4},{7,5},{8,10},{9,11},{10,... | collective-permute-start | bytes 3145736 | tf_op jit(solution)/shard_map/ppermute | solution.py:17
  67.0 35.4 %collective-permute-done.13.refs_11_ = bf16[2,512,1024]{2,1,0:T(8,128)(2,1)} collective-permute-done((bf16[2,512,1024]{2,1,0:T(8,128)(2,1)S(1)}, bf16[2,512,1024]{2,1,0:T(8,128)(2,1)}, u32[]{:S(2)}, u32[]{:S(2)}) %collective-permute-start.13) | collective-permute-done | bytes 2097184 | tf_op jit(solution)/shard_map/ppermute | solution.py:17
  103.5 12.3 %shard_map.121.hidden_ref = bf16[1024,1024]{1,0:T(8,128)(2,1)S(1)} custom-call(bf16[128,2176]{1,0:T(8,128)(2,1)S(1)} %shard_map.113.refs_0_, bf16[128,2176]{1,0:T(8,128)(2,1)S(1)} %shard_map.115.refs_1_, bf16[128,2176]{1,0:T(8,128)(2,1)S(1)} %shard_map.117.refs_2_, bf16[128,2176]{1,0:T(8,128)(2,1)S(1)} %shard_map.119.refs_3_, ...), custom_call_target="tpu_custom_call" | custom-call | flops 1 | bytes 1 | tf_op jit(solution)/shard_map/pallas_call | solution.py:208
  115.8 3.6 %shard_map.123 = (bf16[512,1024]{1,0:T(8,128)(2,1)S(1)}, bf16[512,1024]{1,0:T(8,128)(2,1)S(1)}) custom-call(bf16[1024,1024]{1,0:T(8,128)(2,1)S(1)} %shard_map.121.hidden_ref, bf16[512,1024]{1,0:T(8,128)(2,1)S(1)} %copy-done.7, bf16[512,1024]{1,0:T(8,128)(2,1)} %get-tuple-element.20.refs_1_), custom_call_target="tpu_custom_call" | custom-call | flops 1 | bytes 1 | tf_op jit(solution)/shard_map/pallas_call | solution.py:245
  119.5 5.1 %collective-permute-done.17.refs_0_ = bf16[512,1024]{1,0:T(8,128)(2,1)S(1)} collective-permute-done((bf16[512,1024]{1,0:T(8,128)(2,1)}, bf16[512,1024]{1,0:T(8,128)(2,1)S(1)}, u32[]{:S(2)}, u32[]{:S(2)}) %collective-permute-start.17) | collective-permute-done | bytes 1048608 | tf_op jit(solution)/shard_map/ppermute | solution.py:17
  126.0 1.8 collective-permute-start.22
  128.5 1.8 collective-permute-start.16
  131.3 6.1 %shard_map.126 = (bf16[2,512,1024]{2,1,0:T(8,128)(2,1)}, bf16[2,512,1024]{2,1,0:T(8,128)(2,1)}, bf16[2,512,1024]{2,1,0:T(8,128)(2,1)}) custom-call(s32[16]{0:T(128)} %refs_0_.7, s32[16]{0:T(128)} %refs_1_.7, bf16[3,512,1024]{2,1,0:T(8,128)(2,1)} %collective-permute-done.23.refs_2_, bf16[2,512,1024]{2,1,0:T(8,128)(2,1)} %refs_3_.7, ...), custom_call_target="tpu_custom_call" | custom-call | tf_op jit(solution)/shard_map/pallas_call | solution.py:102
  137.5 10.7 %collective-permute-done.19 = bf16[4,64,512]{2,1,0:T(8,128)(2,1)S(1)} collective-permute-done((bf16[4,64,512]{2,1,0:T(8,128)(2,1)}, bf16[4,64,512]{2,1,0:T(8,128)(2,1)S(1)}, u32[]{:S(2)}, u32[]{:S(2)}) %collective-permute-start.19) | collective-permute-done | bytes 262176 | tf_op jit(solution)/shard_map/ppermute | solution.py:17
  148.4 3.3 %collective-permute-done.22.refs_0_ = bf16[512,1024]{1,0:T(8,128)(2,1)S(1)} collective-permute-done((bf16[512,1024]{1,0:T(8,128)(2,1)}, bf16[512,1024]{1,0:T(8,128)(2,1)S(1)}, u32[]{:S(2)}, u32[]{:S(2)}) %collective-permute-start.22) | collective-permute-done | bytes 1048608 | tf_op jit(solution)/shard_map/ppermute | solution.py:17
  153.1 1.9 %collective-permute-done.24 = bf16[512,512]{1,0:T(8,128)(2,1)S(1)} collective-permute-done((bf16[512,512]{1,0:T(8,128)(2,1)S(1)}, bf16[512,512]{1,0:T(8,128)(2,1)S(1)}, u32[]{:S(2)}, u32[]{:S(2)}) %collective-permute-start.24) | collective-permute-done | bytes 524320 | tf_op jit(solution)/shard_map/ppermute | solution.py:17
  155.2 1.8 collective-permute-start.25
  157.0 2.7 %collective-permute-start.20 = (bf16[2,64,1536]{2,1,0:T(8,128)(2,1)S(1)}, bf16[2,64,1536]{2,1,0:T(8,128)(2,1)S(1)}, u32[]{:S(2)}, u32[]{:S(2)}) collective-permute-start(bf16[2,64,1536]{2,1,0:T(8,128)(2,1)S(1)} %fusion.3), channel_id=1, source_target_pairs={{0,16},{4,20},{8,24},{12,28},{16,0},{20,4},{24,8},{28,12},{1,17},{... | collective-permute-start | bytes 1179656 | tf_op jit(solution)/shard_map/ppermute | solution.py:17
  159.7 3.9 %collective-permute-done.25 = bf16[4,64,512]{2,1,0:T(8,128)(2,1)S(1)} collective-permute-done((bf16[4,64,512]{2,1,0:T(8,128)(2,1)S(1)}, bf16[4,64,512]{2,1,0:T(8,128)(2,1)S(1)}, u32[]{:S(2)}, u32[]{:S(2)}) %collective-permute-start.25) | collective-permute-done | bytes 262176 | tf_op jit(solution)/shard_map/ppermute | solution.py:17
  163.7 2.9 %collective-permute-start.26 = (bf16[2,64,512]{2,1,0:T(8,128)(2,1)S(1)}, bf16[2,64,512]{2,1,0:T(8,128)(2,1)S(1)}, u32[]{:S(2)}, u32[]{:S(2)}) collective-permute-start(bf16[2,64,512]{2,1,0:T(8,128)(2,1)S(1)} %slice.100), channel_id=1, source_target_pairs={{0,16},{4,20},{8,24},{12,28},{16,0},{20,4},{24,8},{28,12},{1,17},{... | collective-permute-start | bytes 393224 | tf_op jit(solution)/shard_map/ppermute | solution.py:17
  166.6 14.6 %collective-permute-done.20 = bf16[2,64,1536]{2,1,0:T(8,128)(2,1)S(1)} collective-permute-done((bf16[2,64,1536]{2,1,0:T(8,128)(2,1)S(1)}, bf16[2,64,1536]{2,1,0:T(8,128)(2,1)S(1)}, u32[]{:S(2)}, u32[]{:S(2)}) %collective-permute-start.20) | collective-permute-done | bytes 393248 | tf_op jit(solution)/shard_map/ppermute | solution.py:17
  183.7 4.1 %collective-permute-done.21 = bf16[1,64,1536]{2,1,0:T(8,128)(2,1)S(1)} collective-permute-done((bf16[1,64,1536]{2,1,0:T(8,128)(2,1)S(1)}, bf16[1,64,1536]{2,1,0:T(8,128)(2,1)S(1)}, u32[]{:S(2)}, u32[]{:S(2)}) %collective-permute-start.21) | collective-permute-done | bytes 196640 | tf_op jit(solution)/shard_map/ppermute | solution.py:17
  (96 shorter events, 24.8 us)
Async XLA Ops:
  4.3 31.1 %collective-permute-start.12 = (bf16[2,512,1024]{2,1,0:T(8,128)(2,1)}, bf16[2,512,1024]{2,1,0:T(8,128)(2,1)S(1)}, u32[]{:S(2)}, u32[]{:S(2)}) collective-permute-start(bf16[2,512,1024]{2,1,0:T(8,128)(2,1)} %get-tuple-element.17), channel_id=1, source_target_pairs={{0,1},{1,0},{2,3},{3,2},{4,5},{5,4},{6,7},{7,6},{8,9},{9,8},{10,11... | collective-permute-start | bytes 6291464 | tf_op jit(solution)/shard_map/ppermute | solution.py:17
  8.1 49.3 %collective-permute-start.1 = (bf16[2,512,1024]{2,1,0:T(8,128)(2,1)}, bf16[2,512,1024]{2,1,0:T(8,128)(2,1)S(1)}, u32[]{:S(2)}, u32[]{:S(2)}) collective-permute-start(bf16[2,512,1024]{2,1,0:T(8,128)(2,1)} %shard_map.112.refs_8_), channel_id=1, source_target_pairs={{0,2},{1,3},{2,0},{3,1},{4,6},{5,7},{6,4},{7,5},{8,10},{9,11},{10,... | collective-permute-start | bytes 6291464 | tf_op jit(solution)/shard_map/ppermute | solution.py:17
  11.4 13.5 %collective-permute-start.2 = (bf16[64,2176]{1,0:T(8,128)(2,1)S(1)}, bf16[64,2176]{1,0:T(8,128)(2,1)S(1)}, u32[]{:S(2)}, u32[]{:S(2)}) collective-permute-start(bf16[64,2176]{1,0:T(8,128)(2,1)S(1)} %shard_map.111), channel_id=1, source_target_pairs={{0,8},{4,12},{8,0},{12,4},{16,24},{20,28},{24,16},{28,20},{1,9},{5... | collective-permute-start | bytes 835592 | tf_op jit(solution)/shard_map/ppermute | solution.py:17
  13.0 11.9 %collective-permute-start = (bf16[64,2176]{1,0:T(8,128)(2,1)S(1)}, bf16[64,2176]{1,0:T(8,128)(2,1)S(1)}, u32[]{:S(2)}, u32[]{:S(2)}) collective-permute-start(bf16[64,2176]{1,0:T(8,128)(2,1)S(1)} %shard_map.111), channel_id=1, source_target_pairs={{0,4},{4,0},{8,12},{12,8},{16,20},{20,16},{24,28},{28,24},{1,5},{5... | collective-permute-start | bytes 835592 | tf_op jit(solution)/shard_map/ppermute | solution.py:17
  14.5 16.5 %collective-permute-start.4 = (bf16[64,2176]{1,0:T(8,128)(2,1)S(1)}, bf16[64,2176]{1,0:T(8,128)(2,1)S(1)}, u32[]{:S(2)}, u32[]{:S(2)}) collective-permute-start(bf16[64,2176]{1,0:T(8,128)(2,1)S(1)} %shard_map.111), channel_id=1, source_target_pairs={{0,16},{4,20},{8,24},{12,28},{16,0},{20,4},{24,8},{28,12},{1,17},{... | collective-permute-start | bytes 835592 | tf_op jit(solution)/shard_map/ppermute | solution.py:17
  24.9 17.6 %copy-start.1 = (bf16[64,2176]{1,0:T(8,128)(2,1)}, bf16[64,2176]{1,0:T(8,128)(2,1)S(1)}, u32[]{:S(2)}) copy-start(bf16[64,2176]{1,0:T(8,128)(2,1)S(1)} %collective-permute-done.refs_1_.refs_5_) | copy-start | bytes 835588
  24.9 8.7 %collective-permute-start.3 = (bf16[64,2176]{1,0:T(8,128)(2,1)S(1)}, bf16[64,2176]{1,0:T(8,128)(2,1)S(1)}, u32[]{:S(2)}, u32[]{:S(2)}) collective-permute-start(bf16[64,2176]{1,0:T(8,128)(2,1)S(1)} %shard_map.114), channel_id=1, source_target_pairs={{0,4},{4,0},{8,12},{12,8},{16,20},{20,16},{24,28},{28,24},{1,5},{5... | collective-permute-start | bytes 835592 | tf_op jit(solution)/shard_map/ppermute | solution.py:17
  27.4 9.6 %collective-permute-start.6 = (bf16[64,2176]{1,0:T(8,128)(2,1)S(1)}, bf16[64,2176]{1,0:T(8,128)(2,1)S(1)}, u32[]{:S(2)}, u32[]{:S(2)}) collective-permute-start(bf16[64,2176]{1,0:T(8,128)(2,1)S(1)} %shard_map.111), channel_id=1, source_target_pairs={{0,24},{4,28},{8,16},{12,20},{16,8},{20,12},{24,0},{28,4},{1,25},{... | collective-permute-start | bytes 835592 | tf_op jit(solution)/shard_map/ppermute | solution.py:17
  33.6 7.3 %collective-permute-start.5 = (bf16[64,2176]{1,0:T(8,128)(2,1)S(1)}, bf16[64,2176]{1,0:T(8,128)(2,1)S(1)}, u32[]{:S(2)}, u32[]{:S(2)}) collective-permute-start(bf16[64,2176]{1,0:T(8,128)(2,1)S(1)} %shard_map.116), channel_id=1, source_target_pairs={{0,4},{4,0},{8,12},{12,8},{16,20},{20,16},{24,28},{28,24},{1,5},{5... | collective-permute-start | bytes 835592 | tf_op jit(solution)/shard_map/ppermute | solution.py:17
  35.4 67.0 %collective-permute-start.13 = (bf16[2,512,1024]{2,1,0:T(8,128)(2,1)S(1)}, bf16[2,512,1024]{2,1,0:T(8,128)(2,1)}, u32[]{:S(2)}, u32[]{:S(2)}) collective-permute-start(bf16[2,512,1024]{2,1,0:T(8,128)(2,1)S(1)} %collective-permute-done.12.refs_9_), channel_id=1, source_target_pairs={{0,2},{1,3},{2,0},{3,1},{4,6},{5,7},{6,4},{7,5},{8,10},{9,11},{10,... | collective-permute-start | bytes 6291464 | tf_op jit(solution)/shard_map/ppermute | solution.py:17
  35.9 22.5 %collective-permute-start.14 = (bf16[1,512,1024]{2,1,0:T(8,128)(2,1)}, bf16[1,512,1024]{2,1,0:T(8,128)(2,1)}, u32[]{:S(2)}, u32[]{:S(2)}) collective-permute-start(bf16[1,512,1024]{2,1,0:T(8,128)(2,1)} %get-tuple-element.18), channel_id=1, source_target_pairs={{0,1},{1,0},{2,3},{3,2},{4,5},{5,4},{6,7},{7,6},{8,9},{9,8},{10,11... | collective-permute-start | bytes 3145736 | tf_op jit(solution)/shard_map/ppermute | solution.py:17
  41.0 6.5 %collective-permute-start.7 = (bf16[64,2176]{1,0:T(8,128)(2,1)S(1)}, bf16[64,2176]{1,0:T(8,128)(2,1)S(1)}, u32[]{:S(2)}, u32[]{:S(2)}) collective-permute-start(bf16[64,2176]{1,0:T(8,128)(2,1)S(1)} %shard_map.118), channel_id=1, source_target_pairs={{0,4},{4,0},{8,12},{12,8},{16,20},{20,16},{24,28},{28,24},{1,5},{5... | collective-permute-start | bytes 835592 | tf_op jit(solution)/shard_map/ppermute | solution.py:17
  51.9 79.5 %collective-permute-start.23 = (bf16[3,512,1024]{2,1,0:T(8,128)(2,1)}, bf16[3,512,1024]{2,1,0:T(8,128)(2,1)}, u32[]{:S(2)}, u32[]{:S(2)}) collective-permute-start(bf16[3,512,1024]{2,1,0:T(8,128)(2,1)} %shard_map.125), channel_id=1, source_target_pairs={{0,4},{4,8},{8,12},{12,16},{16,20},{20,24},{24,28},{28,0},{1,5},{5... | collective-permute-start | bytes 9437192 | tf_op jit(solution)/shard_map/ppermute | solution.py:22
  57.4 6.0 %collective-permute-start.11 = (bf16[128,2176]{1,0:T(8,128)(2,1)S(1)}, bf16[128,2176]{1,0:T(8,128)(2,1)S(1)}, u32[]{:S(2)}, u32[]{:S(2)}) collective-permute-start(bf16[128,2176]{1,0:T(8,128)(2,1)S(1)} %shard_map.119.refs_3_), channel_id=1, source_target_pairs={{0,1},{1,0},{2,3},{3,2},{4,5},{5,4},{6,7},{7,6},{8,9},{9,8},{10,11... | collective-permute-start | bytes 1671176 | tf_op jit(solution)/shard_map/ppermute | solution.py:17
  57.4 6.8 %collective-permute-start.10 = (bf16[128,2176]{1,0:T(8,128)(2,1)S(1)}, bf16[128,2176]{1,0:T(8,128)(2,1)}, u32[]{:S(2)}, u32[]{:S(2)}) collective-permute-start(bf16[128,2176]{1,0:T(8,128)(2,1)S(1)} %shard_map.117.refs_2_), channel_id=1, source_target_pairs={{0,1},{1,0},{2,3},{3,2},{4,5},{5,4},{6,7},{7,6},{8,9},{9,8},{10,11... | collective-permute-start | bytes 1671176 | tf_op jit(solution)/shard_map/ppermute | solution.py:17
  61.3 63.3 %collective-permute-start.17 = (bf16[512,1024]{1,0:T(8,128)(2,1)}, bf16[512,1024]{1,0:T(8,128)(2,1)S(1)}, u32[]{:S(2)}, u32[]{:S(2)}) collective-permute-start(bf16[512,1024]{1,0:T(8,128)(2,1)} %get-tuple-element.19.refs_0_), channel_id=1, source_target_pairs={{0,2},{1,3},{2,0},{3,1},{4,6},{5,7},{6,4},{7,5},{8,10},{9,11},{10,... | collective-permute-start | bytes 3145736 | tf_op jit(solution)/shard_map/ppermute | solution.py:17
  63.4 39.1 %copy-start = (bf16[2,512,1024]{2,1,0:T(8,128)(2,1)S(1)}, bf16[2,512,1024]{2,1,0:T(8,128)(2,1)}, u32[]{:S(2)}) copy-start(bf16[2,512,1024]{2,1,0:T(8,128)(2,1)} %shard_map.112.refs_8_) | copy-start | bytes 6291460
  63.4 52.4 %copy-start.7 = (bf16[512,1024]{1,0:T(8,128)(2,1)S(1)}, bf16[512,1024]{1,0:T(8,128)(2,1)}, u32[]{:S(2)}) copy-start(bf16[512,1024]{1,0:T(8,128)(2,1)} %get-tuple-element.19.refs_0_) | copy-start | bytes 3145732
  64.2 2.0 %collective-permute-start.9 = (bf16[128,2176]{1,0:T(8,128)(2,1)S(1)}, bf16[128,2176]{1,0:T(8,128)(2,1)S(1)}, u32[]{:S(2)}, u32[]{:S(2)}) collective-permute-start(bf16[128,2176]{1,0:T(8,128)(2,1)S(1)} %shard_map.115.refs_1_), channel_id=1, source_target_pairs={{0,1},{1,0},{2,3},{3,2},{4,5},{5,4},{6,7},{7,6},{8,9},{9,8},{10,11... | collective-permute-start | bytes 1671176 | tf_op jit(solution)/shard_map/ppermute | solution.py:17
  64.2 2.7 %collective-permute-start.8 = (bf16[128,2176]{1,0:T(8,128)(2,1)S(1)}, bf16[128,2176]{1,0:T(8,128)(2,1)S(1)}, u32[]{:S(2)}, u32[]{:S(2)}) collective-permute-start(bf16[128,2176]{1,0:T(8,128)(2,1)S(1)} %shard_map.113.refs_0_), channel_id=1, source_target_pairs={{0,1},{1,0},{2,3},{3,2},{4,5},{5,4},{6,7},{7,6},{8,9},{9,8},{10,11... | collective-permute-start | bytes 1671176 | tf_op jit(solution)/shard_map/ppermute | solution.py:17
  119.4 8.6 %collective-permute-start.15 = (bf16[512,1024]{1,0:T(8,128)(2,1)S(1)}, bf16[512,1024]{1,0:T(8,128)(2,1)S(1)}, u32[]{:S(2)}, u32[]{:S(2)}) collective-permute-start(bf16[512,1024]{1,0:T(8,128)(2,1)S(1)} %get-tuple-element.22.refs_1_), channel_id=1, source_target_pairs={{0,1},{1,0},{2,3},{3,2},{4,5},{5,4},{6,7},{7,6},{8,9},{9,8},{10,11... | collective-permute-start | bytes 3145736 | tf_op jit(solution)/shard_map/ppermute | solution.py:17
  125.9 2.0 %collective-permute-start.18 = (bf16[512,512]{1,0:T(8,128)(2,1)S(1)}, bf16[512,512]{1,0:T(8,128)(2,1)S(1)}, u32[]{:S(2)}, u32[]{:S(2)}) collective-permute-start(bf16[512,512]{1,0:T(8,128)(2,1)S(1)} %get-tuple-element.24.refs_1_), channel_id=1, source_target_pairs={{0,1},{1,0},{2,3},{3,2},{4,5},{5,4},{6,7},{7,6},{8,9},{9,8},{10,11... | collective-permute-start | bytes 1572872 | tf_op jit(solution)/shard_map/ppermute | solution.py:17
  126.0 25.8 %collective-permute-start.22 = (bf16[512,1024]{1,0:T(8,128)(2,1)}, bf16[512,1024]{1,0:T(8,128)(2,1)S(1)}, u32[]{:S(2)}, u32[]{:S(2)}) collective-permute-start(bf16[512,1024]{1,0:T(8,128)(2,1)} %get-tuple-element.20.refs_1_), channel_id=1, source_target_pairs={{0,2},{1,3},{2,0},{3,1},{4,6},{5,7},{6,4},{7,5},{8,10},{9,11},{10,... | collective-permute-start | bytes 3145736 | tf_op jit(solution)/shard_map/ppermute | solution.py:17
  128.5 19.7 %collective-permute-start.16 = (bf16[4,64,1024]{2,1,0:T(8,128)(2,1)S(1)}, bf16[4,64,1024]{2,1,0:T(8,128)(2,1)S(1)}, u32[]{:S(2)}, u32[]{:S(2)}) collective-permute-start(bf16[4,64,1024]{2,1,0:T(8,128)(2,1)S(1)} %fusion.4), channel_id=1, source_target_pairs={{0,4},{4,0},{8,12},{12,8},{16,20},{20,16},{24,28},{28,24},{1,5},{5... | collective-permute-start | bytes 1572872 | tf_op jit(solution)/shard_map/ppermute | solution.py:17
  131.0 17.1 %collective-permute-start.19 = (bf16[4,64,512]{2,1,0:T(8,128)(2,1)}, bf16[4,64,512]{2,1,0:T(8,128)(2,1)S(1)}, u32[]{:S(2)}, u32[]{:S(2)}) collective-permute-start(bf16[4,64,512]{2,1,0:T(8,128)(2,1)} %fusion.8), channel_id=1, source_target_pairs={{0,4},{4,0},{8,12},{12,8},{16,20},{20,16},{24,28},{28,24},{1,5},{5... | collective-permute-start | bytes 786440 | tf_op jit(solution)/shard_map/ppermute | solution.py:17
  137.5 14.3 %copy-start.6 = (bf16[2,512,1024]{2,1,0:T(8,128)(2,1)S(1)}, bf16[2,512,1024]{2,1,0:T(8,128)(2,1)}, u32[]{:S(2)}) copy-start(bf16[2,512,1024]{2,1,0:T(8,128)(2,1)} %get-tuple-element.14.refs_2_) | copy-start | bytes 6291460
  153.0 2.0 %collective-permute-start.24 = (bf16[512,512]{1,0:T(8,128)(2,1)S(1)}, bf16[512,512]{1,0:T(8,128)(2,1)S(1)}, u32[]{:S(2)}, u32[]{:S(2)}) collective-permute-start(bf16[512,512]{1,0:T(8,128)(2,1)S(1)} %get-tuple-element.27), channel_id=1, source_target_pairs={{0,1},{1,0},{2,3},{3,2},{4,5},{5,4},{6,7},{7,6},{8,9},{9,8},{10,11... | collective-permute-start | bytes 1572872 | tf_op jit(solution)/shard_map/ppermute | solution.py:17
  155.2 8.4 %collective-permute-start.25 = (bf16[4,64,512]{2,1,0:T(8,128)(2,1)S(1)}, bf16[4,64,512]{2,1,0:T(8,128)(2,1)S(1)}, u32[]{:S(2)}, u32[]{:S(2)}) collective-permute-start(bf16[4,64,512]{2,1,0:T(8,128)(2,1)S(1)} %fusion.9), channel_id=1, source_target_pairs={{0,4},{4,0},{8,12},{12,8},{16,20},{20,16},{24,28},{28,24},{1,5},{5... | collective-permute-start | bytes 786440 | tf_op jit(solution)/shard_map/ppermute | solution.py:17
  157.0 24.2 %collective-permute-start.20 = (bf16[2,64,1536]{2,1,0:T(8,128)(2,1)S(1)}, bf16[2,64,1536]{2,1,0:T(8,128)(2,1)S(1)}, u32[]{:S(2)}, u32[]{:S(2)}) collective-permute-start(bf16[2,64,1536]{2,1,0:T(8,128)(2,1)S(1)} %fusion.3), channel_id=1, source_target_pairs={{0,16},{4,20},{8,24},{12,28},{16,0},{20,4},{24,8},{28,12},{1,17},{... | collective-permute-start | bytes 1179656 | tf_op jit(solution)/shard_map/ppermute | solution.py:17
  163.7 19.3 %collective-permute-start.26 = (bf16[2,64,512]{2,1,0:T(8,128)(2,1)S(1)}, bf16[2,64,512]{2,1,0:T(8,128)(2,1)S(1)}, u32[]{:S(2)}, u32[]{:S(2)}) collective-permute-start(bf16[2,64,512]{2,1,0:T(8,128)(2,1)S(1)} %slice.100), channel_id=1, source_target_pairs={{0,16},{4,20},{8,24},{12,28},{16,0},{20,4},{24,8},{28,12},{1,17},{... | collective-permute-start | bytes 393224 | tf_op jit(solution)/shard_map/ppermute | solution.py:17
  181.3 6.5 %collective-permute-start.21 = (bf16[1,64,1536]{2,1,0:T(8,128)(2,1)S(1)}, bf16[1,64,1536]{2,1,0:T(8,128)(2,1)S(1)}, u32[]{:S(2)}, u32[]{:S(2)}) collective-permute-start(bf16[1,64,1536]{2,1,0:T(8,128)(2,1)S(1)} %slice.99), channel_id=1, source_target_pairs={{0,8},{4,12},{8,0},{12,4},{16,24},{20,28},{24,16},{28,20},{1,9},{5... | collective-permute-start | bytes 589832 | tf_op jit(solution)/shard_map/ppermute | solution.py:17
  183.1 5.5 %collective-permute-start.27 = (bf16[1,64,512]{2,1,0:T(8,128)(2,1)S(1)}, bf16[1,64,512]{2,1,0:T(8,128)(2,1)S(1)}, u32[]{:S(2)}, u32[]{:S(2)}) collective-permute-start(bf16[1,64,512]{2,1,0:T(8,128)(2,1)S(1)} %slice.101), channel_id=1, source_target_pairs={{0,8},{4,12},{8,0},{12,4},{16,24},{20,28},{24,16},{28,20},{1,9},{5... | collective-permute-start | bytes 196616 | tf_op jit(solution)/shard_map/ppermute | solution.py:17
  (11 other events, 55.6 us)

commit v13 on v12

--- a/solution.py
+++ b/solution.py
@@ -263,10 +263,12 @@
 
 
 def over_z(total):
+    bit = 1
     while total.shape[0] > 1:
-        half = total.shape[0] // 2
-        given = flip_z(total[half:].astype(jnp.bfloat16), half)
-        total = total[:half] + given.astype(jnp.float32)
+        pairs = total.reshape((-1, 2) + total.shape[1:])
+        given = flip_z(pairs[:, 1].astype(jnp.bfloat16), bit)
+        total = pairs[:, 0] + given.astype(jnp.float32)
+        bit *= 2
     return total[0].astype(jnp.bfloat16)
 
 
@@ -302,10 +304,10 @@
     n_z = lax.axis_size("dp") // 2
     places = (old_place, new_place)
 
-    (mine,) = copies(((0, "mine", 0, 0), (1, "mine", 0, 1)), places, (w_gate, w_up), (2,))
-    theirs, theirs_down = copies(
-        ((0, "theirs", 0, 0), (1, "theirs", 0, 1), (2, "theirs", 1, 0)),
-        places, (w_gate, w_up, w_down), (2, 1),
+    mine, theirs, theirs_down = copies(
+        ((0, "mine", 0, 0), (1, "mine", 0, 1))
+        + ((0, "theirs", 1, 0), (1, "theirs", 1, 1), (2, "theirs", 2, 0)),
+        places, (w_gate, w_up, w_down), (2, 2, 1),
     )
     near_weights = [mine, swap(theirs, "shard", 1)]
     weights = spread(near_weights)

time: 190 us -> 181 us (0.953)
  waiting for transfers between devices: 108 us -> 98.5 us
  starting transfers between devices: 34.1 us -> 36.5 us
    ppermute x27, waiting for transfers between devices: 108 us -> 98.5 us  [swap(): lax.ppermute(x, axis, [(i, i ^ bit) for i in range(lax.axis_size(axis))])]
    ppermute x27, starting transfers between devices: 32.7 us -> 35 us  [swap(): lax.ppermute(x, axis, [(i, i ^ bit) for i in range(lax.axis_size(axis))])]
    pallas_call x4 -> x3, Pallas kernels: 16.6 us -> 14.9 us  [copies(): pl.pallas_call(functools.partial(copy_kernel, plan, len(ins), len(counts)...]
  transfers between devices with their start and end apart: 28 -> 28, of which waited for: 20 -> 18; matrix products, arithmetic and copies ran while one was open for 2% -> 2% of each run, Pallas kernels for 18% -> 17%
where the time goes in v13:
time: 181 us; the launch traced here: 180 us
  waiting for transfers between devices  98.5 us (54%)
  Pallas kernels  37.7 us (21%)
  starting transfers between devices  36.5 us (20%)
  local copies, waits for them, and re-layouts  4.05 us (2%)
  other arithmetic  2.43 us (1%)
    ppermute x27, waiting for transfers between devices, swap(): lax.ppermute(x, axis, [(i, i ^ bit) for i in range(lax.axis_size(axis))])  98.5 us
    ppermute x27, starting transfers between devices, swap(): lax.ppermute(x, axis, [(i, i ^ bit) for i in range(lax.axis_size(axis))])  35 us
    pallas_call x3, Pallas kernels, copies(): pl.pallas_call(functools.partial(copy_kernel, plan, len(ins), len(counts)...  14.9 us
    pallas_call x1, Pallas kernels, hidden_of(): pl.pallas_call(functools.partial(hidden_kernel, len(pieces)), grid=(ff //...  12.3 us
    pallas_call x3, Pallas kernels, down_of(): pl.pallas_call(functools.partial(down_kernel, len(downs)), in_specs=[vmem...  6.16 us
  transfers between devices with their start and end apart: 28, of which 18 were waited for; matrix products, arithmetic and copies ran while one was open for 2% of the time, Pallas kernels for 17%

profile of v13, /device:TPU:0, one launch (start us, length us, event | category | flops | bytes accessed | tf_op | source)
XLA Modules:
  0.0 180.3 jit_solution(11100574152876610926)
XLA Ops:
  0.7 5.2 %shard_map.112 = (bf16[2,512,1024]{2,1,0:T(8,128)(2,1)}, bf16[2,512,1024]{2,1,0:T(8,128)(2,1)}, bf16[1,512,1024]{2,1,0:T(8,128)(2,1)}) custom-call(s32[16]{0:T(128)} %refs_0_.5, s32[16]{0:T(128)} %refs_1_.5, bf16[2,512,1024]{2,1,0:T(8,128)(2,1)} %refs_3_.5, bf16[2,512,1024]{2,1,0:T(8,128)(2,1)} %refs_4_.5, bf16[2,512,1024]{2,1,0:T(8,128)(2,1)} %refs_5_.1), custom_call_target="tpu_custom_call" | custom-call | tf_op jit(solution)/shard_map/pallas_call | solution.py:102
  6.4 2.6 %collective-permute-start.1 = (bf16[2,512,1024]{2,1,0:T(8,128)(2,1)}, bf16[2,512,1024]{2,1,0:T(8,128)(2,1)S(1)}, u32[]{:S(2)}, u32[]{:S(2)}) collective-permute-start(bf16[2,512,1024]{2,1,0:T(8,128)(2,1)} %get-tuple-element.18.refs_8_), channel_id=1, source_target_pairs={{0,2},{1,3},{2,0},{3,1},{4,6},{5,7},{6,4},{7,5},{8,10},{9,11},{10,... | collective-permute-start | bytes 6291464 | tf_op jit(solution)/shard_map/ppermute | solution.py:17
  9.7 1.6 collective-permute-start.2
  12.8 2.6 %collective-permute-start.4 = (bf16[64,2176]{1,0:T(8,128)(2,1)S(1)}, bf16[64,2176]{1,0:T(8,128)(2,1)S(1)}, u32[]{:S(2)}, u32[]{:S(2)}) collective-permute-start(bf16[64,2176]{1,0:T(8,128)(2,1)S(1)} %shard_map.111), channel_id=1, source_target_pairs={{0,16},{4,20},{8,24},{12,28},{16,0},{20,4},{24,8},{28,12},{1,17},{... | collective-permute-start | bytes 835592 | tf_op jit(solution)/shard_map/ppermute | solution.py:17
  15.4 7.7 %collective-permute-done.2 = bf16[64,2176]{1,0:T(8,128)(2,1)S(1)} collective-permute-done((bf16[64,2176]{1,0:T(8,128)(2,1)S(1)}, bf16[64,2176]{1,0:T(8,128)(2,1)S(1)}, u32[]{:S(2)}, u32[]{:S(2)}) %collective-permute-start.2) | collective-permute-done | bytes 278560 | tf_op jit(solution)/shard_map/ppermute | solution.py:17
  23.2 2.5 %collective-permute-start.3 = (bf16[64,2176]{1,0:T(8,128)(2,1)S(1)}, bf16[64,2176]{1,0:T(8,128)(2,1)S(1)}, u32[]{:S(2)}, u32[]{:S(2)}) collective-permute-start(bf16[64,2176]{1,0:T(8,128)(2,1)S(1)} %shard_map.114), channel_id=1, source_target_pairs={{0,4},{4,0},{8,12},{12,8},{16,20},{20,16},{24,28},{28,24},{1,5},{5... | collective-permute-start | bytes 835592 | tf_op jit(solution)/shard_map/ppermute | solution.py:17
  25.7 2.5 %collective-permute-start.6 = (bf16[64,2176]{1,0:T(8,128)(2,1)S(1)}, bf16[64,2176]{1,0:T(8,128)(2,1)S(1)}, u32[]{:S(2)}, u32[]{:S(2)}) collective-permute-start(bf16[64,2176]{1,0:T(8,128)(2,1)S(1)} %shard_map.111), channel_id=1, source_target_pairs={{0,24},{4,28},{8,16},{12,20},{16,8},{20,12},{24,0},{28,4},{1,25},{... | collective-permute-start | bytes 835592 | tf_op jit(solution)/shard_map/ppermute | solution.py:17
  29.2 2.6 %collective-permute-done.3.refs_1_.refs_6_ = bf16[64,2176]{1,0:T(8,128)(2,1)S(1)} collective-permute-done((bf16[64,2176]{1,0:T(8,128)(2,1)S(1)}, bf16[64,2176]{1,0:T(8,128)(2,1)S(1)}, u32[]{:S(2)}, u32[]{:S(2)}) %collective-permute-start.3) | collective-permute-done | bytes 278560 | tf_op jit(solution)/shard_map/ppermute | solution.py:17
  31.8 1.7 collective-permute-start.5
  35.2 3.9 %collective-permute-done.5.refs_1_.refs_7_ = bf16[64,2176]{1,0:T(8,128)(2,1)S(1)} collective-permute-done((bf16[64,2176]{1,0:T(8,128)(2,1)S(1)}, bf16[64,2176]{1,0:T(8,128)(2,1)S(1)}, u32[]{:S(2)}, u32[]{:S(2)}) %collective-permute-start.5) | collective-permute-done | bytes 278560 | tf_op jit(solution)/shard_map/ppermute | solution.py:17
  40.6 5.1 %collective-permute-done.7.refs_8_ = bf16[64,2176]{1,0:T(8,128)(2,1)S(1)} collective-permute-done((bf16[64,2176]{1,0:T(8,128)(2,1)S(1)}, bf16[64,2176]{1,0:T(8,128)(2,1)S(1)}, u32[]{:S(2)}, u32[]{:S(2)}) %collective-permute-start.7) | collective-permute-done | bytes 278560 | tf_op jit(solution)/shard_map/ppermute | solution.py:17
  46.4 3.6 %shard_map.124 = bf16[3,512,1024]{2,1,0:T(8,128)(2,1)} custom-call(s32[16]{0:T(128)} %refs_0_.5, s32[16]{0:T(128)} %refs_1_.5, bf16[2,512,1024]{2,1,0:T(8,128)(2,1)} %refs_3_.5, bf16[2,512,1024]{2,1,0:T(8,128)(2,1)} %refs_4_.5, bf16[2,512,1024]{2,1,0:T(8,128)(2,1)} %refs_5_.1, bf16[64,2176]{1,0:T(8,128)(2,1)} %copy-done, bf16[64,2176]{1,0:T(8,128)(2,1)} %copy-done.2, ...), custom_call_target="tpu_custom_call" | custom-call | tf_op jit(solution)/shard_map/pallas_call | solution.py:102
  52.5 3.2 %collective-permute-done.1.refs_1_.refs_10_ = bf16[2,512,1024]{2,1,0:T(8,128)(2,1)S(1)} collective-permute-done((bf16[2,512,1024]{2,1,0:T(8,128)(2,1)}, bf16[2,512,1024]{2,1,0:T(8,128)(2,1)S(1)}, u32[]{:S(2)}, u32[]{:S(2)}) %collective-permute-start.1) | collective-permute-done | bytes 2097184 | tf_op jit(solution)/shard_map/ppermute | solution.py:17
  56.7 2.9 %shard_map.121 = (bf16[512,1024]{1,0:T(8,128)(2,1)}, bf16[512,1024]{1,0:T(8,128)(2,1)}) custom-call(bf16[2,512,1024]{2,1,0:T(8,128)(2,1)} %refs_5_.1, bf16[1,512,1024]{2,1,0:T(8,128)(2,1)} %collective-permute-done.14.other_ref), custom_call_target="tpu_custom_call" | custom-call | tf_op jit(solution)/shard_map/pallas_call | solution.py:141
  59.6 2.0 %collective-permute-start.17 = (bf16[512,1024]{1,0:T(8,128)(2,1)}, bf16[512,1024]{1,0:T(8,128)(2,1)S(1)}, u32[]{:S(2)}, u32[]{:S(2)}) collective-permute-start(bf16[512,1024]{1,0:T(8,128)(2,1)} %get-tuple-element.21.refs_0_), channel_id=1, source_target_pairs={{0,2},{1,3},{2,0},{3,1},{4,6},{5,7},{6,4},{7,5},{8,10},{9,11},{10,... | collective-permute-start | bytes 3145736 | tf_op jit(solution)/shard_map/ppermute | solution.py:17
  65.3 35.4 %collective-permute-done.13.refs_11_ = bf16[2,512,1024]{2,1,0:T(8,128)(2,1)} collective-permute-done((bf16[2,512,1024]{2,1,0:T(8,128)(2,1)S(1)}, bf16[2,512,1024]{2,1,0:T(8,128)(2,1)}, u32[]{:S(2)}, u32[]{:S(2)}) %collective-permute-start.13) | collective-permute-done | bytes 2097184 | tf_op jit(solution)/shard_map/ppermute | solution.py:17
  101.8 12.3 %shard_map.120.hidden_ref = bf16[1024,1024]{1,0:T(8,128)(2,1)S(1)} custom-call(bf16[128,2176]{1,0:T(8,128)(2,1)S(1)} %shard_map.113.refs_0_, bf16[128,2176]{1,0:T(8,128)(2,1)S(1)} %shard_map.115.refs_1_, bf16[128,2176]{1,0:T(8,128)(2,1)S(1)} %shard_map.117.refs_2_, bf16[128,2176]{1,0:T(8,128)(2,1)S(1)} %shard_map.119.refs_3_, ...), custom_call_target="tpu_custom_call" | custom-call | flops 1 | bytes 1 | tf_op jit(solution)/shard_map/pallas_call | solution.py:208
  114.1 3.6 %shard_map.122 = (bf16[512,1024]{1,0:T(8,128)(2,1)S(1)}, bf16[512,1024]{1,0:T(8,128)(2,1)S(1)}) custom-call(bf16[1024,1024]{1,0:T(8,128)(2,1)S(1)} %shard_map.120.hidden_ref, bf16[512,1024]{1,0:T(8,128)(2,1)S(1)} %copy-done.7, bf16[512,1024]{1,0:T(8,128)(2,1)} %get-tuple-element.22.refs_1_), custom_call_target="tpu_custom_call" | custom-call | flops 1 | bytes 1 | tf_op jit(solution)/shard_map/pallas_call | solution.py:245
  117.8 5.0 %collective-permute-done.17.refs_0_ = bf16[512,1024]{1,0:T(8,128)(2,1)S(1)} collective-permute-done((bf16[512,1024]{1,0:T(8,128)(2,1)}, bf16[512,1024]{1,0:T(8,128)(2,1)S(1)}, u32[]{:S(2)}, u32[]{:S(2)}) %collective-permute-start.17) | collective-permute-done | bytes 1048608 | tf_op jit(solution)/shard_map/ppermute | solution.py:17
  124.2 1.8 %collective-permute-start.22 = (bf16[512,1024]{1,0:T(8,128)(2,1)}, bf16[512,1024]{1,0:T(8,128)(2,1)S(1)}, u32[]{:S(2)}, u32[]{:S(2)}) collective-permute-start(bf16[512,1024]{1,0:T(8,128)(2,1)} %get-tuple-element.22.refs_1_), channel_id=1, source_target_pairs={{0,2},{1,3},{2,0},{3,1},{4,6},{5,7},{6,4},{7,5},{8,10},{9,11},{10,... | collective-permute-start | bytes 3145736 | tf_op jit(solution)/shard_map/ppermute | solution.py:17
  126.7 1.8 collective-permute-start.16
  129.6 6.1 %shard_map.125 = (bf16[2,512,1024]{2,1,0:T(8,128)(2,1)}, bf16[2,512,1024]{2,1,0:T(8,128)(2,1)}, bf16[2,512,1024]{2,1,0:T(8,128)(2,1)}) custom-call(s32[16]{0:T(128)} %refs_0_.5, s32[16]{0:T(128)} %refs_1_.5, bf16[3,512,1024]{2,1,0:T(8,128)(2,1)} %collective-permute-done.23.refs_2_, bf16[2,512,1024]{2,1,0:T(8,128)(2,1)} %refs_3_.5, ...), custom_call_target="tpu_custom_call" | custom-call | tf_op jit(solution)/shard_map/pallas_call | solution.py:102
  135.7 10.7 %collective-permute-done.19 = bf16[4,64,512]{2,1,0:T(8,128)(2,1)S(1)} collective-permute-done((bf16[4,64,512]{2,1,0:T(8,128)(2,1)}, bf16[4,64,512]{2,1,0:T(8,128)(2,1)S(1)}, u32[]{:S(2)}, u32[]{:S(2)}) %collective-permute-start.19) | collective-permute-done | bytes 262176 | tf_op jit(solution)/shard_map/ppermute | solution.py:17
  146.7 3.3 %collective-permute-done.22.refs_0_ = bf16[512,1024]{1,0:T(8,128)(2,1)S(1)} collective-permute-done((bf16[512,1024]{1,0:T(8,128)(2,1)}, bf16[512,1024]{1,0:T(8,128)(2,1)S(1)}, u32[]{:S(2)}, u32[]{:S(2)}) %collective-permute-start.22) | collective-permute-done | bytes 1048608 | tf_op jit(solution)/shard_map/ppermute | solution.py:17
  151.5 1.9 %collective-permute-start.20 = (bf16[2,64,1536]{2,1,0:T(8,128)(2,1)S(1)}, bf16[2,64,1536]{2,1,0:T(8,128)(2,1)S(1)}, u32[]{:S(2)}, u32[]{:S(2)}) collective-permute-start(bf16[2,64,1536]{2,1,0:T(8,128)(2,1)S(1)} %fusion.6), channel_id=1, source_target_pairs={{0,8},{4,12},{8,0},{12,4},{16,24},{20,28},{24,16},{28,20},{1,9},{5... | collective-permute-start | bytes 1179656 | tf_op jit(solution)/shard_map/ppermute | solution.py:17
  153.6 1.6 collective-permute-start.25
  155.2 8.0 %collective-permute-done.20 = bf16[2,64,1536]{2,1,0:T(8,128)(2,1)S(1)} collective-permute-done((bf16[2,64,1536]{2,1,0:T(8,128)(2,1)S(1)}, bf16[2,64,1536]{2,1,0:T(8,128)(2,1)S(1)}, u32[]{:S(2)}, u32[]{:S(2)}) %collective-permute-start.20) | collective-permute-done | bytes 393248 | tf_op jit(solution)/shard_map/ppermute | solution.py:17
  163.4 1.8 %collective-permute-start.26 = (bf16[2,64,512]{2,1,0:T(8,128)(2,1)S(1)}, bf16[2,64,512]{2,1,0:T(8,128)(2,1)S(1)}, u32[]{:S(2)}, u32[]{:S(2)}) collective-permute-start(bf16[2,64,512]{2,1,0:T(8,128)(2,1)S(1)} %fusion.15), channel_id=1, source_target_pairs={{0,8},{4,12},{8,0},{12,4},{16,24},{20,28},{24,16},{28,20},{1,9},{5... | collective-permute-start | bytes 393224 | tf_op jit(solution)/shard_map/ppermute | solution.py:17
  165.2 2.7 %collective-permute-start.21 = (bf16[1,64,1536]{2,1,0:T(8,128)(2,1)S(1)}, bf16[1,64,1536]{2,1,0:T(8,128)(2,1)S(1)}, u32[]{:S(2)}, u32[]{:S(2)}) collective-permute-start(bf16[1,64,1536]{2,1,0:T(8,128)(2,1)S(1)} %fusion.14), channel_id=1, source_target_pairs={{0,16},{4,20},{8,24},{12,28},{16,0},{20,4},{24,8},{28,12},{1,17},{... | collective-permute-start | bytes 589832 | tf_op jit(solution)/shard_map/ppermute | solution.py:17
  167.9 2.4 %collective-permute-done.26 = bf16[2,64,512]{2,1,0:T(8,128)(2,1)S(1)} collective-permute-done((bf16[2,64,512]{2,1,0:T(8,128)(2,1)S(1)}, bf16[2,64,512]{2,1,0:T(8,128)(2,1)S(1)}, u32[]{:S(2)}, u32[]{:S(2)}) %collective-permute-start.26) | collective-permute-done | bytes 131104 | tf_op jit(solution)/shard_map/ppermute | solution.py:17
  170.3 2.4 %collective-permute-start.27 = (bf16[1,64,512]{2,1,0:T(8,128)(2,1)S(1)}, bf16[1,64,512]{2,1,0:T(8,128)(2,1)S(1)}, u32[]{:S(2)}, u32[]{:S(2)}) collective-permute-start(bf16[1,64,512]{2,1,0:T(8,128)(2,1)S(1)} %fusion.19), channel_id=1, source_target_pairs={{0,16},{4,20},{8,24},{12,28},{16,0},{20,4},{24,8},{28,12},{1,17},{... | collective-permute-start | bytes 196616 | tf_op jit(solution)/shard_map/ppermute | solution.py:17
  172.7 6.1 %collective-permute-done.21 = bf16[1,64,1536]{2,1,0:T(8,128)(2,1)S(1)} collective-permute-done((bf16[1,64,1536]{2,1,0:T(8,128)(2,1)S(1)}, bf16[1,64,1536]{2,1,0:T(8,128)(2,1)S(1)}, u32[]{:S(2)}, u32[]{:S(2)}) %collective-permute-start.21) | collective-permute-done | bytes 196640 | tf_op jit(solution)/shard_map/ppermute | solution.py:17
  (96 shorter events, 22.5 us)
Async XLA Ops:
  5.9 27.7 %collective-permute-start.12 = (bf16[2,512,1024]{2,1,0:T(8,128)(2,1)}, bf16[2,512,1024]{2,1,0:T(8,128)(2,1)S(1)}, u32[]{:S(2)}, u32[]{:S(2)}) collective-permute-start(bf16[2,512,1024]{2,1,0:T(8,128)(2,1)} %get-tuple-element.19), channel_id=1, source_target_pairs={{0,1},{1,0},{2,3},{3,2},{4,5},{5,4},{6,7},{7,6},{8,9},{9,8},{10,11... | collective-permute-start | bytes 6291464 | tf_op jit(solution)/shard_map/ppermute | solution.py:17
  6.4 49.3 %collective-permute-start.1 = (bf16[2,512,1024]{2,1,0:T(8,128)(2,1)}, bf16[2,512,1024]{2,1,0:T(8,128)(2,1)S(1)}, u32[]{:S(2)}, u32[]{:S(2)}) collective-permute-start(bf16[2,512,1024]{2,1,0:T(8,128)(2,1)} %get-tuple-element.18.refs_8_), channel_id=1, source_target_pairs={{0,2},{1,3},{2,0},{3,1},{4,6},{5,7},{6,4},{7,5},{8,10},{9,11},{10,... | collective-permute-start | bytes 6291464 | tf_op jit(solution)/shard_map/ppermute | solution.py:17
  9.7 13.4 %collective-permute-start.2 = (bf16[64,2176]{1,0:T(8,128)(2,1)S(1)}, bf16[64,2176]{1,0:T(8,128)(2,1)S(1)}, u32[]{:S(2)}, u32[]{:S(2)}) collective-permute-start(bf16[64,2176]{1,0:T(8,128)(2,1)S(1)} %shard_map.111), channel_id=1, source_target_pairs={{0,8},{4,12},{8,0},{12,4},{16,24},{20,28},{24,16},{28,20},{1,9},{5... | collective-permute-start | bytes 835592 | tf_op jit(solution)/shard_map/ppermute | solution.py:17
  11.3 11.8 %collective-permute-start = (bf16[64,2176]{1,0:T(8,128)(2,1)S(1)}, bf16[64,2176]{1,0:T(8,128)(2,1)S(1)}, u32[]{:S(2)}, u32[]{:S(2)}) collective-permute-start(bf16[64,2176]{1,0:T(8,128)(2,1)S(1)} %shard_map.111), channel_id=1, source_target_pairs={{0,4},{4,0},{8,12},{12,8},{16,20},{20,16},{24,28},{28,24},{1,5},{5... | collective-permute-start | bytes 835592 | tf_op jit(solution)/shard_map/ppermute | solution.py:17
  12.8 16.4 %collective-permute-start.4 = (bf16[64,2176]{1,0:T(8,128)(2,1)S(1)}, bf16[64,2176]{1,0:T(8,128)(2,1)S(1)}, u32[]{:S(2)}, u32[]{:S(2)}) collective-permute-start(bf16[64,2176]{1,0:T(8,128)(2,1)S(1)} %shard_map.111), channel_id=1, source_target_pairs={{0,16},{4,20},{8,24},{12,28},{16,0},{20,4},{24,8},{28,12},{1,17},{... | collective-permute-start | bytes 835592 | tf_op jit(solution)/shard_map/ppermute | solution.py:17
  23.1 17.5 %copy-start = (bf16[64,2176]{1,0:T(8,128)(2,1)}, bf16[64,2176]{1,0:T(8,128)(2,1)S(1)}, u32[]{:S(2)}) copy-start(bf16[64,2176]{1,0:T(8,128)(2,1)S(1)} %collective-permute-done.refs_1_.refs_5_) | copy-start | bytes 835588
  23.2 8.7 %collective-permute-start.3 = (bf16[64,2176]{1,0:T(8,128)(2,1)S(1)}, bf16[64,2176]{1,0:T(8,128)(2,1)S(1)}, u32[]{:S(2)}, u32[]{:S(2)}) collective-permute-start(bf16[64,2176]{1,0:T(8,128)(2,1)S(1)} %shard_map.114), channel_id=1, source_target_pairs={{0,4},{4,0},{8,12},{12,8},{16,20},{20,16},{24,28},{28,24},{1,5},{5... | collective-permute-start | bytes 835592 | tf_op jit(solution)/shard_map/ppermute | solution.py:17
  25.7 9.5 %collective-permute-start.6 = (bf16[64,2176]{1,0:T(8,128)(2,1)S(1)}, bf16[64,2176]{1,0:T(8,128)(2,1)S(1)}, u32[]{:S(2)}, u32[]{:S(2)}) collective-permute-start(bf16[64,2176]{1,0:T(8,128)(2,1)S(1)} %shard_map.111), channel_id=1, source_target_pairs={{0,24},{4,28},{8,16},{12,20},{16,8},{20,12},{24,0},{28,4},{1,25},{... | collective-permute-start | bytes 835592 | tf_op jit(solution)/shard_map/ppermute | solution.py:17
  31.8 7.3 %collective-permute-start.5 = (bf16[64,2176]{1,0:T(8,128)(2,1)S(1)}, bf16[64,2176]{1,0:T(8,128)(2,1)S(1)}, u32[]{:S(2)}, u32[]{:S(2)}) collective-permute-start(bf16[64,2176]{1,0:T(8,128)(2,1)S(1)} %shard_map.116), channel_id=1, source_target_pairs={{0,4},{4,0},{8,12},{12,8},{16,20},{20,16},{24,28},{28,24},{1,5},{5... | collective-permute-start | bytes 835592 | tf_op jit(solution)/shard_map/ppermute | solution.py:17
  33.6 67.1 %collective-permute-start.13 = (bf16[2,512,1024]{2,1,0:T(8,128)(2,1)S(1)}, bf16[2,512,1024]{2,1,0:T(8,128)(2,1)}, u32[]{:S(2)}, u32[]{:S(2)}) collective-permute-start(bf16[2,512,1024]{2,1,0:T(8,128)(2,1)S(1)} %collective-permute-done.12.refs_9_), channel_id=1, source_target_pairs={{0,2},{1,3},{2,0},{3,1},{4,6},{5,7},{6,4},{7,5},{8,10},{9,11},{10,... | collective-permute-start | bytes 6291464 | tf_op jit(solution)/shard_map/ppermute | solution.py:17
  34.1 22.6 %collective-permute-start.14 = (bf16[1,512,1024]{2,1,0:T(8,128)(2,1)}, bf16[1,512,1024]{2,1,0:T(8,128)(2,1)}, u32[]{:S(2)}, u32[]{:S(2)}) collective-permute-start(bf16[1,512,1024]{2,1,0:T(8,128)(2,1)} %get-tuple-element.20), channel_id=1, source_target_pairs={{0,1},{1,0},{2,3},{3,2},{4,5},{5,4},{6,7},{7,6},{8,9},{9,8},{10,11... | collective-permute-start | bytes 3145736 | tf_op jit(solution)/shard_map/ppermute | solution.py:17
  39.1 6.5 %collective-permute-start.7 = (bf16[64,2176]{1,0:T(8,128)(2,1)S(1)}, bf16[64,2176]{1,0:T(8,128)(2,1)S(1)}, u32[]{:S(2)}, u32[]{:S(2)}) collective-permute-start(bf16[64,2176]{1,0:T(8,128)(2,1)S(1)} %shard_map.118), channel_id=1, source_target_pairs={{0,4},{4,0},{8,12},{12,8},{16,20},{20,16},{24,28},{28,24},{1,5},{5... | collective-permute-start | bytes 835592 | tf_op jit(solution)/shard_map/ppermute | solution.py:17
  50.0 79.6 %collective-permute-start.23 = (bf16[3,512,1024]{2,1,0:T(8,128)(2,1)}, bf16[3,512,1024]{2,1,0:T(8,128)(2,1)}, u32[]{:S(2)}, u32[]{:S(2)}) collective-permute-start(bf16[3,512,1024]{2,1,0:T(8,128)(2,1)} %shard_map.124), channel_id=1, source_target_pairs={{0,4},{4,8},{8,12},{12,16},{16,20},{20,24},{24,28},{28,0},{1,5},{5... | collective-permute-start | bytes 9437192 | tf_op jit(solution)/shard_map/ppermute | solution.py:22
  55.7 6.0 %collective-permute-start.11 = (bf16[128,2176]{1,0:T(8,128)(2,1)S(1)}, bf16[128,2176]{1,0:T(8,128)(2,1)S(1)}, u32[]{:S(2)}, u32[]{:S(2)}) collective-permute-start(bf16[128,2176]{1,0:T(8,128)(2,1)S(1)} %shard_map.119.refs_3_), channel_id=1, source_target_pairs={{0,1},{1,0},{2,3},{3,2},{4,5},{5,4},{6,7},{7,6},{8,9},{9,8},{10,11... | collective-permute-start | bytes 1671176 | tf_op jit(solution)/shard_map/ppermute | solution.py:17
  55.7 6.8 %collective-permute-start.10 = (bf16[128,2176]{1,0:T(8,128)(2,1)S(1)}, bf16[128,2176]{1,0:T(8,128)(2,1)}, u32[]{:S(2)}, u32[]{:S(2)}) collective-permute-start(bf16[128,2176]{1,0:T(8,128)(2,1)S(1)} %shard_map.117.refs_2_), channel_id=1, source_target_pairs={{0,1},{1,0},{2,3},{3,2},{4,5},{5,4},{6,7},{7,6},{8,9},{9,8},{10,11... | collective-permute-start | bytes 1671176 | tf_op jit(solution)/shard_map/ppermute | solution.py:17
  59.6 63.2 %collective-permute-start.17 = (bf16[512,1024]{1,0:T(8,128)(2,1)}, bf16[512,1024]{1,0:T(8,128)(2,1)S(1)}, u32[]{:S(2)}, u32[]{:S(2)}) collective-permute-start(bf16[512,1024]{1,0:T(8,128)(2,1)} %get-tuple-element.21.refs_0_), channel_id=1, source_target_pairs={{0,2},{1,3},{2,0},{3,1},{4,6},{5,7},{6,4},{7,5},{8,10},{9,11},{10,... | collective-permute-start | bytes 3145736 | tf_op jit(solution)/shard_map/ppermute | solution.py:17
  61.7 39.1 %copy-start.5 = (bf16[2,512,1024]{2,1,0:T(8,128)(2,1)S(1)}, bf16[2,512,1024]{2,1,0:T(8,128)(2,1)}, u32[]{:S(2)}) copy-start(bf16[2,512,1024]{2,1,0:T(8,128)(2,1)} %get-tuple-element.18.refs_8_) | copy-start | bytes 6291460
  61.7 52.4 %copy-start.7 = (bf16[512,1024]{1,0:T(8,128)(2,1)S(1)}, bf16[512,1024]{1,0:T(8,128)(2,1)}, u32[]{:S(2)}) copy-start(bf16[512,1024]{1,0:T(8,128)(2,1)} %get-tuple-element.21.refs_0_) | copy-start | bytes 3145732
  62.5 2.0 %collective-permute-start.9 = (bf16[128,2176]{1,0:T(8,128)(2,1)S(1)}, bf16[128,2176]{1,0:T(8,128)(2,1)S(1)}, u32[]{:S(2)}, u32[]{:S(2)}) collective-permute-start(bf16[128,2176]{1,0:T(8,128)(2,1)S(1)} %shard_map.115.refs_1_), channel_id=1, source_target_pairs={{0,1},{1,0},{2,3},{3,2},{4,5},{5,4},{6,7},{7,6},{8,9},{9,8},{10,11... | collective-permute-start | bytes 1671176 | tf_op jit(solution)/shard_map/ppermute | solution.py:17
  62.5 2.7 %collective-permute-start.8 = (bf16[128,2176]{1,0:T(8,128)(2,1)S(1)}, bf16[128,2176]{1,0:T(8,128)(2,1)S(1)}, u32[]{:S(2)}, u32[]{:S(2)}) collective-permute-start(bf16[128,2176]{1,0:T(8,128)(2,1)S(1)} %shard_map.113.refs_0_), channel_id=1, source_target_pairs={{0,1},{1,0},{2,3},{3,2},{4,5},{5,4},{6,7},{7,6},{8,9},{9,8},{10,11... | collective-permute-start | bytes 1671176 | tf_op jit(solution)/shard_map/ppermute | solution.py:17
  117.7 8.5 %collective-permute-start.15 = (bf16[512,1024]{1,0:T(8,128)(2,1)S(1)}, bf16[512,1024]{1,0:T(8,128)(2,1)S(1)}, u32[]{:S(2)}, u32[]{:S(2)}) collective-permute-start(bf16[512,1024]{1,0:T(8,128)(2,1)S(1)} %get-tuple-element.24.refs_1_), channel_id=1, source_target_pairs={{0,1},{1,0},{2,3},{3,2},{4,5},{5,4},{6,7},{7,6},{8,9},{9,8},{10,11... | collective-permute-start | bytes 3145736 | tf_op jit(solution)/shard_map/ppermute | solution.py:17
  124.1 2.0 %collective-permute-start.18 = (bf16[512,512]{1,0:T(8,128)(2,1)S(1)}, bf16[512,512]{1,0:T(8,128)(2,1)S(1)}, u32[]{:S(2)}, u32[]{:S(2)}) collective-permute-start(bf16[512,512]{1,0:T(8,128)(2,1)S(1)} %get-tuple-element.26.refs_1_), channel_id=1, source_target_pairs={{0,1},{1,0},{2,3},{3,2},{4,5},{5,4},{6,7},{7,6},{8,9},{9,8},{10,11... | collective-permute-start | bytes 1572872 | tf_op jit(solution)/shard_map/ppermute | solution.py:17
  124.2 25.8 %collective-permute-start.22 = (bf16[512,1024]{1,0:T(8,128)(2,1)}, bf16[512,1024]{1,0:T(8,128)(2,1)S(1)}, u32[]{:S(2)}, u32[]{:S(2)}) collective-permute-start(bf16[512,1024]{1,0:T(8,128)(2,1)} %get-tuple-element.22.refs_1_), channel_id=1, source_target_pairs={{0,2},{1,3},{2,0},{3,1},{4,6},{5,7},{6,4},{7,5},{8,10},{9,11},{10,... | collective-permute-start | bytes 3145736 | tf_op jit(solution)/shard_map/ppermute | solution.py:17
  126.7 19.7 %collective-permute-start.16 = (bf16[4,64,1024]{2,1,0:T(8,128)(2,1)S(1)}, bf16[4,64,1024]{2,1,0:T(8,128)(2,1)S(1)}, u32[]{:S(2)}, u32[]{:S(2)}) collective-permute-start(bf16[4,64,1024]{2,1,0:T(8,128)(2,1)S(1)} %fusion.3), channel_id=1, source_target_pairs={{0,4},{4,0},{8,12},{12,8},{16,20},{20,16},{24,28},{28,24},{1,5},{5... | collective-permute-start | bytes 1572872 | tf_op jit(solution)/shard_map/ppermute | solution.py:17
  129.3 17.1 %collective-permute-start.19 = (bf16[4,64,512]{2,1,0:T(8,128)(2,1)}, bf16[4,64,512]{2,1,0:T(8,128)(2,1)S(1)}, u32[]{:S(2)}, u32[]{:S(2)}) collective-permute-start(bf16[4,64,512]{2,1,0:T(8,128)(2,1)} %fusion.9), channel_id=1, source_target_pairs={{0,4},{4,0},{8,12},{12,8},{16,20},{20,16},{24,28},{28,24},{1,5},{5... | collective-permute-start | bytes 786440 | tf_op jit(solution)/shard_map/ppermute | solution.py:17
  135.7 14.3 %copy-start.6 = (bf16[2,512,1024]{2,1,0:T(8,128)(2,1)S(1)}, bf16[2,512,1024]{2,1,0:T(8,128)(2,1)}, u32[]{:S(2)}) copy-start(bf16[2,512,1024]{2,1,0:T(8,128)(2,1)} %get-tuple-element.15.refs_2_) | copy-start | bytes 6291460
  151.3 2.1 %collective-permute-start.24 = (bf16[512,512]{1,0:T(8,128)(2,1)S(1)}, bf16[512,512]{1,0:T(8,128)(2,1)S(1)}, u32[]{:S(2)}, u32[]{:S(2)}) collective-permute-start(bf16[512,512]{1,0:T(8,128)(2,1)S(1)} %get-tuple-element.29), channel_id=1, source_target_pairs={{0,1},{1,0},{2,3},{3,2},{4,5},{5,4},{6,7},{7,6},{8,9},{9,8},{10,11... | collective-permute-start | bytes 1572872 | tf_op jit(solution)/shard_map/ppermute | solution.py:17
  151.5 11.7 %collective-permute-start.20 = (bf16[2,64,1536]{2,1,0:T(8,128)(2,1)S(1)}, bf16[2,64,1536]{2,1,0:T(8,128)(2,1)S(1)}, u32[]{:S(2)}, u32[]{:S(2)}) collective-permute-start(bf16[2,64,1536]{2,1,0:T(8,128)(2,1)S(1)} %fusion.6), channel_id=1, source_target_pairs={{0,8},{4,12},{8,0},{12,4},{16,24},{20,28},{24,16},{28,20},{1,9},{5... | collective-permute-start | bytes 1179656 | tf_op jit(solution)/shard_map/ppermute | solution.py:17
  153.6 9.7 %collective-permute-start.25 = (bf16[4,64,512]{2,1,0:T(8,128)(2,1)S(1)}, bf16[4,64,512]{2,1,0:T(8,128)(2,1)S(1)}, u32[]{:S(2)}, u32[]{:S(2)}) collective-permute-start(bf16[4,64,512]{2,1,0:T(8,128)(2,1)S(1)} %fusion.10), channel_id=1, source_target_pairs={{0,4},{4,0},{8,12},{12,8},{16,20},{20,16},{24,28},{28,24},{1,5},{5... | collective-permute-start | bytes 786440 | tf_op jit(solution)/shard_map/ppermute | solution.py:17
  163.4 6.9 %collective-permute-start.26 = (bf16[2,64,512]{2,1,0:T(8,128)(2,1)S(1)}, bf16[2,64,512]{2,1,0:T(8,128)(2,1)S(1)}, u32[]{:S(2)}, u32[]{:S(2)}) collective-permute-start(bf16[2,64,512]{2,1,0:T(8,128)(2,1)S(1)} %fusion.15), channel_id=1, source_target_pairs={{0,8},{4,12},{8,0},{12,4},{16,24},{20,28},{24,16},{28,20},{1,9},{5... | collective-permute-start | bytes 393224 | tf_op jit(solution)/shard_map/ppermute | solution.py:17
  165.2 13.6 %collective-permute-start.21 = (bf16[1,64,1536]{2,1,0:T(8,128)(2,1)S(1)}, bf16[1,64,1536]{2,1,0:T(8,128)(2,1)S(1)}, u32[]{:S(2)}, u32[]{:S(2)}) collective-permute-start(bf16[1,64,1536]{2,1,0:T(8,128)(2,1)S(1)} %fusion.14), channel_id=1, source_target_pairs={{0,16},{4,20},{8,24},{12,28},{16,0},{20,4},{24,8},{28,12},{1,17},{... | collective-permute-start | bytes 589832 | tf_op jit(solution)/shard_map/ppermute | solution.py:17
  170.3 9.2 %collective-permute-start.27 = (bf16[1,64,512]{2,1,0:T(8,128)(2,1)S(1)}, bf16[1,64,512]{2,1,0:T(8,128)(2,1)S(1)}, u32[]{:S(2)}, u32[]{:S(2)}) collective-permute-start(bf16[1,64,512]{2,1,0:T(8,128)(2,1)S(1)} %fusion.19), channel_id=1, source_target_pairs={{0,16},{4,20},{8,24},{12,28},{16,0},{20,4},{24,8},{28,12},{1,17},{... | collective-permute-start | bytes 196616 | tf_op jit(solution)/shard_map/ppermute | solution.py:17
  (11 other events, 63.2 us)

commit v14 on v13

--- a/solution.py
+++ b/solution.py
@@ -252,22 +252,24 @@
     )(hidden, *downs, *after)
 
 
-def over_core(kept, sent):
-    return kept.astype(jnp.float32) + swap(sent, "shard", 1).astype(jnp.float32)
-
-
-def over_x(total, tok):
-    total = total.reshape(-1, 2, tok, total.shape[-1])
-    given = swap(total[:, 1].astype(jnp.bfloat16), "dp", 1)
-    return total[:, 0] + given.astype(jnp.float32)
-
-
-def over_z(total):
-    bit = 1
+def over_core(kept, sent, tok):
+    total = kept.astype(jnp.float32) + swap(sent, "shard", 1).astype(jnp.float32)
+    return total.reshape(-1, 2 * tok, total.shape[-1])
+
+
+def step_z(total, bit):
+    pairs = total.reshape((-1, 2) + total.shape[1:])
+    return pairs[:, 0] + flip_z(pairs[:, 1].astype(jnp.bfloat16), bit).astype(jnp.float32)
+
+
+def over_x(total):
+    halves = total.reshape(total.shape[0], 2, -1, total.shape[-1])
+    return halves[:, 0] + swap(halves[:, 1].astype(jnp.bfloat16), "dp", 1).astype(jnp.float32)
+
+
+def over_z(total, bit):
     while total.shape[0] > 1:
-        pairs = total.reshape((-1, 2) + total.shape[1:])
-        given = flip_z(pairs[:, 1].astype(jnp.bfloat16), bit)
-        total = pairs[:, 0] + given.astype(jnp.float32)
+        total = step_z(total, bit)
         bit *= 2
     return total[0].astype(jnp.bfloat16)
 
@@ -334,14 +336,13 @@
 
     groups = [[d[0] for d in downs]] + [d[1:] for d in downs]
     kept, sent = down_of(hidden, groups[0], ())
-    at_core = over_core(kept, sent)
+    own_rows = step_z(over_core(kept, sent, tok), 1)
     kept, sent = down_of(hidden, groups[1], (sent,))
-    at_x = over_x(at_core, tok)
-    at_core = over_core(kept, sent)
-    at_x2 = over_x(at_core, tok)
-    kept, last = down_of(hidden, groups[2], (sent, news[0], at_x, at_x2))
-    early = over_z(jnp.concatenate([at_x, at_x2], axis=-1))
-    parts = [early, over_z(over_x(over_core(kept, last), tok))]
+    first_rows = step_z(over_core(kept, sent, tok), 1)
+    kept, sent = down_of(hidden, groups[2], (sent, news[0], own_rows, first_rows))
+    early = over_x(jnp.concatenate([own_rows, first_rows], axis=-1))
+    late = over_x(step_z(over_core(kept, sent, tok), 1))
+    parts = [over_z(early, 2), over_z(late, 2)]
     moe_output = placed(parts, depth, width)
 
     return (moe_output, *news)

time: 181 us -> 180 us (level)
  no operation moved by 1% of the time
where the time goes in v14:
time: 180 us
  waiting for transfers between devices  97.8 us (54%)
  Pallas kernels  37.7 us (21%)
  starting transfers between devices  37.1 us (21%)
  local copies, waits for them, and re-layouts  4.05 us (2%)
  other arithmetic  2.42 us (1%)
    ppermute x27, waiting for transfers between devices, swap(): lax.ppermute(x, axis, [(i, i ^ bit) for i in range(lax.axis_size(axis))])  97.8 us
    ppermute x27, starting transfers between devices, swap(): lax.ppermute(x, axis, [(i, i ^ bit) for i in range(lax.axis_size(axis))])  35.6 us
    pallas_call x3, Pallas kernels, copies(): pl.pallas_call(functools.partial(copy_kernel, plan, len(ins), len(counts)...  14.9 us
    pallas_call x1, Pallas kernels, hidden_of(): pl.pallas_call(functools.partial(hidden_kernel, len(pieces)), grid=(ff //...  12.3 us
    pallas_call x3, Pallas kernels, down_of(): pl.pallas_call(functools.partial(down_kernel, len(downs)), in_specs=[vmem...  6.16 us
  transfers between devices with their start and end apart: 28, of which 18 were waited for; matrix products, arithmetic and copies ran while one was open for 2% of the time, Pallas kernels for 17%

profile of v14, /device:TPU:0, one launch (start us, length us, event | category | flops | bytes accessed | tf_op | source)
XLA Modules:
  0.0 180.1 jit_solution(12657059082088910988)
XLA Ops:
  0.7 5.2 %shard_map.112 = (bf16[2,512,1024]{2,1,0:T(8,128)(2,1)}, bf16[2,512,1024]{2,1,0:T(8,128)(2,1)}, bf16[1,512,1024]{2,1,0:T(8,128)(2,1)}) custom-call(s32[16]{0:T(128)} %refs_0_.5, s32[16]{0:T(128)} %refs_1_.5, bf16[2,512,1024]{2,1,0:T(8,128)(2,1)} %refs_3_.5, bf16[2,512,1024]{2,1,0:T(8,128)(2,1)} %refs_4_.5, bf16[2,512,1024]{2,1,0:T(8,128)(2,1)} %refs_5_.1), custom_call_target="tpu_custom_call" | custom-call | tf_op jit(solution)/shard_map/pallas_call | solution.py:102
  6.4 2.6 %collective-permute-start.1 = (bf16[2,512,1024]{2,1,0:T(8,128)(2,1)}, bf16[2,512,1024]{2,1,0:T(8,128)(2,1)S(1)}, u32[]{:S(2)}, u32[]{:S(2)}) collective-permute-start(bf16[2,512,1024]{2,1,0:T(8,128)(2,1)} %get-tuple-element.18.refs_8_), channel_id=1, source_target_pairs={{0,2},{1,3},{2,0},{3,1},{4,6},{5,7},{6,4},{7,5},{8,10},{9,11},{10,... | collective-permute-start | bytes 6291464 | tf_op jit(solution)/shard_map/ppermute | solution.py:17
  9.7 1.6 collective-permute-start.2
  12.8 2.6 %collective-permute-start.4 = (bf16[64,2176]{1,0:T(8,128)(2,1)S(1)}, bf16[64,2176]{1,0:T(8,128)(2,1)S(1)}, u32[]{:S(2)}, u32[]{:S(2)}) collective-permute-start(bf16[64,2176]{1,0:T(8,128)(2,1)S(1)} %shard_map.111), channel_id=1, source_target_pairs={{0,16},{4,20},{8,24},{12,28},{16,0},{20,4},{24,8},{28,12},{1,17},{... | collective-permute-start | bytes 835592 | tf_op jit(solution)/shard_map/ppermute | solution.py:17
  15.4 7.7 %collective-permute-done.2 = bf16[64,2176]{1,0:T(8,128)(2,1)S(1)} collective-permute-done((bf16[64,2176]{1,0:T(8,128)(2,1)S(1)}, bf16[64,2176]{1,0:T(8,128)(2,1)S(1)}, u32[]{:S(2)}, u32[]{:S(2)}) %collective-permute-start.2) | collective-permute-done | bytes 278560 | tf_op jit(solution)/shard_map/ppermute | solution.py:17
  23.2 2.5 %collective-permute-start.3 = (bf16[64,2176]{1,0:T(8,128)(2,1)S(1)}, bf16[64,2176]{1,0:T(8,128)(2,1)S(1)}, u32[]{:S(2)}, u32[]{:S(2)}) collective-permute-start(bf16[64,2176]{1,0:T(8,128)(2,1)S(1)} %shard_map.114), channel_id=1, source_target_pairs={{0,4},{4,0},{8,12},{12,8},{16,20},{20,16},{24,28},{28,24},{1,5},{5... | collective-permute-start | bytes 835592 | tf_op jit(solution)/shard_map/ppermute | solution.py:17
  25.7 2.5 %collective-permute-start.6 = (bf16[64,2176]{1,0:T(8,128)(2,1)S(1)}, bf16[64,2176]{1,0:T(8,128)(2,1)S(1)}, u32[]{:S(2)}, u32[]{:S(2)}) collective-permute-start(bf16[64,2176]{1,0:T(8,128)(2,1)S(1)} %shard_map.111), channel_id=1, source_target_pairs={{0,24},{4,28},{8,16},{12,20},{16,8},{20,12},{24,0},{28,4},{1,25},{... | collective-permute-start | bytes 835592 | tf_op jit(solution)/shard_map/ppermute | solution.py:17
  29.2 2.6 %collective-permute-done.3.refs_1_.refs_6_ = bf16[64,2176]{1,0:T(8,128)(2,1)S(1)} collective-permute-done((bf16[64,2176]{1,0:T(8,128)(2,1)S(1)}, bf16[64,2176]{1,0:T(8,128)(2,1)S(1)}, u32[]{:S(2)}, u32[]{:S(2)}) %collective-permute-start.3) | collective-permute-done | bytes 278560 | tf_op jit(solution)/shard_map/ppermute | solution.py:17
  31.8 1.7 collective-permute-start.5
  35.2 3.9 %collective-permute-done.5.refs_1_.refs_7_ = bf16[64,2176]{1,0:T(8,128)(2,1)S(1)} collective-permute-done((bf16[64,2176]{1,0:T(8,128)(2,1)S(1)}, bf16[64,2176]{1,0:T(8,128)(2,1)S(1)}, u32[]{:S(2)}, u32[]{:S(2)}) %collective-permute-start.5) | collective-permute-done | bytes 278560 | tf_op jit(solution)/shard_map/ppermute | solution.py:17
  40.6 5.1 %collective-permute-done.7.refs_8_ = bf16[64,2176]{1,0:T(8,128)(2,1)S(1)} collective-permute-done((bf16[64,2176]{1,0:T(8,128)(2,1)S(1)}, bf16[64,2176]{1,0:T(8,128)(2,1)S(1)}, u32[]{:S(2)}, u32[]{:S(2)}) %collective-permute-start.7) | collective-permute-done | bytes 278560 | tf_op jit(solution)/shard_map/ppermute | solution.py:17
  46.4 3.6 %shard_map.124 = bf16[3,512,1024]{2,1,0:T(8,128)(2,1)} custom-call(s32[16]{0:T(128)} %refs_0_.5, s32[16]{0:T(128)} %refs_1_.5, bf16[2,512,1024]{2,1,0:T(8,128)(2,1)} %refs_3_.5, bf16[2,512,1024]{2,1,0:T(8,128)(2,1)} %refs_4_.5, bf16[2,512,1024]{2,1,0:T(8,128)(2,1)} %refs_5_.1, bf16[64,2176]{1,0:T(8,128)(2,1)} %copy-done, bf16[64,2176]{1,0:T(8,128)(2,1)} %copy-done.2, ...), custom_call_target="tpu_custom_call" | custom-call | tf_op jit(solution)/shard_map/pallas_call | solution.py:102
  50.0 1.5 collective-permute-start.23
  52.5 3.2 %collective-permute-done.1.refs_1_.refs_10_ = bf16[2,512,1024]{2,1,0:T(8,128)(2,1)S(1)} collective-permute-done((bf16[2,512,1024]{2,1,0:T(8,128)(2,1)}, bf16[2,512,1024]{2,1,0:T(8,128)(2,1)S(1)}, u32[]{:S(2)}, u32[]{:S(2)}) %collective-permute-start.1) | collective-permute-done | bytes 2097184 | tf_op jit(solution)/shard_map/ppermute | solution.py:17
  56.7 2.9 %shard_map.121 = (bf16[512,1024]{1,0:T(8,128)(2,1)}, bf16[512,1024]{1,0:T(8,128)(2,1)}) custom-call(bf16[2,512,1024]{2,1,0:T(8,128)(2,1)} %refs_5_.1, bf16[1,512,1024]{2,1,0:T(8,128)(2,1)} %collective-permute-done.14.other_ref), custom_call_target="tpu_custom_call" | custom-call | tf_op jit(solution)/shard_map/pallas_call | solution.py:141
  59.6 2.0 %collective-permute-start.17 = (bf16[512,1024]{1,0:T(8,128)(2,1)}, bf16[512,1024]{1,0:T(8,128)(2,1)S(1)}, u32[]{:S(2)}, u32[]{:S(2)}) collective-permute-start(bf16[512,1024]{1,0:T(8,128)(2,1)} %get-tuple-element.21.refs_0_), channel_id=1, source_target_pairs={{0,2},{1,3},{2,0},{3,1},{4,6},{5,7},{6,4},{7,5},{8,10},{9,11},{10,... | collective-permute-start | bytes 3145736 | tf_op jit(solution)/shard_map/ppermute | solution.py:17
  65.3 35.4 %collective-permute-done.13.refs_11_ = bf16[2,512,1024]{2,1,0:T(8,128)(2,1)} collective-permute-done((bf16[2,512,1024]{2,1,0:T(8,128)(2,1)S(1)}, bf16[2,512,1024]{2,1,0:T(8,128)(2,1)}, u32[]{:S(2)}, u32[]{:S(2)}) %collective-permute-start.13) | collective-permute-done | bytes 2097184 | tf_op jit(solution)/shard_map/ppermute | solution.py:17
  101.8 12.3 %shard_map.120.hidden_ref = bf16[1024,1024]{1,0:T(8,128)(2,1)S(1)} custom-call(bf16[128,2176]{1,0:T(8,128)(2,1)S(1)} %shard_map.113.refs_0_, bf16[128,2176]{1,0:T(8,128)(2,1)S(1)} %shard_map.115.refs_1_, bf16[128,2176]{1,0:T(8,128)(2,1)S(1)} %shard_map.117.refs_2_, bf16[128,2176]{1,0:T(8,128)(2,1)S(1)} %shard_map.119.refs_3_, ...), custom_call_target="tpu_custom_call" | custom-call | flops 1 | bytes 1 | tf_op jit(solution)/shard_map/pallas_call | solution.py:208
  114.1 3.6 %shard_map.122 = (bf16[512,1024]{1,0:T(8,128)(2,1)S(1)}, bf16[512,1024]{1,0:T(8,128)(2,1)S(1)}) custom-call(bf16[1024,1024]{1,0:T(8,128)(2,1)S(1)} %shard_map.120.hidden_ref, bf16[512,1024]{1,0:T(8,128)(2,1)S(1)} %copy-done.7, bf16[512,1024]{1,0:T(8,128)(2,1)} %get-tuple-element.22.refs_1_), custom_call_target="tpu_custom_call" | custom-call | flops 1 | bytes 1 | tf_op jit(solution)/shard_map/pallas_call | solution.py:245
  117.8 5.0 %collective-permute-done.17.refs_0_ = bf16[512,1024]{1,0:T(8,128)(2,1)S(1)} collective-permute-done((bf16[512,1024]{1,0:T(8,128)(2,1)}, bf16[512,1024]{1,0:T(8,128)(2,1)S(1)}, u32[]{:S(2)}, u32[]{:S(2)}) %collective-permute-start.17) | collective-permute-done | bytes 1048608 | tf_op jit(solution)/shard_map/ppermute | solution.py:17
  124.2 1.8 %collective-permute-start.22 = (bf16[512,1024]{1,0:T(8,128)(2,1)}, bf16[512,1024]{1,0:T(8,128)(2,1)S(1)}, u32[]{:S(2)}, u32[]{:S(2)}) collective-permute-start(bf16[512,1024]{1,0:T(8,128)(2,1)} %get-tuple-element.22.refs_1_), channel_id=1, source_target_pairs={{0,2},{1,3},{2,0},{3,1},{4,6},{5,7},{6,4},{7,5},{8,10},{9,11},{10,... | collective-permute-start | bytes 3145736 | tf_op jit(solution)/shard_map/ppermute | solution.py:17
  126.7 1.9 %collective-permute-start.16 = (bf16[2,128,1024]{2,1,0:T(8,128)(2,1)S(1)}, bf16[2,128,1024]{2,1,0:T(8,128)(2,1)S(1)}, u32[]{:S(2)}, u32[]{:S(2)}) collective-permute-start(bf16[2,128,1024]{2,1,0:T(8,128)(2,1)S(1)} %fusion.3), channel_id=1, source_target_pairs={{0,8},{4,12},{8,0},{12,4},{16,24},{20,28},{24,16},{28,20},{1,9},{5... | collective-permute-start | bytes 1572872 | tf_op jit(solution)/shard_map/ppermute | solution.py:17
  129.6 6.1 %shard_map.125 = (bf16[2,512,1024]{2,1,0:T(8,128)(2,1)}, bf16[2,512,1024]{2,1,0:T(8,128)(2,1)}, bf16[2,512,1024]{2,1,0:T(8,128)(2,1)}) custom-call(s32[16]{0:T(128)} %refs_0_.5, s32[16]{0:T(128)} %refs_1_.5, bf16[3,512,1024]{2,1,0:T(8,128)(2,1)} %collective-permute-done.23.refs_2_, bf16[2,512,1024]{2,1,0:T(8,128)(2,1)} %refs_3_.5, ...), custom_call_target="tpu_custom_call" | custom-call | tf_op jit(solution)/shard_map/pallas_call | solution.py:102
  135.7 10.7 %collective-permute-done.19 = bf16[2,128,512]{2,1,0:T(8,128)(2,1)S(1)} collective-permute-done((bf16[2,128,512]{2,1,0:T(8,128)(2,1)}, bf16[2,128,512]{2,1,0:T(8,128)(2,1)S(1)}, u32[]{:S(2)}, u32[]{:S(2)}) %collective-permute-start.19) | collective-permute-done | bytes 262176 | tf_op jit(solution)/shard_map/ppermute | solution.py:17
  146.7 3.3 %collective-permute-done.22.refs_0_ = bf16[512,1024]{1,0:T(8,128)(2,1)S(1)} collective-permute-done((bf16[512,1024]{1,0:T(8,128)(2,1)}, bf16[512,1024]{1,0:T(8,128)(2,1)S(1)}, u32[]{:S(2)}, u32[]{:S(2)}) %collective-permute-start.22) | collective-permute-done | bytes 1048608 | tf_op jit(solution)/shard_map/ppermute | solution.py:17
  151.5 1.8 collective-permute-start.20
  153.5 1.8 %collective-permute-start.25 = (bf16[2,128,512]{2,1,0:T(8,128)(2,1)S(1)}, bf16[2,128,512]{2,1,0:T(8,128)(2,1)S(1)}, u32[]{:S(2)}, u32[]{:S(2)}) collective-permute-start(bf16[2,128,512]{2,1,0:T(8,128)(2,1)S(1)} %fusion.10), channel_id=1, source_target_pairs={{0,8},{4,12},{8,0},{12,4},{16,24},{20,28},{24,16},{28,20},{1,9},{5... | collective-permute-start | bytes 786440 | tf_op jit(solution)/shard_map/ppermute | solution.py:17
  155.3 7.8 %collective-permute-done.20 = bf16[2,64,1536]{2,1,0:T(8,128)(2,1)S(1)} collective-permute-done((bf16[2,64,1536]{2,1,0:T(8,128)(2,1)S(1)}, bf16[2,64,1536]{2,1,0:T(8,128)(2,1)S(1)}, u32[]{:S(2)}, u32[]{:S(2)}) %collective-permute-start.20) | collective-permute-done | bytes 393248 | tf_op jit(solution)/shard_map/ppermute | solution.py:17
  163.3 1.8 collective-permute-start.26
  165.1 2.7 %collective-permute-start.21 = (bf16[1,64,1536]{2,1,0:T(8,128)(2,1)S(1)}, bf16[1,64,1536]{2,1,0:T(8,128)(2,1)S(1)}, u32[]{:S(2)}, u32[]{:S(2)}) collective-permute-start(bf16[1,64,1536]{2,1,0:T(8,128)(2,1)S(1)} %fusion.14), channel_id=1, source_target_pairs={{0,16},{4,20},{8,24},{12,28},{16,0},{20,4},{24,8},{28,12},{1,17},{... | collective-permute-start | bytes 589832 | tf_op jit(solution)/shard_map/ppermute | solution.py:17
  168.6 2.9 %collective-permute-start.27 = (bf16[1,64,512]{2,1,0:T(8,128)(2,1)S(1)}, bf16[1,64,512]{2,1,0:T(8,128)(2,1)S(1)}, u32[]{:S(2)}, u32[]{:S(2)}) collective-permute-start(bf16[1,64,512]{2,1,0:T(8,128)(2,1)S(1)} %fusion.19), channel_id=1, source_target_pairs={{0,16},{4,20},{8,24},{12,28},{16,0},{20,4},{24,8},{28,12},{1,17},{... | collective-permute-start | bytes 196616 | tf_op jit(solution)/shard_map/ppermute | solution.py:17
  171.5 7.2 %collective-permute-done.21 = bf16[1,64,1536]{2,1,0:T(8,128)(2,1)S(1)} collective-permute-done((bf16[1,64,1536]{2,1,0:T(8,128)(2,1)S(1)}, bf16[1,64,1536]{2,1,0:T(8,128)(2,1)S(1)}, u32[]{:S(2)}, u32[]{:S(2)}) %collective-permute-start.21) | collective-permute-done | bytes 196640 | tf_op jit(solution)/shard_map/ppermute | solution.py:17
  (96 shorter events, 21.7 us)
Async XLA Ops:
  5.9 27.7 %collective-permute-start.12 = (bf16[2,512,1024]{2,1,0:T(8,128)(2,1)}, bf16[2,512,1024]{2,1,0:T(8,128)(2,1)S(1)}, u32[]{:S(2)}, u32[]{:S(2)}) collective-permute-start(bf16[2,512,1024]{2,1,0:T(8,128)(2,1)} %get-tuple-element.19), channel_id=1, source_target_pairs={{0,1},{1,0},{2,3},{3,2},{4,5},{5,4},{6,7},{7,6},{8,9},{9,8},{10,11... | collective-permute-start | bytes 6291464 | tf_op jit(solution)/shard_map/ppermute | solution.py:17
  6.4 49.3 %collective-permute-start.1 = (bf16[2,512,1024]{2,1,0:T(8,128)(2,1)}, bf16[2,512,1024]{2,1,0:T(8,128)(2,1)S(1)}, u32[]{:S(2)}, u32[]{:S(2)}) collective-permute-start(bf16[2,512,1024]{2,1,0:T(8,128)(2,1)} %get-tuple-element.18.refs_8_), channel_id=1, source_target_pairs={{0,2},{1,3},{2,0},{3,1},{4,6},{5,7},{6,4},{7,5},{8,10},{9,11},{10,... | collective-permute-start | bytes 6291464 | tf_op jit(solution)/shard_map/ppermute | solution.py:17
  9.7 13.4 %collective-permute-start.2 = (bf16[64,2176]{1,0:T(8,128)(2,1)S(1)}, bf16[64,2176]{1,0:T(8,128)(2,1)S(1)}, u32[]{:S(2)}, u32[]{:S(2)}) collective-permute-start(bf16[64,2176]{1,0:T(8,128)(2,1)S(1)} %shard_map.111), channel_id=1, source_target_pairs={{0,8},{4,12},{8,0},{12,4},{16,24},{20,28},{24,16},{28,20},{1,9},{5... | collective-permute-start | bytes 835592 | tf_op jit(solution)/shard_map/ppermute | solution.py:17
  11.3 11.8 %collective-permute-start = (bf16[64,2176]{1,0:T(8,128)(2,1)S(1)}, bf16[64,2176]{1,0:T(8,128)(2,1)S(1)}, u32[]{:S(2)}, u32[]{:S(2)}) collective-permute-start(bf16[64,2176]{1,0:T(8,128)(2,1)S(1)} %shard_map.111), channel_id=1, source_target_pairs={{0,4},{4,0},{8,12},{12,8},{16,20},{20,16},{24,28},{28,24},{1,5},{5... | collective-permute-start | bytes 835592 | tf_op jit(solution)/shard_map/ppermute | solution.py:17
  12.8 16.4 %collective-permute-start.4 = (bf16[64,2176]{1,0:T(8,128)(2,1)S(1)}, bf16[64,2176]{1,0:T(8,128)(2,1)S(1)}, u32[]{:S(2)}, u32[]{:S(2)}) collective-permute-start(bf16[64,2176]{1,0:T(8,128)(2,1)S(1)} %shard_map.111), channel_id=1, source_target_pairs={{0,16},{4,20},{8,24},{12,28},{16,0},{20,4},{24,8},{28,12},{1,17},{... | collective-permute-start | bytes 835592 | tf_op jit(solution)/shard_map/ppermute | solution.py:17
  23.1 17.5 %copy-start = (bf16[64,2176]{1,0:T(8,128)(2,1)}, bf16[64,2176]{1,0:T(8,128)(2,1)S(1)}, u32[]{:S(2)}) copy-start(bf16[64,2176]{1,0:T(8,128)(2,1)S(1)} %collective-permute-done.refs_1_.refs_5_) | copy-start | bytes 835588
  23.2 8.7 %collective-permute-start.3 = (bf16[64,2176]{1,0:T(8,128)(2,1)S(1)}, bf16[64,2176]{1,0:T(8,128)(2,1)S(1)}, u32[]{:S(2)}, u32[]{:S(2)}) collective-permute-start(bf16[64,2176]{1,0:T(8,128)(2,1)S(1)} %shard_map.114), channel_id=1, source_target_pairs={{0,4},{4,0},{8,12},{12,8},{16,20},{20,16},{24,28},{28,24},{1,5},{5... | collective-permute-start | bytes 835592 | tf_op jit(solution)/shard_map/ppermute | solution.py:17
  25.7 9.5 %collective-permute-start.6 = (bf16[64,2176]{1,0:T(8,128)(2,1)S(1)}, bf16[64,2176]{1,0:T(8,128)(2,1)S(1)}, u32[]{:S(2)}, u32[]{:S(2)}) collective-permute-start(bf16[64,2176]{1,0:T(8,128)(2,1)S(1)} %shard_map.111), channel_id=1, source_target_pairs={{0,24},{4,28},{8,16},{12,20},{16,8},{20,12},{24,0},{28,4},{1,25},{... | collective-permute-start | bytes 835592 | tf_op jit(solution)/shard_map/ppermute | solution.py:17
  31.8 7.3 %collective-permute-start.5 = (bf16[64,2176]{1,0:T(8,128)(2,1)S(1)}, bf16[64,2176]{1,0:T(8,128)(2,1)S(1)}, u32[]{:S(2)}, u32[]{:S(2)}) collective-permute-start(bf16[64,2176]{1,0:T(8,128)(2,1)S(1)} %shard_map.116), channel_id=1, source_target_pairs={{0,4},{4,0},{8,12},{12,8},{16,20},{20,16},{24,28},{28,24},{1,5},{5... | collective-permute-start | bytes 835592 | tf_op jit(solution)/shard_map/ppermute | solution.py:17
  33.6 67.1 %collective-permute-start.13 = (bf16[2,512,1024]{2,1,0:T(8,128)(2,1)S(1)}, bf16[2,512,1024]{2,1,0:T(8,128)(2,1)}, u32[]{:S(2)}, u32[]{:S(2)}) collective-permute-start(bf16[2,512,1024]{2,1,0:T(8,128)(2,1)S(1)} %collective-permute-done.12.refs_9_), channel_id=1, source_target_pairs={{0,2},{1,3},{2,0},{3,1},{4,6},{5,7},{6,4},{7,5},{8,10},{9,11},{10,... | collective-permute-start | bytes 6291464 | tf_op jit(solution)/shard_map/ppermute | solution.py:17
  34.1 22.6 %collective-permute-start.14 = (bf16[1,512,1024]{2,1,0:T(8,128)(2,1)}, bf16[1,512,1024]{2,1,0:T(8,128)(2,1)}, u32[]{:S(2)}, u32[]{:S(2)}) collective-permute-start(bf16[1,512,1024]{2,1,0:T(8,128)(2,1)} %get-tuple-element.20), channel_id=1, source_target_pairs={{0,1},{1,0},{2,3},{3,2},{4,5},{5,4},{6,7},{7,6},{8,9},{9,8},{10,11... | collective-permute-start | bytes 3145736 | tf_op jit(solution)/shard_map/ppermute | solution.py:17
  39.1 6.5 %collective-permute-start.7 = (bf16[64,2176]{1,0:T(8,128)(2,1)S(1)}, bf16[64,2176]{1,0:T(8,128)(2,1)S(1)}, u32[]{:S(2)}, u32[]{:S(2)}) collective-permute-start(bf16[64,2176]{1,0:T(8,128)(2,1)S(1)} %shard_map.118), channel_id=1, source_target_pairs={{0,4},{4,0},{8,12},{12,8},{16,20},{20,16},{24,28},{28,24},{1,5},{5... | collective-permute-start | bytes 835592 | tf_op jit(solution)/shard_map/ppermute | solution.py:17
  50.0 79.6 %collective-permute-start.23 = (bf16[3,512,1024]{2,1,0:T(8,128)(2,1)}, bf16[3,512,1024]{2,1,0:T(8,128)(2,1)}, u32[]{:S(2)}, u32[]{:S(2)}) collective-permute-start(bf16[3,512,1024]{2,1,0:T(8,128)(2,1)} %shard_map.124), channel_id=1, source_target_pairs={{0,4},{4,8},{8,12},{12,16},{16,20},{20,24},{24,28},{28,0},{1,5},{5... | collective-permute-start | bytes 9437192 | tf_op jit(solution)/shard_map/ppermute | solution.py:22
  55.7 6.0 %collective-permute-start.11 = (bf16[128,2176]{1,0:T(8,128)(2,1)S(1)}, bf16[128,2176]{1,0:T(8,128)(2,1)S(1)}, u32[]{:S(2)}, u32[]{:S(2)}) collective-permute-start(bf16[128,2176]{1,0:T(8,128)(2,1)S(1)} %shard_map.119.refs_3_), channel_id=1, source_target_pairs={{0,1},{1,0},{2,3},{3,2},{4,5},{5,4},{6,7},{7,6},{8,9},{9,8},{10,11... | collective-permute-start | bytes 1671176 | tf_op jit(solution)/shard_map/ppermute | solution.py:17
  55.7 6.8 %collective-permute-start.10 = (bf16[128,2176]{1,0:T(8,128)(2,1)S(1)}, bf16[128,2176]{1,0:T(8,128)(2,1)}, u32[]{:S(2)}, u32[]{:S(2)}) collective-permute-start(bf16[128,2176]{1,0:T(8,128)(2,1)S(1)} %shard_map.117.refs_2_), channel_id=1, source_target_pairs={{0,1},{1,0},{2,3},{3,2},{4,5},{5,4},{6,7},{7,6},{8,9},{9,8},{10,11... | collective-permute-start | bytes 1671176 | tf_op jit(solution)/shard_map/ppermute | solution.py:17
  59.6 63.2 %collective-permute-start.17 = (bf16[512,1024]{1,0:T(8,128)(2,1)}, bf16[512,1024]{1,0:T(8,128)(2,1)S(1)}, u32[]{:S(2)}, u32[]{:S(2)}) collective-permute-start(bf16[512,1024]{1,0:T(8,128)(2,1)} %get-tuple-element.21.refs_0_), channel_id=1, source_target_pairs={{0,2},{1,3},{2,0},{3,1},{4,6},{5,7},{6,4},{7,5},{8,10},{9,11},{10,... | collective-permute-start | bytes 3145736 | tf_op jit(solution)/shard_map/ppermute | solution.py:17
  61.7 39.1 %copy-start.5 = (bf16[2,512,1024]{2,1,0:T(8,128)(2,1)S(1)}, bf16[2,512,1024]{2,1,0:T(8,128)(2,1)}, u32[]{:S(2)}) copy-start(bf16[2,512,1024]{2,1,0:T(8,128)(2,1)} %get-tuple-element.18.refs_8_) | copy-start | bytes 6291460
  61.7 52.4 %copy-start.7 = (bf16[512,1024]{1,0:T(8,128)(2,1)S(1)}, bf16[512,1024]{1,0:T(8,128)(2,1)}, u32[]{:S(2)}) copy-start(bf16[512,1024]{1,0:T(8,128)(2,1)} %get-tuple-element.21.refs_0_) | copy-start | bytes 3145732
  62.5 2.0 %collective-permute-start.9 = (bf16[128,2176]{1,0:T(8,128)(2,1)S(1)}, bf16[128,2176]{1,0:T(8,128)(2,1)S(1)}, u32[]{:S(2)}, u32[]{:S(2)}) collective-permute-start(bf16[128,2176]{1,0:T(8,128)(2,1)S(1)} %shard_map.115.refs_1_), channel_id=1, source_target_pairs={{0,1},{1,0},{2,3},{3,2},{4,5},{5,4},{6,7},{7,6},{8,9},{9,8},{10,11... | collective-permute-start | bytes 1671176 | tf_op jit(solution)/shard_map/ppermute | solution.py:17
  62.5 2.7 %collective-permute-start.8 = (bf16[128,2176]{1,0:T(8,128)(2,1)S(1)}, bf16[128,2176]{1,0:T(8,128)(2,1)S(1)}, u32[]{:S(2)}, u32[]{:S(2)}) collective-permute-start(bf16[128,2176]{1,0:T(8,128)(2,1)S(1)} %shard_map.113.refs_0_), channel_id=1, source_target_pairs={{0,1},{1,0},{2,3},{3,2},{4,5},{5,4},{6,7},{7,6},{8,9},{9,8},{10,11... | collective-permute-start | bytes 1671176 | tf_op jit(solution)/shard_map/ppermute | solution.py:17
  117.7 8.5 %collective-permute-start.15 = (bf16[512,1024]{1,0:T(8,128)(2,1)S(1)}, bf16[512,1024]{1,0:T(8,128)(2,1)S(1)}, u32[]{:S(2)}, u32[]{:S(2)}) collective-permute-start(bf16[512,1024]{1,0:T(8,128)(2,1)S(1)} %get-tuple-element.24.refs_1_), channel_id=1, source_target_pairs={{0,1},{1,0},{2,3},{3,2},{4,5},{5,4},{6,7},{7,6},{8,9},{9,8},{10,11... | collective-permute-start | bytes 3145736 | tf_op jit(solution)/shard_map/ppermute | solution.py:17
  124.1 2.0 %collective-permute-start.18 = (bf16[512,512]{1,0:T(8,128)(2,1)S(1)}, bf16[512,512]{1,0:T(8,128)(2,1)S(1)}, u32[]{:S(2)}, u32[]{:S(2)}) collective-permute-start(bf16[512,512]{1,0:T(8,128)(2,1)S(1)} %get-tuple-element.26.refs_1_), channel_id=1, source_target_pairs={{0,1},{1,0},{2,3},{3,2},{4,5},{5,4},{6,7},{7,6},{8,9},{9,8},{10,11... | collective-permute-start | bytes 1572872 | tf_op jit(solution)/shard_map/ppermute | solution.py:17
  124.2 25.8 %collective-permute-start.22 = (bf16[512,1024]{1,0:T(8,128)(2,1)}, bf16[512,1024]{1,0:T(8,128)(2,1)S(1)}, u32[]{:S(2)}, u32[]{:S(2)}) collective-permute-start(bf16[512,1024]{1,0:T(8,128)(2,1)} %get-tuple-element.22.refs_1_), channel_id=1, source_target_pairs={{0,2},{1,3},{2,0},{3,1},{4,6},{5,7},{6,4},{7,5},{8,10},{9,11},{10,... | collective-permute-start | bytes 3145736 | tf_op jit(solution)/shard_map/ppermute | solution.py:17
  126.7 19.8 %collective-permute-start.16 = (bf16[2,128,1024]{2,1,0:T(8,128)(2,1)S(1)}, bf16[2,128,1024]{2,1,0:T(8,128)(2,1)S(1)}, u32[]{:S(2)}, u32[]{:S(2)}) collective-permute-start(bf16[2,128,1024]{2,1,0:T(8,128)(2,1)S(1)} %fusion.3), channel_id=1, source_target_pairs={{0,8},{4,12},{8,0},{12,4},{16,24},{20,28},{24,16},{28,20},{1,9},{5... | collective-permute-start | bytes 1572872 | tf_op jit(solution)/shard_map/ppermute | solution.py:17
  129.3 17.1 %collective-permute-start.19 = (bf16[2,128,512]{2,1,0:T(8,128)(2,1)}, bf16[2,128,512]{2,1,0:T(8,128)(2,1)S(1)}, u32[]{:S(2)}, u32[]{:S(2)}) collective-permute-start(bf16[2,128,512]{2,1,0:T(8,128)(2,1)} %fusion.9), channel_id=1, source_target_pairs={{0,8},{4,12},{8,0},{12,4},{16,24},{20,28},{24,16},{28,20},{1,9},{5... | collective-permute-start | bytes 786440 | tf_op jit(solution)/shard_map/ppermute | solution.py:17
  135.7 14.3 %copy-start.6 = (bf16[2,512,1024]{2,1,0:T(8,128)(2,1)S(1)}, bf16[2,512,1024]{2,1,0:T(8,128)(2,1)}, u32[]{:S(2)}) copy-start(bf16[2,512,1024]{2,1,0:T(8,128)(2,1)} %get-tuple-element.15.refs_2_) | copy-start | bytes 6291460
  151.3 2.1 %collective-permute-start.24 = (bf16[512,512]{1,0:T(8,128)(2,1)S(1)}, bf16[512,512]{1,0:T(8,128)(2,1)S(1)}, u32[]{:S(2)}, u32[]{:S(2)}) collective-permute-start(bf16[512,512]{1,0:T(8,128)(2,1)S(1)} %get-tuple-element.29), channel_id=1, source_target_pairs={{0,1},{1,0},{2,3},{3,2},{4,5},{5,4},{6,7},{7,6},{8,9},{9,8},{10,11... | collective-permute-start | bytes 1572872 | tf_op jit(solution)/shard_map/ppermute | solution.py:17
  151.5 11.6 %collective-permute-start.20 = (bf16[2,64,1536]{2,1,0:T(8,128)(2,1)S(1)}, bf16[2,64,1536]{2,1,0:T(8,128)(2,1)S(1)}, u32[]{:S(2)}, u32[]{:S(2)}) collective-permute-start(bf16[2,64,1536]{2,1,0:T(8,128)(2,1)S(1)} %fusion.6), channel_id=1, source_target_pairs={{0,4},{4,0},{8,12},{12,8},{16,20},{20,16},{24,28},{28,24},{1,5},{5... | collective-permute-start | bytes 1179656 | tf_op jit(solution)/shard_map/ppermute | solution.py:17
  153.5 9.7 %collective-permute-start.25 = (bf16[2,128,512]{2,1,0:T(8,128)(2,1)S(1)}, bf16[2,128,512]{2,1,0:T(8,128)(2,1)S(1)}, u32[]{:S(2)}, u32[]{:S(2)}) collective-permute-start(bf16[2,128,512]{2,1,0:T(8,128)(2,1)S(1)} %fusion.10), channel_id=1, source_target_pairs={{0,8},{4,12},{8,0},{12,4},{16,24},{20,28},{24,16},{28,20},{1,9},{5... | collective-permute-start | bytes 786440 | tf_op jit(solution)/shard_map/ppermute | solution.py:17
  163.3 5.2 %collective-permute-start.26 = (bf16[2,64,512]{2,1,0:T(8,128)(2,1)S(1)}, bf16[2,64,512]{2,1,0:T(8,128)(2,1)S(1)}, u32[]{:S(2)}, u32[]{:S(2)}) collective-permute-start(bf16[2,64,512]{2,1,0:T(8,128)(2,1)S(1)} %fusion.15), channel_id=1, source_target_pairs={{0,4},{4,0},{8,12},{12,8},{16,20},{20,16},{24,28},{28,24},{1,5},{5... | collective-permute-start | bytes 393224 | tf_op jit(solution)/shard_map/ppermute | solution.py:17
  165.1 13.5 %collective-permute-start.21 = (bf16[1,64,1536]{2,1,0:T(8,128)(2,1)S(1)}, bf16[1,64,1536]{2,1,0:T(8,128)(2,1)S(1)}, u32[]{:S(2)}, u32[]{:S(2)}) collective-permute-start(bf16[1,64,1536]{2,1,0:T(8,128)(2,1)S(1)} %fusion.14), channel_id=1, source_target_pairs={{0,16},{4,20},{8,24},{12,28},{16,0},{20,4},{24,8},{28,12},{1,17},{... | collective-permute-start | bytes 589832 | tf_op jit(solution)/shard_map/ppermute | solution.py:17
  168.6 10.8 %collective-permute-start.27 = (bf16[1,64,512]{2,1,0:T(8,128)(2,1)S(1)}, bf16[1,64,512]{2,1,0:T(8,128)(2,1)S(1)}, u32[]{:S(2)}, u32[]{:S(2)}) collective-permute-start(bf16[1,64,512]{2,1,0:T(8,128)(2,1)S(1)} %fusion.19), channel_id=1, source_target_pairs={{0,16},{4,20},{8,24},{12,28},{16,0},{20,4},{24,8},{28,12},{1,17},{... | collective-permute-start | bytes 196616 | tf_op jit(solution)/shard_map/ppermute | solution.py:17
  (11 other events, 63.2 us)

commit v15 on v14

--- a/solution.py
+++ b/solution.py
@@ -306,11 +306,11 @@
     n_z = lax.axis_size("dp") // 2
     places = (old_place, new_place)
 
-    mine, theirs, theirs_down = copies(
-        ((0, "mine", 0, 0), (1, "mine", 0, 1))
-        + ((0, "theirs", 1, 0), (1, "theirs", 1, 1), (2, "theirs", 2, 0)),
-        places, (w_gate, w_up, w_down), (2, 2, 1),
-    )
+    mine, theirs = copies(
+        ((0, "mine", 0, 0), (1, "mine", 0, 1), (0, "theirs", 1, 0), (1, "theirs", 1, 1)),
+        places, (w_gate, w_up), (2, 2),
+    )
+    (theirs_down,) = copies(((0, "theirs", 0, 0),), places, (w_down,), (1,), (mine,))
     near_weights = [mine, swap(theirs, "shard", 1)]
     weights = spread(near_weights)
     downs = [spread([d]) for d in in_order(w_down, swap(theirs_down, "shard", 1))]

time: 180 us -> 179 us (level)
  waiting for transfers between devices: 97.8 us -> 95.4 us
    ppermute x27, waiting for transfers between devices: 97.8 us -> 95.4 us  [swap(): lax.ppermute(x, axis, [(i, i ^ bit) for i in range(lax.axis_size(axis))])]
    pallas_call x3 -> x4, Pallas kernels: 14.9 us -> 16.7 us  [copies(): pl.pallas_call(functools.partial(copy_kernel, plan, len(ins), len(counts)...]
  transfers between devices with their start and end apart: 28 -> 28, of which waited for: 18 -> 17; matrix products, arithmetic and copies ran while one was open for 2% -> 2% of each run, Pallas kernels for 17% -> 19%
where the time goes in v15:
time: 179 us
  waiting for transfers between devices  95.4 us (53%)
  Pallas kernels  39.5 us (22%)
  starting transfers between devices  36.6 us (20%)
  local copies, waits for them, and re-layouts  4.06 us (2%)
  other arithmetic  2.42 us (1%)
    ppermute x27, waiting for transfers between devices, swap(): lax.ppermute(x, axis, [(i, i ^ bit) for i in range(lax.axis_size(axis))])  95.4 us
    ppermute x27, starting transfers between devices, swap(): lax.ppermute(x, axis, [(i, i ^ bit) for i in range(lax.axis_size(axis))])  35.7 us
    pallas_call x4, Pallas kernels, copies(): pl.pallas_call(functools.partial(copy_kernel, plan, len(ins), len(counts)...  16.7 us
    pallas_call x1, Pallas kernels, hidden_of(): pl.pallas_call(functools.partial(hidden_kernel, len(pieces)), grid=(ff //...  12.3 us
    pallas_call x3, Pallas kernels, down_of(): pl.pallas_call(functools.partial(down_kernel, len(downs)), in_specs=[vmem...  6.16 us
  transfers between devices with their start and end apart: 28, of which 17 were waited for; matrix products, arithmetic and copies ran while one was open for 2% of the time, Pallas kernels for 19%

profile of v15, /device:TPU:0, one launch (start us, length us, event | category | flops | bytes accessed | tf_op | source)
XLA Modules:
  0.0 179.1 jit_solution(12003972788431549647)
XLA Ops:
  0.7 4.1 %shard_map.112 = (bf16[2,512,1024]{2,1,0:T(8,128)(2,1)}, bf16[2,512,1024]{2,1,0:T(8,128)(2,1)}) custom-call(s32[16]{0:T(128)} %refs_0_.7, s32[16]{0:T(128)} %refs_1_.7, bf16[2,512,1024]{2,1,0:T(8,128)(2,1)} %refs_3_.5, bf16[2,512,1024]{2,1,0:T(8,128)(2,1)} %refs_4_.3), custom_call_target="tpu_custom_call" | custom-call | tf_op jit(solution)/shard_map/pallas_call | solution.py:102
  5.3 2.6 %collective-permute-start.1 = (bf16[2,512,1024]{2,1,0:T(8,128)(2,1)}, bf16[2,512,1024]{2,1,0:T(8,128)(2,1)S(1)}, u32[]{:S(2)}, u32[]{:S(2)}) collective-permute-start(bf16[2,512,1024]{2,1,0:T(8,128)(2,1)} %get-tuple-element.17.refs_8_.refs_3_), channel_id=1, source_target_pairs={{0,2},{1,3},{2,0},{3,1},{4,6},{5,7},{6,4},{7,5},{8,10},{9,11},{10,... | collective-permute-start | bytes 6291464 | tf_op jit(solution)/shard_map/ppermute | solution.py:17
  8.6 1.6 collective-permute-start.2
  11.7 2.6 %collective-permute-start.4 = (bf16[64,2176]{1,0:T(8,128)(2,1)S(1)}, bf16[64,2176]{1,0:T(8,128)(2,1)S(1)}, u32[]{:S(2)}, u32[]{:S(2)}) collective-permute-start(bf16[64,2176]{1,0:T(8,128)(2,1)S(1)} %shard_map.111), channel_id=1, source_target_pairs={{0,16},{4,20},{8,24},{12,28},{16,0},{20,4},{24,8},{28,12},{1,17},{... | collective-permute-start | bytes 835592 | tf_op jit(solution)/shard_map/ppermute | solution.py:17
  14.3 7.7 %collective-permute-done.2 = bf16[64,2176]{1,0:T(8,128)(2,1)S(1)} collective-permute-done((bf16[64,2176]{1,0:T(8,128)(2,1)S(1)}, bf16[64,2176]{1,0:T(8,128)(2,1)S(1)}, u32[]{:S(2)}, u32[]{:S(2)}) %collective-permute-start.2) | collective-permute-done | bytes 278560 | tf_op jit(solution)/shard_map/ppermute | solution.py:17
  22.1 2.5 %collective-permute-start.3 = (bf16[64,2176]{1,0:T(8,128)(2,1)S(1)}, bf16[64,2176]{1,0:T(8,128)(2,1)S(1)}, u32[]{:S(2)}, u32[]{:S(2)}) collective-permute-start(bf16[64,2176]{1,0:T(8,128)(2,1)S(1)} %shard_map.114), channel_id=1, source_target_pairs={{0,4},{4,0},{8,12},{12,8},{16,20},{20,16},{24,28},{28,24},{1,5},{5... | collective-permute-start | bytes 835592 | tf_op jit(solution)/shard_map/ppermute | solution.py:17
  24.6 2.5 %collective-permute-start.6 = (bf16[64,2176]{1,0:T(8,128)(2,1)S(1)}, bf16[64,2176]{1,0:T(8,128)(2,1)S(1)}, u32[]{:S(2)}, u32[]{:S(2)}) collective-permute-start(bf16[64,2176]{1,0:T(8,128)(2,1)S(1)} %shard_map.111), channel_id=1, source_target_pairs={{0,24},{4,28},{8,16},{12,20},{16,8},{20,12},{24,0},{28,4},{1,25},{... | collective-permute-start | bytes 835592 | tf_op jit(solution)/shard_map/ppermute | solution.py:17
  28.1 2.7 %collective-permute-done.3.refs_1_.refs_6_ = bf16[64,2176]{1,0:T(8,128)(2,1)S(1)} collective-permute-done((bf16[64,2176]{1,0:T(8,128)(2,1)S(1)}, bf16[64,2176]{1,0:T(8,128)(2,1)S(1)}, u32[]{:S(2)}, u32[]{:S(2)}) %collective-permute-start.3) | collective-permute-done | bytes 278560 | tf_op jit(solution)/shard_map/ppermute | solution.py:17
  30.8 1.7 collective-permute-start.5
  33.0 2.9 %shard_map.121 = bf16[1,512,1024]{2,1,0:T(8,128)(2,1)} custom-call(s32[16]{0:T(128)} %refs_0_.7, s32[16]{0:T(128)} %refs_1_.7, bf16[2,512,1024]{2,1,0:T(8,128)(2,1)} %refs_5_.1, bf16[2,512,1024]{2,1,0:T(8,128)(2,1)} %get-tuple-element.17.refs_8_.refs_3_), custom_call_target="tpu_custom_call" | custom-call | tf_op jit(solution)/shard_map/pallas_call | solution.py:102
  36.0 2.0 %collective-permute-done.5.refs_1_.refs_7_ = bf16[64,2176]{1,0:T(8,128)(2,1)S(1)} collective-permute-done((bf16[64,2176]{1,0:T(8,128)(2,1)S(1)}, bf16[64,2176]{1,0:T(8,128)(2,1)S(1)}, u32[]{:S(2)}, u32[]{:S(2)}) %collective-permute-start.5) | collective-permute-done | bytes 278560 | tf_op jit(solution)/shard_map/ppermute | solution.py:17
  39.5 5.7 %collective-permute-done.7.refs_8_ = bf16[64,2176]{1,0:T(8,128)(2,1)S(1)} collective-permute-done((bf16[64,2176]{1,0:T(8,128)(2,1)S(1)}, bf16[64,2176]{1,0:T(8,128)(2,1)S(1)}, u32[]{:S(2)}, u32[]{:S(2)}) %collective-permute-start.7) | collective-permute-done | bytes 278560 | tf_op jit(solution)/shard_map/ppermute | solution.py:17
  45.9 3.6 %shard_map.125 = bf16[3,512,1024]{2,1,0:T(8,128)(2,1)} custom-call(s32[16]{0:T(128)} %refs_0_.7, s32[16]{0:T(128)} %refs_1_.7, bf16[2,512,1024]{2,1,0:T(8,128)(2,1)} %refs_3_.5, bf16[2,512,1024]{2,1,0:T(8,128)(2,1)} %refs_4_.3, bf16[2,512,1024]{2,1,0:T(8,128)(2,1)} %refs_5_.1, bf16[64,2176]{1,0:T(8,128)(2,1)} %copy-done.1, bf16[64,2176]{1,0:T(8,128)(2,1)} %copy-done.3, ...), custom_call_target="tpu_custom_call" | custom-call | tf_op jit(solution)/shard_map/pallas_call | solution.py:102
  51.4 3.2 %collective-permute-done.1.refs_1_.refs_10_ = bf16[2,512,1024]{2,1,0:T(8,128)(2,1)S(1)} collective-permute-done((bf16[2,512,1024]{2,1,0:T(8,128)(2,1)}, bf16[2,512,1024]{2,1,0:T(8,128)(2,1)S(1)}, u32[]{:S(2)}, u32[]{:S(2)}) %collective-permute-start.1) | collective-permute-done | bytes 2097184 | tf_op jit(solution)/shard_map/ppermute | solution.py:17
  55.6 2.9 %shard_map.122 = (bf16[512,1024]{1,0:T(8,128)(2,1)}, bf16[512,1024]{1,0:T(8,128)(2,1)}) custom-call(bf16[2,512,1024]{2,1,0:T(8,128)(2,1)} %refs_5_.1, bf16[1,512,1024]{2,1,0:T(8,128)(2,1)} %collective-permute-done.14.other_ref), custom_call_target="tpu_custom_call" | custom-call | tf_op jit(solution)/shard_map/pallas_call | solution.py:141
  58.5 2.0 %collective-permute-start.17 = (bf16[512,1024]{1,0:T(8,128)(2,1)}, bf16[512,1024]{1,0:T(8,128)(2,1)S(1)}, u32[]{:S(2)}, u32[]{:S(2)}) collective-permute-start(bf16[512,1024]{1,0:T(8,128)(2,1)} %get-tuple-element.19.refs_0_), channel_id=1, source_target_pairs={{0,2},{1,3},{2,0},{3,1},{4,6},{5,7},{6,4},{7,5},{8,10},{9,11},{10,... | collective-permute-start | bytes 3145736 | tf_op jit(solution)/shard_map/ppermute | solution.py:17
  64.2 35.4 %collective-permute-done.13.refs_11_ = bf16[2,512,1024]{2,1,0:T(8,128)(2,1)} collective-permute-done((bf16[2,512,1024]{2,1,0:T(8,128)(2,1)S(1)}, bf16[2,512,1024]{2,1,0:T(8,128)(2,1)}, u32[]{:S(2)}, u32[]{:S(2)}) %collective-permute-start.13) | collective-permute-done | bytes 2097184 | tf_op jit(solution)/shard_map/ppermute | solution.py:17
  100.7 12.3 %shard_map.120.hidden_ref = bf16[1024,1024]{1,0:T(8,128)(2,1)S(1)} custom-call(bf16[128,2176]{1,0:T(8,128)(2,1)S(1)} %shard_map.113.refs_0_, bf16[128,2176]{1,0:T(8,128)(2,1)S(1)} %shard_map.115.refs_1_, bf16[128,2176]{1,0:T(8,128)(2,1)S(1)} %shard_map.117.refs_2_, bf16[128,2176]{1,0:T(8,128)(2,1)S(1)} %shard_map.119.refs_3_, ...), custom_call_target="tpu_custom_call" | custom-call | flops 1 | bytes 1 | tf_op jit(solution)/shard_map/pallas_call | solution.py:208
  113.0 3.6 %shard_map.123 = (bf16[512,1024]{1,0:T(8,128)(2,1)S(1)}, bf16[512,1024]{1,0:T(8,128)(2,1)S(1)}) custom-call(bf16[1024,1024]{1,0:T(8,128)(2,1)S(1)} %shard_map.120.hidden_ref, bf16[512,1024]{1,0:T(8,128)(2,1)S(1)} %copy-done.7, bf16[512,1024]{1,0:T(8,128)(2,1)} %get-tuple-element.20.refs_1_), custom_call_target="tpu_custom_call" | custom-call | flops 1 | bytes 1 | tf_op jit(solution)/shard_map/pallas_call | solution.py:245
  116.7 5.0 %collective-permute-done.17.refs_0_ = bf16[512,1024]{1,0:T(8,128)(2,1)S(1)} collective-permute-done((bf16[512,1024]{1,0:T(8,128)(2,1)}, bf16[512,1024]{1,0:T(8,128)(2,1)S(1)}, u32[]{:S(2)}, u32[]{:S(2)}) %collective-permute-start.17) | collective-permute-done | bytes 1048608 | tf_op jit(solution)/shard_map/ppermute | solution.py:17
  123.1 1.8 %collective-permute-start.22 = (bf16[512,1024]{1,0:T(8,128)(2,1)}, bf16[512,1024]{1,0:T(8,128)(2,1)S(1)}, u32[]{:S(2)}, u32[]{:S(2)}) collective-permute-start(bf16[512,1024]{1,0:T(8,128)(2,1)} %get-tuple-element.20.refs_1_), channel_id=1, source_target_pairs={{0,2},{1,3},{2,0},{3,1},{4,6},{5,7},{6,4},{7,5},{8,10},{9,11},{10,... | collective-permute-start | bytes 3145736 | tf_op jit(solution)/shard_map/ppermute | solution.py:17
  125.7 1.9 %collective-permute-start.16 = (bf16[2,128,1024]{2,1,0:T(8,128)(2,1)S(1)}, bf16[2,128,1024]{2,1,0:T(8,128)(2,1)S(1)}, u32[]{:S(2)}, u32[]{:S(2)}) collective-permute-start(bf16[2,128,1024]{2,1,0:T(8,128)(2,1)S(1)} %fusion.3), channel_id=1, source_target_pairs={{0,8},{4,12},{8,0},{12,4},{16,24},{20,28},{24,16},{28,20},{1,9},{5... | collective-permute-start | bytes 1572872 | tf_op jit(solution)/shard_map/ppermute | solution.py:17
  128.5 6.1 %shard_map.126 = (bf16[2,512,1024]{2,1,0:T(8,128)(2,1)}, bf16[2,512,1024]{2,1,0:T(8,128)(2,1)}, bf16[2,512,1024]{2,1,0:T(8,128)(2,1)}) custom-call(s32[16]{0:T(128)} %refs_0_.7, s32[16]{0:T(128)} %refs_1_.7, bf16[3,512,1024]{2,1,0:T(8,128)(2,1)} %collective-permute-done.23.refs_2_, bf16[2,512,1024]{2,1,0:T(8,128)(2,1)} %refs_3_.5, ...), custom_call_target="tpu_custom_call" | custom-call | tf_op jit(solution)/shard_map/pallas_call | solution.py:102
  134.6 10.7 %collective-permute-done.19 = bf16[2,128,512]{2,1,0:T(8,128)(2,1)S(1)} collective-permute-done((bf16[2,128,512]{2,1,0:T(8,128)(2,1)}, bf16[2,128,512]{2,1,0:T(8,128)(2,1)S(1)}, u32[]{:S(2)}, u32[]{:S(2)}) %collective-permute-start.19) | collective-permute-done | bytes 262176 | tf_op jit(solution)/shard_map/ppermute | solution.py:17
  145.6 3.3 %collective-permute-done.22.refs_0_ = bf16[512,1024]{1,0:T(8,128)(2,1)S(1)} collective-permute-done((bf16[512,1024]{1,0:T(8,128)(2,1)}, bf16[512,1024]{1,0:T(8,128)(2,1)S(1)}, u32[]{:S(2)}, u32[]{:S(2)}) %collective-permute-start.22) | collective-permute-done | bytes 1048608 | tf_op jit(solution)/shard_map/ppermute | solution.py:17
  150.5 1.8 %collective-permute-start.20 = (bf16[2,64,1536]{2,1,0:T(8,128)(2,1)S(1)}, bf16[2,64,1536]{2,1,0:T(8,128)(2,1)S(1)}, u32[]{:S(2)}, u32[]{:S(2)}) collective-permute-start(bf16[2,64,1536]{2,1,0:T(8,128)(2,1)S(1)} %fusion.6), channel_id=1, source_target_pairs={{0,4},{4,0},{8,12},{12,8},{16,20},{20,16},{24,28},{28,24},{1,5},{5... | collective-permute-start | bytes 1179656 | tf_op jit(solution)/shard_map/ppermute | solution.py:17
  152.5 1.8 %collective-permute-start.25 = (bf16[2,128,512]{2,1,0:T(8,128)(2,1)S(1)}, bf16[2,128,512]{2,1,0:T(8,128)(2,1)S(1)}, u32[]{:S(2)}, u32[]{:S(2)}) collective-permute-start(bf16[2,128,512]{2,1,0:T(8,128)(2,1)S(1)} %fusion.10), channel_id=1, source_target_pairs={{0,8},{4,12},{8,0},{12,4},{16,24},{20,28},{24,16},{28,20},{1,9},{5... | collective-permute-start | bytes 786440 | tf_op jit(solution)/shard_map/ppermute | solution.py:17
  154.2 7.8 %collective-permute-done.20 = bf16[2,64,1536]{2,1,0:T(8,128)(2,1)S(1)} collective-permute-done((bf16[2,64,1536]{2,1,0:T(8,128)(2,1)S(1)}, bf16[2,64,1536]{2,1,0:T(8,128)(2,1)S(1)}, u32[]{:S(2)}, u32[]{:S(2)}) %collective-permute-start.20) | collective-permute-done | bytes 393248 | tf_op jit(solution)/shard_map/ppermute | solution.py:17
  162.3 1.8 %collective-permute-start.26 = (bf16[2,64,512]{2,1,0:T(8,128)(2,1)S(1)}, bf16[2,64,512]{2,1,0:T(8,128)(2,1)S(1)}, u32[]{:S(2)}, u32[]{:S(2)}) collective-permute-start(bf16[2,64,512]{2,1,0:T(8,128)(2,1)S(1)} %fusion.15), channel_id=1, source_target_pairs={{0,4},{4,0},{8,12},{12,8},{16,20},{20,16},{24,28},{28,24},{1,5},{5... | collective-permute-start | bytes 393224 | tf_op jit(solution)/shard_map/ppermute | solution.py:17
  164.1 2.6 %collective-permute-start.21 = (bf16[1,64,1536]{2,1,0:T(8,128)(2,1)S(1)}, bf16[1,64,1536]{2,1,0:T(8,128)(2,1)S(1)}, u32[]{:S(2)}, u32[]{:S(2)}) collective-permute-start(bf16[1,64,1536]{2,1,0:T(8,128)(2,1)S(1)} %fusion.14), channel_id=1, source_target_pairs={{0,16},{4,20},{8,24},{12,28},{16,0},{20,4},{24,8},{28,12},{1,17},{... | collective-permute-start | bytes 589832 | tf_op jit(solution)/shard_map/ppermute | solution.py:17
  167.5 2.9 %collective-permute-start.27 = (bf16[1,64,512]{2,1,0:T(8,128)(2,1)S(1)}, bf16[1,64,512]{2,1,0:T(8,128)(2,1)S(1)}, u32[]{:S(2)}, u32[]{:S(2)}) collective-permute-start(bf16[1,64,512]{2,1,0:T(8,128)(2,1)S(1)} %fusion.19), channel_id=1, source_target_pairs={{0,16},{4,20},{8,24},{12,28},{16,0},{20,4},{24,8},{28,12},{1,17},{... | collective-permute-start | bytes 196616 | tf_op jit(solution)/shard_map/ppermute | solution.py:17
  170.4 7.2 %collective-permute-done.21 = bf16[1,64,1536]{2,1,0:T(8,128)(2,1)S(1)} collective-permute-done((bf16[1,64,1536]{2,1,0:T(8,128)(2,1)S(1)}, bf16[1,64,1536]{2,1,0:T(8,128)(2,1)S(1)}, u32[]{:S(2)}, u32[]{:S(2)}) %collective-permute-start.21) | collective-permute-done | bytes 196640 | tf_op jit(solution)/shard_map/ppermute | solution.py:17
  (97 shorter events, 21.5 us)
Async XLA Ops:
  4.8 27.7 %collective-permute-start.12 = (bf16[2,512,1024]{2,1,0:T(8,128)(2,1)}, bf16[2,512,1024]{2,1,0:T(8,128)(2,1)S(1)}, u32[]{:S(2)}, u32[]{:S(2)}) collective-permute-start(bf16[2,512,1024]{2,1,0:T(8,128)(2,1)} %get-tuple-element.18), channel_id=1, source_target_pairs={{0,1},{1,0},{2,3},{3,2},{4,5},{5,4},{6,7},{7,6},{8,9},{9,8},{10,11... | collective-permute-start | bytes 6291464 | tf_op jit(solution)/shard_map/ppermute | solution.py:17
  5.3 49.3 %collective-permute-start.1 = (bf16[2,512,1024]{2,1,0:T(8,128)(2,1)}, bf16[2,512,1024]{2,1,0:T(8,128)(2,1)S(1)}, u32[]{:S(2)}, u32[]{:S(2)}) collective-permute-start(bf16[2,512,1024]{2,1,0:T(8,128)(2,1)} %get-tuple-element.17.refs_8_.refs_3_), channel_id=1, source_target_pairs={{0,2},{1,3},{2,0},{3,1},{4,6},{5,7},{6,4},{7,5},{8,10},{9,11},{10,... | collective-permute-start | bytes 6291464 | tf_op jit(solution)/shard_map/ppermute | solution.py:17
  8.6 13.4 %collective-permute-start.2 = (bf16[64,2176]{1,0:T(8,128)(2,1)S(1)}, bf16[64,2176]{1,0:T(8,128)(2,1)S(1)}, u32[]{:S(2)}, u32[]{:S(2)}) collective-permute-start(bf16[64,2176]{1,0:T(8,128)(2,1)S(1)} %shard_map.111), channel_id=1, source_target_pairs={{0,8},{4,12},{8,0},{12,4},{16,24},{20,28},{24,16},{28,20},{1,9},{5... | collective-permute-start | bytes 835592 | tf_op jit(solution)/shard_map/ppermute | solution.py:17
  10.2 11.8 %collective-permute-start = (bf16[64,2176]{1,0:T(8,128)(2,1)S(1)}, bf16[64,2176]{1,0:T(8,128)(2,1)S(1)}, u32[]{:S(2)}, u32[]{:S(2)}) collective-permute-start(bf16[64,2176]{1,0:T(8,128)(2,1)S(1)} %shard_map.111), channel_id=1, source_target_pairs={{0,4},{4,0},{8,12},{12,8},{16,20},{20,16},{24,28},{28,24},{1,5},{5... | collective-permute-start | bytes 835592 | tf_op jit(solution)/shard_map/ppermute | solution.py:17
  11.7 16.4 %collective-permute-start.4 = (bf16[64,2176]{1,0:T(8,128)(2,1)S(1)}, bf16[64,2176]{1,0:T(8,128)(2,1)S(1)}, u32[]{:S(2)}, u32[]{:S(2)}) collective-permute-start(bf16[64,2176]{1,0:T(8,128)(2,1)S(1)} %shard_map.111), channel_id=1, source_target_pairs={{0,16},{4,20},{8,24},{12,28},{16,0},{20,4},{24,8},{28,12},{1,17},{... | collective-permute-start | bytes 835592 | tf_op jit(solution)/shard_map/ppermute | solution.py:17
  22.1 13.9 %copy-start.1 = (bf16[64,2176]{1,0:T(8,128)(2,1)}, bf16[64,2176]{1,0:T(8,128)(2,1)S(1)}, u32[]{:S(2)}) copy-start(bf16[64,2176]{1,0:T(8,128)(2,1)S(1)} %collective-permute-done.refs_1_.refs_5_) | copy-start | bytes 835588
  22.1 8.7 %collective-permute-start.3 = (bf16[64,2176]{1,0:T(8,128)(2,1)S(1)}, bf16[64,2176]{1,0:T(8,128)(2,1)S(1)}, u32[]{:S(2)}, u32[]{:S(2)}) collective-permute-start(bf16[64,2176]{1,0:T(8,128)(2,1)S(1)} %shard_map.114), channel_id=1, source_target_pairs={{0,4},{4,0},{8,12},{12,8},{16,20},{20,16},{24,28},{28,24},{1,5},{5... | collective-permute-start | bytes 835592 | tf_op jit(solution)/shard_map/ppermute | solution.py:17
  24.6 11.4 %collective-permute-start.6 = (bf16[64,2176]{1,0:T(8,128)(2,1)S(1)}, bf16[64,2176]{1,0:T(8,128)(2,1)S(1)}, u32[]{:S(2)}, u32[]{:S(2)}) collective-permute-start(bf16[64,2176]{1,0:T(8,128)(2,1)S(1)} %shard_map.111), channel_id=1, source_target_pairs={{0,24},{4,28},{8,16},{12,20},{16,8},{20,12},{24,0},{28,4},{1,25},{... | collective-permute-start | bytes 835592 | tf_op jit(solution)/shard_map/ppermute | solution.py:17
  30.8 7.3 %collective-permute-start.5 = (bf16[64,2176]{1,0:T(8,128)(2,1)S(1)}, bf16[64,2176]{1,0:T(8,128)(2,1)S(1)}, u32[]{:S(2)}, u32[]{:S(2)}) collective-permute-start(bf16[64,2176]{1,0:T(8,128)(2,1)S(1)} %shard_map.116), channel_id=1, source_target_pairs={{0,4},{4,0},{8,12},{12,8},{16,20},{20,16},{24,28},{28,24},{1,5},{5... | collective-permute-start | bytes 835592 | tf_op jit(solution)/shard_map/ppermute | solution.py:17
  32.5 67.1 %collective-permute-start.13 = (bf16[2,512,1024]{2,1,0:T(8,128)(2,1)S(1)}, bf16[2,512,1024]{2,1,0:T(8,128)(2,1)}, u32[]{:S(2)}, u32[]{:S(2)}) collective-permute-start(bf16[2,512,1024]{2,1,0:T(8,128)(2,1)S(1)} %collective-permute-done.12.refs_9_), channel_id=1, source_target_pairs={{0,2},{1,3},{2,0},{3,1},{4,6},{5,7},{6,4},{7,5},{8,10},{9,11},{10,... | collective-permute-start | bytes 6291464 | tf_op jit(solution)/shard_map/ppermute | solution.py:17
  35.9 19.7 %collective-permute-start.14 = (bf16[1,512,1024]{2,1,0:T(8,128)(2,1)}, bf16[1,512,1024]{2,1,0:T(8,128)(2,1)}, u32[]{:S(2)}, u32[]{:S(2)}) collective-permute-start(bf16[1,512,1024]{2,1,0:T(8,128)(2,1)} %shard_map.121), channel_id=1, source_target_pairs={{0,1},{1,0},{2,3},{3,2},{4,5},{5,4},{6,7},{7,6},{8,9},{9,8},{10,11... | collective-permute-start | bytes 3145736 | tf_op jit(solution)/shard_map/ppermute | solution.py:17
  38.0 7.2 %collective-permute-start.7 = (bf16[64,2176]{1,0:T(8,128)(2,1)S(1)}, bf16[64,2176]{1,0:T(8,128)(2,1)S(1)}, u32[]{:S(2)}, u32[]{:S(2)}) collective-permute-start(bf16[64,2176]{1,0:T(8,128)(2,1)S(1)} %shard_map.118), channel_id=1, source_target_pairs={{0,4},{4,0},{8,12},{12,8},{16,20},{20,16},{24,28},{28,24},{1,5},{5... | collective-permute-start | bytes 835592 | tf_op jit(solution)/shard_map/ppermute | solution.py:17
  49.5 79.0 %collective-permute-start.23 = (bf16[3,512,1024]{2,1,0:T(8,128)(2,1)}, bf16[3,512,1024]{2,1,0:T(8,128)(2,1)}, u32[]{:S(2)}, u32[]{:S(2)}) collective-permute-start(bf16[3,512,1024]{2,1,0:T(8,128)(2,1)} %shard_map.125), channel_id=1, source_target_pairs={{0,4},{4,8},{8,12},{12,16},{16,20},{20,24},{24,28},{28,0},{1,5},{5... | collective-permute-start | bytes 9437192 | tf_op jit(solution)/shard_map/ppermute | solution.py:22
  54.6 6.0 %collective-permute-start.11 = (bf16[128,2176]{1,0:T(8,128)(2,1)S(1)}, bf16[128,2176]{1,0:T(8,128)(2,1)S(1)}, u32[]{:S(2)}, u32[]{:S(2)}) collective-permute-start(bf16[128,2176]{1,0:T(8,128)(2,1)S(1)} %shard_map.119.refs_3_), channel_id=1, source_target_pairs={{0,1},{1,0},{2,3},{3,2},{4,5},{5,4},{6,7},{7,6},{8,9},{9,8},{10,11... | collective-permute-start | bytes 1671176 | tf_op jit(solution)/shard_map/ppermute | solution.py:17
  54.6 6.8 %collective-permute-start.10 = (bf16[128,2176]{1,0:T(8,128)(2,1)S(1)}, bf16[128,2176]{1,0:T(8,128)(2,1)}, u32[]{:S(2)}, u32[]{:S(2)}) collective-permute-start(bf16[128,2176]{1,0:T(8,128)(2,1)S(1)} %shard_map.117.refs_2_), channel_id=1, source_target_pairs={{0,1},{1,0},{2,3},{3,2},{4,5},{5,4},{6,7},{7,6},{8,9},{9,8},{10,11... | collective-permute-start | bytes 1671176 | tf_op jit(solution)/shard_map/ppermute | solution.py:17
  58.5 63.2 %collective-permute-start.17 = (bf16[512,1024]{1,0:T(8,128)(2,1)}, bf16[512,1024]{1,0:T(8,128)(2,1)S(1)}, u32[]{:S(2)}, u32[]{:S(2)}) collective-permute-start(bf16[512,1024]{1,0:T(8,128)(2,1)} %get-tuple-element.19.refs_0_), channel_id=1, source_target_pairs={{0,2},{1,3},{2,0},{3,1},{4,6},{5,7},{6,4},{7,5},{8,10},{9,11},{10,... | collective-permute-start | bytes 3145736 | tf_op jit(solution)/shard_map/ppermute | solution.py:17
  60.6 39.1 %copy-start = (bf16[2,512,1024]{2,1,0:T(8,128)(2,1)S(1)}, bf16[2,512,1024]{2,1,0:T(8,128)(2,1)}, u32[]{:S(2)}) copy-start(bf16[2,512,1024]{2,1,0:T(8,128)(2,1)} %get-tuple-element.17.refs_8_.refs_3_) | copy-start | bytes 6291460
  60.6 52.4 %copy-start.7 = (bf16[512,1024]{1,0:T(8,128)(2,1)S(1)}, bf16[512,1024]{1,0:T(8,128)(2,1)}, u32[]{:S(2)}) copy-start(bf16[512,1024]{1,0:T(8,128)(2,1)} %get-tuple-element.19.refs_0_) | copy-start | bytes 3145732
  61.4 2.0 %collective-permute-start.9 = (bf16[128,2176]{1,0:T(8,128)(2,1)S(1)}, bf16[128,2176]{1,0:T(8,128)(2,1)S(1)}, u32[]{:S(2)}, u32[]{:S(2)}) collective-permute-start(bf16[128,2176]{1,0:T(8,128)(2,1)S(1)} %shard_map.115.refs_1_), channel_id=1, source_target_pairs={{0,1},{1,0},{2,3},{3,2},{4,5},{5,4},{6,7},{7,6},{8,9},{9,8},{10,11... | collective-permute-start | bytes 1671176 | tf_op jit(solution)/shard_map/ppermute | solution.py:17
  61.4 2.7 %collective-permute-start.8 = (bf16[128,2176]{1,0:T(8,128)(2,1)S(1)}, bf16[128,2176]{1,0:T(8,128)(2,1)S(1)}, u32[]{:S(2)}, u32[]{:S(2)}) collective-permute-start(bf16[128,2176]{1,0:T(8,128)(2,1)S(1)} %shard_map.113.refs_0_), channel_id=1, source_target_pairs={{0,1},{1,0},{2,3},{3,2},{4,5},{5,4},{6,7},{7,6},{8,9},{9,8},{10,11... | collective-permute-start | bytes 1671176 | tf_op jit(solution)/shard_map/ppermute | solution.py:17
  116.6 8.5 %collective-permute-start.15 = (bf16[512,1024]{1,0:T(8,128)(2,1)S(1)}, bf16[512,1024]{1,0:T(8,128)(2,1)S(1)}, u32[]{:S(2)}, u32[]{:S(2)}) collective-permute-start(bf16[512,1024]{1,0:T(8,128)(2,1)S(1)} %get-tuple-element.22.refs_1_), channel_id=1, source_target_pairs={{0,1},{1,0},{2,3},{3,2},{4,5},{5,4},{6,7},{7,6},{8,9},{9,8},{10,11... | collective-permute-start | bytes 3145736 | tf_op jit(solution)/shard_map/ppermute | solution.py:17
  123.0 2.0 %collective-permute-start.18 = (bf16[512,512]{1,0:T(8,128)(2,1)S(1)}, bf16[512,512]{1,0:T(8,128)(2,1)S(1)}, u32[]{:S(2)}, u32[]{:S(2)}) collective-permute-start(bf16[512,512]{1,0:T(8,128)(2,1)S(1)} %get-tuple-element.24.refs_1_), channel_id=1, source_target_pairs={{0,1},{1,0},{2,3},{3,2},{4,5},{5,4},{6,7},{7,6},{8,9},{9,8},{10,11... | collective-permute-start | bytes 1572872 | tf_op jit(solution)/shard_map/ppermute | solution.py:17
  123.1 25.8 %collective-permute-start.22 = (bf16[512,1024]{1,0:T(8,128)(2,1)}, bf16[512,1024]{1,0:T(8,128)(2,1)S(1)}, u32[]{:S(2)}, u32[]{:S(2)}) collective-permute-start(bf16[512,1024]{1,0:T(8,128)(2,1)} %get-tuple-element.20.refs_1_), channel_id=1, source_target_pairs={{0,2},{1,3},{2,0},{3,1},{4,6},{5,7},{6,4},{7,5},{8,10},{9,11},{10,... | collective-permute-start | bytes 3145736 | tf_op jit(solution)/shard_map/ppermute | solution.py:17
  125.7 19.8 %collective-permute-start.16 = (bf16[2,128,1024]{2,1,0:T(8,128)(2,1)S(1)}, bf16[2,128,1024]{2,1,0:T(8,128)(2,1)S(1)}, u32[]{:S(2)}, u32[]{:S(2)}) collective-permute-start(bf16[2,128,1024]{2,1,0:T(8,128)(2,1)S(1)} %fusion.3), channel_id=1, source_target_pairs={{0,8},{4,12},{8,0},{12,4},{16,24},{20,28},{24,16},{28,20},{1,9},{5... | collective-permute-start | bytes 1572872 | tf_op jit(solution)/shard_map/ppermute | solution.py:17
  128.3 17.1 %collective-permute-start.19 = (bf16[2,128,512]{2,1,0:T(8,128)(2,1)}, bf16[2,128,512]{2,1,0:T(8,128)(2,1)S(1)}, u32[]{:S(2)}, u32[]{:S(2)}) collective-permute-start(bf16[2,128,512]{2,1,0:T(8,128)(2,1)} %fusion.9), channel_id=1, source_target_pairs={{0,8},{4,12},{8,0},{12,4},{16,24},{20,28},{24,16},{28,20},{1,9},{5... | collective-permute-start | bytes 786440 | tf_op jit(solution)/shard_map/ppermute | solution.py:17
  134.6 14.3 %copy-start.6 = (bf16[2,512,1024]{2,1,0:T(8,128)(2,1)S(1)}, bf16[2,512,1024]{2,1,0:T(8,128)(2,1)}, u32[]{:S(2)}) copy-start(bf16[2,512,1024]{2,1,0:T(8,128)(2,1)} %get-tuple-element.14.refs_2_) | copy-start | bytes 6291460
  150.2 2.1 %collective-permute-start.24 = (bf16[512,512]{1,0:T(8,128)(2,1)S(1)}, bf16[512,512]{1,0:T(8,128)(2,1)S(1)}, u32[]{:S(2)}, u32[]{:S(2)}) collective-permute-start(bf16[512,512]{1,0:T(8,128)(2,1)S(1)} %get-tuple-element.27), channel_id=1, source_target_pairs={{0,1},{1,0},{2,3},{3,2},{4,5},{5,4},{6,7},{7,6},{8,9},{9,8},{10,11... | collective-permute-start | bytes 1572872 | tf_op jit(solution)/shard_map/ppermute | solution.py:17
  150.5 11.6 %collective-permute-start.20 = (bf16[2,64,1536]{2,1,0:T(8,128)(2,1)S(1)}, bf16[2,64,1536]{2,1,0:T(8,128)(2,1)S(1)}, u32[]{:S(2)}, u32[]{:S(2)}) collective-permute-start(bf16[2,64,1536]{2,1,0:T(8,128)(2,1)S(1)} %fusion.6), channel_id=1, source_target_pairs={{0,4},{4,0},{8,12},{12,8},{16,20},{20,16},{24,28},{28,24},{1,5},{5... | collective-permute-start | bytes 1179656 | tf_op jit(solution)/shard_map/ppermute | solution.py:17
  152.5 9.7 %collective-permute-start.25 = (bf16[2,128,512]{2,1,0:T(8,128)(2,1)S(1)}, bf16[2,128,512]{2,1,0:T(8,128)(2,1)S(1)}, u32[]{:S(2)}, u32[]{:S(2)}) collective-permute-start(bf16[2,128,512]{2,1,0:T(8,128)(2,1)S(1)} %fusion.10), channel_id=1, source_target_pairs={{0,8},{4,12},{8,0},{12,4},{16,24},{20,28},{24,16},{28,20},{1,9},{5... | collective-permute-start | bytes 786440 | tf_op jit(solution)/shard_map/ppermute | solution.py:17
  162.3 5.2 %collective-permute-start.26 = (bf16[2,64,512]{2,1,0:T(8,128)(2,1)S(1)}, bf16[2,64,512]{2,1,0:T(8,128)(2,1)S(1)}, u32[]{:S(2)}, u32[]{:S(2)}) collective-permute-start(bf16[2,64,512]{2,1,0:T(8,128)(2,1)S(1)} %fusion.15), channel_id=1, source_target_pairs={{0,4},{4,0},{8,12},{12,8},{16,20},{20,16},{24,28},{28,24},{1,5},{5... | collective-permute-start | bytes 393224 | tf_op jit(solution)/shard_map/ppermute | solution.py:17
  164.1 13.5 %collective-permute-start.21 = (bf16[1,64,1536]{2,1,0:T(8,128)(2,1)S(1)}, bf16[1,64,1536]{2,1,0:T(8,128)(2,1)S(1)}, u32[]{:S(2)}, u32[]{:S(2)}) collective-permute-start(bf16[1,64,1536]{2,1,0:T(8,128)(2,1)S(1)} %fusion.14), channel_id=1, source_target_pairs={{0,16},{4,20},{8,24},{12,28},{16,0},{20,4},{24,8},{28,12},{1,17},{... | collective-permute-start | bytes 589832 | tf_op jit(solution)/shard_map/ppermute | solution.py:17
  167.5 10.8 %collective-permute-start.27 = (bf16[1,64,512]{2,1,0:T(8,128)(2,1)S(1)}, bf16[1,64,512]{2,1,0:T(8,128)(2,1)S(1)}, u32[]{:S(2)}, u32[]{:S(2)}) collective-permute-start(bf16[1,64,512]{2,1,0:T(8,128)(2,1)S(1)} %fusion.19), channel_id=1, source_target_pairs={{0,16},{4,20},{8,24},{12,28},{16,0},{20,4},{24,8},{28,12},{1,17},{... | collective-permute-start | bytes 196616 | tf_op jit(solution)/shard_map/ppermute | solution.py:17
  (11 other events, 50.8 us)

commit v16 on v15

--- a/solution.py
+++ b/solution.py
@@ -117,13 +117,18 @@
 
 def order_kernel(mine_ref, other_ref, first_ref, second_ref, held, in_sems, out_sems):
     _, core, _ = position()
+    depth, cut = mine_ref.shape[1], first_ref.shape[0]
+
+    def rows(n):
+        return held.at[pl.ds(pl.multiple_of(n * depth, LANES), depth)]
+
     loads = [
-        pltpu.make_async_copy(mine_ref.at[core], held.at[core], in_sems.at[0]),
-        pltpu.make_async_copy(other_ref.at[0], held.at[1 - core], in_sems.at[1]),
+        pltpu.make_async_copy(mine_ref.at[core], rows(core), in_sems.at[0]),
+        pltpu.make_async_copy(other_ref.at[0], rows(1 - core), in_sems.at[1]),
     ]
     stores = [
-        pltpu.make_async_copy(held.at[n], out, out_sems.at[n])
-        for n, out in enumerate((first_ref, second_ref))
+        pltpu.make_async_copy(held.at[pl.ds(0, cut)], first_ref, out_sems.at[0]),
+        pltpu.make_async_copy(held.at[pl.ds(cut, 2 * depth - cut)], second_ref, out_sems.at[1]),
     ]
     for c in loads:
         c.start()
@@ -135,16 +140,23 @@
         c.wait()
 
 
+def cut_of(depth):
+    return max(LANES, 3 * depth // 4)
+
+
 def in_order(w_down, other):
     anywhere = pl.BlockSpec(memory_space=pl.ANY)
-    slot = w_down.shape[1:]
+    depth, ff = w_down.shape[1:]
+    cut = cut_of(depth)
     return pl.pallas_call(
         order_kernel,
         in_specs=[anywhere] * 2,
         out_specs=(anywhere,) * 2,
-        out_shape=(jax.ShapeDtypeStruct(slot, w_down.dtype),) * 2,
+        out_shape=tuple(
+            jax.ShapeDtypeStruct((n, ff), w_down.dtype) for n in (cut, 2 * depth - cut)
+        ),
         scratch_shapes=[
-            pltpu.VMEM((2,) + slot, w_down.dtype),
+            pltpu.VMEM((2 * depth, ff), w_down.dtype),
             pltpu.SemaphoreType.DMA((2,)),
             pltpu.SemaphoreType.DMA((2,)),
         ],
@@ -223,25 +235,26 @@
 
 def down_kernel(n_downs, hidden_ref, *refs):
     downs, (kept_ref, sent_ref) = refs[:n_downs], refs[-2:]
-    depth = downs[0].shape[0]
     rows = kept_ref.shape[0]
     tile = min(rows, 512)
     contract = (((1,), (1,)), ((), ()))
-    for i, w in enumerate(downs):
+    left = 0
+    for w in downs:
+        right = left + w.shape[0]
         for out, base in ((kept_ref, 0), (sent_ref, rows)):
             for top in range(0, rows, tile):
                 part = lax.dot_general(
                     hidden_ref[base + top : base + top + tile], w[...], contract,
                     preferred_element_type=jnp.float32,
                 )
-                out[top : top + tile, i * depth : (i + 1) * depth] = part.astype(out.dtype)
+                out[top : top + tile, left:right] = part.astype(out.dtype)
+        left = right
 
 
 def down_of(hidden, downs, after):
-    depth, ff = downs[0].shape
     rows = hidden.shape[0] // 2
     vmem = pl.BlockSpec(memory_space=pltpu.VMEM)
-    out = jax.ShapeDtypeStruct((rows, len(downs) * depth), hidden.dtype)
+    out = jax.ShapeDtypeStruct((rows, sum(d.shape[0] for d in downs)), hidden.dtype)
     return pl.pallas_call(
         functools.partial(down_kernel, len(downs)),
         in_specs=[vmem] * (1 + len(downs)) + [pl.BlockSpec(memory_space=pl.ANY)] * len(after),
@@ -275,17 +288,20 @@
 
 
 def place_kernel(depth, *refs):
-    parts, out_ref = refs[:-1], refs[-1]
+    (first_ref, second_ref), out_ref = refs[:2], refs[2]
     pair, _, _ = position()
-    for part, blocks in zip(parts, out_blocks(depth, [p.shape[1] for p in parts])):
-        for n, (j, core) in enumerate(blocks):
-            start = pl.multiple_of((2 * (pair ^ j) + core) * depth, LANES)
-            out_ref[:, pl.ds(start, depth)] = part[:, n * depth : (n + 1) * depth]
-
-
-def out_blocks(depth, widths):
-    others = range(1, widths[1] // depth + 1)
-    return [[(0, 0), (0, 1)] + [(j, 0) for j in others], [(j, 1) for j in others]]
+    cut = cut_of(depth)
+
+    def put(j, offset, block):
+        start = pl.multiple_of(2 * (pair ^ j) * depth + offset, LANES)
+        out_ref[:, pl.ds(start, block.shape[1])] = block
+
+    put(0, 0, first_ref[:, : 2 * depth])
+    rest = 2 * depth - cut
+    for j in range(1, second_ref.shape[1] // rest + 1):
+        left = 2 * depth + (j - 1) * cut
+        put(j, 0, first_ref[:, left : left + cut])
+        put(j, cut, second_ref[:, (j - 1) * rest : j * rest])
 
 
 def placed(parts, depth, width):
@@ -334,12 +350,11 @@
         places, (arrive, w_gate, w_up, w_down), (2, 2, 2),
     )
 
-    groups = [[d[0] for d in downs]] + [d[1:] for d in downs]
-    kept, sent = down_of(hidden, groups[0], ())
+    kept, sent = down_of(hidden, [d[0] for d in downs], ())
     own_rows = step_z(over_core(kept, sent, tok), 1)
-    kept, sent = down_of(hidden, groups[1], (sent,))
+    kept, sent = down_of(hidden, downs[0][1:], (sent,))
     first_rows = step_z(over_core(kept, sent, tok), 1)
-    kept, sent = down_of(hidden, groups[2], (sent, news[0], own_rows, first_rows))
+    kept, sent = down_of(hidden, downs[1][1:], (sent, news[0], own_rows, first_rows))
     early = over_x(jnp.concatenate([own_rows, first_rows], axis=-1))
     late = over_x(step_z(over_core(kept, sent, tok), 1))
     parts = [over_z(early, 2), over_z(late, 2)]

time: 179 us -> 184 us (1.028)
  local copies, waits for them, and re-layouts: 4.06 us -> 6.3 us
    unnamed x33 -> x41, local copies, waits for them, and re-layouts: 3.12 us -> 6.07 us
  transfers between devices with their start and end apart: 28 -> 28, of which waited for: 17 -> 16; matrix products, arithmetic and copies ran while one was open for 2% -> 1% of each run, Pallas kernels for 19% -> 19%
where the time goes in v16:
time: 184 us; the launch traced here: 183 us
  waiting for transfers between devices  95.7 us (52%)
  Pallas kernels  40.7 us (22%)
  starting transfers between devices  37 us (20%)
  local copies, waits for them, and re-layouts  6.3 us (3%)
  other arithmetic  2.26 us (1%)
    ppermute x27, waiting for transfers between devices, swap(): lax.ppermute(x, axis, [(i, i ^ bit) for i in range(lax.axis_size(axis))])  95.7 us
    ppermute x27, starting transfers between devices, swap(): lax.ppermute(x, axis, [(i, i ^ bit) for i in range(lax.axis_size(axis))])  36.1 us
    pallas_call x4, Pallas kernels, copies(): pl.pallas_call(functools.partial(copy_kernel, plan, len(ins), len(counts)...  16.7 us
    pallas_call x1, Pallas kernels, hidden_of(): pl.pallas_call(functools.partial(hidden_kernel, len(pieces)), grid=(ff //...  12.4 us
    pallas_call x3, Pallas kernels, down_of(): pl.pallas_call(functools.partial(down_kernel, len(downs)), in_specs=[vmem...  7.28 us
    unnamed x41, local copies, waits for them, and re-layouts  6.07 us
  transfers between devices with their start and end apart: 28, of which 16 were waited for; matrix products, arithmetic and copies ran while one was open for 1% of the time, Pallas kernels for 19%

profile of v16, /device:TPU:0, one launch (start us, length us, event | category | flops | bytes accessed | tf_op | source)
XLA Modules:
  0.0 183.0 jit_solution(18258330316592181891)
XLA Ops:
  0.7 4.1 %shard_map.112 = (bf16[2,512,1024]{2,1,0:T(8,128)(2,1)}, bf16[2,512,1024]{2,1,0:T(8,128)(2,1)}) custom-call(s32[16]{0:T(128)} %refs_0_.7, s32[16]{0:T(128)} %refs_1_.7, bf16[2,512,1024]{2,1,0:T(8,128)(2,1)} %refs_3_.5, bf16[2,512,1024]{2,1,0:T(8,128)(2,1)} %refs_4_.3), custom_call_target="tpu_custom_call" | custom-call | tf_op jit(solution)/shard_map/pallas_call | solution.py:102
  5.3 2.6 %collective-permute-start.1 = (bf16[2,512,1024]{2,1,0:T(8,128)(2,1)}, bf16[2,512,1024]{2,1,0:T(8,128)(2,1)S(1)}, u32[]{:S(2)}, u32[]{:S(2)}) collective-permute-start(bf16[2,512,1024]{2,1,0:T(8,128)(2,1)} %get-tuple-element.17.refs_8_.refs_3_), channel_id=1, source_target_pairs={{0,2},{1,3},{2,0},{3,1},{4,6},{5,7},{6,4},{7,5},{8,10},{9,11},{10,... | collective-permute-start | bytes 6291464 | tf_op jit(solution)/shard_map/ppermute | solution.py:17
  8.6 1.6 collective-permute-start.2
  11.7 2.6 %collective-permute-start.4 = (bf16[64,2176]{1,0:T(8,128)(2,1)S(1)}, bf16[64,2176]{1,0:T(8,128)(2,1)S(1)}, u32[]{:S(2)}, u32[]{:S(2)}) collective-permute-start(bf16[64,2176]{1,0:T(8,128)(2,1)S(1)} %shard_map.111), channel_id=1, source_target_pairs={{0,16},{4,20},{8,24},{12,28},{16,0},{20,4},{24,8},{28,12},{1,17},{... | collective-permute-start | bytes 835592 | tf_op jit(solution)/shard_map/ppermute | solution.py:17
  14.3 7.7 %collective-permute-done.2 = bf16[64,2176]{1,0:T(8,128)(2,1)S(1)} collective-permute-done((bf16[64,2176]{1,0:T(8,128)(2,1)S(1)}, bf16[64,2176]{1,0:T(8,128)(2,1)S(1)}, u32[]{:S(2)}, u32[]{:S(2)}) %collective-permute-start.2) | collective-permute-done | bytes 278560 | tf_op jit(solution)/shard_map/ppermute | solution.py:17
  22.1 2.5 %collective-permute-start.3 = (bf16[64,2176]{1,0:T(8,128)(2,1)S(1)}, bf16[64,2176]{1,0:T(8,128)(2,1)S(1)}, u32[]{:S(2)}, u32[]{:S(2)}) collective-permute-start(bf16[64,2176]{1,0:T(8,128)(2,1)S(1)} %shard_map.114), channel_id=1, source_target_pairs={{0,4},{4,0},{8,12},{12,8},{16,20},{20,16},{24,28},{28,24},{1,5},{5... | collective-permute-start | bytes 835592 | tf_op jit(solution)/shard_map/ppermute | solution.py:17
  24.6 2.5 %collective-permute-start.6 = (bf16[64,2176]{1,0:T(8,128)(2,1)S(1)}, bf16[64,2176]{1,0:T(8,128)(2,1)S(1)}, u32[]{:S(2)}, u32[]{:S(2)}) collective-permute-start(bf16[64,2176]{1,0:T(8,128)(2,1)S(1)} %shard_map.111), channel_id=1, source_target_pairs={{0,24},{4,28},{8,16},{12,20},{16,8},{20,12},{24,0},{28,4},{1,25},{... | collective-permute-start | bytes 835592 | tf_op jit(solution)/shard_map/ppermute | solution.py:17
  28.1 2.7 %collective-permute-done.3.refs_1_.refs_6_ = bf16[64,2176]{1,0:T(8,128)(2,1)S(1)} collective-permute-done((bf16[64,2176]{1,0:T(8,128)(2,1)S(1)}, bf16[64,2176]{1,0:T(8,128)(2,1)S(1)}, u32[]{:S(2)}, u32[]{:S(2)}) %collective-permute-start.3) | collective-permute-done | bytes 278560 | tf_op jit(solution)/shard_map/ppermute | solution.py:17
  30.8 1.7 collective-permute-start.5
  33.0 2.9 %shard_map.121 = bf16[1,512,1024]{2,1,0:T(8,128)(2,1)} custom-call(s32[16]{0:T(128)} %refs_0_.7, s32[16]{0:T(128)} %refs_1_.7, bf16[2,512,1024]{2,1,0:T(8,128)(2,1)} %refs_5_.1, bf16[2,512,1024]{2,1,0:T(8,128)(2,1)} %get-tuple-element.17.refs_8_.refs_3_), custom_call_target="tpu_custom_call" | custom-call | tf_op jit(solution)/shard_map/pallas_call | solution.py:102
  36.0 2.0 %collective-permute-done.5.refs_1_.refs_7_ = bf16[64,2176]{1,0:T(8,128)(2,1)S(1)} collective-permute-done((bf16[64,2176]{1,0:T(8,128)(2,1)S(1)}, bf16[64,2176]{1,0:T(8,128)(2,1)S(1)}, u32[]{:S(2)}, u32[]{:S(2)}) %collective-permute-start.5) | collective-permute-done | bytes 278560 | tf_op jit(solution)/shard_map/ppermute | solution.py:17
  39.5 5.7 %collective-permute-done.7.refs_8_ = bf16[64,2176]{1,0:T(8,128)(2,1)S(1)} collective-permute-done((bf16[64,2176]{1,0:T(8,128)(2,1)S(1)}, bf16[64,2176]{1,0:T(8,128)(2,1)S(1)}, u32[]{:S(2)}, u32[]{:S(2)}) %collective-permute-start.7) | collective-permute-done | bytes 278560 | tf_op jit(solution)/shard_map/ppermute | solution.py:17
  45.9 3.6 %shard_map.125 = bf16[3,512,1024]{2,1,0:T(8,128)(2,1)} custom-call(s32[16]{0:T(128)} %refs_0_.7, s32[16]{0:T(128)} %refs_1_.7, bf16[2,512,1024]{2,1,0:T(8,128)(2,1)} %refs_3_.5, bf16[2,512,1024]{2,1,0:T(8,128)(2,1)} %refs_4_.3, bf16[2,512,1024]{2,1,0:T(8,128)(2,1)} %refs_5_.1, bf16[64,2176]{1,0:T(8,128)(2,1)} %copy-done.3, bf16[64,2176]{1,0:T(8,128)(2,1)} %copy-done.5, ...), custom_call_target="tpu_custom_call" | custom-call | tf_op jit(solution)/shard_map/pallas_call | solution.py:102
  51.4 3.2 %collective-permute-done.1.refs_1_.refs_10_ = bf16[2,512,1024]{2,1,0:T(8,128)(2,1)S(1)} collective-permute-done((bf16[2,512,1024]{2,1,0:T(8,128)(2,1)}, bf16[2,512,1024]{2,1,0:T(8,128)(2,1)S(1)}, u32[]{:S(2)}, u32[]{:S(2)}) %collective-permute-start.1) | collective-permute-done | bytes 2097184 | tf_op jit(solution)/shard_map/ppermute | solution.py:17
  57.0 2.9 %shard_map.122 = (bf16[384,1024]{1,0:T(8,128)(2,1)}, bf16[640,1024]{1,0:T(8,128)(2,1)}) custom-call(bf16[2,512,1024]{2,1,0:T(8,128)(2,1)} %refs_5_.1, bf16[1,512,1024]{2,1,0:T(8,128)(2,1)} %collective-permute-done.14.other_ref), custom_call_target="tpu_custom_call" | custom-call | tf_op jit(solution)/shard_map/pallas_call | solution.py:151
  59.9 2.0 %collective-permute-start.17 = (bf16[384,1024]{1,0:T(8,128)(2,1)}, bf16[384,1024]{1,0:T(8,128)(2,1)S(1)}, u32[]{:S(2)}, u32[]{:S(2)}) collective-permute-start(bf16[384,1024]{1,0:T(8,128)(2,1)} %get-tuple-element.19.refs_0_), channel_id=1, source_target_pairs={{0,2},{1,3},{2,0},{3,1},{4,6},{5,7},{6,4},{7,5},{8,10},{9,11},{10,... | collective-permute-start | bytes 2359304 | tf_op jit(solution)/shard_map/ppermute | solution.py:17
  62.8 36.9 %collective-permute-done.13.refs_11_ = bf16[2,512,1024]{2,1,0:T(8,128)(2,1)} collective-permute-done((bf16[2,512,1024]{2,1,0:T(8,128)(2,1)}, bf16[2,512,1024]{2,1,0:T(8,128)(2,1)}, u32[]{:S(2)}, u32[]{:S(2)}) %collective-permute-start.13) | collective-permute-done | bytes 2097184 | tf_op jit(solution)/shard_map/ppermute | solution.py:17
  102.8 12.4 %shard_map.120.hidden_ref = bf16[1024,1024]{1,0:T(8,128)(2,1)S(1)} custom-call(bf16[128,2176]{1,0:T(8,128)(2,1)S(1)} %shard_map.113.refs_0_, bf16[128,2176]{1,0:T(8,128)(2,1)S(1)} %copy-done.2, bf16[128,2176]{1,0:T(8,128)(2,1)S(1)} %shard_map.117.refs_2_, bf16[128,2176]{1,0:T(8,128)(2,1)S(1)} %shard_map.119.refs_3_, ...), custom_call_target="tpu_custom_call" | custom-call | flops 1 | bytes 1 | tf_op jit(solution)/shard_map/pallas_call | solution.py:220
  115.3 4.2 %shard_map.123 = (bf16[512,1024]{1,0:T(8,128)(2,1)S(1)}, bf16[512,1024]{1,0:T(8,128)(2,1)S(1)}) custom-call(bf16[1024,1024]{1,0:T(8,128)(2,1)S(1)} %shard_map.120.hidden_ref, bf16[384,1024]{1,0:T(8,128)(2,1)S(1)} %copy-done.9, bf16[640,1024]{1,0:T(8,128)(2,1)} %get-tuple-element.20.refs_1_), custom_call_target="tpu_custom_call" | custom-call | flops 1 | bytes 1 | tf_op jit(solution)/shard_map/pallas_call | solution.py:258
  121.4 1.9 %collective-permute-start.22 = (bf16[640,1024]{1,0:T(8,128)(2,1)}, bf16[640,1024]{1,0:T(8,128)(2,1)S(1)}, u32[]{:S(2)}, u32[]{:S(2)}) collective-permute-start(bf16[640,1024]{1,0:T(8,128)(2,1)} %get-tuple-element.20.refs_1_), channel_id=1, source_target_pairs={{0,2},{1,3},{2,0},{3,1},{4,6},{5,7},{6,4},{7,5},{8,10},{9,11},{10,... | collective-permute-start | bytes 3932168 | tf_op jit(solution)/shard_map/ppermute | solution.py:17
  123.9 1.6 collective-permute-start.16
  126.1 6.1 %shard_map.126 = (bf16[2,512,1024]{2,1,0:T(8,128)(2,1)}, bf16[2,512,1024]{2,1,0:T(8,128)(2,1)}, bf16[2,512,1024]{2,1,0:T(8,128)(2,1)}) custom-call(s32[16]{0:T(128)} %refs_0_.7, s32[16]{0:T(128)} %refs_1_.7, bf16[3,512,1024]{2,1,0:T(8,128)(2,1)} %collective-permute-done.23.refs_2_, bf16[2,512,1024]{2,1,0:T(8,128)(2,1)} %refs_3_.5, ...), custom_call_target="tpu_custom_call" | custom-call | tf_op jit(solution)/shard_map/pallas_call | solution.py:102
  132.2 9.8 %collective-permute-done.19 = bf16[2,128,384]{2,1,0:T(8,128)(2,1)S(1)} collective-permute-done((bf16[2,128,384]{2,1,0:T(8,128)(2,1)S(1)}, bf16[2,128,384]{2,1,0:T(8,128)(2,1)S(1)}, u32[]{:S(2)}, u32[]{:S(2)}) %collective-permute-start.19) | collective-permute-done | bytes 196640 | tf_op jit(solution)/shard_map/ppermute | solution.py:17
  142.3 10.3 %collective-permute-done.22.refs_0_ = bf16[640,1024]{1,0:T(8,128)(2,1)S(1)} collective-permute-done((bf16[640,1024]{1,0:T(8,128)(2,1)}, bf16[640,1024]{1,0:T(8,128)(2,1)S(1)}, u32[]{:S(2)}, u32[]{:S(2)}) %collective-permute-start.22) | collective-permute-done | bytes 1310752 | tf_op jit(solution)/shard_map/ppermute | solution.py:17
  152.6 1.8 shard_map.127
  154.6 1.8 collective-permute-start.20
  156.7 1.9 %collective-permute-start.25 = (bf16[2,128,640]{2,1,0:T(8,128)(2,1)S(1)}, bf16[2,128,640]{2,1,0:T(8,128)(2,1)S(1)}, u32[]{:S(2)}, u32[]{:S(2)}) collective-permute-start(bf16[2,128,640]{2,1,0:T(8,128)(2,1)S(1)} %fusion.9), channel_id=1, source_target_pairs={{0,8},{4,12},{8,0},{12,4},{16,24},{20,28},{24,16},{28,20},{1,9},{5... | collective-permute-start | bytes 983048 | tf_op jit(solution)/shard_map/ppermute | solution.py:17
  158.6 6.9 %collective-permute-done.20 = bf16[2,64,1408]{2,1,0:T(8,128)(2,1)S(1)} collective-permute-done((bf16[2,64,1408]{2,1,0:T(8,128)(2,1)S(1)}, bf16[2,64,1408]{2,1,0:T(8,128)(2,1)S(1)}, u32[]{:S(2)}, u32[]{:S(2)}) %collective-permute-start.20) | collective-permute-done | bytes 360480 | tf_op jit(solution)/shard_map/ppermute | solution.py:17
  166.7 1.7 collective-permute-start.26
  168.4 2.7 %collective-permute-start.21 = (bf16[1,64,1408]{2,1,0:T(8,128)(2,1)S(1)}, bf16[1,64,1408]{2,1,0:T(8,128)(2,1)S(1)}, u32[]{:S(2)}, u32[]{:S(2)}) collective-permute-start(bf16[1,64,1408]{2,1,0:T(8,128)(2,1)S(1)} %fusion.14), channel_id=1, source_target_pairs={{0,16},{4,20},{8,24},{12,28},{16,0},{20,4},{24,8},{28,12},{1,17},{... | collective-permute-start | bytes 540680 | tf_op jit(solution)/shard_map/ppermute | solution.py:17
  172.3 2.8 %collective-permute-start.27 = (bf16[1,64,640]{2,1,0:T(8,128)(2,1)S(1)}, bf16[1,64,640]{2,1,0:T(8,128)(2,1)S(1)}, u32[]{:S(2)}, u32[]{:S(2)}) collective-permute-start(bf16[1,64,640]{2,1,0:T(8,128)(2,1)S(1)} %fusion.19), channel_id=1, source_target_pairs={{0,16},{4,20},{8,24},{12,28},{16,0},{20,4},{24,8},{28,12},{1,17},{... | collective-permute-start | bytes 245768 | tf_op jit(solution)/shard_map/ppermute | solution.py:17
  175.1 6.3 %collective-permute-done.21 = bf16[1,64,1408]{2,1,0:T(8,128)(2,1)S(1)} collective-permute-done((bf16[1,64,1408]{2,1,0:T(8,128)(2,1)S(1)}, bf16[1,64,1408]{2,1,0:T(8,128)(2,1)S(1)}, u32[]{:S(2)}, u32[]{:S(2)}) %collective-permute-start.21) | collective-permute-done | bytes 180256 | tf_op jit(solution)/shard_map/ppermute | solution.py:17
  (105 shorter events, 22.6 us)
Async XLA Ops:
  4.8 27.7 %collective-permute-start.12 = (bf16[2,512,1024]{2,1,0:T(8,128)(2,1)}, bf16[2,512,1024]{2,1,0:T(8,128)(2,1)}, u32[]{:S(2)}, u32[]{:S(2)}) collective-permute-start(bf16[2,512,1024]{2,1,0:T(8,128)(2,1)} %get-tuple-element.18), channel_id=1, source_target_pairs={{0,1},{1,0},{2,3},{3,2},{4,5},{5,4},{6,7},{7,6},{8,9},{9,8},{10,11... | collective-permute-start | bytes 6291464 | tf_op jit(solution)/shard_map/ppermute | solution.py:17
  5.3 49.3 %collective-permute-start.1 = (bf16[2,512,1024]{2,1,0:T(8,128)(2,1)}, bf16[2,512,1024]{2,1,0:T(8,128)(2,1)S(1)}, u32[]{:S(2)}, u32[]{:S(2)}) collective-permute-start(bf16[2,512,1024]{2,1,0:T(8,128)(2,1)} %get-tuple-element.17.refs_8_.refs_3_), channel_id=1, source_target_pairs={{0,2},{1,3},{2,0},{3,1},{4,6},{5,7},{6,4},{7,5},{8,10},{9,11},{10,... | collective-permute-start | bytes 6291464 | tf_op jit(solution)/shard_map/ppermute | solution.py:17
  8.6 13.4 %collective-permute-start.2 = (bf16[64,2176]{1,0:T(8,128)(2,1)S(1)}, bf16[64,2176]{1,0:T(8,128)(2,1)S(1)}, u32[]{:S(2)}, u32[]{:S(2)}) collective-permute-start(bf16[64,2176]{1,0:T(8,128)(2,1)S(1)} %shard_map.111), channel_id=1, source_target_pairs={{0,8},{4,12},{8,0},{12,4},{16,24},{20,28},{24,16},{28,20},{1,9},{5... | collective-permute-start | bytes 835592 | tf_op jit(solution)/shard_map/ppermute | solution.py:17
  10.2 11.8 %collective-permute-start = (bf16[64,2176]{1,0:T(8,128)(2,1)S(1)}, bf16[64,2176]{1,0:T(8,128)(2,1)S(1)}, u32[]{:S(2)}, u32[]{:S(2)}) collective-permute-start(bf16[64,2176]{1,0:T(8,128)(2,1)S(1)} %shard_map.111), channel_id=1, source_target_pairs={{0,4},{4,0},{8,12},{12,8},{16,20},{20,16},{24,28},{28,24},{1,5},{5... | collective-permute-start | bytes 835592 | tf_op jit(solution)/shard_map/ppermute | solution.py:17
  11.7 16.4 %collective-permute-start.4 = (bf16[64,2176]{1,0:T(8,128)(2,1)S(1)}, bf16[64,2176]{1,0:T(8,128)(2,1)S(1)}, u32[]{:S(2)}, u32[]{:S(2)}) collective-permute-start(bf16[64,2176]{1,0:T(8,128)(2,1)S(1)} %shard_map.111), channel_id=1, source_target_pairs={{0,16},{4,20},{8,24},{12,28},{16,0},{20,4},{24,8},{28,12},{1,17},{... | collective-permute-start | bytes 835592 | tf_op jit(solution)/shard_map/ppermute | solution.py:17
  22.1 13.9 %copy-start.3 = (bf16[64,2176]{1,0:T(8,128)(2,1)}, bf16[64,2176]{1,0:T(8,128)(2,1)S(1)}, u32[]{:S(2)}) copy-start(bf16[64,2176]{1,0:T(8,128)(2,1)S(1)} %collective-permute-done.refs_1_.refs_5_) | copy-start | bytes 835588
  22.1 8.7 %collective-permute-start.3 = (bf16[64,2176]{1,0:T(8,128)(2,1)S(1)}, bf16[64,2176]{1,0:T(8,128)(2,1)S(1)}, u32[]{:S(2)}, u32[]{:S(2)}) collective-permute-start(bf16[64,2176]{1,0:T(8,128)(2,1)S(1)} %shard_map.114), channel_id=1, source_target_pairs={{0,4},{4,0},{8,12},{12,8},{16,20},{20,16},{24,28},{28,24},{1,5},{5... | collective-permute-start | bytes 835592 | tf_op jit(solution)/shard_map/ppermute | solution.py:17
  24.6 11.4 %collective-permute-start.6 = (bf16[64,2176]{1,0:T(8,128)(2,1)S(1)}, bf16[64,2176]{1,0:T(8,128)(2,1)S(1)}, u32[]{:S(2)}, u32[]{:S(2)}) collective-permute-start(bf16[64,2176]{1,0:T(8,128)(2,1)S(1)} %shard_map.111), channel_id=1, source_target_pairs={{0,24},{4,28},{8,16},{12,20},{16,8},{20,12},{24,0},{28,4},{1,25},{... | collective-permute-start | bytes 835592 | tf_op jit(solution)/shard_map/ppermute | solution.py:17
  30.8 7.3 %collective-permute-start.5 = (bf16[64,2176]{1,0:T(8,128)(2,1)S(1)}, bf16[64,2176]{1,0:T(8,128)(2,1)S(1)}, u32[]{:S(2)}, u32[]{:S(2)}) collective-permute-start(bf16[64,2176]{1,0:T(8,128)(2,1)S(1)} %shard_map.116), channel_id=1, source_target_pairs={{0,4},{4,0},{8,12},{12,8},{16,20},{20,16},{24,28},{28,24},{1,5},{5... | collective-permute-start | bytes 835592 | tf_op jit(solution)/shard_map/ppermute | solution.py:17
  32.5 67.1 %collective-permute-start.13 = (bf16[2,512,1024]{2,1,0:T(8,128)(2,1)}, bf16[2,512,1024]{2,1,0:T(8,128)(2,1)}, u32[]{:S(2)}, u32[]{:S(2)}) collective-permute-start(bf16[2,512,1024]{2,1,0:T(8,128)(2,1)} %collective-permute-done.12.refs_9_), channel_id=1, source_target_pairs={{0,2},{1,3},{2,0},{3,1},{4,6},{5,7},{6,4},{7,5},{8,10},{9,11},{10,... | collective-permute-start | bytes 6291464 | tf_op jit(solution)/shard_map/ppermute | solution.py:17
  35.9 19.8 %collective-permute-start.14 = (bf16[1,512,1024]{2,1,0:T(8,128)(2,1)}, bf16[1,512,1024]{2,1,0:T(8,128)(2,1)}, u32[]{:S(2)}, u32[]{:S(2)}) collective-permute-start(bf16[1,512,1024]{2,1,0:T(8,128)(2,1)} %shard_map.121), channel_id=1, source_target_pairs={{0,1},{1,0},{2,3},{3,2},{4,5},{5,4},{6,7},{7,6},{8,9},{9,8},{10,11... | collective-permute-start | bytes 3145736 | tf_op jit(solution)/shard_map/ppermute | solution.py:17
  38.0 7.2 %collective-permute-start.7 = (bf16[64,2176]{1,0:T(8,128)(2,1)S(1)}, bf16[64,2176]{1,0:T(8,128)(2,1)S(1)}, u32[]{:S(2)}, u32[]{:S(2)}) collective-permute-start(bf16[64,2176]{1,0:T(8,128)(2,1)S(1)} %shard_map.118), channel_id=1, source_target_pairs={{0,4},{4,0},{8,12},{12,8},{16,20},{20,16},{24,28},{28,24},{1,5},{5... | collective-permute-start | bytes 835592 | tf_op jit(solution)/shard_map/ppermute | solution.py:17
  49.5 76.6 %collective-permute-start.23 = (bf16[3,512,1024]{2,1,0:T(8,128)(2,1)}, bf16[3,512,1024]{2,1,0:T(8,128)(2,1)}, u32[]{:S(2)}, u32[]{:S(2)}) collective-permute-start(bf16[3,512,1024]{2,1,0:T(8,128)(2,1)} %shard_map.125), channel_id=1, source_target_pairs={{0,4},{4,8},{8,12},{12,16},{16,20},{20,24},{24,28},{28,0},{1,5},{5... | collective-permute-start | bytes 9437192 | tf_op jit(solution)/shard_map/ppermute | solution.py:22
  54.6 2.0 %collective-permute-start.11 = (bf16[128,2176]{1,0:T(8,128)(2,1)S(1)}, bf16[128,2176]{1,0:T(8,128)(2,1)S(1)}, u32[]{:S(2)}, u32[]{:S(2)}) collective-permute-start(bf16[128,2176]{1,0:T(8,128)(2,1)S(1)} %shard_map.119.refs_3_), channel_id=1, source_target_pairs={{0,1},{1,0},{2,3},{3,2},{4,5},{5,4},{6,7},{7,6},{8,9},{9,8},{10,11... | collective-permute-start | bytes 1671176 | tf_op jit(solution)/shard_map/ppermute | solution.py:17
  54.6 5.3 %collective-permute-start.10 = (bf16[128,2176]{1,0:T(8,128)(2,1)S(1)}, bf16[128,2176]{1,0:T(8,128)(2,1)}, u32[]{:S(2)}, u32[]{:S(2)}) collective-permute-start(bf16[128,2176]{1,0:T(8,128)(2,1)S(1)} %shard_map.117.refs_2_), channel_id=1, source_target_pairs={{0,1},{1,0},{2,3},{3,2},{4,5},{5,4},{6,7},{7,6},{8,9},{9,8},{10,11... | collective-permute-start | bytes 1671176 | tf_op jit(solution)/shard_map/ppermute | solution.py:17
  55.7 43.9 %copy-start = (bf16[2,512,1024]{2,1,0:T(8,128)(2,1)S(1)}, bf16[2,512,1024]{2,1,0:T(8,128)(2,1)}, u32[]{:S(2)}) copy-start(bf16[2,512,1024]{2,1,0:T(8,128)(2,1)} %get-tuple-element.17.refs_8_.refs_3_) | copy-start | bytes 6291460
  56.5 5.5 %collective-permute-start.9 = (bf16[128,2176]{1,0:T(8,128)(2,1)S(1)}, bf16[128,2176]{1,0:T(8,128)(2,1)S(1)}, u32[]{:S(2)}, u32[]{:S(2)}) collective-permute-start(bf16[128,2176]{1,0:T(8,128)(2,1)S(1)} %shard_map.115.refs_1_), channel_id=1, source_target_pairs={{0,1},{1,0},{2,3},{3,2},{4,5},{5,4},{6,7},{7,6},{8,9},{9,8},{10,11... | collective-permute-start | bytes 1671176 | tf_op jit(solution)/shard_map/ppermute | solution.py:17
  56.6 6.2 %collective-permute-start.8 = (bf16[128,2176]{1,0:T(8,128)(2,1)S(1)}, bf16[128,2176]{1,0:T(8,128)(2,1)}, u32[]{:S(2)}, u32[]{:S(2)}) collective-permute-start(bf16[128,2176]{1,0:T(8,128)(2,1)S(1)} %shard_map.113.refs_0_), channel_id=1, source_target_pairs={{0,1},{1,0},{2,3},{3,2},{4,5},{5,4},{6,7},{7,6},{8,9},{9,8},{10,11... | collective-permute-start | bytes 1671176 | tf_op jit(solution)/shard_map/ppermute | solution.py:17
  59.9 59.6 %collective-permute-start.17 = (bf16[384,1024]{1,0:T(8,128)(2,1)}, bf16[384,1024]{1,0:T(8,128)(2,1)S(1)}, u32[]{:S(2)}, u32[]{:S(2)}) collective-permute-start(bf16[384,1024]{1,0:T(8,128)(2,1)} %get-tuple-element.19.refs_0_), channel_id=1, source_target_pairs={{0,2},{1,3},{2,0},{3,1},{4,6},{5,7},{6,4},{7,5},{8,10},{9,11},{10,... | collective-permute-start | bytes 2359304 | tf_op jit(solution)/shard_map/ppermute | solution.py:17
  102.8 12.5 %copy-start.9 = (bf16[384,1024]{1,0:T(8,128)(2,1)S(1)}, bf16[384,1024]{1,0:T(8,128)(2,1)}, u32[]{:S(2)}) copy-start(bf16[384,1024]{1,0:T(8,128)(2,1)} %get-tuple-element.19.refs_0_) | copy-start | bytes 2359300
  119.5 3.9 %collective-permute-start.15 = (bf16[512,1024]{1,0:T(8,128)(2,1)S(1)}, bf16[512,1024]{1,0:T(8,128)(2,1)S(1)}, u32[]{:S(2)}, u32[]{:S(2)}) collective-permute-start(bf16[512,1024]{1,0:T(8,128)(2,1)S(1)} %get-tuple-element.22.refs_1_), channel_id=1, source_target_pairs={{0,1},{1,0},{2,3},{3,2},{4,5},{5,4},{6,7},{7,6},{8,9},{9,8},{10,11... | collective-permute-start | bytes 3145736 | tf_op jit(solution)/shard_map/ppermute | solution.py:17
  120.8 2.5 %collective-permute-start.18 = (bf16[512,384]{1,0:T(8,128)(2,1)S(1)}, bf16[512,384]{1,0:T(8,128)(2,1)S(1)}, u32[]{:S(2)}, u32[]{:S(2)}) collective-permute-start(bf16[512,384]{1,0:T(8,128)(2,1)S(1)} %get-tuple-element.24.refs_1_), channel_id=1, source_target_pairs={{0,1},{1,0},{2,3},{3,2},{4,5},{5,4},{6,7},{7,6},{8,9},{9,8},{10,11... | collective-permute-start | bytes 1179656 | tf_op jit(solution)/shard_map/ppermute | solution.py:17
  121.4 31.2 %collective-permute-start.22 = (bf16[640,1024]{1,0:T(8,128)(2,1)}, bf16[640,1024]{1,0:T(8,128)(2,1)S(1)}, u32[]{:S(2)}, u32[]{:S(2)}) collective-permute-start(bf16[640,1024]{1,0:T(8,128)(2,1)} %get-tuple-element.20.refs_1_), channel_id=1, source_target_pairs={{0,2},{1,3},{2,0},{3,1},{4,6},{5,7},{6,4},{7,5},{8,10},{9,11},{10,... | collective-permute-start | bytes 3932168 | tf_op jit(solution)/shard_map/ppermute | solution.py:17
  123.9 18.2 %collective-permute-start.16 = (bf16[2,128,1024]{2,1,0:T(8,128)(2,1)S(1)}, bf16[2,128,1024]{2,1,0:T(8,128)(2,1)S(1)}, u32[]{:S(2)}, u32[]{:S(2)}) collective-permute-start(bf16[2,128,1024]{2,1,0:T(8,128)(2,1)S(1)} %fusion.4), channel_id=1, source_target_pairs={{0,8},{4,12},{8,0},{12,4},{16,24},{20,28},{24,16},{28,20},{1,9},{5... | collective-permute-start | bytes 1572872 | tf_op jit(solution)/shard_map/ppermute | solution.py:17
  125.6 16.5 %collective-permute-start.19 = (bf16[2,128,384]{2,1,0:T(8,128)(2,1)S(1)}, bf16[2,128,384]{2,1,0:T(8,128)(2,1)S(1)}, u32[]{:S(2)}, u32[]{:S(2)}) collective-permute-start(bf16[2,128,384]{2,1,0:T(8,128)(2,1)S(1)} %fusion.12), channel_id=1, source_target_pairs={{0,8},{4,12},{8,0},{12,4},{16,24},{20,28},{24,16},{28,20},{1,9},{5... | collective-permute-start | bytes 589832 | tf_op jit(solution)/shard_map/ppermute | solution.py:17
  142.1 10.5 %copy-start.8 = (bf16[2,512,1024]{2,1,0:T(8,128)(2,1)S(1)}, bf16[2,512,1024]{2,1,0:T(8,128)(2,1)}, u32[]{:S(2)}) copy-start(bf16[2,512,1024]{2,1,0:T(8,128)(2,1)} %get-tuple-element.14.refs_2_) | copy-start | bytes 6291460
  154.4 2.2 %collective-permute-start.24 = (bf16[512,640]{1,0:T(8,128)(2,1)S(1)}, bf16[512,640]{1,0:T(8,128)(2,1)S(1)}, u32[]{:S(2)}, u32[]{:S(2)}) collective-permute-start(bf16[512,640]{1,0:T(8,128)(2,1)S(1)} %get-tuple-element.27), channel_id=1, source_target_pairs={{0,1},{1,0},{2,3},{3,2},{4,5},{5,4},{6,7},{7,6},{8,9},{9,8},{10,11... | collective-permute-start | bytes 1966088 | tf_op jit(solution)/shard_map/ppermute | solution.py:17
  154.6 10.9 %collective-permute-start.20 = (bf16[2,64,1408]{2,1,0:T(8,128)(2,1)S(1)}, bf16[2,64,1408]{2,1,0:T(8,128)(2,1)S(1)}, u32[]{:S(2)}, u32[]{:S(2)}) collective-permute-start(bf16[2,64,1408]{2,1,0:T(8,128)(2,1)S(1)} %fusion.6), channel_id=1, source_target_pairs={{0,4},{4,0},{8,12},{12,8},{16,20},{20,16},{24,28},{28,24},{1,5},{5... | collective-permute-start | bytes 1081352 | tf_op jit(solution)/shard_map/ppermute | solution.py:17
  156.7 9.9 %collective-permute-start.25 = (bf16[2,128,640]{2,1,0:T(8,128)(2,1)S(1)}, bf16[2,128,640]{2,1,0:T(8,128)(2,1)S(1)}, u32[]{:S(2)}, u32[]{:S(2)}) collective-permute-start(bf16[2,128,640]{2,1,0:T(8,128)(2,1)S(1)} %fusion.9), channel_id=1, source_target_pairs={{0,8},{4,12},{8,0},{12,4},{16,24},{20,28},{24,16},{28,20},{1,9},{5... | collective-permute-start | bytes 983048 | tf_op jit(solution)/shard_map/ppermute | solution.py:17
  166.7 5.5 %collective-permute-start.26 = (bf16[2,64,640]{2,1,0:T(8,128)(2,1)S(1)}, bf16[2,64,640]{2,1,0:T(8,128)(2,1)S(1)}, u32[]{:S(2)}, u32[]{:S(2)}) collective-permute-start(bf16[2,64,640]{2,1,0:T(8,128)(2,1)S(1)} %fusion.15), channel_id=1, source_target_pairs={{0,4},{4,0},{8,12},{12,8},{16,20},{20,16},{24,28},{28,24},{1,5},{5... | collective-permute-start | bytes 491528 | tf_op jit(solution)/shard_map/ppermute | solution.py:17
  168.4 12.9 %collective-permute-start.21 = (bf16[1,64,1408]{2,1,0:T(8,128)(2,1)S(1)}, bf16[1,64,1408]{2,1,0:T(8,128)(2,1)S(1)}, u32[]{:S(2)}, u32[]{:S(2)}) collective-permute-start(bf16[1,64,1408]{2,1,0:T(8,128)(2,1)S(1)} %fusion.14), channel_id=1, source_target_pairs={{0,16},{4,20},{8,24},{12,28},{16,0},{20,4},{24,8},{28,12},{1,17},{... | collective-permute-start | bytes 540680 | tf_op jit(solution)/shard_map/ppermute | solution.py:17
  172.3 10.0 %collective-permute-start.27 = (bf16[1,64,640]{2,1,0:T(8,128)(2,1)S(1)}, bf16[1,64,640]{2,1,0:T(8,128)(2,1)S(1)}, u32[]{:S(2)}, u32[]{:S(2)}) collective-permute-start(bf16[1,64,640]{2,1,0:T(8,128)(2,1)S(1)} %fusion.19), channel_id=1, source_target_pairs={{0,16},{4,20},{8,24},{12,28},{16,0},{20,4},{24,8},{28,12},{1,17},{... | collective-permute-start | bytes 245768 | tf_op jit(solution)/shard_map/ppermute | solution.py:17
  (15 other events, 52.3 us)

commit v17 on v15

--- a/solution.py
+++ b/solution.py
@@ -284,8 +284,8 @@
 
 
 def out_blocks(depth, widths):
-    others = range(1, widths[1] // depth + 1)
-    return [[(0, 0), (0, 1)] + [(j, 0) for j in others], [(j, 1) for j in others]]
+    others = range(1, widths[1] // (2 * depth) + 1)
+    return [[(0, 0), (0, 1)], [(j, core) for core in range(2) for j in others]]
 
 
 def placed(parts, depth, width):
@@ -338,11 +338,11 @@
     kept, sent = down_of(hidden, groups[0], ())
     own_rows = step_z(over_core(kept, sent, tok), 1)
     kept, sent = down_of(hidden, groups[1], (sent,))
-    first_rows = step_z(over_core(kept, sent, tok), 1)
+    first_rows = over_core(kept, sent, tok)
     kept, sent = down_of(hidden, groups[2], (sent, news[0], own_rows, first_rows))
-    early = over_x(jnp.concatenate([own_rows, first_rows], axis=-1))
-    late = over_x(step_z(over_core(kept, sent, tok), 1))
-    parts = [over_z(early, 2), over_z(late, 2)]
+    second_rows = over_core(kept, sent, tok)
+    late = over_x(step_z(jnp.concatenate([first_rows, second_rows], axis=-1), 1))
+    parts = [over_z(over_x(own_rows), 2), over_z(late, 2)]
     moe_output = placed(parts, depth, width)
 
     return (moe_output, *news)

time: 179 us -> 180 us (level)
    unnamed x33 -> x41, local copies, waits for them, and re-layouts: 3.12 us -> 5.01 us
    ppermute x27 -> x26, waiting for transfers between devices: 95.4 us -> 94.4 us  [swap(): lax.ppermute(x, axis, [(i, i ^ bit) for i in range(lax.axis_size(axis))])]
    ppermute x27 -> x26, starting transfers between devices: 35.7 us -> 35.4 us  [swap(): lax.ppermute(x, axis, [(i, i ^ bit) for i in range(lax.axis_size(axis))])]
  transfers between devices with their start and end apart: 28 -> 27, of which waited for: 17 -> 15; matrix products, arithmetic and copies ran while one was open for 2% -> 1% of each run, Pallas kernels for 19% -> 19%
where the time goes in v17:
time: 180 us; the launch traced here: 179 us
  waiting for transfers between devices  94.5 us (52%)
  Pallas kernels  39.8 us (22%)
  starting transfers between devices  36.3 us (20%)
  local copies, waits for them, and re-layouts  5.24 us (3%)
  other arithmetic  2.45 us (1%)
    ppermute x26, waiting for transfers between devices, swap(): lax.ppermute(x, axis, [(i, i ^ bit) for i in range(lax.axis_size(axis))])  94.4 us
    ppermute x26, starting transfers between devices, swap(): lax.ppermute(x, axis, [(i, i ^ bit) for i in range(lax.axis_size(axis))])  35.4 us
    pallas_call x4, Pallas kernels, copies(): pl.pallas_call(functools.partial(copy_kernel, plan, len(ins), len(counts)...  16.7 us
    pallas_call x1, Pallas kernels, hidden_of(): pl.pallas_call(functools.partial(hidden_kernel, len(pieces)), grid=(ff //...  12.4 us
    pallas_call x3, Pallas kernels, down_of(): pl.pallas_call(functools.partial(down_kernel, len(downs)), in_specs=[vmem...  6.16 us
    unnamed x41, local copies, waits for them, and re-layouts  5.01 us
  transfers between devices with their start and end apart: 27, of which 15 were waited for; matrix products, arithmetic and copies ran while one was open for 1% of the time, Pallas kernels for 19%

profile of v17, /device:TPU:0, one launch (start us, length us, event | category | flops | bytes accessed | tf_op | source)
XLA Modules:
  0.0 179.3 jit_solution(9044472995724423467)
XLA Ops:
  0.7 4.1 %shard_map.112 = (bf16[2,512,1024]{2,1,0:T(8,128)(2,1)}, bf16[2,512,1024]{2,1,0:T(8,128)(2,1)}) custom-call(s32[16]{0:T(128)} %refs_0_.7, s32[16]{0:T(128)} %refs_1_.7, bf16[2,512,1024]{2,1,0:T(8,128)(2,1)} %refs_3_.5, bf16[2,512,1024]{2,1,0:T(8,128)(2,1)} %refs_4_.3), custom_call_target="tpu_custom_call" | custom-call | tf_op jit(solution)/shard_map/pallas_call | solution.py:102
  5.3 2.6 %collective-permute-start.1 = (bf16[2,512,1024]{2,1,0:T(8,128)(2,1)}, bf16[2,512,1024]{2,1,0:T(8,128)(2,1)S(1)}, u32[]{:S(2)}, u32[]{:S(2)}) collective-permute-start(bf16[2,512,1024]{2,1,0:T(8,128)(2,1)} %get-tuple-element.17.refs_8_.refs_3_), channel_id=1, source_target_pairs={{0,2},{1,3},{2,0},{3,1},{4,6},{5,7},{6,4},{7,5},{8,10},{9,11},{10,... | collective-permute-start | bytes 6291464 | tf_op jit(solution)/shard_map/ppermute | solution.py:17
  8.6 1.6 collective-permute-start.2
  11.7 2.6 %collective-permute-start.4 = (bf16[64,2176]{1,0:T(8,128)(2,1)S(1)}, bf16[64,2176]{1,0:T(8,128)(2,1)S(1)}, u32[]{:S(2)}, u32[]{:S(2)}) collective-permute-start(bf16[64,2176]{1,0:T(8,128)(2,1)S(1)} %shard_map.111), channel_id=1, source_target_pairs={{0,16},{4,20},{8,24},{12,28},{16,0},{20,4},{24,8},{28,12},{1,17},{... | collective-permute-start | bytes 835592 | tf_op jit(solution)/shard_map/ppermute | solution.py:17
  14.3 7.7 %collective-permute-done.2 = bf16[64,2176]{1,0:T(8,128)(2,1)S(1)} collective-permute-done((bf16[64,2176]{1,0:T(8,128)(2,1)S(1)}, bf16[64,2176]{1,0:T(8,128)(2,1)S(1)}, u32[]{:S(2)}, u32[]{:S(2)}) %collective-permute-start.2) | collective-permute-done | bytes 278560 | tf_op jit(solution)/shard_map/ppermute | solution.py:17
  22.1 2.5 %collective-permute-start.3 = (bf16[64,2176]{1,0:T(8,128)(2,1)S(1)}, bf16[64,2176]{1,0:T(8,128)(2,1)S(1)}, u32[]{:S(2)}, u32[]{:S(2)}) collective-permute-start(bf16[64,2176]{1,0:T(8,128)(2,1)S(1)} %shard_map.114), channel_id=1, source_target_pairs={{0,4},{4,0},{8,12},{12,8},{16,20},{20,16},{24,28},{28,24},{1,5},{5... | collective-permute-start | bytes 835592 | tf_op jit(solution)/shard_map/ppermute | solution.py:17
  24.6 2.5 %collective-permute-start.6 = (bf16[64,2176]{1,0:T(8,128)(2,1)S(1)}, bf16[64,2176]{1,0:T(8,128)(2,1)S(1)}, u32[]{:S(2)}, u32[]{:S(2)}) collective-permute-start(bf16[64,2176]{1,0:T(8,128)(2,1)S(1)} %shard_map.111), channel_id=1, source_target_pairs={{0,24},{4,28},{8,16},{12,20},{16,8},{20,12},{24,0},{28,4},{1,25},{... | collective-permute-start | bytes 835592 | tf_op jit(solution)/shard_map/ppermute | solution.py:17
  28.1 2.6 %collective-permute-done.3.refs_1_.refs_6_ = bf16[64,2176]{1,0:T(8,128)(2,1)S(1)} collective-permute-done((bf16[64,2176]{1,0:T(8,128)(2,1)S(1)}, bf16[64,2176]{1,0:T(8,128)(2,1)S(1)}, u32[]{:S(2)}, u32[]{:S(2)}) %collective-permute-start.3) | collective-permute-done | bytes 278560 | tf_op jit(solution)/shard_map/ppermute | solution.py:17
  30.8 1.7 collective-permute-start.5
  33.0 2.9 %shard_map.121 = bf16[1,512,1024]{2,1,0:T(8,128)(2,1)} custom-call(s32[16]{0:T(128)} %refs_0_.7, s32[16]{0:T(128)} %refs_1_.7, bf16[2,512,1024]{2,1,0:T(8,128)(2,1)} %refs_5_.1, bf16[2,512,1024]{2,1,0:T(8,128)(2,1)} %get-tuple-element.17.refs_8_.refs_3_), custom_call_target="tpu_custom_call" | custom-call | tf_op jit(solution)/shard_map/pallas_call | solution.py:102
  36.0 2.0 %collective-permute-done.5.refs_1_.refs_7_ = bf16[64,2176]{1,0:T(8,128)(2,1)S(1)} collective-permute-done((bf16[64,2176]{1,0:T(8,128)(2,1)S(1)}, bf16[64,2176]{1,0:T(8,128)(2,1)S(1)}, u32[]{:S(2)}, u32[]{:S(2)}) %collective-permute-start.5) | collective-permute-done | bytes 278560 | tf_op jit(solution)/shard_map/ppermute | solution.py:17
  39.5 5.7 %collective-permute-done.7.refs_8_ = bf16[64,2176]{1,0:T(8,128)(2,1)S(1)} collective-permute-done((bf16[64,2176]{1,0:T(8,128)(2,1)S(1)}, bf16[64,2176]{1,0:T(8,128)(2,1)S(1)}, u32[]{:S(2)}, u32[]{:S(2)}) %collective-permute-start.7) | collective-permute-done | bytes 278560 | tf_op jit(solution)/shard_map/ppermute | solution.py:17
  45.9 3.6 %shard_map.125 = bf16[3,512,1024]{2,1,0:T(8,128)(2,1)} custom-call(s32[16]{0:T(128)} %refs_0_.7, s32[16]{0:T(128)} %refs_1_.7, bf16[2,512,1024]{2,1,0:T(8,128)(2,1)} %refs_3_.5, bf16[2,512,1024]{2,1,0:T(8,128)(2,1)} %refs_4_.3, bf16[2,512,1024]{2,1,0:T(8,128)(2,1)} %refs_5_.1, bf16[64,2176]{1,0:T(8,128)(2,1)} %copy-done.5, bf16[64,2176]{1,0:T(8,128)(2,1)} %copy-done.3, ...), custom_call_target="tpu_custom_call" | custom-call | tf_op jit(solution)/shard_map/pallas_call | solution.py:102
  51.4 3.2 %collective-permute-done.1.refs_1_.refs_10_ = bf16[2,512,1024]{2,1,0:T(8,128)(2,1)S(1)} collective-permute-done((bf16[2,512,1024]{2,1,0:T(8,128)(2,1)}, bf16[2,512,1024]{2,1,0:T(8,128)(2,1)S(1)}, u32[]{:S(2)}, u32[]{:S(2)}) %collective-permute-start.1) | collective-permute-done | bytes 2097184 | tf_op jit(solution)/shard_map/ppermute | solution.py:17
  56.7 3.0 %shard_map.122 = (bf16[512,1024]{1,0:T(8,128)(2,1)}, bf16[512,1024]{1,0:T(8,128)(2,1)}) custom-call(bf16[2,512,1024]{2,1,0:T(8,128)(2,1)} %refs_5_.1, bf16[1,512,1024]{2,1,0:T(8,128)(2,1)} %collective-permute-done.14.other_ref), custom_call_target="tpu_custom_call" | custom-call | tf_op jit(solution)/shard_map/pallas_call | solution.py:141
  60.5 1.9 %collective-permute-start.19 = (bf16[512,1024]{1,0:T(8,128)(2,1)}, bf16[512,1024]{1,0:T(8,128)(2,1)S(1)}, u32[]{:S(2)}, u32[]{:S(2)}) collective-permute-start(bf16[512,1024]{1,0:T(8,128)(2,1)} %get-tuple-element.19.refs_0_), channel_id=1, source_target_pairs={{0,2},{1,3},{2,0},{3,1},{4,6},{5,7},{6,4},{7,5},{8,10},{9,11},{10,... | collective-permute-start | bytes 3145736 | tf_op jit(solution)/shard_map/ppermute | solution.py:17
  62.5 37.1 %collective-permute-done.13.refs_11_ = bf16[2,512,1024]{2,1,0:T(8,128)(2,1)} collective-permute-done((bf16[2,512,1024]{2,1,0:T(8,128)(2,1)}, bf16[2,512,1024]{2,1,0:T(8,128)(2,1)}, u32[]{:S(2)}, u32[]{:S(2)}) %collective-permute-start.13) | collective-permute-done | bytes 2097184 | tf_op jit(solution)/shard_map/ppermute | solution.py:17
  102.8 12.4 %shard_map.120.hidden_ref = bf16[1024,1024]{1,0:T(8,128)(2,1)S(1)} custom-call(bf16[128,2176]{1,0:T(8,128)(2,1)S(1)} %shard_map.113.refs_0_, bf16[128,2176]{1,0:T(8,128)(2,1)S(1)} %shard_map.115.refs_1_, bf16[128,2176]{1,0:T(8,128)(2,1)S(1)} %copy-done.2, bf16[128,2176]{1,0:T(8,128)(2,1)S(1)} %shard_map.119.refs_3_, ...), custom_call_target="tpu_custom_call" | custom-call | flops 1 | bytes 1 | tf_op jit(solution)/shard_map/pallas_call | solution.py:208
  115.3 3.6 %shard_map.123 = (bf16[512,1024]{1,0:T(8,128)(2,1)S(1)}, bf16[512,1024]{1,0:T(8,128)(2,1)S(1)}) custom-call(bf16[1024,1024]{1,0:T(8,128)(2,1)S(1)} %shard_map.120.hidden_ref, bf16[512,1024]{1,0:T(8,128)(2,1)S(1)} %copy-done.9, bf16[512,1024]{1,0:T(8,128)(2,1)} %get-tuple-element.20.refs_1_), custom_call_target="tpu_custom_call" | custom-call | flops 1 | bytes 1 | tf_op jit(solution)/shard_map/pallas_call | solution.py:245
  119.0 2.0 %collective-permute-start.21 = (bf16[512,1024]{1,0:T(8,128)(2,1)}, bf16[512,1024]{1,0:T(8,128)(2,1)S(1)}, u32[]{:S(2)}, u32[]{:S(2)}) collective-permute-start(bf16[512,1024]{1,0:T(8,128)(2,1)} %get-tuple-element.20.refs_1_), channel_id=1, source_target_pairs={{0,2},{1,3},{2,0},{3,1},{4,6},{5,7},{6,4},{7,5},{8,10},{9,11},{10,... | collective-permute-start | bytes 3145736 | tf_op jit(solution)/shard_map/ppermute | solution.py:17
  123.6 1.9 %collective-permute-start.16 = (bf16[2,128,1024]{2,1,0:T(8,128)(2,1)S(1)}, bf16[2,128,1024]{2,1,0:T(8,128)(2,1)S(1)}, u32[]{:S(2)}, u32[]{:S(2)}) collective-permute-start(bf16[2,128,1024]{2,1,0:T(8,128)(2,1)S(1)} %fusion.2), channel_id=1, source_target_pairs={{0,8},{4,12},{8,0},{12,4},{16,24},{20,28},{24,16},{28,20},{1,9},{5... | collective-permute-start | bytes 1572872 | tf_op jit(solution)/shard_map/ppermute | solution.py:17
  125.5 6.1 %shard_map.126 = (bf16[2,512,1024]{2,1,0:T(8,128)(2,1)}, bf16[2,512,1024]{2,1,0:T(8,128)(2,1)}, bf16[2,512,1024]{2,1,0:T(8,128)(2,1)}) custom-call(s32[16]{0:T(128)} %refs_0_.7, s32[16]{0:T(128)} %refs_1_.7, bf16[3,512,1024]{2,1,0:T(8,128)(2,1)} %collective-permute-done.22.refs_2_, bf16[2,512,1024]{2,1,0:T(8,128)(2,1)} %refs_3_.5, ...), custom_call_target="tpu_custom_call" | custom-call | tf_op jit(solution)/shard_map/pallas_call | solution.py:102
  131.8 6.3 %collective-permute-done.16 = bf16[2,128,1024]{2,1,0:T(8,128)(2,1)S(1)} collective-permute-done((bf16[2,128,1024]{2,1,0:T(8,128)(2,1)S(1)}, bf16[2,128,1024]{2,1,0:T(8,128)(2,1)S(1)}, u32[]{:S(2)}, u32[]{:S(2)}) %collective-permute-start.16) | collective-permute-done | bytes 524320 | tf_op jit(solution)/shard_map/ppermute | solution.py:17
  138.2 6.7 %collective-permute-done.21.refs_0_ = bf16[512,1024]{1,0:T(8,128)(2,1)S(1)} collective-permute-done((bf16[512,1024]{1,0:T(8,128)(2,1)}, bf16[512,1024]{1,0:T(8,128)(2,1)S(1)}, u32[]{:S(2)}, u32[]{:S(2)}) %collective-permute-start.21) | collective-permute-done | bytes 1048608 | tf_op jit(solution)/shard_map/ppermute | solution.py:17
  146.3 1.9 %collective-permute-done.23 = bf16[512,512]{1,0:T(8,128)(2,1)S(1)} collective-permute-done((bf16[512,512]{1,0:T(8,128)(2,1)S(1)}, bf16[512,512]{1,0:T(8,128)(2,1)S(1)}, u32[]{:S(2)}, u32[]{:S(2)}) %collective-permute-start.23) | collective-permute-done | bytes 524320 | tf_op jit(solution)/shard_map/ppermute | solution.py:17
  148.6 1.9 %collective-permute-start.24 = (bf16[2,128,1024]{2,1,0:T(8,128)(2,1)S(1)}, bf16[2,128,1024]{2,1,0:T(8,128)(2,1)S(1)}, u32[]{:S(2)}, u32[]{:S(2)}) collective-permute-start(bf16[2,128,1024]{2,1,0:T(8,128)(2,1)S(1)} %fusion.3), channel_id=1, source_target_pairs={{0,8},{4,12},{8,0},{12,4},{16,24},{20,28},{24,16},{28,20},{1,9},{5... | collective-permute-start | bytes 1572872 | tf_op jit(solution)/shard_map/ppermute | solution.py:17
  152.1 10.6 %collective-permute-done.24 = bf16[2,128,1024]{2,1,0:T(8,128)(2,1)S(1)} collective-permute-done((bf16[2,128,1024]{2,1,0:T(8,128)(2,1)S(1)}, bf16[2,128,1024]{2,1,0:T(8,128)(2,1)S(1)}, u32[]{:S(2)}, u32[]{:S(2)}) %collective-permute-start.24) | collective-permute-done | bytes 524320 | tf_op jit(solution)/shard_map/ppermute | solution.py:17
  162.9 1.7 collective-permute-start.25
  164.7 2.7 %collective-permute-start.18 = (bf16[1,64,1024]{2,1,0:T(8,128)(2,1)S(1)}, bf16[1,64,1024]{2,1,0:T(8,128)(2,1)S(1)}, u32[]{:S(2)}, u32[]{:S(2)}) collective-permute-start(bf16[1,64,1024]{2,1,0:T(8,128)(2,1)S(1)} %fusion.15), channel_id=1, source_target_pairs={{0,16},{4,20},{8,24},{12,28},{16,0},{20,4},{24,8},{28,12},{1,17},{... | collective-permute-start | bytes 393224 | tf_op jit(solution)/shard_map/ppermute | solution.py:17
  167.4 3.2 %collective-permute-done.25 = bf16[2,64,1024]{2,1,0:T(8,128)(2,1)S(1)} collective-permute-done((bf16[2,64,1024]{2,1,0:T(8,128)(2,1)S(1)}, bf16[2,64,1024]{2,1,0:T(8,128)(2,1)S(1)}, u32[]{:S(2)}, u32[]{:S(2)}) %collective-permute-start.25) | collective-permute-done | bytes 262176 | tf_op jit(solution)/shard_map/ppermute | solution.py:17
  170.7 2.7 %collective-permute-start.26 = (bf16[1,64,1024]{2,1,0:T(8,128)(2,1)S(1)}, bf16[1,64,1024]{2,1,0:T(8,128)(2,1)S(1)}, u32[]{:S(2)}, u32[]{:S(2)}) collective-permute-start(bf16[1,64,1024]{2,1,0:T(8,128)(2,1)S(1)} %fusion.17), channel_id=1, source_target_pairs={{0,16},{4,20},{8,24},{12,28},{16,0},{20,4},{24,8},{28,12},{1,17},{... | collective-permute-start | bytes 393224 | tf_op jit(solution)/shard_map/ppermute | solution.py:17
  173.4 5.1 %collective-permute-done.26 = bf16[1,64,1024]{2,1,0:T(8,128)(2,1)S(1)} collective-permute-done((bf16[1,64,1024]{2,1,0:T(8,128)(2,1)S(1)}, bf16[1,64,1024]{2,1,0:T(8,128)(2,1)S(1)}, u32[]{:S(2)}, u32[]{:S(2)}) %collective-permute-start.26) | collective-permute-done | bytes 131104 | tf_op jit(solution)/shard_map/ppermute | solution.py:17
  (101 shorter events, 21.9 us)
Async XLA Ops:
  0.6 7.3 %copy-start.15 = (s32[16]{0:T(128)S(1)}, s32[16]{0:T(128)}, u32[]{:S(2)}) copy-start(s32[16]{0:T(128)} %refs_0_.7) | copy-start | bytes 196
  4.8 27.7 %collective-permute-start.12 = (bf16[2,512,1024]{2,1,0:T(8,128)(2,1)}, bf16[2,512,1024]{2,1,0:T(8,128)(2,1)}, u32[]{:S(2)}, u32[]{:S(2)}) collective-permute-start(bf16[2,512,1024]{2,1,0:T(8,128)(2,1)} %get-tuple-element.18), channel_id=1, source_target_pairs={{0,1},{1,0},{2,3},{3,2},{4,5},{5,4},{6,7},{7,6},{8,9},{9,8},{10,11... | collective-permute-start | bytes 6291464 | tf_op jit(solution)/shard_map/ppermute | solution.py:17
  5.3 49.3 %collective-permute-start.1 = (bf16[2,512,1024]{2,1,0:T(8,128)(2,1)}, bf16[2,512,1024]{2,1,0:T(8,128)(2,1)S(1)}, u32[]{:S(2)}, u32[]{:S(2)}) collective-permute-start(bf16[2,512,1024]{2,1,0:T(8,128)(2,1)} %get-tuple-element.17.refs_8_.refs_3_), channel_id=1, source_target_pairs={{0,2},{1,3},{2,0},{3,1},{4,6},{5,7},{6,4},{7,5},{8,10},{9,11},{10,... | collective-permute-start | bytes 6291464 | tf_op jit(solution)/shard_map/ppermute | solution.py:17
  8.6 13.4 %collective-permute-start.2 = (bf16[64,2176]{1,0:T(8,128)(2,1)S(1)}, bf16[64,2176]{1,0:T(8,128)(2,1)S(1)}, u32[]{:S(2)}, u32[]{:S(2)}) collective-permute-start(bf16[64,2176]{1,0:T(8,128)(2,1)S(1)} %shard_map.111), channel_id=1, source_target_pairs={{0,8},{4,12},{8,0},{12,4},{16,24},{20,28},{24,16},{28,20},{1,9},{5... | collective-permute-start | bytes 835592 | tf_op jit(solution)/shard_map/ppermute | solution.py:17
  10.2 11.8 %collective-permute-start = (bf16[64,2176]{1,0:T(8,128)(2,1)S(1)}, bf16[64,2176]{1,0:T(8,128)(2,1)S(1)}, u32[]{:S(2)}, u32[]{:S(2)}) collective-permute-start(bf16[64,2176]{1,0:T(8,128)(2,1)S(1)} %shard_map.111), channel_id=1, source_target_pairs={{0,4},{4,0},{8,12},{12,8},{16,20},{20,16},{24,28},{28,24},{1,5},{5... | collective-permute-start | bytes 835592 | tf_op jit(solution)/shard_map/ppermute | solution.py:17
  11.7 16.4 %collective-permute-start.4 = (bf16[64,2176]{1,0:T(8,128)(2,1)S(1)}, bf16[64,2176]{1,0:T(8,128)(2,1)S(1)}, u32[]{:S(2)}, u32[]{:S(2)}) collective-permute-start(bf16[64,2176]{1,0:T(8,128)(2,1)S(1)} %shard_map.111), channel_id=1, source_target_pairs={{0,16},{4,20},{8,24},{12,28},{16,0},{20,4},{24,8},{28,12},{1,17},{... | collective-permute-start | bytes 835592 | tf_op jit(solution)/shard_map/ppermute | solution.py:17
  22.1 17.4 %copy-start.5 = (bf16[64,2176]{1,0:T(8,128)(2,1)}, bf16[64,2176]{1,0:T(8,128)(2,1)S(1)}, u32[]{:S(2)}) copy-start(bf16[64,2176]{1,0:T(8,128)(2,1)S(1)} %collective-permute-done.refs_1_.refs_5_) | copy-start | bytes 835588
  22.1 8.7 %collective-permute-start.3 = (bf16[64,2176]{1,0:T(8,128)(2,1)S(1)}, bf16[64,2176]{1,0:T(8,128)(2,1)S(1)}, u32[]{:S(2)}, u32[]{:S(2)}) collective-permute-start(bf16[64,2176]{1,0:T(8,128)(2,1)S(1)} %shard_map.114), channel_id=1, source_target_pairs={{0,4},{4,0},{8,12},{12,8},{16,20},{20,16},{24,28},{28,24},{1,5},{5... | collective-permute-start | bytes 835592 | tf_op jit(solution)/shard_map/ppermute | solution.py:17
  24.6 11.4 %collective-permute-start.6 = (bf16[64,2176]{1,0:T(8,128)(2,1)S(1)}, bf16[64,2176]{1,0:T(8,128)(2,1)S(1)}, u32[]{:S(2)}, u32[]{:S(2)}) collective-permute-start(bf16[64,2176]{1,0:T(8,128)(2,1)S(1)} %shard_map.111), channel_id=1, source_target_pairs={{0,24},{4,28},{8,16},{12,20},{16,8},{20,12},{24,0},{28,4},{1,25},{... | collective-permute-start | bytes 835592 | tf_op jit(solution)/shard_map/ppermute | solution.py:17
  30.8 7.3 %collective-permute-start.5 = (bf16[64,2176]{1,0:T(8,128)(2,1)S(1)}, bf16[64,2176]{1,0:T(8,128)(2,1)S(1)}, u32[]{:S(2)}, u32[]{:S(2)}) collective-permute-start(bf16[64,2176]{1,0:T(8,128)(2,1)S(1)} %shard_map.116), channel_id=1, source_target_pairs={{0,4},{4,0},{8,12},{12,8},{16,20},{20,16},{24,28},{28,24},{1,5},{5... | collective-permute-start | bytes 835592 | tf_op jit(solution)/shard_map/ppermute | solution.py:17
  32.5 67.1 %collective-permute-start.13 = (bf16[2,512,1024]{2,1,0:T(8,128)(2,1)}, bf16[2,512,1024]{2,1,0:T(8,128)(2,1)}, u32[]{:S(2)}, u32[]{:S(2)}) collective-permute-start(bf16[2,512,1024]{2,1,0:T(8,128)(2,1)} %collective-permute-done.12.refs_9_), channel_id=1, source_target_pairs={{0,2},{1,3},{2,0},{3,1},{4,6},{5,7},{6,4},{7,5},{8,10},{9,11},{10,... | collective-permute-start | bytes 6291464 | tf_op jit(solution)/shard_map/ppermute | solution.py:17
  35.9 19.6 %collective-permute-start.14 = (bf16[1,512,1024]{2,1,0:T(8,128)(2,1)}, bf16[1,512,1024]{2,1,0:T(8,128)(2,1)}, u32[]{:S(2)}, u32[]{:S(2)}) collective-permute-start(bf16[1,512,1024]{2,1,0:T(8,128)(2,1)} %shard_map.121), channel_id=1, source_target_pairs={{0,1},{1,0},{2,3},{3,2},{4,5},{5,4},{6,7},{7,6},{8,9},{9,8},{10,11... | collective-permute-start | bytes 3145736 | tf_op jit(solution)/shard_map/ppermute | solution.py:17
  38.0 7.1 %collective-permute-start.7 = (bf16[64,2176]{1,0:T(8,128)(2,1)S(1)}, bf16[64,2176]{1,0:T(8,128)(2,1)S(1)}, u32[]{:S(2)}, u32[]{:S(2)}) collective-permute-start(bf16[64,2176]{1,0:T(8,128)(2,1)S(1)} %shard_map.118), channel_id=1, source_target_pairs={{0,4},{4,0},{8,12},{12,8},{16,20},{20,16},{24,28},{28,24},{1,5},{5... | collective-permute-start | bytes 835592 | tf_op jit(solution)/shard_map/ppermute | solution.py:17
  49.5 76.0 %collective-permute-start.22 = (bf16[3,512,1024]{2,1,0:T(8,128)(2,1)}, bf16[3,512,1024]{2,1,0:T(8,128)(2,1)}, u32[]{:S(2)}, u32[]{:S(2)}) collective-permute-start(bf16[3,512,1024]{2,1,0:T(8,128)(2,1)} %shard_map.125), channel_id=1, source_target_pairs={{0,4},{4,8},{8,12},{12,16},{16,20},{20,24},{24,28},{28,0},{1,5},{5... | collective-permute-start | bytes 9437192 | tf_op jit(solution)/shard_map/ppermute | solution.py:22
  54.6 2.0 %collective-permute-start.11 = (bf16[128,2176]{1,0:T(8,128)(2,1)S(1)}, bf16[128,2176]{1,0:T(8,128)(2,1)S(1)}, u32[]{:S(2)}, u32[]{:S(2)}) collective-permute-start(bf16[128,2176]{1,0:T(8,128)(2,1)S(1)} %shard_map.119.refs_3_), channel_id=1, source_target_pairs={{0,1},{1,0},{2,3},{3,2},{4,5},{5,4},{6,7},{7,6},{8,9},{9,8},{10,11... | collective-permute-start | bytes 1671176 | tf_op jit(solution)/shard_map/ppermute | solution.py:17
  54.7 5.0 %collective-permute-start.10 = (bf16[128,2176]{1,0:T(8,128)(2,1)S(1)}, bf16[128,2176]{1,0:T(8,128)(2,1)S(1)}, u32[]{:S(2)}, u32[]{:S(2)}) collective-permute-start(bf16[128,2176]{1,0:T(8,128)(2,1)S(1)} %shard_map.117.refs_2_), channel_id=1, source_target_pairs={{0,1},{1,0},{2,3},{3,2},{4,5},{5,4},{6,7},{7,6},{8,9},{9,8},{10,11... | collective-permute-start | bytes 1671176 | tf_op jit(solution)/shard_map/ppermute | solution.py:17
  55.5 44.1 %copy-start = (bf16[2,512,1024]{2,1,0:T(8,128)(2,1)S(1)}, bf16[2,512,1024]{2,1,0:T(8,128)(2,1)}, u32[]{:S(2)}) copy-start(bf16[2,512,1024]{2,1,0:T(8,128)(2,1)} %get-tuple-element.17.refs_8_.refs_3_) | copy-start | bytes 6291460
  55.5 7.0 %collective-permute-start.9 = (bf16[128,2176]{1,0:T(8,128)(2,1)S(1)}, bf16[128,2176]{1,0:T(8,128)(2,1)}, u32[]{:S(2)}, u32[]{:S(2)}) collective-permute-start(bf16[128,2176]{1,0:T(8,128)(2,1)S(1)} %shard_map.115.refs_1_), channel_id=1, source_target_pairs={{0,1},{1,0},{2,3},{3,2},{4,5},{5,4},{6,7},{7,6},{8,9},{9,8},{10,11... | collective-permute-start | bytes 1671176 | tf_op jit(solution)/shard_map/ppermute | solution.py:17
  56.6 5.9 %collective-permute-start.8 = (bf16[128,2176]{1,0:T(8,128)(2,1)S(1)}, bf16[128,2176]{1,0:T(8,128)(2,1)}, u32[]{:S(2)}, u32[]{:S(2)}) collective-permute-start(bf16[128,2176]{1,0:T(8,128)(2,1)S(1)} %shard_map.113.refs_0_), channel_id=1, source_target_pairs={{0,1},{1,0},{2,3},{3,2},{4,5},{5,4},{6,7},{7,6},{8,9},{9,8},{10,11... | collective-permute-start | bytes 1671176 | tf_op jit(solution)/shard_map/ppermute | solution.py:17
  60.5 61.2 %collective-permute-start.19 = (bf16[512,1024]{1,0:T(8,128)(2,1)}, bf16[512,1024]{1,0:T(8,128)(2,1)S(1)}, u32[]{:S(2)}, u32[]{:S(2)}) collective-permute-start(bf16[512,1024]{1,0:T(8,128)(2,1)} %get-tuple-element.19.refs_0_), channel_id=1, source_target_pairs={{0,2},{1,3},{2,0},{3,1},{4,6},{5,7},{6,4},{7,5},{8,10},{9,11},{10,... | collective-permute-start | bytes 3145736 | tf_op jit(solution)/shard_map/ppermute | solution.py:17
  102.8 12.5 %copy-start.9 = (bf16[512,1024]{1,0:T(8,128)(2,1)S(1)}, bf16[512,1024]{1,0:T(8,128)(2,1)}, u32[]{:S(2)}) copy-start(bf16[512,1024]{1,0:T(8,128)(2,1)} %get-tuple-element.19.refs_0_) | copy-start | bytes 3145732
  118.9 4.2 %collective-permute-start.15 = (bf16[512,1024]{1,0:T(8,128)(2,1)S(1)}, bf16[512,1024]{1,0:T(8,128)(2,1)S(1)}, u32[]{:S(2)}, u32[]{:S(2)}) collective-permute-start(bf16[512,1024]{1,0:T(8,128)(2,1)S(1)} %get-tuple-element.22.refs_1_), channel_id=1, source_target_pairs={{0,1},{1,0},{2,3},{3,2},{4,5},{5,4},{6,7},{7,6},{8,9},{9,8},{10,11... | collective-permute-start | bytes 3145736 | tf_op jit(solution)/shard_map/ppermute | solution.py:17
  119.0 26.0 %collective-permute-start.21 = (bf16[512,1024]{1,0:T(8,128)(2,1)}, bf16[512,1024]{1,0:T(8,128)(2,1)S(1)}, u32[]{:S(2)}, u32[]{:S(2)}) collective-permute-start(bf16[512,1024]{1,0:T(8,128)(2,1)} %get-tuple-element.20.refs_1_), channel_id=1, source_target_pairs={{0,2},{1,3},{2,0},{3,1},{4,6},{5,7},{6,4},{7,5},{8,10},{9,11},{10,... | collective-permute-start | bytes 3145736 | tf_op jit(solution)/shard_map/ppermute | solution.py:17
  123.0 8.6 %collective-permute-start.20 = (bf16[512,512]{1,0:T(8,128)(2,1)S(1)}, bf16[512,512]{1,0:T(8,128)(2,1)S(1)}, u32[]{:S(2)}, u32[]{:S(2)}) collective-permute-start(bf16[512,512]{1,0:T(8,128)(2,1)S(1)} %get-tuple-element.24.refs_1_), channel_id=1, source_target_pairs={{0,1},{1,0},{2,3},{3,2},{4,5},{5,4},{6,7},{7,6},{8,9},{9,8},{10,11... | collective-permute-start | bytes 1572872 | tf_op jit(solution)/shard_map/ppermute | solution.py:17
  123.6 14.5 %collective-permute-start.16 = (bf16[2,128,1024]{2,1,0:T(8,128)(2,1)S(1)}, bf16[2,128,1024]{2,1,0:T(8,128)(2,1)S(1)}, u32[]{:S(2)}, u32[]{:S(2)}) collective-permute-start(bf16[2,128,1024]{2,1,0:T(8,128)(2,1)S(1)} %fusion.2), channel_id=1, source_target_pairs={{0,8},{4,12},{8,0},{12,4},{16,24},{20,28},{24,16},{28,20},{1,9},{5... | collective-permute-start | bytes 1572872 | tf_op jit(solution)/shard_map/ppermute | solution.py:17
  131.6 13.3 %copy-start.8 = (bf16[2,512,1024]{2,1,0:T(8,128)(2,1)S(1)}, bf16[2,512,1024]{2,1,0:T(8,128)(2,1)}, u32[]{:S(2)}) copy-start(bf16[2,512,1024]{2,1,0:T(8,128)(2,1)} %get-tuple-element.14.refs_2_) | copy-start | bytes 6291460
  146.2 2.0 %collective-permute-start.23 = (bf16[512,512]{1,0:T(8,128)(2,1)S(1)}, bf16[512,512]{1,0:T(8,128)(2,1)S(1)}, u32[]{:S(2)}, u32[]{:S(2)}) collective-permute-start(bf16[512,512]{1,0:T(8,128)(2,1)S(1)} %get-tuple-element.27), channel_id=1, source_target_pairs={{0,1},{1,0},{2,3},{3,2},{4,5},{5,4},{6,7},{7,6},{8,9},{9,8},{10,11... | collective-permute-start | bytes 1572872 | tf_op jit(solution)/shard_map/ppermute | solution.py:17
  148.6 14.1 %collective-permute-start.24 = (bf16[2,128,1024]{2,1,0:T(8,128)(2,1)S(1)}, bf16[2,128,1024]{2,1,0:T(8,128)(2,1)S(1)}, u32[]{:S(2)}, u32[]{:S(2)}) collective-permute-start(bf16[2,128,1024]{2,1,0:T(8,128)(2,1)S(1)} %fusion.3), channel_id=1, source_target_pairs={{0,8},{4,12},{8,0},{12,4},{16,24},{20,28},{24,16},{28,20},{1,9},{5... | collective-permute-start | bytes 1572872 | tf_op jit(solution)/shard_map/ppermute | solution.py:17
  150.5 14.1 %collective-permute-start.17 = (bf16[2,64,1024]{2,1,0:T(8,128)(2,1)S(1)}, bf16[2,64,1024]{2,1,0:T(8,128)(2,1)S(1)}, u32[]{:S(2)}, u32[]{:S(2)}) collective-permute-start(bf16[2,64,1024]{2,1,0:T(8,128)(2,1)S(1)} %fusion.8), channel_id=1, source_target_pairs={{0,4},{4,0},{8,12},{12,8},{16,20},{20,16},{24,28},{28,24},{1,5},{5... | collective-permute-start | bytes 786440 | tf_op jit(solution)/shard_map/ppermute | solution.py:17
  162.9 7.7 %collective-permute-start.25 = (bf16[2,64,1024]{2,1,0:T(8,128)(2,1)S(1)}, bf16[2,64,1024]{2,1,0:T(8,128)(2,1)S(1)}, u32[]{:S(2)}, u32[]{:S(2)}) collective-permute-start(bf16[2,64,1024]{2,1,0:T(8,128)(2,1)S(1)} %fusion.9), channel_id=1, source_target_pairs={{0,4},{4,0},{8,12},{12,8},{16,20},{20,16},{24,28},{28,24},{1,5},{5... | collective-permute-start | bytes 786440 | tf_op jit(solution)/shard_map/ppermute | solution.py:17
  164.7 8.7 %collective-permute-start.18 = (bf16[1,64,1024]{2,1,0:T(8,128)(2,1)S(1)}, bf16[1,64,1024]{2,1,0:T(8,128)(2,1)S(1)}, u32[]{:S(2)}, u32[]{:S(2)}) collective-permute-start(bf16[1,64,1024]{2,1,0:T(8,128)(2,1)S(1)} %fusion.15), channel_id=1, source_target_pairs={{0,16},{4,20},{8,24},{12,28},{16,0},{20,4},{24,8},{28,12},{1,17},{... | collective-permute-start | bytes 393224 | tf_op jit(solution)/shard_map/ppermute | solution.py:17
  170.7 7.9 %collective-permute-start.26 = (bf16[1,64,1024]{2,1,0:T(8,128)(2,1)S(1)}, bf16[1,64,1024]{2,1,0:T(8,128)(2,1)S(1)}, u32[]{:S(2)}, u32[]{:S(2)}) collective-permute-start(bf16[1,64,1024]{2,1,0:T(8,128)(2,1)S(1)} %fusion.17), channel_id=1, source_target_pairs={{0,16},{4,20},{8,24},{12,28},{16,0},{20,4},{24,8},{28,12},{1,17},{... | collective-permute-start | bytes 393224 | tf_op jit(solution)/shard_map/ppermute | solution.py:17
  (14 other events, 53.9 us)

commit v18 on v15

--- a/solution.py
+++ b/solution.py
@@ -79,14 +79,14 @@
     moved = (old_ref[second] != new_ref[second]).astype(jnp.int32)
     slots = {"mine": core, "theirs": 1 - core, "leaves": moved, "stays": 1 - moved}
     slots.update({i: i for i in range(3)})
-    loads = [
-        pltpu.make_async_copy(ins[i].at[slots[a]], held.at[n], in_sems.at[n])
-        for n, (i, a, o, b) in enumerate(plan)
-    ]
-    stores = [
-        pltpu.make_async_copy(held.at[n], outs[o].at[slots[b]], out_sems.at[n])
-        for n, (i, a, o, b) in enumerate(plan)
-    ]
+    tall = held.shape[1] // 2
+    parts = [(n, pl.ds(h * tall, tall)) for n in range(len(plan)) for h in range(2)]
+    loads, stores = [], []
+    for k, (n, part) in enumerate(parts):
+        i, a, o, b = plan[n]
+        here = held.at[n, part]
+        loads.append(pltpu.make_async_copy(ins[i].at[slots[a], part], here, in_sems.at[k]))
+        stores.append(pltpu.make_async_copy(here, outs[o].at[slots[b], part], out_sems.at[k]))
     for c in loads:
         c.start()
     for n, c in enumerate(stores):
@@ -107,8 +107,8 @@
         input_output_aliases={2 + len(ins) + i: i for i in range(len(aliases))},
         scratch_shapes=[
             pltpu.VMEM((len(plan),) + slot, kind),
-            pltpu.SemaphoreType.DMA((len(plan),)),
-            pltpu.SemaphoreType.DMA((len(plan),)),
+            pltpu.SemaphoreType.DMA((2 * len(plan),)),
+            pltpu.SemaphoreType.DMA((2 * len(plan),)),
         ],
         compiler_params=params(MOST),
         cost_estimate=NOTHING,

time: 179 us -> 180 us (level)
  transfers between devices with their start and end apart: 28 -> 28, of which waited for: 17 -> 17; matrix products, arithmetic and copies ran while one was open for 2% -> 2% of each run, Pallas kernels for 19% -> 18%
where the time goes in v18:
time: 180 us; the launch traced here: 179 us
  waiting for transfers between devices  95.5 us (53%)
  Pallas kernels  39.5 us (22%)
  starting transfers between devices  36.7 us (20%)
  local copies, waits for them, and re-layouts  4.06 us (2%)
  other arithmetic  2.42 us (1%)
    ppermute x27, waiting for transfers between devices, swap(): lax.ppermute(x, axis, [(i, i ^ bit) for i in range(lax.axis_size(axis))])  95.5 us
    ppermute x27, starting transfers between devices, swap(): lax.ppermute(x, axis, [(i, i ^ bit) for i in range(lax.axis_size(axis))])  35.7 us
    pallas_call x4, Pallas kernels, copies(): pl.pallas_call(functools.partial(copy_kernel, plan, len(ins), len(counts)...  16.7 us
    pallas_call x1, Pallas kernels, hidden_of(): pl.pallas_call(functools.partial(hidden_kernel, len(pieces)), grid=(ff //...  12.3 us
    pallas_call x3, Pallas kernels, down_of(): pl.pallas_call(functools.partial(down_kernel, len(downs)), in_specs=[vmem...  6.16 us
  transfers between devices with their start and end apart: 28, of which 17 were waited for; matrix products, arithmetic and copies ran while one was open for 2% of the time, Pallas kernels for 18%

profile of v18, /device:TPU:0, one launch (start us, length us, event | category | flops | bytes accessed | tf_op | source)
XLA Modules:
  0.0 179.3 jit_solution(16059988456913564221)
XLA Ops:
  0.7 4.4 %shard_map.112 = (bf16[2,512,1024]{2,1,0:T(8,128)(2,1)}, bf16[2,512,1024]{2,1,0:T(8,128)(2,1)}) custom-call(s32[16]{0:T(128)} %refs_0_.7, s32[16]{0:T(128)} %refs_1_.7, bf16[2,512,1024]{2,1,0:T(8,128)(2,1)} %refs_3_.5, bf16[2,512,1024]{2,1,0:T(8,128)(2,1)} %refs_4_.3), custom_call_target="tpu_custom_call" | custom-call | tf_op jit(solution)/shard_map/pallas_call | solution.py:102
  5.6 2.6 %collective-permute-start.1 = (bf16[2,512,1024]{2,1,0:T(8,128)(2,1)}, bf16[2,512,1024]{2,1,0:T(8,128)(2,1)S(1)}, u32[]{:S(2)}, u32[]{:S(2)}) collective-permute-start(bf16[2,512,1024]{2,1,0:T(8,128)(2,1)} %get-tuple-element.17.refs_8_.refs_3_), channel_id=1, source_target_pairs={{0,2},{1,3},{2,0},{3,1},{4,6},{5,7},{6,4},{7,5},{8,10},{9,11},{10,... | collective-permute-start | bytes 6291464 | tf_op jit(solution)/shard_map/ppermute | solution.py:17
  8.9 1.6 collective-permute-start.2
  12.0 2.6 %collective-permute-start.4 = (bf16[64,2176]{1,0:T(8,128)(2,1)S(1)}, bf16[64,2176]{1,0:T(8,128)(2,1)S(1)}, u32[]{:S(2)}, u32[]{:S(2)}) collective-permute-start(bf16[64,2176]{1,0:T(8,128)(2,1)S(1)} %shard_map.111), channel_id=1, source_target_pairs={{0,16},{4,20},{8,24},{12,28},{16,0},{20,4},{24,8},{28,12},{1,17},{... | collective-permute-start | bytes 835592 | tf_op jit(solution)/shard_map/ppermute | solution.py:17
  14.6 7.7 %collective-permute-done.2 = bf16[64,2176]{1,0:T(8,128)(2,1)S(1)} collective-permute-done((bf16[64,2176]{1,0:T(8,128)(2,1)S(1)}, bf16[64,2176]{1,0:T(8,128)(2,1)S(1)}, u32[]{:S(2)}, u32[]{:S(2)}) %collective-permute-start.2) | collective-permute-done | bytes 278560 | tf_op jit(solution)/shard_map/ppermute | solution.py:17
  22.4 2.5 %collective-permute-start.3 = (bf16[64,2176]{1,0:T(8,128)(2,1)S(1)}, bf16[64,2176]{1,0:T(8,128)(2,1)S(1)}, u32[]{:S(2)}, u32[]{:S(2)}) collective-permute-start(bf16[64,2176]{1,0:T(8,128)(2,1)S(1)} %shard_map.114), channel_id=1, source_target_pairs={{0,4},{4,0},{8,12},{12,8},{16,20},{20,16},{24,28},{28,24},{1,5},{5... | collective-permute-start | bytes 835592 | tf_op jit(solution)/shard_map/ppermute | solution.py:17
  24.9 2.5 %collective-permute-start.6 = (bf16[64,2176]{1,0:T(8,128)(2,1)S(1)}, bf16[64,2176]{1,0:T(8,128)(2,1)S(1)}, u32[]{:S(2)}, u32[]{:S(2)}) collective-permute-start(bf16[64,2176]{1,0:T(8,128)(2,1)S(1)} %shard_map.111), channel_id=1, source_target_pairs={{0,24},{4,28},{8,16},{12,20},{16,8},{20,12},{24,0},{28,4},{1,25},{... | collective-permute-start | bytes 835592 | tf_op jit(solution)/shard_map/ppermute | solution.py:17
  28.4 2.7 %collective-permute-done.3.refs_1_.refs_6_ = bf16[64,2176]{1,0:T(8,128)(2,1)S(1)} collective-permute-done((bf16[64,2176]{1,0:T(8,128)(2,1)S(1)}, bf16[64,2176]{1,0:T(8,128)(2,1)S(1)}, u32[]{:S(2)}, u32[]{:S(2)}) %collective-permute-start.3) | collective-permute-done | bytes 278560 | tf_op jit(solution)/shard_map/ppermute | solution.py:17
  31.0 1.7 collective-permute-start.5
  33.3 2.7 %shard_map.121 = bf16[1,512,1024]{2,1,0:T(8,128)(2,1)} custom-call(s32[16]{0:T(128)} %refs_0_.7, s32[16]{0:T(128)} %refs_1_.7, bf16[2,512,1024]{2,1,0:T(8,128)(2,1)} %refs_5_.1, bf16[2,512,1024]{2,1,0:T(8,128)(2,1)} %get-tuple-element.17.refs_8_.refs_3_), custom_call_target="tpu_custom_call" | custom-call | tf_op jit(solution)/shard_map/pallas_call | solution.py:102
  36.2 2.2 %collective-permute-done.5.refs_1_.refs_7_ = bf16[64,2176]{1,0:T(8,128)(2,1)S(1)} collective-permute-done((bf16[64,2176]{1,0:T(8,128)(2,1)S(1)}, bf16[64,2176]{1,0:T(8,128)(2,1)S(1)}, u32[]{:S(2)}, u32[]{:S(2)}) %collective-permute-start.5) | collective-permute-done | bytes 278560 | tf_op jit(solution)/shard_map/ppermute | solution.py:17
  39.8 5.5 %collective-permute-done.7.refs_8_ = bf16[64,2176]{1,0:T(8,128)(2,1)S(1)} collective-permute-done((bf16[64,2176]{1,0:T(8,128)(2,1)S(1)}, bf16[64,2176]{1,0:T(8,128)(2,1)S(1)}, u32[]{:S(2)}, u32[]{:S(2)}) %collective-permute-start.7) | collective-permute-done | bytes 278560 | tf_op jit(solution)/shard_map/ppermute | solution.py:17
  46.0 3.5 %shard_map.125 = bf16[3,512,1024]{2,1,0:T(8,128)(2,1)} custom-call(s32[16]{0:T(128)} %refs_0_.7, s32[16]{0:T(128)} %refs_1_.7, bf16[2,512,1024]{2,1,0:T(8,128)(2,1)} %refs_3_.5, bf16[2,512,1024]{2,1,0:T(8,128)(2,1)} %refs_4_.3, bf16[2,512,1024]{2,1,0:T(8,128)(2,1)} %refs_5_.1, bf16[64,2176]{1,0:T(8,128)(2,1)} %copy-done.1, bf16[64,2176]{1,0:T(8,128)(2,1)} %copy-done.3, ...), custom_call_target="tpu_custom_call" | custom-call | tf_op jit(solution)/shard_map/pallas_call | solution.py:102
  51.5 3.3 %collective-permute-done.1.refs_1_.refs_10_ = bf16[2,512,1024]{2,1,0:T(8,128)(2,1)S(1)} collective-permute-done((bf16[2,512,1024]{2,1,0:T(8,128)(2,1)}, bf16[2,512,1024]{2,1,0:T(8,128)(2,1)S(1)}, u32[]{:S(2)}, u32[]{:S(2)}) %collective-permute-start.1) | collective-permute-done | bytes 2097184 | tf_op jit(solution)/shard_map/ppermute | solution.py:17
  55.9 2.9 %shard_map.122 = (bf16[512,1024]{1,0:T(8,128)(2,1)}, bf16[512,1024]{1,0:T(8,128)(2,1)}) custom-call(bf16[2,512,1024]{2,1,0:T(8,128)(2,1)} %refs_5_.1, bf16[1,512,1024]{2,1,0:T(8,128)(2,1)} %collective-permute-done.14.other_ref), custom_call_target="tpu_custom_call" | custom-call | tf_op jit(solution)/shard_map/pallas_call | solution.py:141
  58.8 2.0 %collective-permute-start.17 = (bf16[512,1024]{1,0:T(8,128)(2,1)}, bf16[512,1024]{1,0:T(8,128)(2,1)S(1)}, u32[]{:S(2)}, u32[]{:S(2)}) collective-permute-start(bf16[512,1024]{1,0:T(8,128)(2,1)} %get-tuple-element.19.refs_0_), channel_id=1, source_target_pairs={{0,2},{1,3},{2,0},{3,1},{4,6},{5,7},{6,4},{7,5},{8,10},{9,11},{10,... | collective-permute-start | bytes 3145736 | tf_op jit(solution)/shard_map/ppermute | solution.py:17
  64.5 35.4 %collective-permute-done.13.refs_11_ = bf16[2,512,1024]{2,1,0:T(8,128)(2,1)} collective-permute-done((bf16[2,512,1024]{2,1,0:T(8,128)(2,1)S(1)}, bf16[2,512,1024]{2,1,0:T(8,128)(2,1)}, u32[]{:S(2)}, u32[]{:S(2)}) %collective-permute-start.13) | collective-permute-done | bytes 2097184 | tf_op jit(solution)/shard_map/ppermute | solution.py:17
  101.0 12.3 %shard_map.120.hidden_ref = bf16[1024,1024]{1,0:T(8,128)(2,1)S(1)} custom-call(bf16[128,2176]{1,0:T(8,128)(2,1)S(1)} %shard_map.113.refs_0_, bf16[128,2176]{1,0:T(8,128)(2,1)S(1)} %shard_map.115.refs_1_, bf16[128,2176]{1,0:T(8,128)(2,1)S(1)} %shard_map.117.refs_2_, bf16[128,2176]{1,0:T(8,128)(2,1)S(1)} %shard_map.119.refs_3_, ...), custom_call_target="tpu_custom_call" | custom-call | flops 1 | bytes 1 | tf_op jit(solution)/shard_map/pallas_call | solution.py:208
  113.3 3.6 %shard_map.123 = (bf16[512,1024]{1,0:T(8,128)(2,1)S(1)}, bf16[512,1024]{1,0:T(8,128)(2,1)S(1)}) custom-call(bf16[1024,1024]{1,0:T(8,128)(2,1)S(1)} %shard_map.120.hidden_ref, bf16[512,1024]{1,0:T(8,128)(2,1)S(1)} %copy-done.7, bf16[512,1024]{1,0:T(8,128)(2,1)} %get-tuple-element.20.refs_1_), custom_call_target="tpu_custom_call" | custom-call | flops 1 | bytes 1 | tf_op jit(solution)/shard_map/pallas_call | solution.py:245
  117.0 5.0 %collective-permute-done.17.refs_0_ = bf16[512,1024]{1,0:T(8,128)(2,1)S(1)} collective-permute-done((bf16[512,1024]{1,0:T(8,128)(2,1)}, bf16[512,1024]{1,0:T(8,128)(2,1)S(1)}, u32[]{:S(2)}, u32[]{:S(2)}) %collective-permute-start.17) | collective-permute-done | bytes 1048608 | tf_op jit(solution)/shard_map/ppermute | solution.py:17
  123.4 1.8 %collective-permute-start.22 = (bf16[512,1024]{1,0:T(8,128)(2,1)}, bf16[512,1024]{1,0:T(8,128)(2,1)S(1)}, u32[]{:S(2)}, u32[]{:S(2)}) collective-permute-start(bf16[512,1024]{1,0:T(8,128)(2,1)} %get-tuple-element.20.refs_1_), channel_id=1, source_target_pairs={{0,2},{1,3},{2,0},{3,1},{4,6},{5,7},{6,4},{7,5},{8,10},{9,11},{10,... | collective-permute-start | bytes 3145736 | tf_op jit(solution)/shard_map/ppermute | solution.py:17
  125.9 1.9 %collective-permute-start.16 = (bf16[2,128,1024]{2,1,0:T(8,128)(2,1)S(1)}, bf16[2,128,1024]{2,1,0:T(8,128)(2,1)S(1)}, u32[]{:S(2)}, u32[]{:S(2)}) collective-permute-start(bf16[2,128,1024]{2,1,0:T(8,128)(2,1)S(1)} %fusion.3), channel_id=1, source_target_pairs={{0,8},{4,12},{8,0},{12,4},{16,24},{20,28},{24,16},{28,20},{1,9},{5... | collective-permute-start | bytes 1572872 | tf_op jit(solution)/shard_map/ppermute | solution.py:17
  128.8 6.1 %shard_map.126 = (bf16[2,512,1024]{2,1,0:T(8,128)(2,1)}, bf16[2,512,1024]{2,1,0:T(8,128)(2,1)}, bf16[2,512,1024]{2,1,0:T(8,128)(2,1)}) custom-call(s32[16]{0:T(128)} %refs_0_.7, s32[16]{0:T(128)} %refs_1_.7, bf16[3,512,1024]{2,1,0:T(8,128)(2,1)} %collective-permute-done.23.refs_2_, bf16[2,512,1024]{2,1,0:T(8,128)(2,1)} %refs_3_.5, ...), custom_call_target="tpu_custom_call" | custom-call | tf_op jit(solution)/shard_map/pallas_call | solution.py:102
  134.9 10.7 %collective-permute-done.19 = bf16[2,128,512]{2,1,0:T(8,128)(2,1)S(1)} collective-permute-done((bf16[2,128,512]{2,1,0:T(8,128)(2,1)}, bf16[2,128,512]{2,1,0:T(8,128)(2,1)S(1)}, u32[]{:S(2)}, u32[]{:S(2)}) %collective-permute-start.19) | collective-permute-done | bytes 262176 | tf_op jit(solution)/shard_map/ppermute | solution.py:17
  145.9 3.3 %collective-permute-done.22.refs_0_ = bf16[512,1024]{1,0:T(8,128)(2,1)S(1)} collective-permute-done((bf16[512,1024]{1,0:T(8,128)(2,1)}, bf16[512,1024]{1,0:T(8,128)(2,1)S(1)}, u32[]{:S(2)}, u32[]{:S(2)}) %collective-permute-start.22) | collective-permute-done | bytes 1048608 | tf_op jit(solution)/shard_map/ppermute | solution.py:17
  150.7 1.8 %collective-permute-start.20 = (bf16[2,64,1536]{2,1,0:T(8,128)(2,1)S(1)}, bf16[2,64,1536]{2,1,0:T(8,128)(2,1)S(1)}, u32[]{:S(2)}, u32[]{:S(2)}) collective-permute-start(bf16[2,64,1536]{2,1,0:T(8,128)(2,1)S(1)} %fusion.6), channel_id=1, source_target_pairs={{0,4},{4,0},{8,12},{12,8},{16,20},{20,16},{24,28},{28,24},{1,5},{5... | collective-permute-start | bytes 1179656 | tf_op jit(solution)/shard_map/ppermute | solution.py:17
  152.7 1.8 %collective-permute-start.25 = (bf16[2,128,512]{2,1,0:T(8,128)(2,1)S(1)}, bf16[2,128,512]{2,1,0:T(8,128)(2,1)S(1)}, u32[]{:S(2)}, u32[]{:S(2)}) collective-permute-start(bf16[2,128,512]{2,1,0:T(8,128)(2,1)S(1)} %fusion.10), channel_id=1, source_target_pairs={{0,8},{4,12},{8,0},{12,4},{16,24},{20,28},{24,16},{28,20},{1,9},{5... | collective-permute-start | bytes 786440 | tf_op jit(solution)/shard_map/ppermute | solution.py:17
  154.5 7.8 %collective-permute-done.20 = bf16[2,64,1536]{2,1,0:T(8,128)(2,1)S(1)} collective-permute-done((bf16[2,64,1536]{2,1,0:T(8,128)(2,1)S(1)}, bf16[2,64,1536]{2,1,0:T(8,128)(2,1)S(1)}, u32[]{:S(2)}, u32[]{:S(2)}) %collective-permute-start.20) | collective-permute-done | bytes 393248 | tf_op jit(solution)/shard_map/ppermute | solution.py:17
  162.5 1.8 %collective-permute-start.26 = (bf16[2,64,512]{2,1,0:T(8,128)(2,1)S(1)}, bf16[2,64,512]{2,1,0:T(8,128)(2,1)S(1)}, u32[]{:S(2)}, u32[]{:S(2)}) collective-permute-start(bf16[2,64,512]{2,1,0:T(8,128)(2,1)S(1)} %fusion.15), channel_id=1, source_target_pairs={{0,4},{4,0},{8,12},{12,8},{16,20},{20,16},{24,28},{28,24},{1,5},{5... | collective-permute-start | bytes 393224 | tf_op jit(solution)/shard_map/ppermute | solution.py:17
  164.4 2.6 %collective-permute-start.21 = (bf16[1,64,1536]{2,1,0:T(8,128)(2,1)S(1)}, bf16[1,64,1536]{2,1,0:T(8,128)(2,1)S(1)}, u32[]{:S(2)}, u32[]{:S(2)}) collective-permute-start(bf16[1,64,1536]{2,1,0:T(8,128)(2,1)S(1)} %fusion.14), channel_id=1, source_target_pairs={{0,16},{4,20},{8,24},{12,28},{16,0},{20,4},{24,8},{28,12},{1,17},{... | collective-permute-start | bytes 589832 | tf_op jit(solution)/shard_map/ppermute | solution.py:17
  167.8 2.9 %collective-permute-start.27 = (bf16[1,64,512]{2,1,0:T(8,128)(2,1)S(1)}, bf16[1,64,512]{2,1,0:T(8,128)(2,1)S(1)}, u32[]{:S(2)}, u32[]{:S(2)}) collective-permute-start(bf16[1,64,512]{2,1,0:T(8,128)(2,1)S(1)} %fusion.19), channel_id=1, source_target_pairs={{0,16},{4,20},{8,24},{12,28},{16,0},{20,4},{24,8},{28,12},{1,17},{... | collective-permute-start | bytes 196616 | tf_op jit(solution)/shard_map/ppermute | solution.py:17
  170.7 7.2 %collective-permute-done.21 = bf16[1,64,1536]{2,1,0:T(8,128)(2,1)S(1)} collective-permute-done((bf16[1,64,1536]{2,1,0:T(8,128)(2,1)S(1)}, bf16[1,64,1536]{2,1,0:T(8,128)(2,1)S(1)}, u32[]{:S(2)}, u32[]{:S(2)}) %collective-permute-start.21) | collective-permute-done | bytes 196640 | tf_op jit(solution)/shard_map/ppermute | solution.py:17
  (97 shorter events, 21.7 us)
Async XLA Ops:
  5.1 27.7 %collective-permute-start.12 = (bf16[2,512,1024]{2,1,0:T(8,128)(2,1)}, bf16[2,512,1024]{2,1,0:T(8,128)(2,1)S(1)}, u32[]{:S(2)}, u32[]{:S(2)}) collective-permute-start(bf16[2,512,1024]{2,1,0:T(8,128)(2,1)} %get-tuple-element.18), channel_id=1, source_target_pairs={{0,1},{1,0},{2,3},{3,2},{4,5},{5,4},{6,7},{7,6},{8,9},{9,8},{10,11... | collective-permute-start | bytes 6291464 | tf_op jit(solution)/shard_map/ppermute | solution.py:17
  5.6 49.3 %collective-permute-start.1 = (bf16[2,512,1024]{2,1,0:T(8,128)(2,1)}, bf16[2,512,1024]{2,1,0:T(8,128)(2,1)S(1)}, u32[]{:S(2)}, u32[]{:S(2)}) collective-permute-start(bf16[2,512,1024]{2,1,0:T(8,128)(2,1)} %get-tuple-element.17.refs_8_.refs_3_), channel_id=1, source_target_pairs={{0,2},{1,3},{2,0},{3,1},{4,6},{5,7},{6,4},{7,5},{8,10},{9,11},{10,... | collective-permute-start | bytes 6291464 | tf_op jit(solution)/shard_map/ppermute | solution.py:17
  8.9 13.4 %collective-permute-start.2 = (bf16[64,2176]{1,0:T(8,128)(2,1)S(1)}, bf16[64,2176]{1,0:T(8,128)(2,1)S(1)}, u32[]{:S(2)}, u32[]{:S(2)}) collective-permute-start(bf16[64,2176]{1,0:T(8,128)(2,1)S(1)} %shard_map.111), channel_id=1, source_target_pairs={{0,8},{4,12},{8,0},{12,4},{16,24},{20,28},{24,16},{28,20},{1,9},{5... | collective-permute-start | bytes 835592 | tf_op jit(solution)/shard_map/ppermute | solution.py:17
  10.5 11.8 %collective-permute-start = (bf16[64,2176]{1,0:T(8,128)(2,1)S(1)}, bf16[64,2176]{1,0:T(8,128)(2,1)S(1)}, u32[]{:S(2)}, u32[]{:S(2)}) collective-permute-start(bf16[64,2176]{1,0:T(8,128)(2,1)S(1)} %shard_map.111), channel_id=1, source_target_pairs={{0,4},{4,0},{8,12},{12,8},{16,20},{20,16},{24,28},{28,24},{1,5},{5... | collective-permute-start | bytes 835592 | tf_op jit(solution)/shard_map/ppermute | solution.py:17
  12.0 16.4 %collective-permute-start.4 = (bf16[64,2176]{1,0:T(8,128)(2,1)S(1)}, bf16[64,2176]{1,0:T(8,128)(2,1)S(1)}, u32[]{:S(2)}, u32[]{:S(2)}) collective-permute-start(bf16[64,2176]{1,0:T(8,128)(2,1)S(1)} %shard_map.111), channel_id=1, source_target_pairs={{0,16},{4,20},{8,24},{12,28},{16,0},{20,4},{24,8},{28,12},{1,17},{... | collective-permute-start | bytes 835592 | tf_op jit(solution)/shard_map/ppermute | solution.py:17
  22.3 13.7 %copy-start.1 = (bf16[64,2176]{1,0:T(8,128)(2,1)}, bf16[64,2176]{1,0:T(8,128)(2,1)S(1)}, u32[]{:S(2)}) copy-start(bf16[64,2176]{1,0:T(8,128)(2,1)S(1)} %collective-permute-done.refs_1_.refs_5_) | copy-start | bytes 835588
  22.4 8.7 %collective-permute-start.3 = (bf16[64,2176]{1,0:T(8,128)(2,1)S(1)}, bf16[64,2176]{1,0:T(8,128)(2,1)S(1)}, u32[]{:S(2)}, u32[]{:S(2)}) collective-permute-start(bf16[64,2176]{1,0:T(8,128)(2,1)S(1)} %shard_map.114), channel_id=1, source_target_pairs={{0,4},{4,0},{8,12},{12,8},{16,20},{20,16},{24,28},{28,24},{1,5},{5... | collective-permute-start | bytes 835592 | tf_op jit(solution)/shard_map/ppermute | solution.py:17
  24.9 11.2 %collective-permute-start.6 = (bf16[64,2176]{1,0:T(8,128)(2,1)S(1)}, bf16[64,2176]{1,0:T(8,128)(2,1)S(1)}, u32[]{:S(2)}, u32[]{:S(2)}) collective-permute-start(bf16[64,2176]{1,0:T(8,128)(2,1)S(1)} %shard_map.111), channel_id=1, source_target_pairs={{0,24},{4,28},{8,16},{12,20},{16,8},{20,12},{24,0},{28,4},{1,25},{... | collective-permute-start | bytes 835592 | tf_op jit(solution)/shard_map/ppermute | solution.py:17
  31.0 7.3 %collective-permute-start.5 = (bf16[64,2176]{1,0:T(8,128)(2,1)S(1)}, bf16[64,2176]{1,0:T(8,128)(2,1)S(1)}, u32[]{:S(2)}, u32[]{:S(2)}) collective-permute-start(bf16[64,2176]{1,0:T(8,128)(2,1)S(1)} %shard_map.116), channel_id=1, source_target_pairs={{0,4},{4,0},{8,12},{12,8},{16,20},{20,16},{24,28},{28,24},{1,5},{5... | collective-permute-start | bytes 835592 | tf_op jit(solution)/shard_map/ppermute | solution.py:17
  32.8 67.1 %collective-permute-start.13 = (bf16[2,512,1024]{2,1,0:T(8,128)(2,1)S(1)}, bf16[2,512,1024]{2,1,0:T(8,128)(2,1)}, u32[]{:S(2)}, u32[]{:S(2)}) collective-permute-start(bf16[2,512,1024]{2,1,0:T(8,128)(2,1)S(1)} %collective-permute-done.12.refs_9_), channel_id=1, source_target_pairs={{0,2},{1,3},{2,0},{3,1},{4,6},{5,7},{6,4},{7,5},{8,10},{9,11},{10,... | collective-permute-start | bytes 6291464 | tf_op jit(solution)/shard_map/ppermute | solution.py:17
  36.0 19.8 %collective-permute-start.14 = (bf16[1,512,1024]{2,1,0:T(8,128)(2,1)}, bf16[1,512,1024]{2,1,0:T(8,128)(2,1)}, u32[]{:S(2)}, u32[]{:S(2)}) collective-permute-start(bf16[1,512,1024]{2,1,0:T(8,128)(2,1)} %shard_map.121), channel_id=1, source_target_pairs={{0,1},{1,0},{2,3},{3,2},{4,5},{5,4},{6,7},{7,6},{8,9},{9,8},{10,11... | collective-permute-start | bytes 3145736 | tf_op jit(solution)/shard_map/ppermute | solution.py:17
  38.3 7.0 %collective-permute-start.7 = (bf16[64,2176]{1,0:T(8,128)(2,1)S(1)}, bf16[64,2176]{1,0:T(8,128)(2,1)S(1)}, u32[]{:S(2)}, u32[]{:S(2)}) collective-permute-start(bf16[64,2176]{1,0:T(8,128)(2,1)S(1)} %shard_map.118), channel_id=1, source_target_pairs={{0,4},{4,0},{8,12},{12,8},{16,20},{20,16},{24,28},{28,24},{1,5},{5... | collective-permute-start | bytes 835592 | tf_op jit(solution)/shard_map/ppermute | solution.py:17
  49.5 79.3 %collective-permute-start.23 = (bf16[3,512,1024]{2,1,0:T(8,128)(2,1)}, bf16[3,512,1024]{2,1,0:T(8,128)(2,1)}, u32[]{:S(2)}, u32[]{:S(2)}) collective-permute-start(bf16[3,512,1024]{2,1,0:T(8,128)(2,1)} %shard_map.125), channel_id=1, source_target_pairs={{0,4},{4,8},{8,12},{12,16},{16,20},{20,24},{24,28},{28,0},{1,5},{5... | collective-permute-start | bytes 9437192 | tf_op jit(solution)/shard_map/ppermute | solution.py:22
  54.9 6.0 %collective-permute-start.11 = (bf16[128,2176]{1,0:T(8,128)(2,1)S(1)}, bf16[128,2176]{1,0:T(8,128)(2,1)S(1)}, u32[]{:S(2)}, u32[]{:S(2)}) collective-permute-start(bf16[128,2176]{1,0:T(8,128)(2,1)S(1)} %shard_map.119.refs_3_), channel_id=1, source_target_pairs={{0,1},{1,0},{2,3},{3,2},{4,5},{5,4},{6,7},{7,6},{8,9},{9,8},{10,11... | collective-permute-start | bytes 1671176 | tf_op jit(solution)/shard_map/ppermute | solution.py:17
  54.9 6.8 %collective-permute-start.10 = (bf16[128,2176]{1,0:T(8,128)(2,1)S(1)}, bf16[128,2176]{1,0:T(8,128)(2,1)}, u32[]{:S(2)}, u32[]{:S(2)}) collective-permute-start(bf16[128,2176]{1,0:T(8,128)(2,1)S(1)} %shard_map.117.refs_2_), channel_id=1, source_target_pairs={{0,1},{1,0},{2,3},{3,2},{4,5},{5,4},{6,7},{7,6},{8,9},{9,8},{10,11... | collective-permute-start | bytes 1671176 | tf_op jit(solution)/shard_map/ppermute | solution.py:17
  58.8 63.2 %collective-permute-start.17 = (bf16[512,1024]{1,0:T(8,128)(2,1)}, bf16[512,1024]{1,0:T(8,128)(2,1)S(1)}, u32[]{:S(2)}, u32[]{:S(2)}) collective-permute-start(bf16[512,1024]{1,0:T(8,128)(2,1)} %get-tuple-element.19.refs_0_), channel_id=1, source_target_pairs={{0,2},{1,3},{2,0},{3,1},{4,6},{5,7},{6,4},{7,5},{8,10},{9,11},{10,... | collective-permute-start | bytes 3145736 | tf_op jit(solution)/shard_map/ppermute | solution.py:17
  60.9 39.1 %copy-start = (bf16[2,512,1024]{2,1,0:T(8,128)(2,1)S(1)}, bf16[2,512,1024]{2,1,0:T(8,128)(2,1)}, u32[]{:S(2)}) copy-start(bf16[2,512,1024]{2,1,0:T(8,128)(2,1)} %get-tuple-element.17.refs_8_.refs_3_) | copy-start | bytes 6291460
  60.9 52.4 %copy-start.7 = (bf16[512,1024]{1,0:T(8,128)(2,1)S(1)}, bf16[512,1024]{1,0:T(8,128)(2,1)}, u32[]{:S(2)}) copy-start(bf16[512,1024]{1,0:T(8,128)(2,1)} %get-tuple-element.19.refs_0_) | copy-start | bytes 3145732
  61.7 2.0 %collective-permute-start.9 = (bf16[128,2176]{1,0:T(8,128)(2,1)S(1)}, bf16[128,2176]{1,0:T(8,128)(2,1)S(1)}, u32[]{:S(2)}, u32[]{:S(2)}) collective-permute-start(bf16[128,2176]{1,0:T(8,128)(2,1)S(1)} %shard_map.115.refs_1_), channel_id=1, source_target_pairs={{0,1},{1,0},{2,3},{3,2},{4,5},{5,4},{6,7},{7,6},{8,9},{9,8},{10,11... | collective-permute-start | bytes 1671176 | tf_op jit(solution)/shard_map/ppermute | solution.py:17
  61.7 2.7 %collective-permute-start.8 = (bf16[128,2176]{1,0:T(8,128)(2,1)S(1)}, bf16[128,2176]{1,0:T(8,128)(2,1)S(1)}, u32[]{:S(2)}, u32[]{:S(2)}) collective-permute-start(bf16[128,2176]{1,0:T(8,128)(2,1)S(1)} %shard_map.113.refs_0_), channel_id=1, source_target_pairs={{0,1},{1,0},{2,3},{3,2},{4,5},{5,4},{6,7},{7,6},{8,9},{9,8},{10,11... | collective-permute-start | bytes 1671176 | tf_op jit(solution)/shard_map/ppermute | solution.py:17
  116.9 8.5 %collective-permute-start.15 = (bf16[512,1024]{1,0:T(8,128)(2,1)S(1)}, bf16[512,1024]{1,0:T(8,128)(2,1)S(1)}, u32[]{:S(2)}, u32[]{:S(2)}) collective-permute-start(bf16[512,1024]{1,0:T(8,128)(2,1)S(1)} %get-tuple-element.22.refs_1_), channel_id=1, source_target_pairs={{0,1},{1,0},{2,3},{3,2},{4,5},{5,4},{6,7},{7,6},{8,9},{9,8},{10,11... | collective-permute-start | bytes 3145736 | tf_op jit(solution)/shard_map/ppermute | solution.py:17
  123.3 2.0 %collective-permute-start.18 = (bf16[512,512]{1,0:T(8,128)(2,1)S(1)}, bf16[512,512]{1,0:T(8,128)(2,1)S(1)}, u32[]{:S(2)}, u32[]{:S(2)}) collective-permute-start(bf16[512,512]{1,0:T(8,128)(2,1)S(1)} %get-tuple-element.24.refs_1_), channel_id=1, source_target_pairs={{0,1},{1,0},{2,3},{3,2},{4,5},{5,4},{6,7},{7,6},{8,9},{9,8},{10,11... | collective-permute-start | bytes 1572872 | tf_op jit(solution)/shard_map/ppermute | solution.py:17
  123.4 25.8 %collective-permute-start.22 = (bf16[512,1024]{1,0:T(8,128)(2,1)}, bf16[512,1024]{1,0:T(8,128)(2,1)S(1)}, u32[]{:S(2)}, u32[]{:S(2)}) collective-permute-start(bf16[512,1024]{1,0:T(8,128)(2,1)} %get-tuple-element.20.refs_1_), channel_id=1, source_target_pairs={{0,2},{1,3},{2,0},{3,1},{4,6},{5,7},{6,4},{7,5},{8,10},{9,11},{10,... | collective-permute-start | bytes 3145736 | tf_op jit(solution)/shard_map/ppermute | solution.py:17
  125.9 19.8 %collective-permute-start.16 = (bf16[2,128,1024]{2,1,0:T(8,128)(2,1)S(1)}, bf16[2,128,1024]{2,1,0:T(8,128)(2,1)S(1)}, u32[]{:S(2)}, u32[]{:S(2)}) collective-permute-start(bf16[2,128,1024]{2,1,0:T(8,128)(2,1)S(1)} %fusion.3), channel_id=1, source_target_pairs={{0,8},{4,12},{8,0},{12,4},{16,24},{20,28},{24,16},{28,20},{1,9},{5... | collective-permute-start | bytes 1572872 | tf_op jit(solution)/shard_map/ppermute | solution.py:17
  128.5 17.1 %collective-permute-start.19 = (bf16[2,128,512]{2,1,0:T(8,128)(2,1)}, bf16[2,128,512]{2,1,0:T(8,128)(2,1)S(1)}, u32[]{:S(2)}, u32[]{:S(2)}) collective-permute-start(bf16[2,128,512]{2,1,0:T(8,128)(2,1)} %fusion.9), channel_id=1, source_target_pairs={{0,8},{4,12},{8,0},{12,4},{16,24},{20,28},{24,16},{28,20},{1,9},{5... | collective-permute-start | bytes 786440 | tf_op jit(solution)/shard_map/ppermute | solution.py:17
  134.9 14.3 %copy-start.6 = (bf16[2,512,1024]{2,1,0:T(8,128)(2,1)S(1)}, bf16[2,512,1024]{2,1,0:T(8,128)(2,1)}, u32[]{:S(2)}) copy-start(bf16[2,512,1024]{2,1,0:T(8,128)(2,1)} %get-tuple-element.14.refs_2_) | copy-start | bytes 6291460
  150.5 2.1 %collective-permute-start.24 = (bf16[512,512]{1,0:T(8,128)(2,1)S(1)}, bf16[512,512]{1,0:T(8,128)(2,1)S(1)}, u32[]{:S(2)}, u32[]{:S(2)}) collective-permute-start(bf16[512,512]{1,0:T(8,128)(2,1)S(1)} %get-tuple-element.27), channel_id=1, source_target_pairs={{0,1},{1,0},{2,3},{3,2},{4,5},{5,4},{6,7},{7,6},{8,9},{9,8},{10,11... | collective-permute-start | bytes 1572872 | tf_op jit(solution)/shard_map/ppermute | solution.py:17
  150.7 11.6 %collective-permute-start.20 = (bf16[2,64,1536]{2,1,0:T(8,128)(2,1)S(1)}, bf16[2,64,1536]{2,1,0:T(8,128)(2,1)S(1)}, u32[]{:S(2)}, u32[]{:S(2)}) collective-permute-start(bf16[2,64,1536]{2,1,0:T(8,128)(2,1)S(1)} %fusion.6), channel_id=1, source_target_pairs={{0,4},{4,0},{8,12},{12,8},{16,20},{20,16},{24,28},{28,24},{1,5},{5... | collective-permute-start | bytes 1179656 | tf_op jit(solution)/shard_map/ppermute | solution.py:17
  152.7 9.7 %collective-permute-start.25 = (bf16[2,128,512]{2,1,0:T(8,128)(2,1)S(1)}, bf16[2,128,512]{2,1,0:T(8,128)(2,1)S(1)}, u32[]{:S(2)}, u32[]{:S(2)}) collective-permute-start(bf16[2,128,512]{2,1,0:T(8,128)(2,1)S(1)} %fusion.10), channel_id=1, source_target_pairs={{0,8},{4,12},{8,0},{12,4},{16,24},{20,28},{24,16},{28,20},{1,9},{5... | collective-permute-start | bytes 786440 | tf_op jit(solution)/shard_map/ppermute | solution.py:17
  162.5 5.2 %collective-permute-start.26 = (bf16[2,64,512]{2,1,0:T(8,128)(2,1)S(1)}, bf16[2,64,512]{2,1,0:T(8,128)(2,1)S(1)}, u32[]{:S(2)}, u32[]{:S(2)}) collective-permute-start(bf16[2,64,512]{2,1,0:T(8,128)(2,1)S(1)} %fusion.15), channel_id=1, source_target_pairs={{0,4},{4,0},{8,12},{12,8},{16,20},{20,16},{24,28},{28,24},{1,5},{5... | collective-permute-start | bytes 393224 | tf_op jit(solution)/shard_map/ppermute | solution.py:17
  164.4 13.5 %collective-permute-start.21 = (bf16[1,64,1536]{2,1,0:T(8,128)(2,1)S(1)}, bf16[1,64,1536]{2,1,0:T(8,128)(2,1)S(1)}, u32[]{:S(2)}, u32[]{:S(2)}) collective-permute-start(bf16[1,64,1536]{2,1,0:T(8,128)(2,1)S(1)} %fusion.14), channel_id=1, source_target_pairs={{0,16},{4,20},{8,24},{12,28},{16,0},{20,4},{24,8},{28,12},{1,17},{... | collective-permute-start | bytes 589832 | tf_op jit(solution)/shard_map/ppermute | solution.py:17
  167.8 10.8 %collective-permute-start.27 = (bf16[1,64,512]{2,1,0:T(8,128)(2,1)S(1)}, bf16[1,64,512]{2,1,0:T(8,128)(2,1)S(1)}, u32[]{:S(2)}, u32[]{:S(2)}) collective-permute-start(bf16[1,64,512]{2,1,0:T(8,128)(2,1)S(1)} %fusion.19), channel_id=1, source_target_pairs={{0,16},{4,20},{8,24},{12,28},{16,0},{20,4},{24,8},{28,12},{1,17},{... | collective-permute-start | bytes 196616 | tf_op jit(solution)/shard_map/ppermute | solution.py:17
  (11 other events, 51.6 us)
